TPU v7x, 32 devices: a whole 2x2x4 slice. The times are simulated.
32 devices in a mesh: groups: 2 (over y), expert: 4 (over x, core), section: 4 (over z).
Axes of the slice: x: 2, y: 2, z: 4, core: 2. Of those that a mesh axis runs over, the one named last changes fastest.
Arguments:
- prompts: bfloat16 [32, 128, 3584], P(('groups', 'expert', 'section')), parts along dimension 0, may hold values from -6 to 6
- owners: int32 [32], P('groups'), parts along dimension 0, may hold values from 0 to 3, as said below
- lengths: int32 [32], P('groups'), parts along dimension 0, may hold values from 1 to 128, 1024 in all
- residual: bfloat16 [2, 32, 3584], P(None, ('groups', 'expert')), parts along dimension 1, may hold values from -6 to 6
- queries: bfloat16 [2, 32, 64, 192], P(None, ('groups', 'expert'), 'section'), parts along dimension 1, may hold values from -170 to 170
- expert_ids: int32 [2, 32, 8], P(None, ('groups', 'expert')), parts along dimension 1, may hold values from 0 to 15, all different within a row; in each aligned block of 4 rows (0 to 3, 4 to 7, ..., all dimensions but the last counted through in order) at most 3 rows name the same one
- route_scores: float32 [2, 32, 8], P(None, ('groups', 'expert')), parts along dimension 1, may hold values from 0.02 to 1
- attn_gain: bfloat16 [3584], replicated, may hold values from 0.25 to 1.75
- w_dkv: bfloat16 [3584, 576], P('section'), may hold values from -0.09375 to 0.09375
- kv_gain: bfloat16 [512], replicated, may hold values from 0.25 to 1.75
- w_uk: bfloat16 [64, 128, 512], P('section', None, 'expert'), may hold values from -0.5 to 0.5
- w_uv: bfloat16 [64, 128, 512], P('section', None, 'expert'), may hold values from -0.25 to 0.25
- w_o: bfloat16 [8192, 3584], P('section', 'expert'), may hold values from -0.0625 to 0.0625
- moe_gain: bfloat16 [3584], replicated, may hold values from 0.25 to 1.75
- w_gate: bfloat16 [16, 3584, 1024], P('expert', None, 'section'), may hold values from -0.09375 to 0.09375
- w_up: bfloat16 [16, 3584, 1024], P('expert', None, 'section'), may hold values from -0.09375 to 0.09375
- w_down: bfloat16 [16, 1024, 3584], P('expert', 'section'), may hold values from -0.1875 to 0.1875
Outputs:
- layer_out: bfloat16 [2, 32, 3584], P(None, ('groups', 'expert'), 'section'), parts along dimension 1
There are 2 independent parts, one for each index of `groups`. A program takes and returns all parts, laid end to end along the dimension named above; an argument that names none is the same for every part. Nothing has to cross between parts.
Inputs may be any that keep to these rules, and one draw needn't show every extreme that they name: `owners`: requests j * 4 to j * 4 + 3 name every owner exactly once. `expert_ids`: each token names 8 different experts; within one step the 4 tokens of one owner name one expert at most 3 times.
All inputs are finite; a program needn't handle non-finite values.
Results may differ from a plain program's by a relative error of at most 0.012.
The roundings to bfloat16 on the way count: a program that leaves them out, or rounds other values in their place, can miss the bound.
Values may be sent and summed in bfloat16 or wider, within the bound.
No kernel may reach another device: no remote copies, remote signals or barrier semaphores. Data moves between devices by JAX's collectives and lax.ppermute only.
A program may use at most 192 MiB of HBM per device.

v0:
```python
import jax
import jax.numpy as jnp
from jax import lax
from jax.sharding import PartitionSpec as P

epsilon = 1e-06
masked_value = -1e30
route_scale = 2.5


def rotate_pairs(values, position):
    halfway = values.shape[-1] // 2
    frequency = 10000.0 ** (-2.0 * jnp.arange(halfway).astype(jnp.float32) / values.shape[-1])
    angles = position.astype(jnp.float32)[..., None] * frequency
    cosine = jnp.cos(angles)
    sine_part = jnp.sin(angles)
    first_half = values[..., :halfway]
    second_half = values[..., halfway:]
    return jnp.concatenate(
        [
            first_half * cosine - second_half * sine_part,
            second_half * cosine + first_half * sine_part,
        ],
        axis=-1,
    )


def rms_scaled(values, gain):
    return (
        values
        * lax.rsqrt(jnp.mean(values * values, axis=-1, keepdims=True) + epsilon)
        * gain.astype(jnp.float32)
    )


def latent_rows(projected, kv_gain, position):
    gain_width = kv_gain.shape[0]
    scaled = rms_scaled(projected[..., :gain_width], kv_gain)
    return jnp.concatenate(
        [scaled, rotate_pairs(projected[..., gain_width:], position)], axis=-1
    ).astype(jnp.bfloat16)


def key_scores(query_cat, latent_cache, recent, cache_pos, token_len, recent_live, score_scale):
    prompt_scores = (
        jnp.einsum("rhc,rpc->rhp", query_cat, latent_cache, preferred_element_type=jnp.float32)
        * score_scale
    )
    prompt_scores = jnp.where(
        cache_pos[None, None, :] < token_len[:, None, None], prompt_scores, masked_value
    )
    recent_scores = (
        jnp.einsum("rhc,rtc->rht", query_cat, recent, preferred_element_type=jnp.float32)
        * score_scale
    )
    recent_scores = jnp.where(recent_live[None, None, :], recent_scores, masked_value)
    return (prompt_scores, recent_scores)


def weighted_latent(prompt_prob, recent_prob, latent_cache, recent, latent_width):
    first_term = jnp.einsum(
        "rhp,rpc->rhc",
        prompt_prob,
        latent_cache[..., :latent_width],
        preferred_element_type=jnp.float32,
    )
    second_term = jnp.einsum(
        "rht,rtc->rhc", recent_prob, recent[..., :latent_width], preferred_element_type=jnp.float32
    )
    return first_term + second_term


def local(
    prompts,
    owners,
    lengths,
    residual,
    queries,
    expert_ids,
    route_scores,
    attn_gain,
    w_dkv,
    kv_gain,
    w_uk,
    w_uv,
    w_o,
    moe_gain,
    w_gate,
    w_up,
    w_down,
):
    expert_rank = lax.axis_index("expert")
    section_rank = lax.axis_index("section")
    expert_count = lax.axis_size("expert")
    section_count = lax.axis_size("section")
    prompt_count, full_length, model_width = prompts.shape
    requests_here = residual.shape[1]
    latent_width = kv_gain.shape[0]
    nope_width = w_uk.shape[1]
    full_dkv = lax.all_gather(w_dkv, "section", axis=0, tiled=True)
    projected = jnp.dot(
        prompts.reshape(-1, model_width), full_dkv, preferred_element_type=jnp.float32
    )
    projected = projected.reshape(prompt_count, full_length, -1)
    whole_pos = jnp.arange(full_length)
    whole_rows = latent_rows(projected, kv_gain, whole_pos[None, :])
    cache_rows = lax.all_to_all(whole_rows, "section", split_axis=1, concat_axis=0, tiled=True)
    my_owners = lax.dynamic_slice_in_dim(owners, expert_rank * requests_here, requests_here)
    sending = jnp.take(cache_rows, jnp.argsort(my_owners), axis=0)
    landed = lax.all_to_all(sending, "expert", split_axis=0, concat_axis=0, tiled=True)
    owner_table = owners.reshape(expert_count, requests_here)
    length_table = lengths.reshape(expert_count, requests_here)
    token_len = jnp.sum(jnp.where(owner_table == expert_rank, length_table, 0), axis=1)
    latent_cache = lax.all_gather(landed, "section", axis=1, tiled=True)
    uk_full, uv_full = (
        lax.all_gather(w_uk, "expert", axis=2, tiled=True),
        lax.all_gather(w_uv, "expert", axis=2, tiled=True),
    )
    steps_total = residual.shape[0]
    recent = jnp.zeros((requests_here, steps_total, latent_cache.shape[-1]), jnp.bfloat16)
    recent_pos = jnp.arange(steps_total)
    score_scale = queries.shape[-1] ** (-0.5)
    expert_local = w_gate.shape[0]
    expert_total = expert_local * expert_count
    capacity = 3 * requests_here // 4
    column_width = model_width // section_count
    expert_range = jnp.arange(expert_total)
    slot_range = jnp.arange(capacity).astype(jnp.float32)
    outputs = []
    for step_index in range(steps_total):
        hidden = residual[step_index].astype(jnp.float32)
        normed = rms_scaled(hidden, attn_gain).astype(jnp.bfloat16)
        fresh_latent = latent_rows(
            jnp.dot(normed, full_dkv, preferred_element_type=jnp.float32),
            kv_gain,
            token_len + step_index,
        )
        recent = recent.at[:, step_index].set(fresh_latent)
        query_now = queries[step_index]
        query_latent = jnp.einsum(
            "rhn,hnc->rhc", query_now[..., :nope_width], uk_full, preferred_element_type=jnp.float32
        )
        query_rot = rotate_pairs(
            query_now[..., nope_width:].astype(jnp.float32), (token_len + step_index)[:, None]
        )
        query_cat = jnp.concatenate([query_latent, query_rot], axis=-1).astype(jnp.bfloat16)
        recent_live = recent_pos <= step_index
        cache_pos = jnp.arange(latent_cache.shape[1])
        prompt_scores, recent_scores = key_scores(
            query_cat, latent_cache, recent, cache_pos, token_len, recent_live, score_scale
        )
        maxima = jnp.maximum(prompt_scores.max(axis=-1), recent_scores.max(axis=-1))[..., None]
        prompt_exp = jnp.exp(prompt_scores - maxima)
        recent_exp = jnp.exp(recent_scores - maxima)
        totals = prompt_exp.sum(axis=-1, keepdims=True) + recent_exp.sum(axis=-1, keepdims=True)
        prompt_prob = (prompt_exp / totals).astype(jnp.bfloat16)
        recent_prob = (recent_exp / totals).astype(jnp.bfloat16)
        out_latent = weighted_latent(
            prompt_prob, recent_prob, latent_cache, recent, latent_width
        ).astype(jnp.bfloat16)
        head_values = jnp.einsum(
            "rhc,hvc->rhv", out_latent, uv_full, preferred_element_type=jnp.float32
        )
        head_values = head_values.astype(jnp.bfloat16).reshape(requests_here, -1)
        partial_out = jnp.dot(
            lax.all_gather(head_values, "expert", axis=0, tiled=True),
            w_o,
            preferred_element_type=jnp.float32,
        )
        exchanged = lax.all_to_all(partial_out, "expert", split_axis=0, concat_axis=1, tiled=True)
        attended = lax.psum(exchanged, "section")
        mixed = hidden + attended
        moe_in = rms_scaled(mixed, moe_gain).astype(jnp.bfloat16)
        match_table = (expert_ids[step_index][:, :, None] == expert_range[None, None, :]).astype(
            jnp.float32
        )
        member = match_table.sum(axis=1)
        scores_now = route_scores[step_index]
        weights = route_scale * scores_now / jnp.sum(scores_now, axis=-1, keepdims=True)
        weight_map = jnp.einsum("rk,rke->re", weights, match_table)
        slot_rank = jnp.cumsum(member, axis=0) - member
        slot_map = member[None] * (slot_rank[None] == slot_range[:, None, None]).astype(jnp.float32)
        buffer = jnp.einsum(
            "cte,td->ecd", slot_map.astype(jnp.bfloat16), moe_in, preferred_element_type=jnp.float32
        )
        buffer = buffer.astype(jnp.bfloat16).reshape(
            expert_count, expert_local, capacity, model_width
        )
        arrived = lax.all_to_all(buffer, "expert", split_axis=0, concat_axis=0, tiled=True)
        gate_part = jnp.einsum(
            "oxcd,xdf->oxcf", arrived, w_gate, preferred_element_type=jnp.float32
        )
        up_part = jnp.einsum("oxcd,xdf->oxcf", arrived, w_up, preferred_element_type=jnp.float32)
        activated = (jax.nn.silu(gate_part) * up_part).astype(jnp.bfloat16)
        partial_units = jnp.einsum(
            "oxcf,xfd->oxcd", activated, w_down, preferred_element_type=jnp.float32
        )
        summed = lax.psum_scatter(partial_units, "section", scatter_dimension=3, tiled=True).astype(
            jnp.bfloat16
        )
        returned = lax.all_to_all(
            summed, "expert", split_axis=0, concat_axis=0, tiled=True
        ).reshape(expert_total, capacity, -1)
        combined = jnp.einsum(
            "cte,ecd->td", slot_map * weight_map[None], returned.astype(jnp.float32)
        )
        own_mixed = lax.dynamic_slice_in_dim(mixed, section_rank * column_width, column_width, 1)
        outputs.append((own_mixed + combined).astype(jnp.bfloat16))
    return jnp.stack(outputs)


def solution(mesh):
    placed = (
        P(("groups", "expert", "section"), None, None),
        P("groups"),
        P("groups"),
        P(None, ("groups", "expert"), None),
        P(None, ("groups", "expert"), "section", None),
        P(None, ("groups", "expert"), None),
        P(None, ("groups", "expert"), None),
        P(),
        P("section", None),
        P(),
        P("section", None, "expert"),
        P("section", None, "expert"),
        P("section", "expert"),
        P(),
        P("expert", None, "section"),
        P("expert", None, "section"),
        P("expert", "section", None),
    )
    return jax.shard_map(
        local,
        mesh=mesh,
        in_specs=placed,
        out_specs=P(None, ("groups", "expert"), "section"),
        check_vma=False,
    )
```

profile of v0, /device:TPU:0, one launch (start us, length us, event | category | flops | bytes accessed | tf_op | source)
XLA Modules:
  0.0 438.1 jit_solution(14945170909277291244)
XLA Ops:
  15.2 19.4 %all-gather.6.cloned.1.call-done = bf16[16,128,512]{2,1,0:T(8,128)(2,1)} async-done(((bf16[16,128,128]{2,1,0:T(8,128)(2,1)}), bf16[16,128,512]{2,1,0:T(8,128)(2,1)}) %all-gather.6.cloned.1.call-update) | async-done | bytes 2097168 | tf_op jit(solution)/shard_map/all_gather | solution.py:116
  38.5 77.4 %all-gather.8.cloned.1.call-done = bf16[3584,576]{0,1:T(8,128)(2,1)} async-done(((bf16[896,576]{0,1:T(8,128)(2,1)}), bf16[3584,576]{0,1:T(8,128)(2,1)}) %all-gather.8.cloned.1.call-update) | async-done | bytes 4128784 | tf_op jit(solution)/shard_map/all_gather | solution.py:100
  129.9 5.5 %all-to-all-done = bf16[4,2,9216]{2,1,0:T(2,128)(2,1)S(1)} async-done(((bf16[4,2,9216]{2,1,0:T(2,128)(2,1)}), bf16[4,2,9216]{2,1,0:T(2,128)(2,1)S(1)}, u32[]{:S(2)}, u32[]{:S(2)}) %all-to-all-start) | async-done | bytes 147488 | tf_op jit(solution)/shard_map/all_to_all | solution.py:107
  140.6 4.8 %all-to-all-done.1 = bf16[4,32,576]{2,1,0:T(8,128)(2,1)S(1)} async-done(((bf16[4,32,576]{2,1,0:T(8,128)(2,1)}), bf16[4,32,576]{2,1,0:T(8,128)(2,1)S(1)}, u32[]{:S(2)}, u32[]{:S(2)}) %all-to-all-start.1) | async-done | bytes 147488 | tf_op jit(solution)/shard_map/all_to_all | solution.py:110
  145.4 16.2 %all_gather.20 = bf16[4,128,576]{2,1,0:T(8,128)(2,1)S(1)} all-gather(bf16[4,32,576]{2,1,0:T(8,128)(2,1)S(1)} %all-to-all-done.1), channel_id=1, replica_groups=mesh['groups'=2,'expert'=4,'section'=4] {'section'}, dimensions={1}, use_global_device_ids=true | all-gather | bytes 737280 | tf_op jit(solution)/shard_map/all_gather | solution.py:114
  165.5 5.2 %all-gather = bf16[4,4,2048]{2,1,0:T(4,128)(2,1)S(1)} all-gather(bf16[1,4,2048]{2,1,0:T(4,128)(2,1)S(1)} %fusion.51), channel_id=1, replica_groups=mesh['groups'=2,'expert'=4,'section'=4] {'expert'}, dimensions={0}, use_global_device_ids=true | all-gather | bytes 81920 | tf_op jit(solution)/shard_map/all_gather | solution.py:166
  178.7 5.3 %all-gather.1 = bf16[4,4,2048]{2,1,0:T(4,128)(2,1)S(1)} all-gather(bf16[1,4,2048]{2,1,0:T(4,128)(2,1)S(1)} %fusion.50), channel_id=1, replica_groups=mesh['groups'=2,'expert'=4,'section'=4] {'expert'}, dimensions={0}, use_global_device_ids=true | all-gather | bytes 81920 | tf_op jit(solution)/shard_map/all_gather | solution.py:166
  190.7 3.9 all-to-all-done.5
  195.5 32.5 %all-reduce.4.cloned.1.call-done = (f32[4,3584]{1,0:T(4,128)}, f32[4,3584]{1,0:T(4,128)}) async-done(((f32[4,3584]{1,0:T(4,128)}, f32[4,3584]{1,0:T(4,128)}), (f32[4,3584]{1,0:T(4,128)}, f32[4,3584]{1,0:T(4,128)})) %all-reduce.4.cloned.1.call-update) | async-done | bytes 114704 | tf_op jit(solution)/shard_map/psum | solution.py:171
  235.1 5.5 %all-to-all-done.3 = bf16[4,4,3,3584]{3,1,2,0:T(4,128)(2,1)S(1)} async-done(((bf16[4,4,3,3584]{3,1,2,0:T(4,128)(2,1)}), bf16[4,4,3,3584]{3,1,2,0:T(4,128)(2,1)S(1)}, u32[]{:S(2)}, u32[]{:S(2)}) %all-to-all-start.3) | async-done | bytes 344096 | tf_op jit(solution)/shard_map/all_to_all | solution.py:189
  244.3 4.2 fusion.24
  248.5 7.2 %fusion.12 = f32[4,4,3,3584]{3,0,2,1:T(4,128)S(1)} fusion(bf16[4,256,3584]{2,1,0:T(8,128)(2,1)} %param.37, bf16[4,3584,256]{2,1,0:T(8,128)(2,1)} %param.36, bf16[4,4,3,3584]{3,1,2,0:T(4,128)(2,1)S(1)} %all-to-all-done.3, f32[4,4,3,256]{3,0,2,1:T(4,128)S(1)} %fusion.24), kind=kOutput, calls=%fused_computation.13 | convolution fusion | flops 176234496 | bytes 15761408 | tf_op jit(solution)/shard_map/oxcf,xfd->oxcd/dot_general | solution.py:195
  255.7 19.4 %copy.121 = f32[4,4,3,3584]{0,2,1,3:T(4,128)} copy(f32[4,4,3,3584]{3,0,2,1:T(4,128)S(1)} %fusion.12) | data formatting | bytes 1376256
  275.2 31.7 %reshape.645 = f32[3584,48]{1,0:T(8,128)} reshape(f32[3584,4,3,4]{3,2,1,0:T(4,128)} %bitcast.210) | data formatting | bytes 1376256
  306.9 4.2 fusion.27
  311.1 7.6 %fusion.15 = f32[4,4,3,3584]{3,0,2,1:T(4,128)S(1)} fusion(bf16[4,256,3584]{2,1,0:T(8,128)(2,1)} %param.37, bf16[4,3584,256]{2,1,0:T(8,128)(2,1)} %param.36, bf16[4,4,3,3584]{3,1,2,0:T(4,128)(2,1)S(1)} %all-to-all-done.6, f32[4,4,3,256]{3,0,2,1:T(4,128)S(1)} %fusion.27), kind=kOutput, calls=%fused_computation.14 | convolution fusion | flops 176234496 | bytes 15761408 | tf_op jit(solution)/shard_map/oxcf,xfd->oxcd/dot_general | solution.py:195
  318.7 19.4 %copy.123 = f32[4,4,3,3584]{0,2,1,3:T(4,128)} copy(f32[4,4,3,3584]{3,0,2,1:T(4,128)S(1)} %fusion.15) | data formatting | bytes 1376256
  338.1 31.7 %reshape.647 = f32[3584,48]{1,0:T(8,128)} reshape(f32[3584,4,3,4]{3,2,1,0:T(4,128)} %bitcast.211) | data formatting | bytes 1376256
  370.1 6.4 %reshape.646 = bf16[896,4,3,4]{3,2,1,0:T(4,128)(2,1)} reshape(f32[896,48]{1,0:T(8,128)} %reduce-scatter.7.cloned.1.call-done) | data formatting | bytes 258048
  376.5 5.7 %copy.122 = bf16[4,4,3,896]{3,0,2,1:T(4,128)(2,1)S(1)} copy(bf16[4,4,3,896]{0,2,1,3:T(4,128)(2,1)} %bitcast.212) | data formatting | bytes 172032
  386.4 23.4 %reduce-scatter.9.cloned.1.call-done = f32[896,48]{1,0:T(8,128)} async-done(((f32[3584,48]{1,0:T(8,128)}), f32[896,48]{1,0:T(8,128)}) %reduce-scatter.9.cloned.1.call-update) | async-done | bytes 172048
  409.8 6.4 %reshape.648 = bf16[896,4,3,4]{3,2,1,0:T(4,128)(2,1)} reshape(f32[896,48]{1,0:T(8,128)} %reduce-scatter.9.cloned.1.call-done) | data formatting | bytes 258048
  416.1 5.7 %copy.124 = bf16[4,4,3,896]{3,0,2,1:T(4,128)(2,1)S(1)} copy(bf16[4,4,3,896]{0,2,1,3:T(4,128)(2,1)} %bitcast.213) | data formatting | bytes 172032
  426.1 3.9 all-to-all-done.7
  (152 shorter events, 71.5 us)
Async XLA Ops:
  6.5 114.3 %copy-start = (bf16[1,128,3584]{2,1,0:T(8,128)(2,1)S(1)}, bf16[1,128,3584]{2,1,0:T(8,128)(2,1)}, u32[]{:S(2)}) copy-start(bf16[1,128,3584]{2,1,0:T(8,128)(2,1)} %param.21) | copy-start | bytes 2752516
  6.5 109.3 %copy-start.4 = (bf16[2,4,3584]{2,1,0:T(4,128)(2,1)S(1)}, bf16[2,4,3584]{2,1,0:T(4,128)(2,1)}, u32[]{:S(2)}) copy-start(bf16[2,4,3584]{2,1,0:T(4,128)(2,1)} %param.24) | copy-start | bytes 172036
  6.5 28.0 %all-gather.6.cloned.1.call-start = ((), (), s32[]{:S(2)}) async-start(), calls=%async_computation.10 | async-start | bytes 2621440 | tf_op jit(solution)/shard_map/all_gather | solution.py:116
  7.3 108.6 %all-gather.8.cloned.1.call-start = ((), (), s32[]{:S(2)}) async-start(), calls=%async_computation.11 | async-start | bytes 5160960 | tf_op jit(solution)/shard_map/all_gather | solution.py:100
  8.0 155.1 %all-gather.10.cloned.1.call-start = ((), (), s32[]{:S(2)}) async-start(), calls=%async_computation.12 | async-start | bytes 2621440 | tf_op jit(solution)/shard_map/all_gather | solution.py:117
  115.8 3.6 copy-start.2
  125.8 9.7 %all-to-all-start = ((bf16[4,2,9216]{2,1,0:T(2,128)(2,1)}), bf16[4,2,9216]{2,1,0:T(2,128)(2,1)S(1)}, u32[]{:S(2)}, u32[]{:S(2)}) async-start(bf16[4,2,9216]{2,1,0:T(2,128)(2,1)} %reshape.649), calls=%async_computation | async-start | bytes 294912 | tf_op jit(solution)/shard_map/all_to_all | solution.py:107
  137.1 8.3 %all-to-all-start.1 = ((bf16[4,32,576]{2,1,0:T(8,128)(2,1)}), bf16[4,32,576]{2,1,0:T(8,128)(2,1)S(1)}, u32[]{:S(2)}, u32[]{:S(2)}) async-start(bf16[4,32,576]{2,1,0:T(8,128)(2,1)} %broadcast_select_fusion), calls=%async_computation.1 | async-start | bytes 327680 | tf_op jit(solution)/shard_map/all_to_all | solution.py:110
  163.1 14.9 %copy-start.3 = (bf16[16,128,512]{2,1,0:T(8,128)(2,1)S(1)}, bf16[16,128,512]{2,1,0:T(8,128)(2,1)}, u32[]{:S(2)}) copy-start(bf16[16,128,512]{2,1,0:T(8,128)(2,1)} %all-gather.10.cloned.1.call-done) | copy-start | bytes 6291460
  173.4 22.0 %copy-start.8 = (bf16[3584]{0:T(1024)(128)(2,1)S(1)}, bf16[3584]{0:T(1024)(128)(2,1)}, u32[]{:S(2)}) copy-start(bf16[3584]{0:T(1024)(128)(2,1)} %param.34) | copy-start | bytes 21508
  174.1 13.2 %all-to-all-start.2 = ((f32[4,4,896]{2,1,0:T(4,128)}), f32[4,4,896]{2,1,0:T(4,128)S(1)}, u32[]{:S(2)}, u32[]{:S(2)}) async-start(f32[4,4,896]{2,1,0:T(4,128)} %all_to_all.55), calls=%async_computation.2 | async-start | bytes 114688 | tf_op jit(solution)/shard_map/all_to_all | solution.py:170
  187.3 7.3 %copy-start.5 = (f32[4,4,896]{2,1,0:T(4,128)}, f32[4,4,896]{2,1,0:T(4,128)S(1)}, u32[]{:S(2)}) copy-start(f32[4,4,896]{2,1,0:T(4,128)S(1)} %all-to-all-done.2) | copy-start | bytes 172036
  187.3 7.3 %all-to-all-start.5 = ((f32[4,4,896]{2,1,0:T(4,128)}), f32[4,4,896]{2,1,0:T(4,128)S(1)}, u32[]{:S(2)}, u32[]{:S(2)}) async-start(f32[4,4,896]{2,1,0:T(4,128)} %all_to_all.61), calls=%async_computation.5 | async-start | bytes 114688 | tf_op jit(solution)/shard_map/all_to_all | solution.py:170
  190.6 37.3 %all-reduce.4.cloned.1.call-start = ((), (), s32[]{:S(2)}) async-start(), calls=%async_computation.15 | async-start | bytes 229376 | tf_op jit(solution)/shard_map/psum | solution.py:171
  194.6 0.6 copy-start.6
  230.3 10.3 %all-to-all-start.3 = ((bf16[4,4,3,3584]{3,1,2,0:T(4,128)(2,1)}), bf16[4,4,3,3584]{3,1,2,0:T(4,128)(2,1)S(1)}, u32[]{:S(2)}, u32[]{:S(2)}) async-start(bf16[4,4,3,3584]{3,1,2,0:T(4,128)(2,1)} %copy.98), calls=%async_computation.3 | async-start | bytes 688128 | tf_op jit(solution)/shard_map/all_to_all | solution.py:189
  240.6 66.3 %all-to-all-start.6 = ((bf16[4,4,3,3584]{3,1,2,0:T(4,128)(2,1)}), bf16[4,4,3,3584]{3,1,2,0:T(4,128)(2,1)S(1)}, u32[]{:S(2)}, u32[]{:S(2)}) async-start(bf16[4,4,3,3584]{3,1,2,0:T(4,128)(2,1)} %copy.109), calls=%async_computation.6 | async-start | bytes 688128 | tf_op jit(solution)/shard_map/all_to_all | solution.py:189
  244.1 126.0 %reduce-scatter.7.cloned.1.call-start = ((), (), s32[]{:S(2)}) async-start(), calls=%async_computation.13 | async-start | bytes 2293760
  306.9 102.9 %reduce-scatter.9.cloned.1.call-start = ((), (), s32[]{:S(2)}) async-start(), calls=%async_computation.14 | async-start | bytes 2293760
  338.1 31.8 %copy-start.7 = (f32[2,4,8]{2,1,0:T(4,128)S(1)}, f32[2,4,8]{2,1,0:T(4,128)}, u32[]{:S(2)}) copy-start(f32[2,4,8]{2,1,0:T(4,128)} %param.27) | copy-start | bytes 772
  382.9 39.6 %all-to-all-start.4 = ((bf16[4,4,3,896]{3,1,2,0:T(4,128)(2,1)}), bf16[4,4,3,896]{3,1,2,0:T(4,128)(2,1)S(1)}, u32[]{:S(2)}, u32[]{:S(2)}) async-start(bf16[4,4,3,896]{3,1,2,0:T(4,128)(2,1)} %copy.101), calls=%async_computation.4 | async-start | bytes 172032 | tf_op jit(solution)/shard_map/all_to_all | solution.py:201
  386.2 45.1 %copy-start.1 = (bf16[1,128,3584]{2,1,0:T(8,128)(2,1)S(1)}, bf16[1,128,3584]{2,1,0:T(8,128)(2,1)}, u32[]{:S(2)}) copy-start(bf16[1,128,3584]{2,1,0:T(8,128)(2,1)} %param.21) | copy-start | bytes 2752516
  422.5 7.5 %all-to-all-start.7 = ((bf16[4,4,3,896]{3,1,2,0:T(4,128)(2,1)}), bf16[4,4,3,896]{3,1,2,0:T(4,128)(2,1)S(1)}, u32[]{:S(2)}, u32[]{:S(2)}) async-start(bf16[4,4,3,896]{3,1,2,0:T(4,128)(2,1)} %copy.112), calls=%async_computation.7 | async-start | bytes 172032 | tf_op jit(solution)/shard_map/all_to_all | solution.py:201
Sparse Core Ops, SparseCore 0:
  8.9 25.5 all-gather.5
  36.1 79.6 all-gather.7
  117.4 21.3 all-gather.9
  195.4 32.4 all-reduce.3
  307.0 39.6 reduce-scatter.6
  370.0 39.7 reduce-scatter.8
where the time goes:
time: 442 us; the launch traced here: 438 us
  waiting for transfers between devices  178 us (40%)
  local copies, waits for them, and re-layouts  137 us (31%)
  matrix products  45 us (10%)
  starting transfers between devices  27.1 us (6%)
  blocking collectives  26.8 us (6%)
  between operations  13.9 us (3%)
  other arithmetic  10.3 us (2%)
    unnamed x32, local copies, waits for them, and re-layouts  129 us
    all_gather x1, waiting for transfers between devices, local(): full_dkv = lax.all_gather(w_dkv, 'section', axis=0, tiled=True)  77.4 us
    psum x1, waiting for transfers between devices, local(): attended = lax.psum(exchanged, 'section')  32.5 us
    unnamed x8, waiting for transfers between devices  25.5 us
    all_gather x1, waiting for transfers between devices, local(): lax.all_gather(w_uk, 'expert', axis=2, tiled=True)  19.4 us
    all_gather x1, blocking collectives, local(): latent_cache = lax.all_gather(landed, 'section', axis=1, tiled=True)  16.2 us
    dot_general x2, matrix products, local(): jnp.einsum('oxcf,xfd->oxcd', activated, w_down, preferred_element_type=jn...  14.8 us
    all_gather x2, blocking collectives, local(): lax.all_gather(head_values, 'expert', axis=0, tiled=True)  10.6 us
  transfers between devices with their start and end apart: 14, of which 9 were waited for; matrix products, arithmetic and copies ran while one was open for 41% of the time, Pallas kernels for 0%

commit v1 on v0

v1 whole, which is shorter than its diff:
```python
import jax
import jax.numpy as jnp
from jax import lax
from jax.sharding import PartitionSpec as P

epsilon = 1e-06
masked_value = -1e30
route_scale = 2.5


def rotation(position, width):
    halfway = width // 2
    frequency = 10000.0 ** (-2.0 * jnp.arange(halfway).astype(jnp.float32) / width)
    angles = position.astype(jnp.float32)[..., None] * frequency
    return jnp.cos(angles), jnp.sin(angles)


def rotate_pairs(values, position):
    halfway = values.shape[-1] // 2
    cosine, sine_part = rotation(position, values.shape[-1])
    first_half = values[..., :halfway]
    second_half = values[..., halfway:]
    return jnp.concatenate(
        [
            first_half * cosine - second_half * sine_part,
            second_half * cosine + first_half * sine_part,
        ],
        axis=-1,
    )


def rms_scaled(values, gain):
    return (
        values
        * lax.rsqrt(jnp.mean(values * values, axis=-1, keepdims=True) + epsilon)
        * gain.astype(jnp.float32)
    )


def latent_rows(projected, kv_gain, position):
    gain_width = kv_gain.shape[0]
    scaled = rms_scaled(projected[..., :gain_width], kv_gain)
    return jnp.concatenate(
        [scaled, rotate_pairs(projected[..., gain_width:], position)], axis=-1
    ).astype(jnp.bfloat16)


def local(
    prompts,
    owners,
    lengths,
    residual,
    queries,
    expert_ids,
    route_scores,
    attn_gain,
    w_dkv,
    kv_gain,
    w_uk,
    w_uv,
    w_o,
    moe_gain,
    w_gate,
    w_up,
    w_down,
):
    bf16, f32 = jnp.bfloat16, jnp.float32
    plane = ("groups", "expert")
    block = ("expert", "section")
    expert_rank = lax.axis_index("expert")
    section_rank = lax.axis_index("section")
    plane_rank = lax.axis_index(plane)
    experts = lax.axis_size("expert")
    sections = lax.axis_size("section")
    members = lax.axis_size("groups") * experts
    prompt_count, full_length, width = prompts.shape
    steps, tokens_here, _ = residual.shape
    heads = queries.shape[2]
    nope = w_uk.shape[1]
    rope = queries.shape[3] - nope
    latent = kv_gain.shape[0]
    cache_width = latent + rope
    depth = w_dkv.shape[0]
    piece = depth // members
    everyone = experts * sections

    w_turned = w_dkv.T
    w_piece = lax.dynamic_slice_in_dim(w_turned, plane_rank * piece, piece, 1)
    w_set = lax.all_gather(w_piece, "section", axis=0)
    rows = prompt_count * full_length
    cut = prompts.reshape(rows, sections, members, piece).transpose(2, 1, 0, 3)
    cut = lax.all_to_all(cut, plane, 0, 0, tiled=True)

    uv_full = lax.all_gather(w_uv, "expert", axis=0)

    table = owners.reshape(experts, tokens_here)
    length_table = lengths.reshape(experts, tokens_here)
    my_owner = lax.dynamic_slice(
        table, (expert_rank, section_rank * prompt_count), (1, prompt_count)
    )[0]
    my_length = lax.dynamic_slice(
        length_table, (expert_rank, section_rank * prompt_count), (1, prompt_count)
    )[0]

    residual_all = lax.all_gather(residual, "expert", axis=0)
    queries_all = lax.all_gather(queries, "expert", axis=0)
    expert_total = w_gate.shape[0] * experts
    match_table = (expert_ids[..., None] == jnp.arange(expert_total)).astype(f32)
    weights = route_scale * route_scores / jnp.sum(route_scores, axis=-1, keepdims=True)
    weight_map = jnp.sum(weights[..., None] * match_table, axis=2)
    weights_all = lax.all_gather(weight_map, "expert", axis=0)

    picked = jnp.take_along_axis(
        queries_all.transpose(2, 0, 1, 3, 4), table[:, :, None, None, None], axis=1
    )
    query_latent = jnp.einsum(
        "ejthn,hnc->ejthc", picked[..., :nope], w_uk, preferred_element_type=f32
    ).astype(bf16)
    rope_piece = rope // experts
    query_rope = lax.dynamic_slice_in_dim(picked[..., nope:], expert_rank * rope_piece, rope_piece, 4)
    query_part = jnp.concatenate([query_latent, query_rope], axis=-1).reshape(
        everyone, prompt_count, steps, heads, -1
    )
    query_part = lax.all_to_all(query_part, block, 0, 0, tiled=True)
    query_part = query_part.reshape(experts, sections, prompt_count, steps, heads, -1)
    query_part = query_part.transpose(2, 3, 1, 4, 0, 5)
    chunk = w_uk.shape[2]
    query_cat = query_part[..., :chunk].reshape(prompt_count, steps, sections * heads, latent)
    query_rope = query_part[..., chunk:].reshape(prompt_count, steps, sections * heads, rope)
    token_pos = my_length[:, None] + jnp.arange(steps)[None, :]
    query_cat = jnp.concatenate(
        [
            query_cat,
            rotate_pairs(query_rope.astype(f32), token_pos[:, :, None]).astype(bf16),
        ],
        axis=-1,
    )

    normed = rms_scaled(residual.astype(f32), attn_gain).astype(bf16)
    normed = lax.dynamic_slice_in_dim(normed, section_rank * depth, depth, 2)
    fresh = jnp.einsum("ted,kd->etk", normed, w_turned, preferred_element_type=f32).astype(bf16)
    fresh = jnp.broadcast_to(
        fresh[:, None], (experts, sections, steps, cache_width)
    ).reshape(everyone, steps, cache_width)
    fresh = lax.all_to_all(fresh, block, 0, 0, tiled=True)
    fresh = fresh.reshape(experts, sections, steps, cache_width)
    fresh = jnp.sum(jnp.take(fresh, my_owner, axis=0).astype(f32), axis=1)
    recent = latent_rows(fresh, kv_gain, token_pos)

    partial = jnp.einsum("dsrc,skc->drk", cut, w_set, preferred_element_type=f32).astype(bf16)
    partial = lax.all_to_all(partial, plane, 0, 0, tiled=True)
    projected = jnp.sum(partial.astype(f32), axis=0).reshape(prompt_count, full_length, cache_width)
    cache = latent_rows(projected, kv_gain, jnp.arange(full_length)[None, :])

    score_scale = queries.shape[-1] ** (-0.5)
    prompt_scores = (
        jnp.einsum("pthc,plc->pthl", query_cat, cache, preferred_element_type=f32) * score_scale
    )
    live = jnp.arange(full_length)[None, :] < my_length[:, None]
    prompt_scores = jnp.where(live[:, None, None, :], prompt_scores, masked_value)
    recent_scores = (
        jnp.einsum("pthc,puc->pthu", query_cat, recent, preferred_element_type=f32) * score_scale
    )
    seen = jnp.arange(steps)[None, :] <= jnp.arange(steps)[:, None]
    recent_scores = jnp.where(seen[None, :, None, :], recent_scores, masked_value)
    maxima = jnp.maximum(prompt_scores.max(axis=-1), recent_scores.max(axis=-1))[..., None]
    prompt_exp = jnp.exp(prompt_scores - maxima)
    recent_exp = jnp.exp(recent_scores - maxima)
    totals = prompt_exp.sum(axis=-1, keepdims=True) + recent_exp.sum(axis=-1, keepdims=True)
    prompt_prob = (prompt_exp / totals).astype(bf16)
    recent_prob = (recent_exp / totals).astype(bf16)
    out_latent = (
        jnp.einsum(
            "pthl,plc->pthc", prompt_prob, cache[..., :latent], preferred_element_type=f32
        )
        + jnp.einsum(
            "pthu,puc->pthc", recent_prob, recent[..., :latent], preferred_element_type=f32
        )
    ).astype(bf16)

    out_latent = out_latent.reshape(prompt_count, steps, sections, heads, latent)
    out_latent = out_latent.transpose(2, 0, 1, 3, 4)
    out_latent = lax.all_to_all(out_latent, "section", 0, 0, tiled=True)
    row = lax.dynamic_slice_in_dim(table, expert_rank, 1, 0)[0]
    out_latent = out_latent.reshape(tokens_here, steps, heads, latent)
    out_latent = jnp.take(out_latent, jnp.argsort(row), axis=0)
    out_latent = out_latent.reshape(tokens_here, steps, heads, experts, chunk)
    head_values = jnp.einsum(
        "othxc,xhvc->othv", out_latent, uv_full, preferred_element_type=f32
    ).astype(bf16)
    head_values = head_values.reshape(tokens_here * steps, -1)
    head_values = lax.all_gather(head_values, "expert", axis=0, tiled=True)

    attended = jnp.dot(head_values, w_o, preferred_element_type=f32).astype(bf16)
    attended = lax.all_gather(attended, "section", axis=0)
    attended = jnp.sum(attended.astype(f32), axis=0).astype(bf16)
    attended = lax.all_gather(attended, "expert", axis=1, tiled=True)
    hidden = residual_all.transpose(2, 0, 1, 3).reshape(-1, width).astype(f32)
    mixed = hidden + attended.astype(f32)
    moe_in = rms_scaled(mixed, moe_gain).astype(bf16)

    gate_part = jnp.einsum("td,xdf->xtf", moe_in, w_gate, preferred_element_type=f32)
    up_part = jnp.einsum("td,xdf->xtf", moe_in, w_up, preferred_element_type=f32)
    route = weights_all.transpose(2, 0, 1, 3).reshape(-1, expert_total)
    route = lax.dynamic_slice_in_dim(route, expert_rank * w_gate.shape[0], w_gate.shape[0], 1)
    activated = (jax.nn.silu(gate_part) * up_part * route.T[:, :, None]).astype(bf16)
    combined = jnp.einsum("xtf,xfd->td", activated, w_down, preferred_element_type=f32).astype(bf16)
    column = width // sections
    combined = combined.reshape(experts, experts, steps, sections, column)
    combined = combined.transpose(1, 3, 0, 2, 4).reshape(everyone, experts, steps, column)
    combined = lax.all_to_all(combined, block, 0, 0, tiled=True)
    combined = jnp.sum(combined.astype(f32), axis=0)
    own = mixed.reshape(experts, experts, steps, sections, column)
    own = lax.dynamic_slice(
        own,
        (0, expert_rank, 0, section_rank, 0),
        (experts, 1, steps, 1, column),
    )[:, 0, :, 0]
    return (own + combined).transpose(1, 0, 2).astype(bf16)


def solution(mesh):
    placed = (
        P(("groups", "expert", "section"), None, None),
        P("groups"),
        P("groups"),
        P(None, ("groups", "expert"), None),
        P(None, ("groups", "expert"), "section", None),
        P(None, ("groups", "expert"), None),
        P(None, ("groups", "expert"), None),
        P(),
        P("section", None),
        P(),
        P("section", None, "expert"),
        P("section", None, "expert"),
        P("section", "expert"),
        P(),
        P("expert", None, "section"),
        P("expert", None, "section"),
        P("expert", "section", None),
    )
    return jax.shard_map(
        local,
        mesh=mesh,
        in_specs=placed,
        out_specs=P(None, ("groups", "expert"), "section"),
        check_vma=False,
    )
```

time: 442 us -> 195 us (0.44)
  waiting for transfers between devices: 178 us -> 47.7 us
  local copies, waits for them, and re-layouts: 137 us -> 12.7 us
  blocking collectives: 26.8 us -> 60.9 us
  matrix products: 45 us -> 23.3 us
    unnamed x32 -> x15, local copies, waits for them, and re-layouts: 129 us -> 0.81 us
    all_gather x3 -> x1, waiting for transfers between devices: 96.7 us -> 0.02 us  [local(): uv_full = lax.all_gather(w_uv, 'expert', axis=0)]
    all_gather x3 -> x7, blocking collectives: 26.8 us -> 60.9 us  [the longest x1 17.1 us: local(): w_set = lax.all_gather(w_piece, 'section', axis=0)]
    psum x1 -> x0, waiting for transfers between devices: 32.5 us -> none  [local(): attended = lax.psum(exchanged, 'section')]
    unnamed x8 -> x1, waiting for transfers between devices: 25.5 us -> 0.68 us
    all_to_all x8 -> x6, waiting for transfers between devices: 23.7 us -> 47 us  [the longest x1 15.6 us: local(): partial = lax.all_to_all(partial, plane, 0, 0, tiled=True)]
    dot_general x27 -> x11, matrix products: 45 us -> 23.3 us  [the longest x1 7.87 us: local(): jnp.einsum('xtf,xfd->td', activated, w_down, preferred_element_type=f32)]
    all_to_all x8 -> x6, starting transfers between devices: 26.7 us -> 27.1 us  [the longest x1 7.36 us: local(): fresh = lax.all_to_all(fresh, block, 0, 0, tiled=True)]
  transfers between devices with their start and end apart: 14 -> 7, of which waited for: 9 -> 5; matrix products, arithmetic and copies ran while one was open for 41% -> 10% of each run, Pallas kernels for 0% -> 0%
where the time goes in v1:
time: 195 us; the launch traced here: 194 us
  blocking collectives  60.9 us (31%)
  waiting for transfers between devices  47.7 us (24%)
  starting transfers between devices  27.2 us (14%)
  matrix products  23.3 us (12%)
  between operations  15.8 us (8%)
  local copies, waits for them, and re-layouts  12.7 us (7%)
  other arithmetic  6.6 us (3%)
    all_gather x1, blocking collectives, local(): w_set = lax.all_gather(w_piece, 'section', axis=0)  17.1 us
    all_to_all x1, waiting for transfers between devices, local(): partial = lax.all_to_all(partial, plane, 0, 0, tiled=True)  15.6 us
    all_gather x1, blocking collectives, local(): attended = lax.all_gather(attended, 'section', axis=0)  13.7 us
    all_to_all x1, waiting for transfers between devices, local(): cut = lax.all_to_all(cut, plane, 0, 0, tiled=True)  9.64 us
    all_to_all x1, waiting for transfers between devices, local(): combined = lax.all_to_all(combined, block, 0, 0, tiled=True)  8.96 us
    dot_general x1, matrix products, local(): jnp.einsum('xtf,xfd->td', activated, w_down, preferred_element_type=f32)  7.87 us
    all_gather x1, blocking collectives, local(): queries_all = lax.all_gather(queries, 'expert', axis=0)  7.55 us
    all_to_all x1, starting transfers between devices, local(): fresh = lax.all_to_all(fresh, block, 0, 0, tiled=True)  7.36 us
  transfers between devices with their start and end apart: 7, of which 5 were waited for; matrix products, arithmetic and copies ran while one was open for 10% of the time, Pallas kernels for 0%

profile of v1, /device:TPU:0, one launch (start us, length us, event | category | flops | bytes accessed | tf_op | source)
XLA Modules:
  0.0 194.1 jit_solution(10242273725579722770)
XLA Ops:
  10.3 7.4 %all-to-all-start.3 = ((bf16[16,2,576]{2,1,0:T(2,128)(2,1)}), bf16[16,2,576]{2,1,0:T(2,128)(2,1)S(1)}, u32[]{:S(2)}, u32[]{:S(2)}) async-start(bf16[16,2,576]{2,1,0:T(2,128)(2,1)} %bitcast.33), calls=%async_computation.3 | async-start | bytes 81920 | tf_op jit(solution)/shard_map/all_to_all | solution.py:145
  19.9 6.3 %all-gather = bf16[8,4,3584]{2,1,0:T(4,128)(2,1)S(1)} all-gather(bf16[2,4,3584]{2,1,0:T(4,128)(2,1)} %param.20), channel_id=2, replica_groups=mesh['groups'=2,'expert'=4,'section'=4] {'expert'}, dimensions={0}, use_global_device_ids=true | all-gather | bytes 286720 | tf_op jit(solution)/shard_map/all_gather | solution.py:105
  28.1 7.5 %all-gather.1 = bf16[8,4,16,192]{3,2,1,0:T(8,128)(2,1)S(1)} all-gather(bf16[2,4,16,192]{3,2,1,0:T(8,128)(2,1)} %param.21), channel_id=3, replica_groups=mesh['groups'=2,'expert'=4,'section'=4] {'expert'}, dimensions={0}, use_global_device_ids=true | all-gather | bytes 245760 | tf_op jit(solution)/shard_map/all_gather | solution.py:106
  36.7 1.3 fusion.5
  38.3 17.1 %all-gather.6 = bf16[4,576,112]{1,2,0:T(8,128)(2,1)} all-gather(bf16[1,576,112]{1,2,0:T(8,128)(2,1)S(1)} %bitcast.178), channel_id=4, replica_groups=mesh['groups'=2,'expert'=4,'section'=4] {'section'}, dimensions={0}, use_global_device_ids=true | all-gather | bytes 645120 | tf_op jit(solution)/shard_map/all_gather | solution.py:89
  58.1 5.2 %all-gather.5 = f32[8,4,16]{2,1,0:T(4,128)S(1)} all-gather(f32[2,4,16]{2,1,0:T(4,128)S(1)} %select_reduce_fusion), channel_id=7, replica_groups=mesh['groups'=2,'expert'=4,'section'=4] {'expert'}, dimensions={0}, use_global_device_ids=true | all-gather | bytes 2560 | tf_op jit(solution)/shard_map/all_gather | solution.py:111
  64.4 4.2 %all-to-all-start.1 = ((bf16[8,4,128,112]{2,3,1,0:T(8,128)(2,1)}), bf16[8,4,128,112]{2,3,1,0:T(8,128)(2,1)}, u32[]{:S(2)}, u32[]{:S(2)}) async-start(bf16[8,4,128,112]{2,3,1,0:T(8,128)(2,1)} %bitcast.163), calls=%async_computation.1 | async-start | bytes 1835008 | tf_op jit(solution)/shard_map/all_to_all | solution.py:92
  73.0 9.6 %all-to-all-done.1 = bf16[8,4,128,112]{2,3,1,0:T(8,128)(2,1)} async-done(((bf16[8,4,128,112]{2,3,1,0:T(8,128)(2,1)}), bf16[8,4,128,112]{2,3,1,0:T(8,128)(2,1)}, u32[]{:S(2)}, u32[]{:S(2)}) %all-to-all-start.1) | async-done | bytes 917536 | tf_op jit(solution)/shard_map/all_to_all | solution.py:92
  82.6 5.1 %all-to-all-start = ((bf16[16,1,2,16,144]{4,3,2,1,0:T(8,128)(2,1)}), bf16[16,1,2,16,144]{4,3,2,1,0:T(8,128)(2,1)S(1)}, u32[]{:S(2)}, u32[]{:S(2)}) async-start(bf16[16,1,2,16,144]{4,3,2,1,0:T(8,128)(2,1)} %bitcast.11), calls=%async_computation | async-start | bytes 524288 | tf_op jit(solution)/shard_map/all_to_all | solution.py:124
  87.7 3.2 %fusion.3 = bf16[8,128,576]{1,2,0:T(8,128)(2,1)} fusion(bf16[8,4,128,112]{2,3,1,0:T(8,128)(2,1)} %all-to-all-done.1, bf16[4,576,112]{1,2,0:T(8,128)(2,1)} %all-gather.6), kind=kOutput, calls=%fused_computation.8 | convolution fusion | flops 529072128 | bytes 2613248 | tf_op jit(solution)/shard_map/dsrc,skc->drk/dot_general | solution.py:150
  90.9 6.9 %all-to-all-done = bf16[16,1,2,16,144]{4,3,2,1,0:T(8,128)(2,1)S(1)} async-done(((bf16[16,1,2,16,144]{4,3,2,1,0:T(8,128)(2,1)}), bf16[16,1,2,16,144]{4,3,2,1,0:T(8,128)(2,1)S(1)}, u32[]{:S(2)}, u32[]{:S(2)}) %all-to-all-start) | async-done | bytes 147488 | tf_op jit(solution)/shard_map/all_to_all | solution.py:124
  97.8 3.6 %all-to-all-start.2 = ((bf16[8,128,576]{1,2,0:T(8,128)(2,1)}), bf16[8,128,576]{1,2,0:T(8,128)(2,1)S(1)}, u32[]{:S(2)}, u32[]{:S(2)}) async-start(bf16[8,128,576]{1,2,0:T(8,128)(2,1)} %fusion.3), calls=%async_computation.2 | async-start | bytes 2359296 | tf_op jit(solution)/shard_map/all_to_all | solution.py:151
  102.5 15.6 %all-to-all-done.2 = bf16[8,128,576]{1,2,0:T(8,128)(2,1)S(1)} async-done(((bf16[8,128,576]{1,2,0:T(8,128)(2,1)}), bf16[8,128,576]{1,2,0:T(8,128)(2,1)S(1)}, u32[]{:S(2)}, u32[]{:S(2)}) %all-to-all-start.2) | async-done | bytes 1179680 | tf_op jit(solution)/shard_map/all_to_all | solution.py:151
  120.4 3.3 %all-to-all-start.4 = ((bf16[4,1,2,16,512]{4,3,2,1,0:T(8,128)(2,1)}), bf16[4,1,2,16,512]{4,3,2,1,0:T(8,128)(2,1)S(1)}, u32[]{:S(2)}, u32[]{:S(2)}) async-start(bf16[4,1,2,16,512]{4,3,2,1,0:T(8,128)(2,1)} %bitcast.164), calls=%async_computation.4 | async-start | bytes 262144 | tf_op jit(solution)/shard_map/all_to_all | solution.py:183
  123.7 5.9 %all-to-all-done.4 = bf16[4,1,2,16,512]{4,3,2,1,0:T(8,128)(2,1)S(1)} async-done(((bf16[4,1,2,16,512]{4,3,2,1,0:T(8,128)(2,1)}), bf16[4,1,2,16,512]{4,3,2,1,0:T(8,128)(2,1)S(1)}, u32[]{:S(2)}, u32[]{:S(2)}) %all-to-all-start.4) | async-done | bytes 131104 | tf_op jit(solution)/shard_map/all_to_all | solution.py:183
  130.4 2.3 %fusion.16 = bf16[4,2,16,128]{3,0,1,2:T(4,128)(2,1)S(1)} fusion(bf16[4,16,128,128,1]{3,2,1,0,4:T(8,128)(2,1)} %bitcast.189, bf16[4,2,16,4,128]{4,3,2,1,0:T(4,128)(2,1)S(1)} %broadcast_select_fusion), kind=kOutput, calls=%fused_computation.23 | convolution fusion | flops 16793600 | bytes 2260992 | tf_op jit(solution)/shard_map/othxc,xhvc->othv/dot_general | solution.py:188
  132.7 5.4 %all_gather.50 = bf16[32,2048]{1,0:T(8,128)(2,1)S(1)} all-gather(bf16[8,2048]{1,0:T(8,128)(2,1)S(1)} %bitcast.181), channel_id=1, replica_groups=mesh['groups'=2,'expert'=4,'section'=4] {'expert'}, dimensions={0}, use_global_device_ids=true | all-gather | bytes 163840 | tf_op jit(solution)/shard_map/all_gather | solution.py:192
  138.1 2.7 %convolution_convert_fusion.1 = bf16[32,896]{1,0:T(8,128)(2,1)S(1)} fusion(bf16[32,2048]{1,0:T(8,128)(2,1)S(1)} %all_gather.50, bf16[2048,896]{1,0:T(8,128)(2,1)} %param.29), kind=kOutput, calls=%fused_computation.18 | convolution fusion | flops 117469184 | bytes 3858432 | tf_op jit(solution)/shard_map/dot_general | solution.py:194
  140.8 13.7 %all-gather.4 = bf16[128,896]{1,0:T(8,128)(2,1)S(1)} all-gather(bf16[32,896]{1,0:T(8,128)(2,1)S(1)} %convolution_convert_fusion.1), channel_id=6, replica_groups=mesh['groups'=2,'expert'=4,'section'=4] {'section'}, dimensions={0}, use_global_device_ids=true | all-gather | bytes 286720 | tf_op jit(solution)/shard_map/all_gather | solution.py:195
  154.5 5.7 %all_gather.53 = bf16[32,3584]{1,0:T(8,128)(2,1)S(1)} all-gather(bf16[32,896]{1,0:T(8,128)(2,1)S(1)} %reduce_sum.121), channel_id=1, replica_groups=mesh['groups'=2,'expert'=4,'section'=4] {'expert'}, dimensions={1}, use_global_device_ids=true | all-gather | bytes 286720 | tf_op jit(solution)/shard_map/all_gather | solution.py:197
  160.4 4.5 %convolution_bitcast_fusion.2 = f32[4,32,256]{2,1,0:T(8,128)S(1)} fusion(bf16[4,3584,256]{2,1,0:T(8,128)(2,1)} %param.31, f32[32,3584]{1,0:T(8,128)S(1)} %get-tuple-element.19, f32[3584]{0:T(1024)S(1)} %convert_element_type.226, f32[32]{0:T(128)S(1)} %add_rsqrt_fusion.1), kind=kOutput, calls=%fused_computation.16 | convolution fusion | flops 235225088 | bytes 7944320 | tf_op jit(solution)/shard_map/td,xdf->xtf/dot_general | solution.py:202
  164.9 7.9 %fusion = bf16[32,3584]{1,0:T(8,128)(2,1)S(1)} fusion(bf16[4,256,3584]{2,1,0:T(8,128)(2,1)} %param.33, bf16[4,3584,256]{2,1,0:T(8,128)(2,1)} %param.32, f32[4,32,256]{2,1,0:T(8,128)S(1)} %convolution_bitcast_fusion.2, f32[4,32]{1,0:T(4,128)S(1)} %copy.118, f32[32,3584]{1,0:T(8,128)S(1)} %get-tuple-element.19, f32[3584]{0:T(1024)S(1)} %convert_element_type.226, ...), kind=kOutput, calls=%fused_computation.3 | convolution fusion | flops 470450176 | bytes 15514240 | tf_op jit(solution)/shard_map/xtf,xfd->td/dot_general | solution.py:207
  173.7 3.5 %all-to-all-start.5 = ((bf16[16,4,2,896]{3,2,1,0:T(2,128)(2,1)}), bf16[16,4,2,896]{3,2,1,0:T(2,128)(2,1)S(1)}, u32[]{:S(2)}, u32[]{:S(2)}) async-start(bf16[16,4,2,896]{3,2,1,0:T(2,128)(2,1)} %bitcast.62), calls=%async_computation.5 | async-start | bytes 458752 | tf_op jit(solution)/shard_map/all_to_all | solution.py:211
  177.5 9.0 %all-to-all-done.5 = bf16[16,4,2,896]{3,2,1,0:T(2,128)(2,1)S(1)} async-done(((bf16[16,4,2,896]{3,2,1,0:T(2,128)(2,1)}), bf16[16,4,2,896]{3,2,1,0:T(2,128)(2,1)S(1)}, u32[]{:S(2)}, u32[]{:S(2)}) %all-to-all-start.5) | async-done | bytes 229408 | tf_op jit(solution)/shard_map/all_to_all | solution.py:211
  (105 shorter events, 21.5 us)
Async XLA Ops:
  6.5 2.7 %copy-start = (bf16[896,576]{0,1:T(8,128)(2,1)S(1)}, bf16[896,576]{0,1:T(8,128)(2,1)}, u32[]{:S(2)}) copy-start(bf16[896,576]{0,1:T(8,128)(2,1)} %param.25) | copy-start | bytes 3096580
  6.5 48.8 %copy-start.1 = (bf16[1,128,3584]{2,1,0:T(8,128)(2,1)S(1)}, bf16[1,128,3584]{2,1,0:T(8,128)(2,1)}, u32[]{:S(2)}) copy-start(bf16[1,128,3584]{2,1,0:T(8,128)(2,1)} %param.17) | copy-start | bytes 2752516
  10.3 54.1 %all-to-all-start.3 = ((bf16[16,2,576]{2,1,0:T(2,128)(2,1)}), bf16[16,2,576]{2,1,0:T(2,128)(2,1)S(1)}, u32[]{:S(2)}, u32[]{:S(2)}) async-start(bf16[16,2,576]{2,1,0:T(2,128)(2,1)} %bitcast.33), calls=%async_computation.3 | async-start | bytes 81920 | tf_op jit(solution)/shard_map/all_to_all | solution.py:145
  17.6 112.7 %all-gather.9.cloned.1.call-start = ((), (), s32[]{:S(2)}) async-start(), calls=%async_computation.6 | async-start | bytes 2621440 | tf_op jit(solution)/shard_map/all_gather | solution.py:94
  36.4 21.5 %copy-start.5 = (f32[2,4,8]{2,1,0:T(4,128)S(1)}, f32[2,4,8]{2,1,0:T(4,128)}, u32[]{:S(2)}) copy-start(f32[2,4,8]{2,1,0:T(4,128)} %param.23) | copy-start | bytes 772
  36.4 21.6 %copy-start.3 = (s32[2,4,8]{2,1,0:T(4,128)S(1)}, s32[2,4,8]{2,1,0:T(4,128)}, u32[]{:S(2)}) copy-start(s32[2,4,8]{2,1,0:T(4,128)} %param.22) | copy-start | bytes 772
  55.4 15.8 %copy-start.4 = (bf16[512]{0:T(512)(128)(2,1)S(1)}, bf16[512]{0:T(512)(128)(2,1)}, u32[]{:S(2)}) copy-start(bf16[512]{0:T(512)(128)(2,1)} %param.26) | copy-start | bytes 3076
  56.0 16.6 %copy-start.2 = (bf16[3584]{0:T(1024)(128)(2,1)S(1)}, bf16[3584]{0:T(1024)(128)(2,1)}, u32[]{:S(2)}) copy-start(bf16[3584]{0:T(1024)(128)(2,1)} %param.30) | copy-start | bytes 21508
  64.4 18.3 %all-to-all-start.1 = ((bf16[8,4,128,112]{2,3,1,0:T(8,128)(2,1)}), bf16[8,4,128,112]{2,3,1,0:T(8,128)(2,1)}, u32[]{:S(2)}, u32[]{:S(2)}) async-start(bf16[8,4,128,112]{2,3,1,0:T(8,128)(2,1)} %bitcast.163), calls=%async_computation.1 | async-start | bytes 1835008 | tf_op jit(solution)/shard_map/all_to_all | solution.py:92
  82.6 15.2 %all-to-all-start = ((bf16[16,1,2,16,144]{4,3,2,1,0:T(8,128)(2,1)}), bf16[16,1,2,16,144]{4,3,2,1,0:T(8,128)(2,1)S(1)}, u32[]{:S(2)}, u32[]{:S(2)}) async-start(bf16[16,1,2,16,144]{4,3,2,1,0:T(8,128)(2,1)} %bitcast.11), calls=%async_computation | async-start | bytes 524288 | tf_op jit(solution)/shard_map/all_to_all | solution.py:124
  97.8 20.3 %all-to-all-start.2 = ((bf16[8,128,576]{1,2,0:T(8,128)(2,1)}), bf16[8,128,576]{1,2,0:T(8,128)(2,1)S(1)}, u32[]{:S(2)}, u32[]{:S(2)}) async-start(bf16[8,128,576]{1,2,0:T(8,128)(2,1)} %fusion.3), calls=%async_computation.2 | async-start | bytes 2359296 | tf_op jit(solution)/shard_map/all_to_all | solution.py:151
  120.4 9.2 %all-to-all-start.4 = ((bf16[4,1,2,16,512]{4,3,2,1,0:T(8,128)(2,1)}), bf16[4,1,2,16,512]{4,3,2,1,0:T(8,128)(2,1)S(1)}, u32[]{:S(2)}, u32[]{:S(2)}) async-start(bf16[4,1,2,16,512]{4,3,2,1,0:T(8,128)(2,1)} %bitcast.164), calls=%async_computation.4 | async-start | bytes 262144 | tf_op jit(solution)/shard_map/all_to_all | solution.py:183
  173.7 12.7 %all-to-all-start.5 = ((bf16[16,4,2,896]{3,2,1,0:T(2,128)(2,1)}), bf16[16,4,2,896]{3,2,1,0:T(2,128)(2,1)S(1)}, u32[]{:S(2)}, u32[]{:S(2)}) async-start(bf16[16,4,2,896]{3,2,1,0:T(2,128)(2,1)} %bitcast.62), calls=%async_computation.5 | async-start | bytes 458752 | tf_op jit(solution)/shard_map/all_to_all | solution.py:211
Sparse Core Ops, SparseCore 0:
  20.0 25.3 all-gather.8

commit v2 on v1

--- a/solution.py
+++ b/solution.py
@@ -1,6 +1,10 @@
+import functools
+
 import jax
 import jax.numpy as jnp
 from jax import lax
+from jax.experimental import pallas as pl
+from jax.experimental.pallas import tpu as pltpu
 from jax.sharding import PartitionSpec as P
 
 epsilon = 1e-06
@@ -43,6 +47,94 @@
     return jnp.concatenate(
         [scaled, rotate_pairs(projected[..., gain_width:], position)], axis=-1
     ).astype(jnp.bfloat16)
+
+
+def swap(block, axis, mask):
+    size = lax.axis_size(axis)
+    return lax.ppermute(block, axis, [(i, i ^ mask) for i in range(size)])
+
+
+def exchange(blocks, axis):
+    here = lax.axis_index(axis)
+    landed = [lax.dynamic_index_in_dim(blocks, here, 0, keepdims=False)]
+    for mask in range(1, lax.axis_size(axis)):
+        sent = lax.dynamic_index_in_dim(blocks, here ^ mask, 0, keepdims=False)
+        landed.append(swap(sent, axis, mask))
+    return landed
+
+
+def spread(block, axis):
+    return [block] + [swap(block, axis, mask) for mask in range(1, lax.axis_size(axis))]
+
+
+def attend_kernel(parts, heads_rows, steps, latent, score_scale, *refs):
+    part_refs = refs[:parts]
+    length_ref, gain_ref, cosine_ref, sine_ref, query_ref, recent_ref, out_ref = refs[parts:]
+    f32, bf16 = jnp.float32, jnp.bfloat16
+    nt = (((1,), (1,)), ((), ()))
+    projected = part_refs[0][0].astype(f32)
+    for ref in part_refs[1:]:
+        projected = projected + ref[0].astype(f32)
+    wide = projected[:, :latent]
+    scale = lax.rsqrt(jnp.mean(wide * wide, axis=-1, keepdims=True) + epsilon)
+    keys = (wide * scale * gain_ref[...].astype(f32)).astype(bf16)
+    turn = projected[:, latent:]
+    half = turn.shape[1] // 2
+    turned = jnp.concatenate([turn[:, half:], turn[:, :half]], axis=1)
+    key_rope = (turn * cosine_ref[...] + turned * sine_ref[...]).astype(bf16)
+    query = query_ref[0]
+    recent = recent_ref[0]
+    scores = lax.dot_general(query[:, :latent], keys, nt, preferred_element_type=f32)
+    scores = scores + lax.dot_general(
+        query[:, latent:], key_rope, nt, preferred_element_type=f32
+    )
+    fresh = lax.dot_general(query, recent, nt, preferred_element_type=f32)
+    place = lax.broadcasted_iota(jnp.int32, scores.shape, 1)
+    scores = jnp.where(place < length_ref[pl.program_id(0)], scores * score_scale, masked_value)
+    step = lax.broadcasted_iota(jnp.int32, fresh.shape, 0) // heads_rows
+    place = lax.broadcasted_iota(jnp.int32, fresh.shape, 1)
+    fresh = jnp.where(place <= step, fresh * score_scale, masked_value)
+    most = jnp.maximum(
+        jnp.max(scores, axis=-1, keepdims=True), jnp.max(fresh, axis=-1, keepdims=True)
+    )
+    scores = jnp.exp(scores - most)
+    fresh = jnp.exp(fresh - most)
+    total = jnp.sum(scores, axis=-1, keepdims=True) + jnp.sum(fresh, axis=-1, keepdims=True)
+    scores = (scores / total).astype(bf16)
+    fresh = (fresh / total).astype(bf16)
+    mixed = jnp.dot(scores, keys, preferred_element_type=f32)
+    mixed = mixed + jnp.dot(fresh, recent[:, :latent], preferred_element_type=f32)
+    out_ref[0] = mixed.astype(bf16)
+
+
+def attend(parts, lengths, kv_gain, query_cat, recent, steps, score_scale):
+    prompts, positions, width = parts[0].shape
+    latent = kv_gain.shape[0]
+    rows = query_cat.shape[1]
+    cosine, sine = rotation(jnp.arange(positions), width - latent)
+    cosine = jnp.concatenate([cosine, cosine], axis=-1)
+    sine = jnp.concatenate([-sine, sine], axis=-1)
+    one = lambda shape: pl.BlockSpec((1,) + shape, lambda i: (i, 0, 0))
+    whole = lambda shape: pl.BlockSpec(shape, lambda i: (0, 0))
+    return pl.pallas_call(
+        functools.partial(
+            attend_kernel, len(parts), rows // steps, steps, latent, score_scale
+        ),
+        grid=(prompts,),
+        out_shape=jax.ShapeDtypeStruct((prompts, rows, latent), jnp.bfloat16),
+        in_specs=[one((positions, width))] * len(parts)
+        + [
+            pl.BlockSpec(memory_space=pltpu.SMEM),
+            whole((1, latent)),
+            whole(cosine.shape),
+            whole(sine.shape),
+            one((rows, width)),
+            one(recent.shape[1:]),
+        ],
+        out_specs=one((rows, latent)),
+        compiler_params=pltpu.CompilerParams(vmem_limit_bytes=32 * 1024 * 1024),
+        name="attend",
+    )(*parts, lengths, kv_gain[None], cosine, sine, query_cat, recent)
 
 
 def local(
@@ -65,14 +157,13 @@
     w_down,
 ):
     bf16, f32 = jnp.bfloat16, jnp.float32
-    plane = ("groups", "expert")
     block = ("expert", "section")
     expert_rank = lax.axis_index("expert")
     section_rank = lax.axis_index("section")
-    plane_rank = lax.axis_index(plane)
+    group_rank = lax.axis_index("groups")
     experts = lax.axis_size("expert")
     sections = lax.axis_size("section")
-    members = lax.axis_size("groups") * experts
+    groups = lax.axis_size("groups")
     prompt_count, full_length, width = prompts.shape
     steps, tokens_here, _ = residual.shape
     heads = queries.shape[2]
@@ -81,15 +172,18 @@
     latent = kv_gain.shape[0]
     cache_width = latent + rope
     depth = w_dkv.shape[0]
-    piece = depth // members
+    piece = depth // (groups * experts)
     everyone = experts * sections
 
     w_turned = w_dkv.T
-    w_piece = lax.dynamic_slice_in_dim(w_turned, plane_rank * piece, piece, 1)
-    w_set = lax.all_gather(w_piece, "section", axis=0)
+    w_piece = lax.dynamic_slice_in_dim(
+        w_turned, (expert_rank * groups + group_rank) * piece, piece, 1
+    )
     rows = prompt_count * full_length
-    cut = prompts.reshape(rows, sections, members, piece).transpose(2, 1, 0, 3)
-    cut = lax.all_to_all(cut, plane, 0, 0, tiled=True)
+    cut = prompts.reshape(rows, sections, experts, groups * piece).transpose(2, 1, 0, 3)
+    cut = lax.all_to_all(cut, "expert", 0, 0, tiled=True)
+    w_parts = spread(w_piece, "section")
+    w_parts = [spread(part, "groups") for part in w_parts]
 
     uv_full = lax.all_gather(w_uv, "expert", axis=0)
 
@@ -119,9 +213,20 @@
     rope_piece = rope // experts
     query_rope = lax.dynamic_slice_in_dim(picked[..., nope:], expert_rank * rope_piece, rope_piece, 4)
     query_part = jnp.concatenate([query_latent, query_rope], axis=-1).reshape(
-        everyone, prompt_count, steps, heads, -1
+        everyone, prompt_count * steps * heads, -1
+    )
+    normed = rms_scaled(residual.astype(f32), attn_gain).astype(bf16)
+    normed = lax.dynamic_slice_in_dim(normed, section_rank * depth, depth, 2)
+    fresh = jnp.einsum("ted,kd->etk", normed, w_turned, preferred_element_type=f32).astype(bf16)
+    fresh = fresh.reshape(experts, 1, -1, query_part.shape[-1])
+    fresh = jnp.broadcast_to(fresh, (experts, sections) + fresh.shape[2:])
+    query_part = jnp.concatenate(
+        [query_part, fresh.reshape((everyone,) + fresh.shape[2:])], axis=1
     )
     query_part = lax.all_to_all(query_part, block, 0, 0, tiled=True)
+    fresh = query_part[:, prompt_count * steps * heads :]
+    fresh = fresh.reshape(experts, sections, steps, cache_width)
+    query_part = query_part[:, : prompt_count * steps * heads]
     query_part = query_part.reshape(experts, sections, prompt_count, steps, heads, -1)
     query_part = query_part.transpose(2, 3, 1, 4, 0, 5)
     chunk = w_uk.shape[2]
@@ -136,47 +241,29 @@
         axis=-1,
     )
 
-    normed = rms_scaled(residual.astype(f32), attn_gain).astype(bf16)
-    normed = lax.dynamic_slice_in_dim(normed, section_rank * depth, depth, 2)
-    fresh = jnp.einsum("ted,kd->etk", normed, w_turned, preferred_element_type=f32).astype(bf16)
-    fresh = jnp.broadcast_to(
-        fresh[:, None], (experts, sections, steps, cache_width)
-    ).reshape(everyone, steps, cache_width)
-    fresh = lax.all_to_all(fresh, block, 0, 0, tiled=True)
-    fresh = fresh.reshape(experts, sections, steps, cache_width)
     fresh = jnp.sum(jnp.take(fresh, my_owner, axis=0).astype(f32), axis=1)
     recent = latent_rows(fresh, kv_gain, token_pos)
-
-    partial = jnp.einsum("dsrc,skc->drk", cut, w_set, preferred_element_type=f32).astype(bf16)
-    partial = lax.all_to_all(partial, plane, 0, 0, tiled=True)
-    projected = jnp.sum(partial.astype(f32), axis=0).reshape(prompt_count, full_length, cache_width)
-    cache = latent_rows(projected, kv_gain, jnp.arange(full_length)[None, :])
-
-    score_scale = queries.shape[-1] ** (-0.5)
-    prompt_scores = (
-        jnp.einsum("pthc,plc->pthl", query_cat, cache, preferred_element_type=f32) * score_scale
-    )
-    live = jnp.arange(full_length)[None, :] < my_length[:, None]
-    prompt_scores = jnp.where(live[:, None, None, :], prompt_scores, masked_value)
-    recent_scores = (
-        jnp.einsum("pthc,puc->pthu", query_cat, recent, preferred_element_type=f32) * score_scale
-    )
-    seen = jnp.arange(steps)[None, :] <= jnp.arange(steps)[:, None]
-    recent_scores = jnp.where(seen[None, :, None, :], recent_scores, masked_value)
-    maxima = jnp.maximum(prompt_scores.max(axis=-1), recent_scores.max(axis=-1))[..., None]
-    prompt_exp = jnp.exp(prompt_scores - maxima)
-    recent_exp = jnp.exp(recent_scores - maxima)
-    totals = prompt_exp.sum(axis=-1, keepdims=True) + recent_exp.sum(axis=-1, keepdims=True)
-    prompt_prob = (prompt_exp / totals).astype(bf16)
-    recent_prob = (recent_exp / totals).astype(bf16)
-    out_latent = (
-        jnp.einsum(
-            "pthl,plc->pthc", prompt_prob, cache[..., :latent], preferred_element_type=f32
-        )
-        + jnp.einsum(
-            "pthu,puc->pthc", recent_prob, recent[..., :latent], preferred_element_type=f32
-        )
-    ).astype(bf16)
+    recent = jnp.pad(recent, ((0, 0), (0, -steps % 16), (0, 0)))
+
+    partial = 0
+    for mask, pair in enumerate(w_parts):
+        share = lax.dynamic_index_in_dim(cut, section_rank ^ mask, 1, keepdims=False)
+        for other, part in enumerate(pair):
+            some = lax.dynamic_slice_in_dim(share, (group_rank ^ other) * piece, piece, 2)
+            partial = partial + jnp.einsum(
+                "drc,kc->drk", some, part, preferred_element_type=f32
+            )
+    parts = exchange(partial.astype(bf16), "expert")
+    parts = [part.reshape(prompt_count, full_length, cache_width) for part in parts]
+    out_latent = attend(
+        parts,
+        my_length,
+        kv_gain,
+        query_cat.reshape(prompt_count, -1, cache_width),
+        recent,
+        steps,
+        queries.shape[-1] ** (-0.5),
+    )
 
     out_latent = out_latent.reshape(prompt_count, steps, sections, heads, latent)
     out_latent = out_latent.transpose(2, 0, 1, 3, 4)
@@ -192,19 +279,22 @@
     head_values = lax.all_gather(head_values, "expert", axis=0, tiled=True)
 
     attended = jnp.dot(head_values, w_o, preferred_element_type=f32).astype(bf16)
-    attended = lax.all_gather(attended, "section", axis=0)
-    attended = jnp.sum(attended.astype(f32), axis=0).astype(bf16)
+    attended = sum(part.astype(f32) for part in spread(attended, "section")).astype(bf16)
     attended = lax.all_gather(attended, "expert", axis=1, tiled=True)
     hidden = residual_all.transpose(2, 0, 1, 3).reshape(-1, width).astype(f32)
     mixed = hidden + attended.astype(f32)
     moe_in = rms_scaled(mixed, moe_gain).astype(bf16)
 
-    gate_part = jnp.einsum("td,xdf->xtf", moe_in, w_gate, preferred_element_type=f32)
-    up_part = jnp.einsum("td,xdf->xtf", moe_in, w_up, preferred_element_type=f32)
+    gate_part = jnp.einsum("td,xdf->txf", moe_in, w_gate, preferred_element_type=f32)
+    up_part = jnp.einsum("td,xdf->txf", moe_in, w_up, preferred_element_type=f32)
     route = weights_all.transpose(2, 0, 1, 3).reshape(-1, expert_total)
     route = lax.dynamic_slice_in_dim(route, expert_rank * w_gate.shape[0], w_gate.shape[0], 1)
-    activated = (jax.nn.silu(gate_part) * up_part * route.T[:, :, None]).astype(bf16)
-    combined = jnp.einsum("xtf,xfd->td", activated, w_down, preferred_element_type=f32).astype(bf16)
+    activated = (jax.nn.silu(gate_part) * up_part * route[:, :, None]).astype(bf16)
+    combined = jnp.dot(
+        activated.reshape(activated.shape[0], -1),
+        w_down.reshape(-1, width),
+        preferred_element_type=f32,
+    ).astype(bf16)
     column = width // sections
     combined = combined.reshape(experts, experts, steps, sections, column)
     combined = combined.transpose(1, 3, 0, 2, 4).reshape(everyone, experts, steps, column)

time: 195 us -> 171 us (0.88)
  blocking collectives: 60.9 us -> 29.2 us
  waiting for transfers between devices: 47.7 us -> 38.3 us
  starting transfers between devices: 27.2 us -> 33.6 us
  matrix products: 23.3 us -> 27.4 us
  local copies, waits for them, and re-layouts: 12.7 us -> 16 us
  other arithmetic: 6.6 us -> 8.66 us
    all_gather x2 -> x0, blocking collectives: 30.8 us -> none  [the longest x1 17.1 us: local(): w_set = lax.all_gather(w_piece, 'section', axis=0)]
    ppermute x0 -> x13, starting transfers between devices: none -> 16.3 us  [swap(): return lax.ppermute(block, axis, [(i, i ^ mask) for i in range(size)])]
    all_to_all x3 -> x1, waiting for transfers between devices: 25.3 us -> 10.8 us  [local(): cut = lax.all_to_all(cut, 'expert', 0, 0, tiled=True)]
    all_to_all x3 -> x1, starting transfers between devices: 15.2 us -> 3.51 us  [local(): cut = lax.all_to_all(cut, 'expert', 0, 0, tiled=True)]
    ppermute x0 -> x13, waiting for transfers between devices: none -> 11.6 us  [swap(): return lax.ppermute(block, axis, [(i, i ^ mask) for i in range(size)])]
    all_to_all x1, waiting for transfers between devices: 6.87 us -> 0.01 us  [local(): query_part = lax.all_to_all(query_part, block, 0, 0, tiled=True)]
    dot_general x7 -> x10, matrix products: 16.7 us -> 21.7 us  [the longest x8 9.38 us: local(): jnp.einsum('drc,kc->drk', some, part, preferred_element_type=f32)]
    unnamed x15 -> x57, local copies, waits for them, and re-layouts: 0.81 us -> 2.82 us
  transfers between devices with their start and end apart: 7 -> 18, of which waited for: 5 -> 6; matrix products, arithmetic and copies ran while one was open for 10% -> 18% of each run, Pallas kernels for 0% -> 1%
where the time goes in v2:
time: 171 us; the launch traced here: 170 us
  waiting for transfers between devices  38.3 us (22%)
  starting transfers between devices  33.6 us (20%)
  blocking collectives  29.2 us (17%)
  matrix products  27.4 us (16%)
  local copies, waits for them, and re-layouts  16 us (9%)
  between operations  15.9 us (9%)
  other arithmetic  8.66 us (5%)
    ppermute x13, starting transfers between devices, swap(): return lax.ppermute(block, axis, [(i, i ^ mask) for i in range(size)])  16.3 us
    ppermute x13, waiting for transfers between devices, swap(): return lax.ppermute(block, axis, [(i, i ^ mask) for i in range(size)])  11.6 us
    all_to_all x1, waiting for transfers between devices, local(): cut = lax.all_to_all(cut, 'expert', 0, 0, tiled=True)  10.8 us
    dot_general x8, matrix products, local(): jnp.einsum('drc,kc->drk', some, part, preferred_element_type=f32)  9.38 us
    all_to_all x1, waiting for transfers between devices, local(): combined = lax.all_to_all(combined, block, 0, 0, tiled=True)  8.78 us
    dot_general x1, matrix products, local(): jnp.dot(activated.reshape(activated.shape[0], -1), w_down.reshape(-1, wid...  7.87 us
    all_gather x1, blocking collectives, local(): residual_all = lax.all_gather(residual, 'expert', axis=0)  6.91 us
    all_to_all x1, waiting for transfers between devices, local(): out_latent = lax.all_to_all(out_latent, 'section', 0, 0, tiled=True)  6.34 us
  transfers between devices with their start and end apart: 18, of which 6 were waited for; matrix products, arithmetic and copies ran while one was open for 18% of the time, Pallas kernels for 1%

profile of v2, /device:TPU:0, one launch (start us, length us, event | category | flops | bytes accessed | tf_op | source)
XLA Modules:
  0.0 170.5 jit_solution(7005329583885481088)
XLA Ops:
  8.7 3.0 %collective-permute-start = (bf16[576,112]{0,1:T(8,128)(2,1)}, bf16[576,112]{0,1:T(8,128)(2,1)}, u32[]{:S(2)}, u32[]{:S(2)}) collective-permute-start(bf16[576,112]{0,1:T(8,128)(2,1)} %bitcast.8), channel_id=1, source_target_pairs={{0,16},{16,0},{1,17},{17,1},{2,18},{18,2},{3,19},{19,3},{4,20},{20... | collective-permute-start | bytes 387080 | tf_op jit(solution)/shard_map/ppermute | solution.py:54
  13.2 2.6 %collective-permute-start.3 = (bf16[576,112]{0,1:T(8,128)(2,1)}, bf16[576,112]{0,1:T(8,128)(2,1)}, u32[]{:S(2)}, u32[]{:S(2)}) collective-permute-start(bf16[576,112]{0,1:T(8,128)(2,1)} %bitcast.8), channel_id=1, source_target_pairs={{0,2},{1,3},{2,0},{3,1},{4,6},{5,7},{6,4},{7,5},{8,10},{9,11},{10,... | collective-permute-start | bytes 387080 | tf_op jit(solution)/shard_map/ppermute | solution.py:54
  20.6 5.8 %all-gather.1 = bf16[8,4,16,192]{3,2,1,0:T(8,128)(2,1)S(1)} all-gather(bf16[2,4,16,192]{3,2,1,0:T(8,128)(2,1)S(1)} %copy-done.11), channel_id=3, replica_groups=mesh['groups'=2,'expert'=4,'section'=4] {'expert'}, dimensions={0}, use_global_device_ids=true | all-gather | bytes 245760 | tf_op jit(solution)/shard_map/all_gather | solution.py:200
  29.0 5.9 %all-to-all-start.1 = ((bf16[16,40,144]{2,1,0:T(8,128)(2,1)}), bf16[16,40,144]{2,1,0:T(8,128)(2,1)S(1)}, u32[]{:S(2)}, u32[]{:S(2)}) async-start(bf16[16,40,144]{2,1,0:T(8,128)(2,1)} %pad_maximum_fusion), calls=%async_computation.1 | async-start | bytes 655360 | tf_op jit(solution)/shard_map/all_to_all | solution.py:226
  39.1 6.9 %all-gather = bf16[8,4,3584]{2,1,0:T(4,128)(2,1)} all-gather(bf16[2,4,3584]{2,1,0:T(4,128)(2,1)S(1)} %copy-done.7), channel_id=2, replica_groups=mesh['groups'=2,'expert'=4,'section'=4] {'expert'}, dimensions={0}, use_global_device_ids=true | all-gather | bytes 286720 | tf_op jit(solution)/shard_map/all_gather | solution.py:199
  51.9 5.2 %all-gather.3 = f32[8,4,16]{2,1,0:T(4,128)S(1)} all-gather(f32[2,4,16]{2,1,0:T(4,128)S(1)} %select_reduce_fusion), channel_id=5, replica_groups=mesh['groups'=2,'expert'=4,'section'=4] {'expert'}, dimensions={0}, use_global_device_ids=true | all-gather | bytes 2560 | tf_op jit(solution)/shard_map/all_gather | solution.py:205
  60.4 3.5 %all-to-all-start = ((bf16[4,4,128,224]{2,3,1,0:T(8,128)(2,1)}), bf16[4,4,128,224]{2,3,1,0:T(8,128)(2,1)S(1)}, u32[]{:S(2)}, u32[]{:S(2)}) async-start(bf16[4,4,128,224]{2,3,1,0:T(8,128)(2,1)} %copy.125), calls=%async_computation | async-start | bytes 1835008 | tf_op jit(solution)/shard_map/all_to_all | solution.py:184
  66.1 10.8 %all-to-all-done = bf16[4,4,128,224]{2,3,1,0:T(8,128)(2,1)S(1)} async-done(((bf16[4,4,128,224]{2,3,1,0:T(8,128)(2,1)}), bf16[4,4,128,224]{2,3,1,0:T(8,128)(2,1)S(1)}, u32[]{:S(2)}, u32[]{:S(2)}) %all-to-all-start) | async-done | bytes 917536 | tf_op jit(solution)/shard_map/all_to_all | solution.py:184
  77.3 2.3 %convolution_add_fusion.4 = f32[4,128,576]{1,2,0:T(8,128)} fusion(f32[4,128,576]{1,2,0:T(8,128)S(1)} %fusion.22, bf16[576,112]{0,1:T(8,128)(2,1)} %collective-permute-done, bf16[4,4,128,224]{2,3,1,0:T(8,128)(2,1)S(1)} %all-to-all-done, s32[]{:T(128)S(6)} %select_n.124, s32[]{:T(128)S(6)} %select_n.129), kind=kOutput, calls=%fused_computation.12 | convolution fusion | flops 66355200 | bytes 2603016 | tf_op jit(solution)/shard_map/drc,kc->drk/dot_general | solution.py:253
  79.6 1.7 copy.127
  90.6 4.8 %collective-permute-done.8 = bf16[128,576]{1,0:T(8,128)(2,1)S(1)} collective-permute-done((bf16[128,576]{1,0:T(8,128)(2,1)S(1)}, bf16[128,576]{1,0:T(8,128)(2,1)S(1)}, u32[]{:S(2)}, u32[]{:S(2)}) %collective-permute-start.8) | collective-permute-done | bytes 147488 | tf_op jit(solution)/shard_map/ppermute | solution.py:54
  95.4 2.6 %collective-permute-done.9 = bf16[128,576]{1,0:T(8,128)(2,1)S(1)} collective-permute-done((bf16[128,576]{1,0:T(8,128)(2,1)S(1)}, bf16[128,576]{1,0:T(8,128)(2,1)S(1)}, u32[]{:S(2)}, u32[]{:S(2)}) %collective-permute-start.9) | collective-permute-done | bytes 147488 | tf_op jit(solution)/shard_map/ppermute | solution.py:54
  100.1 4.2 %all-to-all-start.2 = ((bf16[4,1,2,16,512]{4,3,2,1,0:T(8,128)(2,1)}), bf16[4,1,2,16,512]{4,3,2,1,0:T(8,128)(2,1)S(1)}, u32[]{:S(2)}, u32[]{:S(2)}) async-start(bf16[4,1,2,16,512]{4,3,2,1,0:T(8,128)(2,1)} %bitcast.154), calls=%async_computation.2 | async-start | bytes 262144 | tf_op jit(solution)/shard_map/all_to_all | solution.py:270
  104.4 6.3 %all-to-all-done.2 = bf16[4,1,2,16,512]{4,3,2,1,0:T(8,128)(2,1)S(1)} async-done(((bf16[4,1,2,16,512]{4,3,2,1,0:T(8,128)(2,1)}), bf16[4,1,2,16,512]{4,3,2,1,0:T(8,128)(2,1)S(1)}, u32[]{:S(2)}, u32[]{:S(2)}) %all-to-all-start.2) | async-done | bytes 131104 | tf_op jit(solution)/shard_map/all_to_all | solution.py:270
  111.5 2.3 %fusion.15 = bf16[4,2,16,128]{3,0,1,2:T(4,128)(2,1)S(1)} fusion(bf16[4,16,128,128,1]{3,2,1,0,4:T(8,128)(2,1)} %bitcast.179, bf16[4,2,16,4,128]{4,3,2,1,0:T(4,128)(2,1)S(1)} %broadcast_select_fusion), kind=kOutput, calls=%fused_computation.22 | convolution fusion | flops 16793600 | bytes 2260992 | tf_op jit(solution)/shard_map/othxc,xhvc->othv/dot_general | solution.py:275
  113.8 5.4 %all_gather.36 = bf16[32,2048]{1,0:T(8,128)(2,1)S(1)} all-gather(bf16[8,2048]{1,0:T(8,128)(2,1)S(1)} %bitcast.171), channel_id=1, replica_groups=mesh['groups'=2,'expert'=4,'section'=4] {'expert'}, dimensions={0}, use_global_device_ids=true | all-gather | bytes 163840 | tf_op jit(solution)/shard_map/all_gather | solution.py:279
  119.2 2.8 %convolution_convert_fusion.1 = bf16[32,896]{1,0:T(8,128)(2,1)S(1)} fusion(bf16[32,2048]{1,0:T(8,128)(2,1)S(1)} %all_gather.36, bf16[2048,896]{1,0:T(8,128)(2,1)} %param.29), kind=kOutput, calls=%fused_computation.19 | convolution fusion | flops 117469184 | bytes 3858432 | tf_op jit(solution)/shard_map/dot_general | solution.py:281
  124.2 2.2 %collective-permute-start.12 = (bf16[32,896]{1,0:T(8,128)(2,1)S(1)}, bf16[32,896]{1,0:T(8,128)(2,1)S(1)}, u32[]{:S(2)}, u32[]{:S(2)}) collective-permute-start(bf16[32,896]{1,0:T(8,128)(2,1)S(1)} %convolution_convert_fusion.1), channel_id=1, source_target_pairs={{0,3},{1,2},{2,1},{3,0},{4,7},{5,6},{6,5},{7,4},{8,11},{9,10},{10,... | collective-permute-start | bytes 172040 | tf_op jit(solution)/shard_map/ppermute | solution.py:54
  126.6 4.2 %collective-permute-done.11 = bf16[32,896]{1,0:T(8,128)(2,1)S(1)} collective-permute-done((bf16[32,896]{1,0:T(8,128)(2,1)S(1)}, bf16[32,896]{1,0:T(8,128)(2,1)S(1)}, u32[]{:S(2)}, u32[]{:S(2)}) %collective-permute-start.11) | collective-permute-done | bytes 57376 | tf_op jit(solution)/shard_map/ppermute | solution.py:54
  130.9 5.9 %all_gather.37 = bf16[32,3584]{1,0:T(8,128)(2,1)S(1)} all-gather(bf16[32,896]{1,0:T(8,128)(2,1)S(1)} %add_convert_fusion), channel_id=1, replica_groups=mesh['groups'=2,'expert'=4,'section'=4] {'expert'}, dimensions={1}, use_global_device_ids=true | all-gather | bytes 286720 | tf_op jit(solution)/shard_map/all_gather | solution.py:283
  137.0 4.5 %fusion.96 = f32[32,4,256]{2,0,1:T(8,128)S(1)} fusion(bf16[4,3584,256]{2,1,0:T(8,128)(2,1)} %param.31, f32[32,3584]{1,0:T(8,128)S(1)} %get-tuple-element.19, f32[3584]{0:T(1024)S(1)} %copy-done.8, f32[32]{0:T(128)S(1)} %add_rsqrt_fusion.1), kind=kOutput, calls=%fused_computation.156 | convolution fusion | flops 235225088 | bytes 7944320 | tf_op jit(solution)/shard_map/td,xdf->txf/dot_general | solution.py:288
  141.4 7.9 %fusion = bf16[32,3584]{1,0:T(8,128)(2,1)S(1)} fusion(bf16[4,256,3584]{2,1,0:T(8,128)(2,1)} %param.33, bf16[4,3584,256]{2,1,0:T(8,128)(2,1)} %param.32, f32[32,4,256]{2,0,1:T(8,128)S(1)} %fusion.96, f32[32,4]{0,1:T(4,128)S(1)} %copy.145, f32[32,3584]{1,0:T(8,128)S(1)} %get-tuple-element.19, f32[3584]{0:T(1024)S(1)} %copy-done.8, f32[32]{0:T(128)S(1)} %add_rsqrt_fusion.1), kind=kOutput, calls=%fused_computation.3 | convolution fusion | flops 470450176 | bytes 15514240 | tf_op jit(solution)/shard_map/dot_general | solution.py:293
  150.3 3.5 %all-to-all-start.3 = ((bf16[16,4,2,896]{3,2,1,0:T(2,128)(2,1)}), bf16[16,4,2,896]{3,2,1,0:T(2,128)(2,1)S(1)}, u32[]{:S(2)}, u32[]{:S(2)}) async-start(bf16[16,4,2,896]{3,2,1,0:T(2,128)(2,1)} %bitcast.63), calls=%async_computation.3 | async-start | bytes 458752 | tf_op jit(solution)/shard_map/all_to_all | solution.py:301
  154.0 8.8 %all-to-all-done.3 = bf16[16,4,2,896]{3,2,1,0:T(2,128)(2,1)S(1)} async-done(((bf16[16,4,2,896]{3,2,1,0:T(2,128)(2,1)}), bf16[16,4,2,896]{3,2,1,0:T(2,128)(2,1)S(1)}, u32[]{:S(2)}, u32[]{:S(2)}) %all-to-all-start.3) | async-done | bytes 229408 | tf_op jit(solution)/shard_map/all_to_all | solution.py:301
  (170 shorter events, 41.5 us)
Async XLA Ops:
  6.5 14.0 %copy-start.11 = (bf16[2,4,16,192]{3,2,1,0:T(8,128)(2,1)S(1)}, bf16[2,4,16,192]{3,2,1,0:T(8,128)(2,1)}, u32[]{:S(2)}) copy-start(bf16[2,4,16,192]{3,2,1,0:T(8,128)(2,1)} %param.21) | copy-start | bytes 147460
  8.7 68.6 %collective-permute-start = (bf16[576,112]{0,1:T(8,128)(2,1)}, bf16[576,112]{0,1:T(8,128)(2,1)}, u32[]{:S(2)}, u32[]{:S(2)}) collective-permute-start(bf16[576,112]{0,1:T(8,128)(2,1)} %bitcast.8), channel_id=1, source_target_pairs={{0,16},{16,0},{1,17},{17,1},{2,18},{18,2},{3,19},{19,3},{4,20},{20... | collective-permute-start | bytes 387080 | tf_op jit(solution)/shard_map/ppermute | solution.py:54
  11.6 46.2 %collective-permute-start.1 = (bf16[576,112]{0,1:T(8,128)(2,1)}, bf16[576,112]{0,1:T(8,128)(2,1)}, u32[]{:S(2)}, u32[]{:S(2)}) collective-permute-start(bf16[576,112]{0,1:T(8,128)(2,1)} %bitcast.8), channel_id=1, source_target_pairs={{0,1},{1,0},{2,3},{3,2},{4,5},{5,4},{6,7},{7,6},{8,9},{9,8},{10,11... | collective-permute-start | bytes 387080 | tf_op jit(solution)/shard_map/ppermute | solution.py:54
  13.2 45.2 %collective-permute-start.3 = (bf16[576,112]{0,1:T(8,128)(2,1)}, bf16[576,112]{0,1:T(8,128)(2,1)}, u32[]{:S(2)}, u32[]{:S(2)}) collective-permute-start(bf16[576,112]{0,1:T(8,128)(2,1)} %bitcast.8), channel_id=1, source_target_pairs={{0,2},{1,3},{2,0},{3,1},{4,6},{5,7},{6,4},{7,5},{8,10},{9,11},{10,... | collective-permute-start | bytes 387080 | tf_op jit(solution)/shard_map/ppermute | solution.py:54
  15.8 44.1 %collective-permute-start.5 = (bf16[576,112]{0,1:T(8,128)(2,1)}, bf16[576,112]{0,1:T(8,128)(2,1)}, u32[]{:S(2)}, u32[]{:S(2)}) collective-permute-start(bf16[576,112]{0,1:T(8,128)(2,1)} %bitcast.8), channel_id=1, source_target_pairs={{0,3},{1,2},{2,1},{3,0},{4,7},{5,6},{6,5},{7,4},{8,11},{9,10},{10,... | collective-permute-start | bytes 387080 | tf_op jit(solution)/shard_map/ppermute | solution.py:54
  28.1 18.4 %copy-start.19 = (bf16[512]{0:T(512)(128)(2,1)S(1)}, bf16[512]{0:T(512)(128)(2,1)}, u32[]{:S(2)}) copy-start(bf16[512]{0:T(512)(128)(2,1)} %param.26) | copy-start | bytes 3076
  28.2 18.4 %copy-start.4 = (bf16[1,128,3584]{2,1,0:T(8,128)(2,1)S(1)}, bf16[1,128,3584]{2,1,0:T(8,128)(2,1)}, u32[]{:S(2)}) copy-start(bf16[1,128,3584]{2,1,0:T(8,128)(2,1)} %param.17) | copy-start | bytes 2752516
  29.0 31.5 %all-to-all-start.1 = ((bf16[16,40,144]{2,1,0:T(8,128)(2,1)}), bf16[16,40,144]{2,1,0:T(8,128)(2,1)S(1)}, u32[]{:S(2)}, u32[]{:S(2)}) async-start(bf16[16,40,144]{2,1,0:T(8,128)(2,1)} %pad_maximum_fusion), calls=%async_computation.1 | async-start | bytes 655360 | tf_op jit(solution)/shard_map/all_to_all | solution.py:226
  34.9 76.6 %all-gather.6.cloned.1.call-start = ((), (), s32[]{:S(2)}) async-start(), calls=%async_computation.4 | async-start | bytes 2621440 | tf_op jit(solution)/shard_map/all_gather | solution.py:188
  57.8 26.0 %collective-permute-start.2 = (bf16[576,112]{0,1:T(8,128)(2,1)}, bf16[576,112]{0,1:T(8,128)(2,1)}, u32[]{:S(2)}, u32[]{:S(2)}) collective-permute-start(bf16[576,112]{0,1:T(8,128)(2,1)} %collective-permute-done.1), channel_id=1, source_target_pairs={{0,16},{16,0},{1,17},{17,1},{2,18},{18,2},{3,19},{19,3},{4,20},{20... | collective-permute-start | bytes 387080 | tf_op jit(solution)/shard_map/ppermute | solution.py:54
  58.4 28.0 %collective-permute-start.4 = (bf16[576,112]{0,1:T(8,128)(2,1)}, bf16[576,112]{0,1:T(8,128)(2,1)}, u32[]{:S(2)}, u32[]{:S(2)}) collective-permute-start(bf16[576,112]{0,1:T(8,128)(2,1)} %collective-permute-done.3), channel_id=1, source_target_pairs={{0,16},{16,0},{1,17},{17,1},{2,18},{18,2},{3,19},{19,3},{4,20},{20... | collective-permute-start | bytes 387080 | tf_op jit(solution)/shard_map/ppermute | solution.py:54
  59.9 27.8 %collective-permute-start.6 = (bf16[576,112]{0,1:T(8,128)(2,1)}, bf16[576,112]{0,1:T(8,128)(2,1)S(1)}, u32[]{:S(2)}, u32[]{:S(2)}) collective-permute-start(bf16[576,112]{0,1:T(8,128)(2,1)} %collective-permute-done.5), channel_id=1, source_target_pairs={{0,16},{16,0},{1,17},{17,1},{2,18},{18,2},{3,19},{19,3},{4,20},{20... | collective-permute-start | bytes 387080 | tf_op jit(solution)/shard_map/ppermute | solution.py:54
  60.4 16.5 %all-to-all-start = ((bf16[4,4,128,224]{2,3,1,0:T(8,128)(2,1)}), bf16[4,4,128,224]{2,3,1,0:T(8,128)(2,1)S(1)}, u32[]{:S(2)}, u32[]{:S(2)}) async-start(bf16[4,4,128,224]{2,3,1,0:T(8,128)(2,1)} %copy.125), calls=%async_computation | async-start | bytes 1835008 | tf_op jit(solution)/shard_map/all_to_all | solution.py:184
  88.2 2.3 %collective-permute-start.7 = (bf16[128,576]{1,0:T(8,128)(2,1)S(1)}, bf16[128,576]{1,0:T(8,128)(2,1)S(1)}, u32[]{:S(2)}, u32[]{:S(2)}) collective-permute-start(bf16[128,576]{1,0:T(8,128)(2,1)S(1)} %get-tuple-element.22), channel_id=1, source_target_pairs={{0,4},{4,0},{8,12},{12,8},{1,5},{5,1},{9,13},{13,9},{2,6},{6,2},{1... | collective-permute-start | bytes 442376 | tf_op jit(solution)/shard_map/ppermute | solution.py:54
  88.3 7.1 %collective-permute-start.8 = (bf16[128,576]{1,0:T(8,128)(2,1)S(1)}, bf16[128,576]{1,0:T(8,128)(2,1)S(1)}, u32[]{:S(2)}, u32[]{:S(2)}) collective-permute-start(bf16[128,576]{1,0:T(8,128)(2,1)S(1)} %get-tuple-element.21), channel_id=1, source_target_pairs={{0,8},{4,12},{8,0},{12,4},{1,9},{5,13},{9,1},{13,5},{2,10},{6,14},... | collective-permute-start | bytes 442376 | tf_op jit(solution)/shard_map/ppermute | solution.py:54
  88.8 9.2 %collective-permute-start.9 = (bf16[128,576]{1,0:T(8,128)(2,1)S(1)}, bf16[128,576]{1,0:T(8,128)(2,1)S(1)}, u32[]{:S(2)}, u32[]{:S(2)}) collective-permute-start(bf16[128,576]{1,0:T(8,128)(2,1)S(1)} %get-tuple-element.20), channel_id=1, source_target_pairs={{0,12},{4,8},{8,4},{12,0},{1,13},{5,9},{9,5},{13,1},{2,14},{6,10},... | collective-permute-start | bytes 442376 | tf_op jit(solution)/shard_map/ppermute | solution.py:54
  90.3 14.1 %copy-start.26 = (s32[4]{0:T(128)S(1)}, s32[4]{0:T(128)}, u32[]{:S(2)}) copy-start(s32[4]{0:T(128)} %copy-done.25) | copy-start | bytes 52
  100.1 10.6 %all-to-all-start.2 = ((bf16[4,1,2,16,512]{4,3,2,1,0:T(8,128)(2,1)}), bf16[4,1,2,16,512]{4,3,2,1,0:T(8,128)(2,1)S(1)}, u32[]{:S(2)}, u32[]{:S(2)}) async-start(bf16[4,1,2,16,512]{4,3,2,1,0:T(8,128)(2,1)} %bitcast.154), calls=%async_computation.2 | async-start | bytes 262144 | tf_op jit(solution)/shard_map/all_to_all | solution.py:270
  119.2 17.5 %copy-start.1 = (f32[32,3584]{1,0:T(8,128)S(1)}, f32[32,3584]{1,0:T(8,128)}, u32[]{:S(2)}) copy-start(f32[32,3584]{1,0:T(8,128)} %reshape.538) | copy-start | bytes 1376260
  122.0 15.0 %copy-start.8 = (f32[3584]{0:T(1024)S(1)}, f32[3584]{0:T(1024)}, u32[]{:S(2)}) copy-start(f32[3584]{0:T(1024)} %convert_element_type.214) | copy-start | bytes 43012
  122.0 4.6 %collective-permute-start.10 = (bf16[32,896]{1,0:T(8,128)(2,1)S(1)}, bf16[32,896]{1,0:T(8,128)(2,1)S(1)}, u32[]{:S(2)}, u32[]{:S(2)}) collective-permute-start(bf16[32,896]{1,0:T(8,128)(2,1)S(1)} %convolution_convert_fusion.1), channel_id=1, source_target_pairs={{0,1},{1,0},{2,3},{3,2},{4,5},{5,4},{6,7},{7,6},{8,9},{9,8},{10,11... | collective-permute-start | bytes 172040 | tf_op jit(solution)/shard_map/ppermute | solution.py:54
  123.0 7.9 %collective-permute-start.11 = (bf16[32,896]{1,0:T(8,128)(2,1)S(1)}, bf16[32,896]{1,0:T(8,128)(2,1)S(1)}, u32[]{:S(2)}, u32[]{:S(2)}) collective-permute-start(bf16[32,896]{1,0:T(8,128)(2,1)S(1)} %convolution_convert_fusion.1), channel_id=1, source_target_pairs={{0,2},{1,3},{2,0},{3,1},{4,6},{5,7},{6,4},{7,5},{8,10},{9,11},{10,... | collective-permute-start | bytes 172040 | tf_op jit(solution)/shard_map/ppermute | solution.py:54
  124.2 6.6 %collective-permute-start.12 = (bf16[32,896]{1,0:T(8,128)(2,1)S(1)}, bf16[32,896]{1,0:T(8,128)(2,1)S(1)}, u32[]{:S(2)}, u32[]{:S(2)}) collective-permute-start(bf16[32,896]{1,0:T(8,128)(2,1)S(1)} %convolution_convert_fusion.1), channel_id=1, source_target_pairs={{0,3},{1,2},{2,1},{3,0},{4,7},{5,6},{6,5},{7,4},{8,11},{9,10},{10,... | collective-permute-start | bytes 172040 | tf_op jit(solution)/shard_map/ppermute | solution.py:54
  150.3 12.5 %all-to-all-start.3 = ((bf16[16,4,2,896]{3,2,1,0:T(2,128)(2,1)}), bf16[16,4,2,896]{3,2,1,0:T(2,128)(2,1)S(1)}, u32[]{:S(2)}, u32[]{:S(2)}) async-start(bf16[16,4,2,896]{3,2,1,0:T(2,128)(2,1)} %bitcast.63), calls=%async_computation.3 | async-start | bytes 458752 | tf_op jit(solution)/shard_map/all_to_all | solution.py:301
  (21 other events, 111.1 us)
Sparse Core Ops, SparseCore 0:
  37.3 23.0 all-gather.5

commit v3 on v2

--- a/solution.py
+++ b/solution.py
@@ -2,6 +2,7 @@
 
 import jax
 import jax.numpy as jnp
+import numpy as np
 from jax import lax
 from jax.experimental import pallas as pl
 from jax.experimental.pallas import tpu as pltpu
@@ -54,22 +55,81 @@
     return lax.ppermute(block, axis, [(i, i ^ mask) for i in range(size)])
 
 
-def exchange(blocks, axis):
-    here = lax.axis_index(axis)
-    landed = [lax.dynamic_index_in_dim(blocks, here, 0, keepdims=False)]
-    for mask in range(1, lax.axis_size(axis)):
-        sent = lax.dynamic_index_in_dim(blocks, here ^ mask, 0, keepdims=False)
-        landed.append(swap(sent, axis, mask))
-    return landed
+def deliver(blocks, axis):
+    return [blocks[0]] + [swap(blocks[mask], axis, mask) for mask in range(1, len(blocks))]
 
 
 def spread(block, axis):
     return [block] + [swap(block, axis, mask) for mask in range(1, lax.axis_size(axis))]
 
 
-def attend_kernel(parts, heads_rows, steps, latent, score_scale, *refs):
+def params():
+    return pltpu.CompilerParams(vmem_limit_bytes=40 * 1024 * 1024)
+
+
+def cut_kernel(sections, experts, piece, x_ref, *refs):
+    out_refs, held = refs[:experts], refs[experts]
+    rank = lax.axis_index("expert")
+    for target in range(experts):
+        for section in range(sections):
+            at = (section * experts + target) * piece
+            held[target, section] = x_ref[:, at : at + piece]
+    for mask, ref in enumerate(out_refs):
+        ref[...] = held[rank ^ mask]
+
+
+def cut_columns(x, sections, experts):
+    rows, width = x.shape
+    piece = width // (sections * experts)
+    block = jax.ShapeDtypeStruct((sections, rows, piece), x.dtype)
+    return pl.pallas_call(
+        functools.partial(cut_kernel, sections, experts, piece),
+        out_shape=[block] * experts,
+        scratch_shapes=[pltpu.VMEM((experts,) + block.shape, x.dtype)],
+        compiler_params=params(),
+        name="cut_columns",
+    )(x)
+
+
+def project_kernel(count, sections, groups, *refs):
+    x_refs = refs[:count]
+    w_refs = refs[count : count + sections * groups]
+    out_refs = refs[count + sections * groups :]
+    section_rank = lax.axis_index("section")
+    group_rank = lax.axis_index("groups")
+    rows = x_refs[0].shape[1]
+    total = 0
+    for mask in range(sections):
+        held = [w_refs[mask * groups + other][...] for other in range(groups)]
+        columns = []
+        for group in range(groups):
+            chosen = held[0]
+            for other in range(1, groups):
+                chosen = jnp.where((group_rank ^ other) == group, held[other], chosen)
+            columns.append(chosen)
+        weights = jnp.concatenate(columns, axis=1)
+        x = jnp.concatenate([ref[section_rank ^ mask] for ref in x_refs], axis=0)
+        total = total + lax.dot_general(
+            x, weights, (((1,), (1,)), ((), ())), preferred_element_type=jnp.float32
+        )
+    for index, ref in enumerate(out_refs):
+        ref[...] = total[index * rows : (index + 1) * rows].astype(ref.dtype)
+
+
+def project(blocks, w_parts, sections, groups):
+    out = jax.ShapeDtypeStruct((blocks[0].shape[1], w_parts[0].shape[0]), jnp.bfloat16)
+    return pl.pallas_call(
+        functools.partial(project_kernel, len(blocks), sections, groups),
+        out_shape=[out] * len(blocks),
+        compiler_params=params(),
+        name="project",
+    )(*blocks, *w_parts)
+
+
+def attend_kernel(parts, sections, heads, steps, latent, score_scale, *refs):
     part_refs = refs[:parts]
-    length_ref, gain_ref, cosine_ref, sine_ref, query_ref, recent_ref, out_ref = refs[parts:]
+    length_ref, gain_ref, cosine_ref, sine_ref, query_ref, recent_ref = refs[parts : parts + 6]
+    out_refs, held = refs[parts + 6 : -1], refs[-1]
     f32, bf16 = jnp.float32, jnp.bfloat16
     nt = (((1,), (1,)), ((), ()))
     projected = part_refs[0][0].astype(f32)
@@ -91,9 +151,12 @@
     fresh = lax.dot_general(query, recent, nt, preferred_element_type=f32)
     place = lax.broadcasted_iota(jnp.int32, scores.shape, 1)
     scores = jnp.where(place < length_ref[pl.program_id(0)], scores * score_scale, masked_value)
-    step = lax.broadcasted_iota(jnp.int32, fresh.shape, 0) // heads_rows
+    row = lax.broadcasted_iota(jnp.int32, fresh.shape, 0)
     place = lax.broadcasted_iota(jnp.int32, fresh.shape, 1)
-    fresh = jnp.where(place <= step, fresh * score_scale, masked_value)
+    seen = place < 1
+    for step in range(1, steps):
+        seen = seen | ((place <= step) & (row >= step * sections * heads))
+    fresh = jnp.where(seen, fresh * score_scale, masked_value)
     most = jnp.maximum(
         jnp.max(scores, axis=-1, keepdims=True), jnp.max(fresh, axis=-1, keepdims=True)
     )
@@ -104,24 +167,33 @@
     fresh = (fresh / total).astype(bf16)
     mixed = jnp.dot(scores, keys, preferred_element_type=f32)
     mixed = mixed + jnp.dot(fresh, recent[:, :latent], preferred_element_type=f32)
-    out_ref[0] = mixed.astype(bf16)
-
-
-def attend(parts, lengths, kv_gain, query_cat, recent, steps, score_scale):
+    mixed = mixed.astype(bf16)
+    for section in range(sections):
+        for step in range(steps):
+            at = (step * sections + section) * heads
+            held[section, step * heads : (step + 1) * heads] = mixed[at : at + heads]
+    rank = lax.axis_index("section")
+    for mask, ref in enumerate(out_refs):
+        ref[0] = held[rank ^ mask]
+
+
+def attend(parts, lengths, kv_gain, query_cat, recent, steps, sections, score_scale):
     prompts, positions, width = parts[0].shape
     latent = kv_gain.shape[0]
     rows = query_cat.shape[1]
+    heads = rows // (steps * sections)
     cosine, sine = rotation(jnp.arange(positions), width - latent)
     cosine = jnp.concatenate([cosine, cosine], axis=-1)
     sine = jnp.concatenate([-sine, sine], axis=-1)
     one = lambda shape: pl.BlockSpec((1,) + shape, lambda i: (i, 0, 0))
     whole = lambda shape: pl.BlockSpec(shape, lambda i: (0, 0))
+    out = (steps * heads, latent)
     return pl.pallas_call(
         functools.partial(
-            attend_kernel, len(parts), rows // steps, steps, latent, score_scale
+            attend_kernel, len(parts), sections, heads, steps, latent, score_scale
         ),
         grid=(prompts,),
-        out_shape=jax.ShapeDtypeStruct((prompts, rows, latent), jnp.bfloat16),
+        out_shape=[jax.ShapeDtypeStruct((prompts,) + out, jnp.bfloat16)] * sections,
         in_specs=[one((positions, width))] * len(parts)
         + [
             pl.BlockSpec(memory_space=pltpu.SMEM),
@@ -131,10 +203,143 @@
             one((rows, width)),
             one(recent.shape[1:]),
         ],
-        out_specs=one((rows, latent)),
-        compiler_params=pltpu.CompilerParams(vmem_limit_bytes=32 * 1024 * 1024),
+        out_specs=[one(out)] * sections,
+        scratch_shapes=[pltpu.VMEM((sections,) + out, jnp.bfloat16)],
+        compiler_params=params(),
         name="attend",
     )(*parts, lengths, kv_gain[None], cosine, sine, query_cat, recent)
+
+
+def output_kernel(order_ref, value_ref, weight_ref, out_ref, ordered, total):
+    step = pl.program_id(0)
+    depth = weight_ref.shape[0]
+
+    @pl.when(step == 0)
+    def _():
+        moved = jnp.dot(order_ref[...], value_ref[...], preferred_element_type=jnp.float32)
+        moved = moved.astype(jnp.bfloat16)
+        for index in range(ordered.shape[0]):
+            ordered[index] = moved[:, index * depth : (index + 1) * depth]
+        total[...] = jnp.zeros_like(total)
+
+    total[...] += jnp.dot(ordered[step], weight_ref[...], preferred_element_type=jnp.float32)
+
+    @pl.when(step == pl.num_programs(0) - 1)
+    def _():
+        out_ref[...] = total[...].astype(out_ref.dtype)
+
+
+def output_product(values, order, weight):
+    rows, depth = values.shape
+    width = weight.shape[1]
+    pieces = 4
+    whole = lambda shape: pl.BlockSpec(shape, lambda i: (0, 0))
+    return pl.pallas_call(
+        output_kernel,
+        grid=(pieces,),
+        out_shape=jax.ShapeDtypeStruct((rows, width), jnp.bfloat16),
+        in_specs=[
+            whole(order.shape),
+            whole(values.shape),
+            pl.BlockSpec((depth // pieces, width), lambda i: (i, 0)),
+        ],
+        out_specs=whole((rows, width)),
+        scratch_shapes=[
+            pltpu.VMEM((pieces, rows, depth // pieces), jnp.bfloat16),
+            pltpu.VMEM((rows, width), jnp.float32),
+        ],
+        compiler_params=params(),
+        name="output_product",
+    )(order, values, weight)
+
+
+def expert_kernel(experts, sections, *refs):
+    attended_ref, hidden_ref, gain_ref, route_ref, gate_ref, up_ref, down_ref = refs[:7]
+    out_refs, own_ref = refs[7 : 7 + experts], refs[7 + experts]
+    gate_held, up_held, down_held, staged, sems = refs[8 + experts :]
+    f32, bf16 = jnp.float32, jnp.bfloat16
+    count = gate_held.shape[0]
+    copies = []
+    for x in range(count):
+        for kind, (source, held) in enumerate(
+            ((gate_ref, gate_held), (up_ref, up_held), (down_ref, down_held))
+        ):
+            copies.append(pltpu.make_async_copy(source.at[x], held.at[x], sems.at[x, kind]))
+            copies[-1].start()
+    rank = lax.axis_index("expert")
+    attended = jnp.concatenate([attended_ref[i] for i in range(experts)], axis=1).astype(f32)
+    mixed = hidden_ref[...].astype(f32) + attended
+    scale = lax.rsqrt(jnp.mean(mixed * mixed, axis=-1, keepdims=True) + epsilon)
+    rows_in = (mixed * scale * gain_ref[...].astype(f32)).astype(bf16)
+    block, column = staged.shape[2:]
+
+    def stage(values):
+        for owner in range(experts):
+            for section in range(sections):
+                staged[owner, section] = values[
+                    owner * block : (owner + 1) * block, section * column : (section + 1) * column
+                ]
+
+    stage(attended)
+    own_ref[...] = staged[rank].astype(bf16)
+    total = 0
+    for x in range(count):
+        copies[3 * x].wait()
+        gate = jnp.dot(rows_in, gate_held[x], preferred_element_type=f32)
+        copies[3 * x + 1].wait()
+        up = jnp.dot(rows_in, up_held[x], preferred_element_type=f32)
+        hidden = gate / (1.0 + jnp.exp(-gate)) * up * route_ref[:, x : x + 1]
+        copies[3 * x + 2].wait()
+        total = total + jnp.dot(hidden.astype(bf16), down_held[x], preferred_element_type=f32)
+    stage(total)
+    for mask, ref in enumerate(out_refs):
+        ref[...] = staged[rank ^ mask].astype(bf16)
+
+
+def run_experts(attended, hidden, gain, route, w_gate, w_up, w_down, sections):
+    experts, rows, _ = attended.shape
+    width = hidden.shape[1]
+    shape = (sections, rows // experts, width // sections)
+    out = jax.ShapeDtypeStruct(shape, jnp.bfloat16)
+    held = pl.BlockSpec(memory_space=pltpu.VMEM)
+    away = pl.BlockSpec(memory_space=pl.ANY)
+    outs = pl.pallas_call(
+        functools.partial(expert_kernel, experts, sections),
+        out_shape=[out] * (experts + 1),
+        in_specs=[held] * 4 + [away] * 3,
+        scratch_shapes=[
+            pltpu.VMEM(w_gate.shape, w_gate.dtype),
+            pltpu.VMEM(w_up.shape, w_up.dtype),
+            pltpu.VMEM(w_down.shape, w_down.dtype),
+            pltpu.VMEM((experts,) + shape, jnp.float32),
+            pltpu.SemaphoreType.DMA((w_gate.shape[0], 3)),
+        ],
+        compiler_params=params(),
+        name="run_experts",
+    )(attended, hidden, gain[None], route, w_gate, w_up, w_down)
+    return outs[:experts], outs[experts]
+
+
+def fold_kernel(sections, count, *refs):
+    in_refs, out_refs, held = refs[:count], refs[count:-1], refs[-1]
+    rank = lax.axis_index("section")
+    total = in_refs[0][...].astype(jnp.float32)
+    for ref in in_refs[1:]:
+        total = total + ref[...].astype(jnp.float32)
+    held[...] = total
+    for mask, ref in enumerate(out_refs):
+        ref[...] = held[rank ^ mask].astype(ref.dtype)
+
+
+def fold(blocks):
+    sections, rows, column = blocks[0].shape
+    return pl.pallas_call(
+        functools.partial(fold_kernel, sections, len(blocks)),
+        out_shape=[jax.ShapeDtypeStruct((rows, column), jnp.bfloat16)] * sections,
+        scratch_shapes=[pltpu.VMEM((sections, rows, column), jnp.float32)],
+        compiler_params=params(),
+        name="fold",
+    )(*blocks)
 
 
 def local(
@@ -175,17 +380,15 @@
     piece = depth // (groups * experts)
     everyone = experts * sections
 
+    rows = prompt_count * full_length
     w_turned = w_dkv.T
     w_piece = lax.dynamic_slice_in_dim(
         w_turned, (expert_rank * groups + group_rank) * piece, piece, 1
     )
-    rows = prompt_count * full_length
-    cut = prompts.reshape(rows, sections, experts, groups * piece).transpose(2, 1, 0, 3)
-    cut = lax.all_to_all(cut, "expert", 0, 0, tiled=True)
     w_parts = spread(w_piece, "section")
-    w_parts = [spread(part, "groups") for part in w_parts]
-
-    uv_full = lax.all_gather(w_uv, "expert", axis=0)
+    cut = cut_columns(prompts.reshape(rows, width), sections, experts)
+    cut = deliver(cut, "expert")
+    w_parts = [part for half in w_parts for part in spread(half, "groups")]
 
     table = owners.reshape(experts, tokens_here)
     length_table = lengths.reshape(experts, tokens_here)
@@ -196,13 +399,32 @@
         length_table, (expert_rank, section_rank * prompt_count), (1, prompt_count)
     )[0]
 
-    residual_all = lax.all_gather(residual, "expert", axis=0)
-    queries_all = lax.all_gather(queries, "expert", axis=0)
     expert_total = w_gate.shape[0] * experts
     match_table = (expert_ids[..., None] == jnp.arange(expert_total)).astype(f32)
     weights = route_scale * route_scores / jnp.sum(route_scores, axis=-1, keepdims=True)
-    weight_map = jnp.sum(weights[..., None] * match_table, axis=2)
-    weights_all = lax.all_gather(weight_map, "expert", axis=0)
+    weight_map = jnp.sum(weights[..., None] * match_table, axis=2).reshape(-1, expert_total)
+    weight_high = weight_map.astype(bf16)
+    weight_low = (weight_map - weight_high.astype(f32)).astype(bf16)
+    own_rows = steps * tokens_here
+    packed = jnp.concatenate(
+        [
+            residual.reshape(own_rows, width),
+            queries.reshape(own_rows, -1),
+            weight_high,
+            weight_low,
+        ],
+        axis=1,
+    )
+    packed, cut[0] = lax.optimization_barrier((packed, cut[0]))
+    packed = lax.all_gather(packed, "expert", axis=0, tiled=True)
+    hidden = packed[:, :width]
+    at = width + queries.shape[2] * queries.shape[3]
+    queries_all = packed[:, width:at].reshape((experts,) + queries.shape)
+    weights_all = packed[:, at : at + expert_total].astype(f32)
+    weights_all = weights_all + packed[:, at + expert_total :].astype(f32)
+    route = lax.dynamic_slice_in_dim(
+        weights_all, expert_rank * w_gate.shape[0], w_gate.shape[0], 1
+    )
 
     picked = jnp.take_along_axis(
         queries_all.transpose(2, 0, 1, 3, 4), table[:, :, None, None, None], axis=1
@@ -245,16 +467,10 @@
     recent = latent_rows(fresh, kv_gain, token_pos)
     recent = jnp.pad(recent, ((0, 0), (0, -steps % 16), (0, 0)))
 
-    partial = 0
-    for mask, pair in enumerate(w_parts):
-        share = lax.dynamic_index_in_dim(cut, section_rank ^ mask, 1, keepdims=False)
-        for other, part in enumerate(pair):
-            some = lax.dynamic_slice_in_dim(share, (group_rank ^ other) * piece, piece, 2)
-            partial = partial + jnp.einsum(
-                "drc,kc->drk", some, part, preferred_element_type=f32
-            )
-    parts = exchange(partial.astype(bf16), "expert")
-    parts = [part.reshape(prompt_count, full_length, cache_width) for part in parts]
+    uv_full = lax.all_gather(w_uv, "expert", axis=0)
+    away = project(cut[1:], w_parts, sections, groups)
+    near = project(cut[:1], w_parts, sections, groups)
+    parts = [part.reshape(prompt_count, full_length, -1) for part in deliver(near + away, "expert")]
     out_latent = attend(
         parts,
         my_length,
@@ -262,15 +478,15 @@
         query_cat.reshape(prompt_count, -1, cache_width),
         recent,
         steps,
+        sections,
         queries.shape[-1] ** (-0.5),
     )
 
-    out_latent = out_latent.reshape(prompt_count, steps, sections, heads, latent)
-    out_latent = out_latent.transpose(2, 0, 1, 3, 4)
-    out_latent = lax.all_to_all(out_latent, "section", 0, 0, tiled=True)
+    out_latent = jnp.stack(deliver(out_latent, "section"))
     row = lax.dynamic_slice_in_dim(table, expert_rank, 1, 0)[0]
-    out_latent = out_latent.reshape(tokens_here, steps, heads, latent)
-    out_latent = jnp.take(out_latent, jnp.argsort(row), axis=0)
+    source = jnp.argsort(row)
+    source = (section_rank ^ (source // prompt_count)) * prompt_count + source % prompt_count
+    out_latent = jnp.take(out_latent.reshape(tokens_here, steps, heads, -1), source, axis=0)
     out_latent = out_latent.reshape(tokens_here, steps, heads, experts, chunk)
     head_values = jnp.einsum(
         "othxc,xhvc->othv", out_latent, uv_full, preferred_element_type=f32
@@ -278,35 +494,22 @@
     head_values = head_values.reshape(tokens_here * steps, -1)
     head_values = lax.all_gather(head_values, "expert", axis=0, tiled=True)
 
-    attended = jnp.dot(head_values, w_o, preferred_element_type=f32).astype(bf16)
+    total_rows = head_values.shape[0]
+    order = np.arange(total_rows).reshape(experts, tokens_here, steps).transpose(1, 2, 0)
+    order = np.eye(total_rows, dtype=np.float32)[order.reshape(-1)]
+    attended = output_product(head_values, jnp.asarray(order, bf16), w_o)
     attended = sum(part.astype(f32) for part in spread(attended, "section")).astype(bf16)
-    attended = lax.all_gather(attended, "expert", axis=1, tiled=True)
-    hidden = residual_all.transpose(2, 0, 1, 3).reshape(-1, width).astype(f32)
-    mixed = hidden + attended.astype(f32)
-    moe_in = rms_scaled(mixed, moe_gain).astype(bf16)
-
-    gate_part = jnp.einsum("td,xdf->txf", moe_in, w_gate, preferred_element_type=f32)
-    up_part = jnp.einsum("td,xdf->txf", moe_in, w_up, preferred_element_type=f32)
-    route = weights_all.transpose(2, 0, 1, 3).reshape(-1, expert_total)
-    route = lax.dynamic_slice_in_dim(route, expert_rank * w_gate.shape[0], w_gate.shape[0], 1)
-    activated = (jax.nn.silu(gate_part) * up_part * route[:, :, None]).astype(bf16)
-    combined = jnp.dot(
-        activated.reshape(activated.shape[0], -1),
-        w_down.reshape(-1, width),
-        preferred_element_type=f32,
-    ).astype(bf16)
+    attended = lax.all_gather(attended, "expert", axis=0)
+    blocks, own = run_experts(
+        attended, hidden, moe_gain, route, w_gate, w_up, w_down, sections
+    )
+    blocks = deliver(fold(deliver(blocks, "expert")), "section")
     column = width // sections
-    combined = combined.reshape(experts, experts, steps, sections, column)
-    combined = combined.transpose(1, 3, 0, 2, 4).reshape(everyone, experts, steps, column)
-    combined = lax.all_to_all(combined, block, 0, 0, tiled=True)
-    combined = jnp.sum(combined.astype(f32), axis=0)
-    own = mixed.reshape(experts, experts, steps, sections, column)
-    own = lax.dynamic_slice(
-        own,
-        (0, expert_rank, 0, section_rank, 0),
-        (experts, 1, steps, 1, column),
-    )[:, 0, :, 0]
-    return (own + combined).transpose(1, 0, 2).astype(bf16)
+    base = lax.dynamic_slice_in_dim(residual, section_rank * column, column, 2)
+    own = lax.dynamic_index_in_dim(own, section_rank, 0, keepdims=False)
+    total = base.reshape(own_rows, column).astype(f32) + own.astype(f32)
+    total = total + sum(part.astype(f32) for part in blocks)
+    return total.astype(bf16).reshape(steps, tokens_here, column)
 
 
 def solution(mesh):

time: 171 us -> 152 us (0.89)
  matrix products: 27.4 us -> 4.63 us
  blocking collectives: 29.2 us -> 18 us
  Pallas kernels: 1.48 us -> 12.2 us
  local copies, waits for them, and re-layouts: 16 us -> 20.2 us
  waiting for transfers between devices: 38.3 us -> 34.5 us
  starting transfers between devices: 33.6 us -> 35.9 us
    all_to_all x3 -> x0, waiting for transfers between devices: 25.9 us -> none  [the longest x1 10.8 us: local(): cut = lax.all_to_all(cut, 'expert', 0, 0, tiled=True)]
    dot_general x11 -> x0, matrix products: 24.5 us -> none  [the longest x8 9.38 us: local(): jnp.einsum('drc,kc->drk', some, part, preferred_element_type=f32)]
    ppermute x13 -> x25, waiting for transfers between devices: 11.6 us -> 34.3 us  [swap(): return lax.ppermute(block, axis, [(i, i ^ mask) for i in range(size)])]
    ppermute x13 -> x25, starting transfers between devices: 16.3 us -> 30.4 us  [swap(): return lax.ppermute(block, axis, [(i, i ^ mask) for i in range(size)])]
    all_to_all x3 -> x0, starting transfers between devices: 11.3 us -> none  [the longest x1 4.24 us: local(): out_latent = lax.all_to_all(out_latent, 'section', 0, 0, tiled=True)]
    all_gather x4 -> x2, blocking collectives: 23.8 us -> 12.5 us  [the longest x1 6.67 us: local(): packed = lax.all_gather(packed, 'expert', axis=0, tiled=True)]
    pallas_call x1 -> x7, Pallas kernels: 1.48 us -> 12.2 us  [the longest x1 7.4 us: run_experts(): pl.pallas_call(functools.partial(expert_kernel, experts, sections), out_s...]
    unnamed x57 -> x29, local copies, waits for them, and re-layouts: 2.82 us -> 7.08 us
  transfers between devices with their start and end apart: 18 -> 27, of which waited for: 6 -> 12; matrix products, arithmetic and copies ran while one was open for 18% -> 16% of each run, Pallas kernels for 1% -> 2%
where the time goes in v3:
time: 152 us; the launch traced here: 151 us
  starting transfers between devices  35.9 us (24%)
  waiting for transfers between devices  34.5 us (23%)
  local copies, waits for them, and re-layouts  20.2 us (13%)
  blocking collectives  18 us (12%)
  between operations  15.8 us (10%)
  Pallas kernels  12.2 us (8%)
  other arithmetic  10.1 us (7%)
  matrix products  4.63 us (3%)
    ppermute x25, waiting for transfers between devices, swap(): return lax.ppermute(block, axis, [(i, i ^ mask) for i in range(size)])  34.3 us
    ppermute x25, starting transfers between devices, swap(): return lax.ppermute(block, axis, [(i, i ^ mask) for i in range(size)])  30.4 us
    pallas_call x1, Pallas kernels, run_experts(): pl.pallas_call(functools.partial(expert_kernel, experts, sections), out_s...  7.4 us
    unnamed x29, local copies, waits for them, and re-layouts  7.08 us
    all_gather x1, blocking collectives, local(): packed = lax.all_gather(packed, 'expert', axis=0, tiled=True)  6.67 us
    all_gather x1, blocking collectives, local(): attended = lax.all_gather(attended, 'expert', axis=0)  5.88 us
    all_to_all x1, starting transfers between devices, local(): query_part = lax.all_to_all(query_part, block, 0, 0, tiled=True)  5.53 us
    all_gather x1, blocking collectives, local(): head_values = lax.all_gather(head_values, 'expert', axis=0, tiled=True)  5.43 us
  transfers between devices with their start and end apart: 27, of which 12 were waited for; matrix products, arithmetic and copies ran while one was open for 16% of the time, Pallas kernels for 2%

profile of v3, /device:TPU:0, one launch (start us, length us, event | category | flops | bytes accessed | tf_op | source)
XLA Modules:
  0.0 151.3 jit_solution(9093795959219662633)
XLA Ops:
  7.9 3.1 %collective-permute-start.1 = (bf16[576,112]{1,0:T(8,128)(2,1)S(1)}, bf16[576,112]{1,0:T(8,128)(2,1)S(1)}, u32[]{:S(2)}, u32[]{:S(2)}) collective-permute-start(bf16[576,112]{1,0:T(8,128)(2,1)S(1)} %dynamic-slice_bitcast_fusion.refs_1_.refs_3_), channel_id=1, source_target_pairs={{0,1},{1,0},{2,3},{3,2},{4,5},{5,4},{6,7},{7,6},{8,9},{9,8},{10,11... | collective-permute-start | bytes 387080 | tf_op jit(solution)/shard_map/ppermute | solution.py:55
  11.0 2.6 %collective-permute-start.3 = (bf16[576,112]{1,0:T(8,128)(2,1)S(1)}, bf16[576,112]{1,0:T(8,128)(2,1)S(1)}, u32[]{:S(2)}, u32[]{:S(2)}) collective-permute-start(bf16[576,112]{1,0:T(8,128)(2,1)S(1)} %dynamic-slice_bitcast_fusion.refs_1_.refs_3_), channel_id=1, source_target_pairs={{0,2},{1,3},{2,0},{3,1},{4,6},{5,7},{6,4},{7,5},{8,10},{9,11},{10,... | collective-permute-start | bytes 387080 | tf_op jit(solution)/shard_map/ppermute | solution.py:55
  24.6 6.7 %all_gather.18 = bf16[32,6688]{1,0:T(8,128)(2,1)S(1)} all-gather(bf16[8,6688]{1,0:T(8,128)(2,1)S(1)} %concatenate.50), channel_id=1, replica_groups=mesh['groups'=2,'expert'=4,'section'=4] {'expert'}, dimensions={0}, use_global_device_ids=true | all-gather | bytes 535040 | tf_op jit(solution)/shard_map/all_gather | solution.py:419
  34.9 2.0 %fusion.2 = bf16[4,4,2,16,128]{4,1,2,0,3:T(4,128)(2,1)} fusion(bf16[16,128,128]{2,1,0:T(8,128)(2,1)} %param.28, bf16[4,4,2,16,192]{4,1,2,0,3:T(4,128)(2,1)S(1)} %copy_select_fusion), kind=kOutput, calls=%fused_computation.5 | convolution fusion | flops 16842752 | bytes 786432 | tf_op jit(solution)/shard_map/ejthn,hnc->ejthc/dot_general | solution.py:432
  39.9 5.5 %all-to-all-start = ((bf16[16,40,144]{2,1,0:T(8,128)(2,1)}), bf16[16,40,144]{2,1,0:T(8,128)(2,1)}, u32[]{:S(2)}, u32[]{:S(2)}) async-start(bf16[16,40,144]{2,1,0:T(8,128)(2,1)} %pad_maximum_fusion), calls=%async_computation | async-start | bytes 655360 | tf_op jit(solution)/shard_map/all_to_all | solution.py:448
  48.9 1.9 %collective-permute-start.8 = (bf16[4,128,224]{2,1,0:T(8,128)(2,1)S(1)}, bf16[4,128,224]{2,1,0:T(8,128)(2,1)S(1)}, u32[]{:S(2)}, u32[]{:S(2)}) collective-permute-start(bf16[4,128,224]{2,1,0:T(8,128)(2,1)S(1)} %get-tuple-element.32), channel_id=1, source_target_pairs={{0,8},{4,12},{8,0},{12,4},{1,9},{5,13},{9,1},{13,5},{2,10},{6,14},... | collective-permute-start | bytes 688136 | tf_op jit(solution)/shard_map/ppermute | solution.py:55
  56.0 4.1 %collective-permute-done.8.refs_1_ = bf16[4,128,224]{2,1,0:T(8,128)(2,1)S(1)} collective-permute-done((bf16[4,128,224]{2,1,0:T(8,128)(2,1)S(1)}, bf16[4,128,224]{2,1,0:T(8,128)(2,1)S(1)}, u32[]{:S(2)}, u32[]{:S(2)}) %collective-permute-start.8) | collective-permute-done | bytes 229408 | tf_op jit(solution)/shard_map/ppermute | solution.py:55
  60.1 10.8 %collective-permute-done.9.refs_2_ = bf16[4,128,224]{2,1,0:T(8,128)(2,1)S(1)} collective-permute-done((bf16[4,128,224]{2,1,0:T(8,128)(2,1)S(1)}, bf16[4,128,224]{2,1,0:T(8,128)(2,1)S(1)}, u32[]{:S(2)}, u32[]{:S(2)}) %collective-permute-start.9) | collective-permute-done | bytes 229408 | tf_op jit(solution)/shard_map/ppermute | solution.py:55
  72.2 2.4 %collective-permute-start.11 = (bf16[128,576]{1,0:T(8,128)(2,1)S(1)}, bf16[128,576]{1,0:T(8,128)(2,1)S(1)}, u32[]{:S(2)}, u32[]{:S(2)}) collective-permute-start(bf16[128,576]{1,0:T(8,128)(2,1)S(1)} %get-tuple-element.35), channel_id=1, source_target_pairs={{0,8},{4,12},{8,0},{12,4},{1,9},{5,13},{9,1},{13,5},{2,10},{6,14},... | collective-permute-start | bytes 442376 | tf_op jit(solution)/shard_map/ppermute | solution.py:55
  79.6 2.7 %collective-permute-done.12 = bf16[128,576]{1,0:T(8,128)(2,1)S(1)} collective-permute-done((bf16[128,576]{1,0:T(8,128)(2,1)S(1)}, bf16[128,576]{1,0:T(8,128)(2,1)S(1)}, u32[]{:S(2)}, u32[]{:S(2)}) %collective-permute-start.12) | collective-permute-done | bytes 147488 | tf_op jit(solution)/shard_map/ppermute | solution.py:55
  83.9 1.8 %collective-permute-start.13 = (bf16[1,32,512]{2,1,0:T(8,128)(2,1)S(1)}, bf16[1,32,512]{2,1,0:T(8,128)(2,1)S(1)}, u32[]{:S(2)}, u32[]{:S(2)}) collective-permute-start(bf16[1,32,512]{2,1,0:T(8,128)(2,1)S(1)} %get-tuple-element.39), channel_id=1, source_target_pairs={{0,1},{1,0},{2,3},{3,2},{4,5},{5,4},{6,7},{7,6},{8,9},{9,8},{10,11... | collective-permute-start | bytes 98312 | tf_op jit(solution)/shard_map/ppermute | solution.py:55
  85.7 2.0 %collective-permute-start.14 = (bf16[1,32,512]{2,1,0:T(8,128)(2,1)S(1)}, bf16[1,32,512]{2,1,0:T(8,128)(2,1)S(1)}, u32[]{:S(2)}, u32[]{:S(2)}) collective-permute-start(bf16[1,32,512]{2,1,0:T(8,128)(2,1)S(1)} %get-tuple-element.40), channel_id=1, source_target_pairs={{0,2},{1,3},{2,0},{3,1},{4,6},{5,7},{6,4},{7,5},{8,10},{9,11},{10,... | collective-permute-start | bytes 98312 | tf_op jit(solution)/shard_map/ppermute | solution.py:55
  88.4 2.5 %collective-permute-done.14 = bf16[1,32,512]{2,1,0:T(8,128)(2,1)S(1)} collective-permute-done((bf16[1,32,512]{2,1,0:T(8,128)(2,1)S(1)}, bf16[1,32,512]{2,1,0:T(8,128)(2,1)S(1)}, u32[]{:S(2)}, u32[]{:S(2)}) %collective-permute-start.14) | collective-permute-done | bytes 32800 | tf_op jit(solution)/shard_map/ppermute | solution.py:55
  90.9 2.5 %collective-permute-done.15 = bf16[1,32,512]{2,1,0:T(8,128)(2,1)S(1)} collective-permute-done((bf16[1,32,512]{2,1,0:T(8,128)(2,1)S(1)}, bf16[1,32,512]{2,1,0:T(8,128)(2,1)S(1)}, u32[]{:S(2)}, u32[]{:S(2)}) %collective-permute-start.15) | collective-permute-done | bytes 32800 | tf_op jit(solution)/shard_map/ppermute | solution.py:55
  94.1 2.3 %fusion.9 = bf16[4,2,16,128]{3,0,1,2:T(4,128)(2,1)S(1)} fusion(bf16[4,16,128,128,1]{3,2,1,0,4:T(8,128)(2,1)} %bitcast.93, bf16[4,2,16,4,128]{4,3,2,1,0:T(4,128)(2,1)S(1)} %broadcast_select_fusion), kind=kOutput, calls=%fused_computation.8 | convolution fusion | flops 16793600 | bytes 2260992 | tf_op jit(solution)/shard_map/othxc,xhvc->othv/dot_general | solution.py:491
  96.4 5.4 %all_gather.21.value_ref = bf16[32,2048]{1,0:T(8,128)(2,1)S(1)} all-gather(bf16[8,2048]{1,0:T(8,128)(2,1)S(1)} %bitcast.82), channel_id=1, replica_groups=mesh['groups'=2,'expert'=4,'section'=4] {'expert'}, dimensions={0}, use_global_device_ids=true | all-gather | bytes 163840 | tf_op jit(solution)/shard_map/all_gather | solution.py:495
  101.9 2.0 %copy-done.2 = bf16[2048,896]{1,0:T(8,128)(2,1)S(1)} copy-done((bf16[2048,896]{1,0:T(8,128)(2,1)S(1)}, bf16[2048,896]{1,0:T(8,128)(2,1)}, u32[]{:S(2)}) %copy-start.2) | copy-done | bytes 3670040
  106.6 3.1 %collective-permute-start.18 = (bf16[32,896]{1,0:T(8,128)(2,1)S(1)}, bf16[32,896]{1,0:T(8,128)(2,1)S(1)}, u32[]{:S(2)}, u32[]{:S(2)}) collective-permute-start(bf16[32,896]{1,0:T(8,128)(2,1)S(1)} %output_product.1), channel_id=1, source_target_pairs={{0,3},{1,2},{2,1},{3,0},{4,7},{5,6},{6,5},{7,4},{8,11},{9,10},{10,... | collective-permute-start | bytes 172040 | tf_op jit(solution)/shard_map/ppermute | solution.py:55
  110.4 3.1 %collective-permute-done.17 = bf16[32,896]{1,0:T(8,128)(2,1)S(1)} collective-permute-done((bf16[32,896]{1,0:T(8,128)(2,1)S(1)}, bf16[32,896]{1,0:T(8,128)(2,1)S(1)}, u32[]{:S(2)}, u32[]{:S(2)}) %collective-permute-start.17) | collective-permute-done | bytes 57376 | tf_op jit(solution)/shard_map/ppermute | solution.py:55
  113.5 5.9 %all-gather.1 = bf16[128,896]{1,0:T(8,128)(2,1)S(1)} all-gather(bf16[32,896]{1,0:T(8,128)(2,1)S(1)} %add_convert_fusion), channel_id=3, replica_groups=mesh['groups'=2,'expert'=4,'section'=4] {'expert'}, dimensions={0}, use_global_device_ids=true | all-gather | bytes 286720 | tf_op jit(solution)/shard_map/all_gather | solution.py:502
  119.4 3.1 %copy-done.1 = bf16[4,3584,256]{2,1,0:T(8,128)(2,1)S(1)} copy-done((bf16[4,3584,256]{2,1,0:T(8,128)(2,1)S(1)}, bf16[4,3584,256]{2,1,0:T(8,128)(2,1)}, u32[]{:S(2)}) %copy-start.1) | copy-done | bytes 7340056
  122.4 7.4 %run_experts.1 = (bf16[4,8,896]{2,1,0:T(8,128)(2,1)S(1)}, bf16[4,8,896]{2,1,0:T(8,128)(2,1)S(1)}, bf16[4,8,896]{2,1,0:T(8,128)(2,1)S(1)}, bf16[4,8,896]{2,1,0:T(8,128)(2,1)S(1)}, bf16[4,8,896]{2,1,0:T(8,128)(2,1)S(1)}) custom-call(bf16[4,32,896]{2,1,0:T(8,128)(2,1)S(1)} %bitcast.70, bf16[32,3584]{1,0:T(8,128)(2,1)S(1)} %slice.90.refs_1_, ...), custom_call_target="tpu_custom_call" | custom-call | tf_op jit(solution)/shard_map/run_experts/pallas_call | solution.py:306
  131.8 3.0 %collective-permute-done.20.refs_2_ = bf16[4,8,896]{2,1,0:T(8,128)(2,1)S(1)} collective-permute-done((bf16[4,8,896]{2,1,0:T(8,128)(2,1)S(1)}, bf16[4,8,896]{2,1,0:T(8,128)(2,1)S(1)}, u32[]{:S(2)}, u32[]{:S(2)}) %collective-permute-start.20) | collective-permute-done | bytes 57376 | tf_op jit(solution)/shard_map/ppermute | solution.py:55
  141.3 2.6 %collective-permute-done.24 = bf16[8,896]{1,0:T(8,128)(2,1)S(1)} collective-permute-done((bf16[8,896]{1,0:T(8,128)(2,1)S(1)}, bf16[8,896]{1,0:T(8,128)(2,1)S(1)}, u32[]{:S(2)}, u32[]{:S(2)}) %collective-permute-start.24) | collective-permute-done | bytes 14368 | tf_op jit(solution)/shard_map/ppermute | solution.py:55
  (148 shorter events, 47.2 us)
Async XLA Ops:
  7.9 41.0 %collective-permute-start.1 = (bf16[576,112]{1,0:T(8,128)(2,1)S(1)}, bf16[576,112]{1,0:T(8,128)(2,1)S(1)}, u32[]{:S(2)}, u32[]{:S(2)}) collective-permute-start(bf16[576,112]{1,0:T(8,128)(2,1)S(1)} %dynamic-slice_bitcast_fusion.refs_1_.refs_3_), channel_id=1, source_target_pairs={{0,1},{1,0},{2,3},{3,2},{4,5},{5,4},{6,7},{7,6},{8,9},{9,8},{10,11... | collective-permute-start | bytes 387080 | tf_op jit(solution)/shard_map/ppermute | solution.py:55
  11.0 39.8 %collective-permute-start.3 = (bf16[576,112]{1,0:T(8,128)(2,1)S(1)}, bf16[576,112]{1,0:T(8,128)(2,1)S(1)}, u32[]{:S(2)}, u32[]{:S(2)}) collective-permute-start(bf16[576,112]{1,0:T(8,128)(2,1)S(1)} %dynamic-slice_bitcast_fusion.refs_1_.refs_3_), channel_id=1, source_target_pairs={{0,2},{1,3},{2,0},{3,1},{4,6},{5,7},{6,4},{7,5},{8,10},{9,11},{10,... | collective-permute-start | bytes 387080 | tf_op jit(solution)/shard_map/ppermute | solution.py:55
  13.6 37.2 %collective-permute-start.5 = (bf16[576,112]{1,0:T(8,128)(2,1)S(1)}, bf16[576,112]{1,0:T(8,128)(2,1)S(1)}, u32[]{:S(2)}, u32[]{:S(2)}) collective-permute-start(bf16[576,112]{1,0:T(8,128)(2,1)S(1)} %dynamic-slice_bitcast_fusion.refs_1_.refs_3_), channel_id=1, source_target_pairs={{0,3},{1,2},{2,1},{3,0},{4,7},{5,6},{6,5},{7,4},{8,11},{9,10},{10,... | collective-permute-start | bytes 387080 | tf_op jit(solution)/shard_map/ppermute | solution.py:55
  13.6 37.8 %collective-permute-start = (bf16[576,112]{1,0:T(8,128)(2,1)S(1)}, bf16[576,112]{1,0:T(8,128)(2,1)S(1)}, u32[]{:S(2)}, u32[]{:S(2)}) collective-permute-start(bf16[576,112]{1,0:T(8,128)(2,1)S(1)} %dynamic-slice_bitcast_fusion.refs_1_.refs_3_), channel_id=1, source_target_pairs={{0,16},{16,0},{1,17},{17,1},{2,18},{18,2},{3,19},{19,3},{4,20},{20... | collective-permute-start | bytes 387080 | tf_op jit(solution)/shard_map/ppermute | solution.py:55
  39.9 35.2 %all-to-all-start = ((bf16[16,40,144]{2,1,0:T(8,128)(2,1)}), bf16[16,40,144]{2,1,0:T(8,128)(2,1)}, u32[]{:S(2)}, u32[]{:S(2)}) async-start(bf16[16,40,144]{2,1,0:T(8,128)(2,1)} %pad_maximum_fusion), calls=%async_computation | async-start | bytes 655360 | tf_op jit(solution)/shard_map/all_to_all | solution.py:448
  45.5 48.6 %all-gather.4.cloned.1.call-start = ((), (), s32[]{:S(2)}) async-start(), calls=%async_computation.1 | async-start | bytes 2621440 | tf_op jit(solution)/shard_map/all_gather | solution.py:470
  45.6 7.3 %collective-permute-start.7 = (bf16[4,128,224]{2,1,0:T(8,128)(2,1)S(1)}, bf16[4,128,224]{2,1,0:T(8,128)(2,1)S(1)}, u32[]{:S(2)}, u32[]{:S(2)}) collective-permute-start(bf16[4,128,224]{2,1,0:T(8,128)(2,1)S(1)} %copy-done.6), channel_id=1, source_target_pairs={{0,4},{4,0},{8,12},{12,8},{1,5},{5,1},{9,13},{13,9},{2,6},{6,2},{1... | collective-permute-start | bytes 688136 | tf_op jit(solution)/shard_map/ppermute | solution.py:55
  48.9 11.2 %collective-permute-start.8 = (bf16[4,128,224]{2,1,0:T(8,128)(2,1)S(1)}, bf16[4,128,224]{2,1,0:T(8,128)(2,1)S(1)}, u32[]{:S(2)}, u32[]{:S(2)}) collective-permute-start(bf16[4,128,224]{2,1,0:T(8,128)(2,1)S(1)} %get-tuple-element.32), channel_id=1, source_target_pairs={{0,8},{4,12},{8,0},{12,4},{1,9},{5,13},{9,1},{13,5},{2,10},{6,14},... | collective-permute-start | bytes 688136 | tf_op jit(solution)/shard_map/ppermute | solution.py:55
  50.8 20.1 %collective-permute-start.9 = (bf16[4,128,224]{2,1,0:T(8,128)(2,1)S(1)}, bf16[4,128,224]{2,1,0:T(8,128)(2,1)S(1)}, u32[]{:S(2)}, u32[]{:S(2)}) collective-permute-start(bf16[4,128,224]{2,1,0:T(8,128)(2,1)S(1)} %get-tuple-element.33), channel_id=1, source_target_pairs={{0,12},{4,8},{8,4},{12,0},{1,13},{5,9},{9,5},{13,1},{2,14},{6,10},... | collective-permute-start | bytes 688136 | tf_op jit(solution)/shard_map/ppermute | solution.py:55
  50.8 20.1 %collective-permute-start.2 = (bf16[576,112]{1,0:T(8,128)(2,1)S(1)}, bf16[576,112]{1,0:T(8,128)(2,1)S(1)}, u32[]{:S(2)}, u32[]{:S(2)}) collective-permute-start(bf16[576,112]{1,0:T(8,128)(2,1)S(1)} %collective-permute-done.1.refs_3_.refs_5_), channel_id=1, source_target_pairs={{0,16},{16,0},{1,17},{17,1},{2,18},{18,2},{3,19},{19,3},{4,20},{20... | collective-permute-start | bytes 387080 | tf_op jit(solution)/shard_map/ppermute | solution.py:55
  51.4 19.6 %collective-permute-start.4 = (bf16[576,112]{1,0:T(8,128)(2,1)S(1)}, bf16[576,112]{1,0:T(8,128)(2,1)S(1)}, u32[]{:S(2)}, u32[]{:S(2)}) collective-permute-start(bf16[576,112]{1,0:T(8,128)(2,1)S(1)} %collective-permute-done.3.refs_5_.refs_7_), channel_id=1, source_target_pairs={{0,16},{16,0},{1,17},{17,1},{2,18},{18,2},{3,19},{19,3},{4,20},{20... | collective-permute-start | bytes 387080 | tf_op jit(solution)/shard_map/ppermute | solution.py:55
  52.9 18.0 %collective-permute-start.6 = (bf16[576,112]{1,0:T(8,128)(2,1)S(1)}, bf16[576,112]{1,0:T(8,128)(2,1)S(1)}, u32[]{:S(2)}, u32[]{:S(2)}) collective-permute-start(bf16[576,112]{1,0:T(8,128)(2,1)S(1)} %collective-permute-done.5.refs_7_.refs_9_), channel_id=1, source_target_pairs={{0,16},{16,0},{1,17},{17,1},{2,18},{18,2},{3,19},{19,3},{4,20},{20... | collective-permute-start | bytes 387080 | tf_op jit(solution)/shard_map/ppermute | solution.py:55
  71.8 6.6 %collective-permute-start.10 = (bf16[128,576]{1,0:T(8,128)(2,1)S(1)}, bf16[128,576]{1,0:T(8,128)(2,1)S(1)}, u32[]{:S(2)}, u32[]{:S(2)}) collective-permute-start(bf16[128,576]{1,0:T(8,128)(2,1)S(1)} %get-tuple-element.34), channel_id=1, source_target_pairs={{0,4},{4,0},{8,12},{12,8},{1,5},{5,1},{9,13},{13,9},{2,6},{6,2},{1... | collective-permute-start | bytes 442376 | tf_op jit(solution)/shard_map/ppermute | solution.py:55
  72.2 7.4 %collective-permute-start.11 = (bf16[128,576]{1,0:T(8,128)(2,1)S(1)}, bf16[128,576]{1,0:T(8,128)(2,1)S(1)}, u32[]{:S(2)}, u32[]{:S(2)}) collective-permute-start(bf16[128,576]{1,0:T(8,128)(2,1)S(1)} %get-tuple-element.35), channel_id=1, source_target_pairs={{0,8},{4,12},{8,0},{12,4},{1,9},{5,13},{9,1},{13,5},{2,10},{6,14},... | collective-permute-start | bytes 442376 | tf_op jit(solution)/shard_map/ppermute | solution.py:55
  74.6 7.7 %collective-permute-start.12 = (bf16[128,576]{1,0:T(8,128)(2,1)S(1)}, bf16[128,576]{1,0:T(8,128)(2,1)S(1)}, u32[]{:S(2)}, u32[]{:S(2)}) collective-permute-start(bf16[128,576]{1,0:T(8,128)(2,1)S(1)} %get-tuple-element.36), channel_id=1, source_target_pairs={{0,12},{4,8},{8,4},{12,0},{1,13},{5,9},{9,5},{13,1},{2,14},{6,10},... | collective-permute-start | bytes 442376 | tf_op jit(solution)/shard_map/ppermute | solution.py:55
  83.9 4.5 %collective-permute-start.13 = (bf16[1,32,512]{2,1,0:T(8,128)(2,1)S(1)}, bf16[1,32,512]{2,1,0:T(8,128)(2,1)S(1)}, u32[]{:S(2)}, u32[]{:S(2)}) collective-permute-start(bf16[1,32,512]{2,1,0:T(8,128)(2,1)S(1)} %get-tuple-element.39), channel_id=1, source_target_pairs={{0,1},{1,0},{2,3},{3,2},{4,5},{5,4},{6,7},{7,6},{8,9},{9,8},{10,11... | collective-permute-start | bytes 98312 | tf_op jit(solution)/shard_map/ppermute | solution.py:55
  85.7 5.2 %collective-permute-start.14 = (bf16[1,32,512]{2,1,0:T(8,128)(2,1)S(1)}, bf16[1,32,512]{2,1,0:T(8,128)(2,1)S(1)}, u32[]{:S(2)}, u32[]{:S(2)}) collective-permute-start(bf16[1,32,512]{2,1,0:T(8,128)(2,1)S(1)} %get-tuple-element.40), channel_id=1, source_target_pairs={{0,2},{1,3},{2,0},{3,1},{4,6},{5,7},{6,4},{7,5},{8,10},{9,11},{10,... | collective-permute-start | bytes 98312 | tf_op jit(solution)/shard_map/ppermute | solution.py:55
  87.6 5.7 %collective-permute-start.15 = (bf16[1,32,512]{2,1,0:T(8,128)(2,1)S(1)}, bf16[1,32,512]{2,1,0:T(8,128)(2,1)S(1)}, u32[]{:S(2)}, u32[]{:S(2)}) collective-permute-start(bf16[1,32,512]{2,1,0:T(8,128)(2,1)S(1)} %get-tuple-element.41), channel_id=1, source_target_pairs={{0,3},{1,2},{2,1},{3,0},{4,7},{5,6},{6,5},{7,4},{8,11},{9,10},{10,... | collective-permute-start | bytes 98312 | tf_op jit(solution)/shard_map/ppermute | solution.py:55
  105.2 5.1 %collective-permute-start.16 = (bf16[32,896]{1,0:T(8,128)(2,1)S(1)}, bf16[32,896]{1,0:T(8,128)(2,1)S(1)}, u32[]{:S(2)}, u32[]{:S(2)}) collective-permute-start(bf16[32,896]{1,0:T(8,128)(2,1)S(1)} %output_product.1), channel_id=1, source_target_pairs={{0,1},{1,0},{2,3},{3,2},{4,5},{5,4},{6,7},{7,6},{8,9},{9,8},{10,11... | collective-permute-start | bytes 172040 | tf_op jit(solution)/shard_map/ppermute | solution.py:55
  105.3 8.2 %collective-permute-start.17 = (bf16[32,896]{1,0:T(8,128)(2,1)S(1)}, bf16[32,896]{1,0:T(8,128)(2,1)S(1)}, u32[]{:S(2)}, u32[]{:S(2)}) collective-permute-start(bf16[32,896]{1,0:T(8,128)(2,1)S(1)} %output_product.1), channel_id=1, source_target_pairs={{0,2},{1,3},{2,0},{3,1},{4,6},{5,7},{6,4},{7,5},{8,10},{9,11},{10,... | collective-permute-start | bytes 172040 | tf_op jit(solution)/shard_map/ppermute | solution.py:55
  106.6 6.9 %collective-permute-start.18 = (bf16[32,896]{1,0:T(8,128)(2,1)S(1)}, bf16[32,896]{1,0:T(8,128)(2,1)S(1)}, u32[]{:S(2)}, u32[]{:S(2)}) collective-permute-start(bf16[32,896]{1,0:T(8,128)(2,1)S(1)} %output_product.1), channel_id=1, source_target_pairs={{0,3},{1,2},{2,1},{3,0},{4,7},{5,6},{6,5},{7,4},{8,11},{9,10},{10,... | collective-permute-start | bytes 172040 | tf_op jit(solution)/shard_map/ppermute | solution.py:55
  135.4 5.2 %collective-permute-start.22 = (bf16[8,896]{1,0:T(8,128)(2,1)S(1)}, bf16[8,896]{1,0:T(8,128)(2,1)S(1)}, u32[]{:S(2)}, u32[]{:S(2)}) collective-permute-start(bf16[8,896]{1,0:T(8,128)(2,1)S(1)} %get-tuple-element.48), channel_id=1, source_target_pairs={{0,1},{1,0},{2,3},{3,2},{4,5},{5,4},{6,7},{7,6},{8,9},{9,8},{10,11... | collective-permute-start | bytes 43016 | tf_op jit(solution)/shard_map/ppermute | solution.py:55
  136.6 4.6 %collective-permute-start.23 = (bf16[8,896]{1,0:T(8,128)(2,1)S(1)}, bf16[8,896]{1,0:T(8,128)(2,1)S(1)}, u32[]{:S(2)}, u32[]{:S(2)}) collective-permute-start(bf16[8,896]{1,0:T(8,128)(2,1)S(1)} %get-tuple-element.49), channel_id=1, source_target_pairs={{0,2},{1,3},{2,0},{3,1},{4,6},{5,7},{6,4},{7,5},{8,10},{9,11},{10,... | collective-permute-start | bytes 43016 | tf_op jit(solution)/shard_map/ppermute | solution.py:55
  138.3 5.5 %collective-permute-start.24 = (bf16[8,896]{1,0:T(8,128)(2,1)S(1)}, bf16[8,896]{1,0:T(8,128)(2,1)S(1)}, u32[]{:S(2)}, u32[]{:S(2)}) collective-permute-start(bf16[8,896]{1,0:T(8,128)(2,1)S(1)} %get-tuple-element.50), channel_id=1, source_target_pairs={{0,3},{1,2},{2,1},{3,0},{4,7},{5,6},{6,5},{7,4},{8,11},{9,10},{10,... | collective-permute-start | bytes 43016 | tf_op jit(solution)/shard_map/ppermute | solution.py:55
  (17 other events, 141.1 us)
Sparse Core Ops, SparseCore 0:
  47.9 29.3 all-gather.3

commit v4 on v3

v4 whole, which is shorter than its diff:
```python
import functools

import jax
import jax.numpy as jnp
from jax import lax
from jax.experimental import pallas as pl
from jax.experimental.pallas import tpu as pltpu
from jax.sharding import PartitionSpec as P

epsilon = 1e-06
masked_value = -1e30
route_scale = 2.5


def rotation(position, width):
    halfway = width // 2
    frequency = 10000.0 ** (-2.0 * jnp.arange(halfway).astype(jnp.float32) / width)
    angles = position.astype(jnp.float32)[..., None] * frequency
    return jnp.cos(angles), jnp.sin(angles)


def swap(block, axis, mask):
    size = lax.axis_size(axis)
    return lax.ppermute(block, axis, [(i, i ^ mask) for i in range(size)])


def deliver(blocks, axis):
    return [blocks[0]] + [swap(blocks[mask], axis, mask) for mask in range(1, len(blocks))]


def spread(block, axis):
    return [block] + [swap(block, axis, mask) for mask in range(1, lax.axis_size(axis))]


def params(mebibytes=40):
    return pltpu.CompilerParams(vmem_limit_bytes=mebibytes * 1024 * 1024)


def doubled(block, axis):
    held = {0: block}
    size = lax.axis_size(axis)
    masks = [1 << bit for bit in range(size.bit_length() - 1)]
    for mask in masks[1:] + masks[:1]:
        for other in list(held):
            held[other ^ mask] = swap(held[other], axis, mask)
    return [held[mask] for mask in range(size)]


def cut_kernel(sections, experts, piece, x_ref, *refs):
    out_refs, held = refs[:experts], refs[experts]
    rank = lax.axis_index("expert")
    for target in range(experts):
        for section in range(sections):
            at = (section * experts + target) * piece
            held[target, section] = x_ref[:, at : at + piece]
    for mask, ref in enumerate(out_refs):
        ref[...] = held[rank ^ mask]


def cut_columns(x, sections, experts):
    rows, width = x.shape
    piece = width // (sections * experts)
    block = jax.ShapeDtypeStruct((sections, rows, piece), x.dtype)
    return pl.pallas_call(
        functools.partial(cut_kernel, sections, experts, piece),
        out_shape=[block] * experts,
        scratch_shapes=[pltpu.VMEM((experts,) + block.shape, x.dtype)],
        compiler_params=params(),
        name="cut_columns",
    )(x)


def project_kernel(count, sections, groups, *refs):
    x_refs = refs[:count]
    w_refs = refs[count : count + sections * groups]
    out_refs = refs[count + sections * groups :]
    section_rank = lax.axis_index("section")
    group_rank = lax.axis_index("groups")
    rows = x_refs[0].shape[1]
    total = 0
    for mask in range(sections):
        held = [w_refs[mask * groups + other][...] for other in range(groups)]
        columns = []
        for group in range(groups):
            chosen = held[0]
            for other in range(1, groups):
                chosen = jnp.where((group_rank ^ other) == group, held[other], chosen)
            columns.append(chosen)
        weights = jnp.concatenate(columns, axis=1)
        x = jnp.concatenate([ref[section_rank ^ mask] for ref in x_refs], axis=0)
        total = total + lax.dot_general(
            x, weights, (((1,), (1,)), ((), ())), preferred_element_type=jnp.float32
        )
    for index, ref in enumerate(out_refs):
        ref[...] = total[index * rows : (index + 1) * rows].astype(ref.dtype)


def project(blocks, w_parts, sections, groups):
    out = jax.ShapeDtypeStruct((blocks[0].shape[1], w_parts[0].shape[0]), jnp.bfloat16)
    return pl.pallas_call(
        functools.partial(project_kernel, len(blocks), sections, groups),
        out_shape=[out] * len(blocks),
        compiler_params=params(),
        name="project",
    )(*blocks, *w_parts)


def query_kernel(
    experts, sections, prompts, nope, table_ref, query_ref, uk_ref, own_ref, gain_ref, wt_ref,
    out_ref, picked, ropes, made, normed
):
    f32, bf16 = jnp.float32, jnp.bfloat16
    _, steps, sources, heads, wide = query_ref.shape
    rope = wide - nope
    chunk = uk_ref.shape[2]
    width = out_ref.shape[2]
    count = experts * sources
    block = prompts * steps * heads
    rank = lax.axis_index("expert")

    def pick(index, carry):
        owner = table_ref[index]
        for step in range(steps):
            value = query_ref[owner, step, index // sources].astype(f32)
            at = pl.ds(pl.multiple_of((index * steps + step) * heads, heads), heads)
            picked[at, :] = value[:, :nope]
            ropes[at, :] = value[:, nope:].astype(bf16)
        return carry

    if count <= 16:
        for index in range(count):
            pick(index, 0)
    else:
        lax.fori_loop(0, count, pick, 0)
    for head in range(heads):
        at = pl.ds(head, count * steps, stride=heads)
        value = jnp.dot(picked[at, :].astype(bf16), uk_ref[head], preferred_element_type=f32)
        if chunk < made.shape[1]:
            spare = jnp.zeros((count * steps, made.shape[1] - chunk), f32)
            value = jnp.concatenate([value, spare], axis=1)
        made[at, :] = value
    small = width - chunk
    pair = lax.broadcasted_iota(jnp.int32, (rope, small), 0)
    pair = pair == lax.broadcasted_iota(jnp.int32, (rope, small), 1) + rank * small
    turned = jnp.dot(
        ropes[...], jnp.where(pair, 1.0, 0.0).astype(bf16), preferred_element_type=f32
    )
    own = own_ref[...].astype(f32)
    scale = lax.rsqrt(jnp.mean(own * own, axis=-1, keepdims=True) + epsilon)
    own = (own * scale * gain_ref[...].astype(f32)).astype(bf16)
    depth = wt_ref.shape[1]
    for section in range(sections):
        normed[section] = own[:, section * depth : (section + 1) * depth]
    fresh = lax.dot_general(
        normed[lax.axis_index("section")],
        wt_ref[...],
        (((1,), (1,)), ((), ())),
        preferred_element_type=f32,
    )
    for source in range(experts):
        lines = [
            fresh[step * sources + source :, part * width : (part + 1) * width][:1]
            for step in range(steps)
            for part in range(experts)
        ]
        lines = jnp.concatenate(lines, axis=0).astype(bf16)
        for section in range(sections):
            index = source * sections + section
            at = slice(index * block, (index + 1) * block)
            value = jnp.concatenate([made[at, :chunk], turned[at]], axis=1)
            out_ref[index, :block, :] = value.astype(bf16)
            out_ref[index, block:, :] = lines


def absorb_queries(table, queries, w_uk, own, gain, w_turned, prompts, sections):
    experts, steps, sources, heads, wide = queries.shape
    _, nope, chunk = w_uk.shape
    width = chunk + (wide - nope) // experts
    rows = prompts * steps * heads + steps * experts
    count = experts * sources * steps * heads
    held = pl.BlockSpec(memory_space=pltpu.VMEM)
    return pl.pallas_call(
        functools.partial(query_kernel, experts, sections, prompts, nope),
        out_shape=jax.ShapeDtypeStruct((experts * sections, rows, width), jnp.bfloat16),
        in_specs=[pl.BlockSpec(memory_space=pltpu.SMEM)] + [held] * 5,
        out_specs=held,
        scratch_shapes=[
            pltpu.VMEM((count, nope), jnp.float32),
            pltpu.VMEM((count, wide - nope), jnp.bfloat16),
            pltpu.VMEM((count, max(chunk, 128)), jnp.float32),
            pltpu.VMEM((sections, own.shape[0], w_turned.shape[1]), jnp.bfloat16),
        ],
        compiler_params=params(),
        name="absorb_queries",
    )(table, queries, w_uk, own, gain[None], w_turned)


def attend_kernel(parts, experts, sections, heads, steps, latent, score_scale, *refs):
    part_refs = refs[:parts]
    (length_ref, owner_ref, gain_ref, cosine_ref, sine_ref, token_cosine_ref, token_sine_ref,
     block_ref) = refs[parts : parts + 8]
    out_refs, held = refs[parts + 8 : -1], refs[-1]
    f32, bf16 = jnp.float32, jnp.bfloat16
    nt = (((1,), (1,)), ((), ()))
    prompt = pl.program_id(0)
    gain = gain_ref[...].astype(f32)
    rows = steps * heads
    chunk = latent // experts
    whole = pl.num_programs(0) * rows

    def turn(values, cosine, sine):
        half = values.shape[1] // 2
        other = jnp.concatenate([values[:, half:], values[:, :half]], axis=1)
        return values * cosine + other * sine

    def scaled(values):
        scale = lax.rsqrt(jnp.mean(values * values, axis=-1, keepdims=True) + epsilon)
        return values * scale * gain

    at = pl.ds(pl.multiple_of(prompt * rows, rows), rows)
    token_cosine, token_sine = token_cosine_ref[0], token_sine_ref[0]
    latents, ropes = [], []
    for section in range(sections):
        pieces = [block_ref[i * sections + section, at, :] for i in range(experts)]
        latents.append(jnp.concatenate([piece[:, :chunk] for piece in pieces], axis=1))
        rope = jnp.concatenate([piece[:, chunk:].astype(f32) for piece in pieces], axis=1)
        ropes.append(turn(rope, token_cosine, token_sine).astype(bf16))
    query = jnp.concatenate(latents, axis=0)
    query_rope = jnp.concatenate(ropes, axis=0)

    owner = owner_ref[prompt]
    lines = 0
    for section in range(sections):
        lines = lines + block_ref[owner * sections + section, whole:, :].astype(f32)
    recent, recent_rope = [], []
    for step in range(steps):
        line = jnp.concatenate(
            [lines[step * experts + part :][:1] for part in range(experts)], axis=1
        )
        recent.append(scaled(line[:, :latent]))
        recent_rope.append(
            turn(
                line[:, latent:],
                token_cosine[step * heads : step * heads + 1],
                token_sine[step * heads : step * heads + 1],
            )
        )
    spare = -steps % 16
    recent = jnp.concatenate(recent + [jnp.zeros((spare, latent), f32)], axis=0).astype(bf16)
    rope = recent_rope[0].shape[1]
    recent_rope = jnp.concatenate(
        recent_rope + [jnp.zeros((spare, rope), f32)], axis=0
    ).astype(bf16)

    projected = part_refs[0][0].astype(f32)
    for ref in part_refs[1:]:
        projected = projected + ref[0].astype(f32)
    keys = scaled(projected[:, :latent]).astype(bf16)
    key_rope = turn(projected[:, latent:], cosine_ref[...], sine_ref[...]).astype(bf16)
    scores = lax.dot_general(query, keys, nt, preferred_element_type=f32)
    scores = scores + lax.dot_general(query_rope, key_rope, nt, preferred_element_type=f32)
    fresh = lax.dot_general(query, recent, nt, preferred_element_type=f32)
    fresh = fresh + lax.dot_general(query_rope, recent_rope, nt, preferred_element_type=f32)
    place = lax.broadcasted_iota(jnp.int32, scores.shape, 1)
    scores = jnp.where(place < length_ref[prompt], scores * score_scale, masked_value)
    row = lax.broadcasted_iota(jnp.int32, (rows, fresh.shape[1]), 0)
    place = lax.broadcasted_iota(jnp.int32, (rows, fresh.shape[1]), 1)
    seen = jnp.where(place < 1, 1.0, 0.0)
    for step in range(1, steps):
        seen = jnp.where((place <= step) & (row >= step * heads), 1.0, seen)
    seen = jnp.concatenate([seen] * sections, axis=0)
    fresh = jnp.where(seen > 0.5, fresh * score_scale, masked_value)
    most = jnp.maximum(
        jnp.max(scores, axis=-1, keepdims=True), jnp.max(fresh, axis=-1, keepdims=True)
    )
    scores = jnp.exp(scores - most)
    fresh = jnp.exp(fresh - most)
    total = jnp.sum(scores, axis=-1, keepdims=True) + jnp.sum(fresh, axis=-1, keepdims=True)
    scores = (scores / total).astype(bf16)
    fresh = (fresh / total).astype(bf16)
    mixed = jnp.dot(scores, keys, preferred_element_type=f32)
    mixed = mixed + jnp.dot(fresh, recent, preferred_element_type=f32)
    mixed = mixed.astype(bf16)
    for section in range(sections):
        held[section] = mixed[section * rows : (section + 1) * rows]
    rank = lax.axis_index("section")
    for mask, ref in enumerate(out_refs):
        ref[0] = held[rank ^ mask]


def attend(parts, lengths, owners, kv_gain, blocks, steps, heads, experts, sections, score_scale):
    prompts, positions, width = parts[0].shape
    latent = kv_gain.shape[0]
    cosine, sine = rotation(jnp.arange(positions), width - latent)
    cosine = jnp.concatenate([cosine, cosine], axis=-1)
    sine = jnp.concatenate([-sine, sine], axis=-1)
    token_pos = lengths[:, None] + jnp.arange(steps * heads)[None, :] // heads
    token_cosine, token_sine = rotation(token_pos, width - latent)
    token_cosine = jnp.concatenate([token_cosine, token_cosine], axis=-1)
    token_sine = jnp.concatenate([-token_sine, token_sine], axis=-1)
    one = lambda shape: pl.BlockSpec((1,) + shape, lambda i: (i, 0, 0))
    whole = lambda shape: pl.BlockSpec(shape, lambda i: (0,) * len(shape))
    out = (steps * heads, latent)
    return pl.pallas_call(
        functools.partial(
            attend_kernel, len(parts), experts, sections, heads, steps, latent, score_scale
        ),
        grid=(prompts,),
        out_shape=[jax.ShapeDtypeStruct((prompts,) + out, jnp.bfloat16)] * sections,
        in_specs=[one((positions, width))] * len(parts)
        + [pl.BlockSpec(memory_space=pltpu.SMEM)] * 2
        + [
            whole((1, latent)),
            whole(cosine.shape),
            whole(sine.shape),
            one(token_cosine.shape[1:]),
            one(token_sine.shape[1:]),
            whole(blocks.shape),
        ],
        out_specs=[one(out)] * sections,
        scratch_shapes=[pltpu.VMEM((sections,) + out, jnp.bfloat16)],
        compiler_params=params(),
        name="attend",
    )(*parts, lengths, owners, kv_gain[None], cosine, sine, token_cosine, token_sine, blocks)


def value_kernel(experts, sections, heads, *refs):
    latent_refs, uv_refs = refs[:sections], refs[sections : sections + experts]
    order_ref, out_ref, held = refs[sections + experts :]
    f32, bf16 = jnp.float32, jnp.bfloat16
    chunk = uv_refs[0].shape[2]
    rows = latent_refs[0].shape[0]
    for mask, ref in enumerate(latent_refs):
        for index in range(experts):
            held[index, mask * rows : (mask + 1) * rows, :chunk] = ref[
                :, index * chunk : (index + 1) * chunk
            ].astype(f32)
    rank = lax.axis_index("expert")
    values = []
    for head in range(heads):
        at = pl.ds(head, sections * rows // heads, stride=heads)
        total = 0
        for mask, ref in enumerate(uv_refs):
            total = total + lax.dot_general(
                held[rank ^ mask, at, :][:, :chunk].astype(bf16),
                ref[head],
                (((1,), (1,)), ((), ())),
                preferred_element_type=f32,
            )
        values.append(total.astype(bf16))
    values = jnp.concatenate(values, axis=1)
    out_ref[...] = jnp.dot(order_ref[...], values, preferred_element_type=f32).astype(bf16)


def head_products(latents, uv_parts, order):
    rows, width = latents[0].shape
    heads, value, _ = uv_parts[0].shape
    held = pl.BlockSpec(memory_space=pltpu.VMEM)
    total = rows * len(latents)
    return pl.pallas_call(
        functools.partial(value_kernel, len(uv_parts), len(latents), heads),
        out_shape=jax.ShapeDtypeStruct((total // heads, heads * value), jnp.bfloat16),
        in_specs=[held] * (len(latents) + len(uv_parts) + 1),
        out_specs=held,
        scratch_shapes=[
            pltpu.VMEM((len(uv_parts), total, max(width // len(uv_parts), 128)), jnp.float32)
        ],
        compiler_params=params(),
        name="head_products",
    )(*latents, *uv_parts, order)


def output_kernel(count, order_ref, *refs):
    value_refs = refs[:count]
    weight_ref, out_ref, held, sems = refs[count:]
    pieces, depth, _ = held.shape
    copies = []
    for piece in range(pieces):
        source = weight_ref.at[pl.ds(piece * depth, depth)]
        copies.append(pltpu.make_async_copy(source, held.at[piece], sems.at[piece]))
        copies[-1].start()
    values = jnp.concatenate([ref[...] for ref in value_refs], axis=0)
    values = jnp.dot(order_ref[...], values, preferred_element_type=jnp.float32)
    values = values.astype(jnp.bfloat16)
    total = 0
    for piece in range(pieces):
        copies[piece].wait()
        total = total + jnp.dot(
            values[:, piece * depth : (piece + 1) * depth],
            held[piece],
            preferred_element_type=jnp.float32,
        )
    out_ref[...] = total.astype(out_ref.dtype)


def output_product(values, order, weight):
    rows = sum(value.shape[0] for value in values)
    depth, width = weight.shape
    pieces = 4
    held = pl.BlockSpec(memory_space=pltpu.VMEM)
    return pl.pallas_call(
        functools.partial(output_kernel, len(values)),
        out_shape=jax.ShapeDtypeStruct((rows, width), jnp.bfloat16),
        in_specs=[held] * (len(values) + 1) + [pl.BlockSpec(memory_space=pltpu.HBM)],
        out_specs=held,
        scratch_shapes=[
            pltpu.VMEM((pieces, depth // pieces, width), weight.dtype),
            pltpu.SemaphoreType.DMA((pieces,)),
        ],
        compiler_params=params(),
        name="output_product",
    )(order, *values, weight)


def expert_kernel(experts, sections, *refs):
    attended_refs, own_refs = refs[:experts], refs[experts : 2 * experts]
    gain_ref, gate_ref, up_ref, down_ref = refs[2 * experts : 2 * experts + 4]
    out_refs = refs[2 * experts + 4 : 3 * experts + 4]
    near_ref = refs[3 * experts + 4]
    gate_held, up_held, down_held, columns, sems = refs[3 * experts + 5 :]
    f32, bf16 = jnp.float32, jnp.bfloat16
    count = gate_held.shape[0]
    copies = []
    for x in range(count):
        for kind, (source, held) in enumerate(
            ((gate_ref, gate_held), (up_ref, up_held), (down_ref, down_held))
        ):
            copies.append(pltpu.make_async_copy(source.at[x], held.at[x], sems.at[x, kind]))
            copies[-1].start()
    rank = lax.axis_index("expert")
    width = gain_ref.shape[1]
    block = own_refs[0].shape[0]
    for mask, ref in enumerate(attended_refs):
        columns[rank ^ mask] = ref[...]
    attended, hidden, route = [], [], []
    for mask, ref in enumerate(own_refs):
        attended.append(
            jnp.concatenate([columns[i, rank ^ mask] for i in range(experts)], axis=1).astype(f32)
        )
        own = ref[...].astype(f32)
        hidden.append(own[:, :width])
        route.append(own[:, width:])
    near = attended[0]
    mixed = jnp.concatenate(hidden, axis=0) + jnp.concatenate(attended, axis=0)
    route = jnp.concatenate(route, axis=0)
    total_experts = route.shape[1] // 2
    route = route[:, :total_experts] + route[:, total_experts:]
    place = lax.broadcasted_iota(jnp.int32, route.shape, 1)
    scale = lax.rsqrt(jnp.mean(mixed * mixed, axis=-1, keepdims=True) + epsilon)
    rows_in = (mixed * scale * gain_ref[...].astype(f32)).astype(bf16)
    column = width // sections
    total = 0
    for x in range(count):
        weight = jnp.where(place == rank * count + x, route, 0.0)
        weight = jnp.sum(weight, axis=-1, keepdims=True)
        copies[3 * x].wait()
        gate = jnp.dot(rows_in, gate_held[x], preferred_element_type=f32)
        copies[3 * x + 1].wait()
        up = jnp.dot(rows_in, up_held[x], preferred_element_type=f32)
        inner = gate / (1.0 + jnp.exp(-gate)) * up * weight
        copies[3 * x + 2].wait()
        total = total + jnp.dot(inner.astype(bf16), down_held[x], preferred_element_type=f32)
    for section in range(sections):
        at = slice(section * column, (section + 1) * column)
        near_ref[section] = near[:, at].astype(bf16)
        for mask, ref in enumerate(out_refs):
            ref[section] = total[mask * block : (mask + 1) * block, at].astype(bf16)


def run_experts(attended, own, gain, w_gate, w_up, w_down, sections):
    experts = len(own)
    width = gain.shape[0]
    out = jax.ShapeDtypeStruct((sections, own[0].shape[0], width // sections), jnp.bfloat16)
    held = pl.BlockSpec(memory_space=pltpu.VMEM)
    away = pl.BlockSpec(memory_space=pltpu.HBM)
    outs = pl.pallas_call(
        functools.partial(expert_kernel, experts, sections),
        out_shape=[out] * (experts + 1),
        in_specs=[held] * (2 * experts + 1) + [away] * 3,
        out_specs=[held] * (experts + 1),
        scratch_shapes=[
            pltpu.VMEM(w_gate.shape, w_gate.dtype),
            pltpu.VMEM(w_up.shape, w_up.dtype),
            pltpu.VMEM(w_down.shape, w_down.dtype),
            pltpu.VMEM((experts,) + attended[0].shape, jnp.bfloat16),
            pltpu.SemaphoreType.DMA((w_gate.shape[0], 3)),
        ],
        compiler_params=params(48),
        name="run_experts",
    )(*attended, *own, gain[None], w_gate, w_up, w_down)
    return outs[:experts], outs[experts]


def fold_kernel(sections, count, *refs):
    in_refs, out_refs, held = refs[:count], refs[count:-1], refs[-1]
    rank = lax.axis_index("section")
    total = in_refs[0][...].astype(jnp.float32)
    for ref in in_refs[1:]:
        total = total + ref[...].astype(jnp.float32)
    held[...] = total
    for mask, ref in enumerate(out_refs):
        ref[...] = held[rank ^ mask].astype(ref.dtype)


def fold(blocks):
    sections, rows, column = blocks[0].shape
    return pl.pallas_call(
        functools.partial(fold_kernel, sections, len(blocks)),
        out_shape=[jax.ShapeDtypeStruct((rows, column), jnp.bfloat16)] * sections,
        scratch_shapes=[pltpu.VMEM((sections, rows, column), jnp.float32)],
        compiler_params=params(),
        name="fold",
    )(*blocks)


def local(
    prompts,
    owners,
    lengths,
    residual,
    queries,
    expert_ids,
    route_scores,
    attn_gain,
    w_dkv,
    kv_gain,
    w_uk,
    w_uv,
    w_o,
    moe_gain,
    w_gate,
    w_up,
    w_down,
):
    bf16, f32 = jnp.bfloat16, jnp.float32
    expert_rank = lax.axis_index("expert")
    section_rank = lax.axis_index("section")
    group_rank = lax.axis_index("groups")
    experts = lax.axis_size("expert")
    sections = lax.axis_size("section")
    groups = lax.axis_size("groups")
    prompt_count, full_length, width = prompts.shape
    steps, tokens_here, heads, _ = queries.shape
    depth = w_dkv.shape[0]
    piece = depth // (groups * experts)
    rows = prompt_count * full_length
    own_rows = steps * tokens_here

    w_turned = w_dkv.T
    w_piece = lax.dynamic_slice_in_dim(
        w_turned, (expert_rank * groups + group_rank) * piece, piece, 1
    )
    w_parts = spread(w_piece, "section")
    cut = list(cut_columns(prompts.reshape(rows, width), sections, experts))
    queries, cut[0] = lax.optimization_barrier((queries, cut[0]))
    queries_all = lax.all_gather(queries, "expert", axis=0)
    cut = deliver(cut, "expert")
    w_parts = [part for half in w_parts for part in spread(half, "groups")]

    table = owners.reshape(experts, tokens_here)
    length_table = lengths.reshape(experts, tokens_here)
    at = (expert_rank, section_rank * prompt_count)
    my_owner = lax.dynamic_slice(table, at, (1, prompt_count))[0]
    my_length = lax.dynamic_slice(length_table, at, (1, prompt_count))[0]

    queries_all, *cut = lax.optimization_barrier((queries_all, *cut))
    own = residual.reshape(own_rows, width)
    blocks = absorb_queries(
        owners, queries_all, w_uk, own, attn_gain, w_turned, prompt_count, sections
    )
    blocks = lax.all_to_all(blocks, ("expert", "section"), 0, 0, tiled=True)

    expert_total = w_gate.shape[0] * experts
    match_table = (expert_ids[..., None] == jnp.arange(expert_total)).astype(f32)
    weights = route_scale * route_scores / jnp.sum(route_scores, axis=-1, keepdims=True)
    weight_map = jnp.sum(weights[..., None] * match_table, axis=2).reshape(-1, expert_total)
    weight_high = weight_map.astype(bf16)
    weight_low = (weight_map - weight_high.astype(f32)).astype(bf16)
    packed = jnp.concatenate([own, weight_high, weight_low], axis=1)
    w_uv, packed, cut[0] = lax.optimization_barrier((w_uv, packed, cut[0]))
    uv_parts = doubled(w_uv, "expert")

    away = list(project(cut[1:], w_parts, sections, groups))
    near = list(project(cut[:1], w_parts, sections, groups))
    parts = [part.reshape(prompt_count, full_length, -1) for part in deliver(near + away, "expert")]
    blocks, uv_parts[2] = lax.optimization_barrier((blocks, uv_parts[2]))
    out_latent = attend(
        parts,
        my_length,
        my_owner,
        kv_gain,
        blocks,
        steps,
        heads,
        experts,
        sections,
        queries.shape[-1] ** (-0.5),
    )

    out_latent = deliver(out_latent, "section")
    row = lax.dynamic_slice_in_dim(table, expert_rank, 1, 0)[0]
    place = jnp.arange(tokens_here)
    place = (section_rank ^ (place // prompt_count)) * prompt_count + place % prompt_count
    step = jnp.arange(own_rows) % steps
    order = jnp.take(row, place)[jnp.arange(own_rows) // steps] * steps + step
    order = (jnp.arange(own_rows)[:, None] == order[None, :]).astype(bf16)
    head_values = head_products(
        [part.reshape(-1, part.shape[-1]) for part in out_latent], uv_parts, order
    )
    head_values = spread(head_values, "expert")

    total_rows = own_rows * experts
    row = jnp.arange(total_rows)
    source = (row % experts) ^ expert_rank
    order = source * own_rows + row // experts
    order = (order[:, None] == row[None, :]).astype(bf16)
    attended = output_product(head_values, order, w_o)
    attended = sum(part.astype(f32) for part in spread(attended, "section")).astype(bf16)
    attended = attended.reshape(experts, own_rows, -1)
    blocks, near = run_experts(
        spread(attended, "expert"),
        spread(packed, "expert"),
        moe_gain,
        w_gate,
        w_up,
        w_down,
        sections,
    )
    blocks = deliver(fold(deliver(blocks, "expert")), "section")
    column = width // sections
    base = lax.dynamic_slice_in_dim(residual, section_rank * column, column, 2)
    near = lax.dynamic_index_in_dim(near, section_rank, 0, keepdims=False)
    total = base.reshape(own_rows, column).astype(f32) + near.astype(f32)
    total = total + sum(part.astype(f32) for part in blocks)
    return total.astype(bf16).reshape(steps, tokens_here, column)


def solution(mesh):
    placed = (
        P(("groups", "expert", "section"), None, None),
        P("groups"),
        P("groups"),
        P(None, ("groups", "expert"), None),
        P(None, ("groups", "expert"), "section", None),
        P(None, ("groups", "expert"), None),
        P(None, ("groups", "expert"), None),
        P(),
        P("section", None),
        P(),
        P("section", None, "expert"),
        P("section", None, "expert"),
        P("section", "expert"),
        P(),
        P("expert", None, "section"),
        P("expert", None, "section"),
        P("expert", "section", None),
    )
    return jax.shard_map(
        local,
        mesh=mesh,
        in_specs=placed,
        out_specs=P(None, ("groups", "expert"), "section"),
        check_vma=False,
    )
```

time: 152 us -> 127 us (0.84)
  between operations: 15.8 us -> 0.26 us
  waiting for transfers between devices: 34.5 us -> 24.1 us
  blocking collectives: 18 us -> 9.65 us
  Pallas kernels: 12.2 us -> 20.5 us
  starting transfers between devices: 35.9 us -> 42 us
  matrix products: 4.63 us -> 0 us
  other arithmetic: 10.1 us -> 7.41 us
  local copies, waits for them, and re-layouts: 20.2 us -> 22.2 us
    ppermute x25 -> x37, waiting for transfers between devices: 34.3 us -> 24.1 us  [swap(): return lax.ppermute(block, axis, [(i, i ^ mask) for i in range(size)])]
    all_gather x3 -> x1, blocking collectives: 18 us -> 9.65 us  [local(): queries_all = lax.all_gather(queries, 'expert', axis=0)]
    ppermute x25 -> x37, starting transfers between devices: 30.4 us -> 38 us  [swap(): return lax.ppermute(block, axis, [(i, i ^ mask) for i in range(size)])]
    pallas_call x2 -> x4, Pallas kernels: 2.82 us -> 9.59 us  [the longest x1 3.21 us: attend(): pl.pallas_call(functools.partial(attend_kernel, len(parts), experts, sect...]
    unnamed x29 -> x32, local copies, waits for them, and re-layouts: 7.08 us -> 13.6 us
    dot_general x3 -> x0, matrix products: 4.63 us -> none  [the longest x1 2.26 us: local(): jnp.einsum('othxc,xhvc->othv', out_latent, uv_full, preferred_element_typ...]
    slice x8 -> x0, local copies, waits for them, and re-layouts: 2.81 us -> none  [the longest x1 1.03 us: local(): query_part = query_part[:, :prompt_count * steps * heads]]
    dynamic_slice x4 -> x2, local copies, waits for them, and re-layouts: 3.02 us -> 1.18 us  [the longest x1 0.59 us: local(): my_owner = lax.dynamic_slice(table, at, (1, prompt_count))[0]]
  transfers between devices with their start and end apart: 27 -> 38, of which waited for: 12 -> 14; matrix products, arithmetic and copies ran while one was open for 16% -> 11% of each run, Pallas kernels for 2% -> 6%
where the time goes in v4:
time: 127 us; the launch traced here: 126 us
  starting transfers between devices  42 us (33%)
  waiting for transfers between devices  24.1 us (19%)
  local copies, waits for them, and re-layouts  22.2 us (17%)
  Pallas kernels  20.5 us (16%)
  blocking collectives  9.65 us (8%)
  other arithmetic  7.41 us (6%)
    ppermute x37, starting transfers between devices, swap(): return lax.ppermute(block, axis, [(i, i ^ mask) for i in range(size)])  38 us
    ppermute x37, waiting for transfers between devices, swap(): return lax.ppermute(block, axis, [(i, i ^ mask) for i in range(size)])  24.1 us
    unnamed x32, local copies, waits for them, and re-layouts  13.6 us
    all_gather x1, blocking collectives, local(): queries_all = lax.all_gather(queries, 'expert', axis=0)  9.65 us
    pallas_call x1, Pallas kernels, run_experts(): pl.pallas_call(functools.partial(expert_kernel, experts, sections), out_s...  8.24 us
    all_to_all x1, starting transfers between devices, local(): blocks = lax.all_to_all(blocks, ('expert', 'section'), 0, 0, tiled=True)  4.02 us
    pallas_call x1, Pallas kernels, attend(): pl.pallas_call(functools.partial(attend_kernel, len(parts), experts, sect...  3.21 us
  transfers between devices with their start and end apart: 38, of which 14 were waited for; matrix products, arithmetic and copies ran while one was open for 11% of the time, Pallas kernels for 6%

profile of v4, /device:TPU:0, one launch (start us, length us, event | category | flops | bytes accessed | tf_op | source)
XLA Modules:
  0.0 126.1 jit_solution(3225187413930888232)
XLA Ops:
  1.1 3.1 %collective-permute-start.4 = (bf16[576,112]{1,0:T(8,128)(2,1)S(1)}, bf16[576,112]{1,0:T(8,128)(2,1)S(1)}, u32[]{:S(2)}, u32[]{:S(2)}) collective-permute-start(bf16[576,112]{1,0:T(8,128)(2,1)S(1)} %dynamic-slice_bitcast_fusion.refs_1_.refs_3_), channel_id=1, source_target_pairs={{0,1},{1,0},{2,3},{3,2},{4,5},{5,4},{6,7},{7,6},{8,9},{9,8},{10,11... | collective-permute-start | bytes 387080 | tf_op jit(solution)/shard_map/ppermute | solution.py:24
  4.2 2.6 %collective-permute-start.6 = (bf16[576,112]{1,0:T(8,128)(2,1)S(1)}, bf16[576,112]{1,0:T(8,128)(2,1)S(1)}, u32[]{:S(2)}, u32[]{:S(2)}) collective-permute-start(bf16[576,112]{1,0:T(8,128)(2,1)S(1)} %dynamic-slice_bitcast_fusion.refs_1_.refs_3_), channel_id=1, source_target_pairs={{0,2},{1,3},{2,0},{3,1},{4,6},{5,7},{6,4},{7,5},{8,10},{9,11},{10,... | collective-permute-start | bytes 387080 | tf_op jit(solution)/shard_map/ppermute | solution.py:24
  15.4 9.7 %all-gather = bf16[8,4,16,192]{3,2,1,0:T(8,128)(2,1)S(1)} all-gather(bf16[2,4,16,192]{3,2,1,0:T(8,128)(2,1)} %param.21), channel_id=2, replica_groups=mesh['groups'=2,'expert'=4,'section'=4] {'expert'}, dimensions={0}, use_global_device_ids=true | all-gather | bytes 245760 | tf_op jit(solution)/shard_map/all_gather | solution.py:556
  30.2 1.7 %collective-permute-start.3 = (bf16[576,112]{1,0:T(8,128)(2,1)S(1)}, bf16[576,112]{1,0:T(8,128)(2,1)S(1)}, u32[]{:S(2)}, u32[]{:S(2)}) collective-permute-start(bf16[576,112]{1,0:T(8,128)(2,1)S(1)} %dynamic-slice_bitcast_fusion.refs_1_.refs_3_), channel_id=1, source_target_pairs={{0,16},{16,0},{1,17},{17,1},{2,18},{18,2},{3,19},{19,3},{4,20},{20... | collective-permute-start | bytes 387080 | tf_op jit(solution)/shard_map/ppermute | solution.py:24
  41.9 2.0 %absorb_queries.1 = bf16[16,40,144]{2,1,0:T(8,128)(2,1)} custom-call(s32[16]{0:T(128)S(1)} %copy-done.14, bf16[4,2,4,16,192]{4,3,2,1,0:T(8,128)(2,1)S(1)} %bitcast.30, bf16[16,128,128]{2,1,0:T(8,128)(2,1)S(1)} %copy-done.4, bf16[8,3584]{1,0:T(8,128)(2,1)S(1)} %reshape.353.own_ref, bf16[1,3584]{1,0:T(2,128)(2,1)S(1)} %broadcast_in_dim.8.gain_ref, ...), custom_call_target="tpu_custom_call" | custom-call | tf_op jit(solution)/shard_map/absorb_queries/pallas_call | solution.py:182
  43.8 4.0 %all-to-all-start = ((bf16[16,40,144]{2,1,0:T(8,128)(2,1)}), bf16[16,40,144]{2,1,0:T(8,128)(2,1)S(1)}, u32[]{:S(2)}, u32[]{:S(2)}) async-start(bf16[16,40,144]{2,1,0:T(8,128)(2,1)} %absorb_queries.1), calls=%async_computation | async-start | bytes 655360 | tf_op jit(solution)/shard_map/all_to_all | solution.py:571
  53.3 1.7 %collective-permute-start.11 = (bf16[128,576]{1,0:T(8,128)(2,1)}, bf16[128,576]{1,0:T(8,128)(2,1)}, u32[]{:S(2)}, u32[]{:S(2)}) collective-permute-start(bf16[128,576]{1,0:T(8,128)(2,1)} %get-tuple-element.49), channel_id=1, source_target_pairs={{0,8},{4,12},{8,0},{12,4},{1,9},{5,13},{9,1},{13,5},{2,10},{6,14},... | collective-permute-start | bytes 442376 | tf_op jit(solution)/shard_map/ppermute | solution.py:24
  57.1 1.7 %pad_maximum_fusion = (f32[128,64]{1,0:T(8,128)}, f32[128,64]{1,0:T(8,128)}) fusion(f32[128,32]{1,0:T(8,128)} %get-tuple-element.76, f32[128,32]{1,0:T(8,128)S(1)} %get-tuple-element.75, f32[128,32]{1,0:T(8,128)S(1)} %get-tuple-element.74), kind=kLoop, calls=%fused_computation.6 | loop fusion | flops 16384 | bytes 114688 | tf_op jit(solution)/shard_map/concatenate | solution.py:295
  59.4 1.7 %collective-permute-done.11 = bf16[128,576]{1,0:T(8,128)(2,1)} collective-permute-done((bf16[128,576]{1,0:T(8,128)(2,1)}, bf16[128,576]{1,0:T(8,128)(2,1)}, u32[]{:S(2)}, u32[]{:S(2)}) %collective-permute-start.11) | collective-permute-done | bytes 147488 | tf_op jit(solution)/shard_map/ppermute | solution.py:24
  61.1 2.7 %collective-permute-done.12 = bf16[128,576]{1,0:T(8,128)(2,1)} collective-permute-done((bf16[128,576]{1,0:T(8,128)(2,1)}, bf16[128,576]{1,0:T(8,128)(2,1)}, u32[]{:S(2)}, u32[]{:S(2)}) %collective-permute-start.12) | collective-permute-done | bytes 147488 | tf_op jit(solution)/shard_map/ppermute | solution.py:24
  65.4 3.2 %attend.1 = (bf16[1,32,512]{2,1,0:T(8,128)(2,1)S(1)}, bf16[1,32,512]{2,1,0:T(8,128)(2,1)S(1)}, bf16[1,32,512]{2,1,0:T(8,128)(2,1)S(1)}, bf16[1,32,512]{2,1,0:T(8,128)(2,1)S(1)}) custom-call(bf16[1,128,576]{2,1,0:T(8,128)(2,1)S(1)} %bitcast.32, bf16[1,128,576]{2,1,0:T(8,128)(2,1)} %bitcast.5.refs_1_, bf16[1,128,576]{2,1,0:T(8,128)(2,1)} %bitcast.6.refs_2_, ...), custom_call_target="tpu_custom_call" | custom-call | tf_op jit(solution)/shard_map/attend/pallas_call | solution.py:304
  68.7 1.8 %collective-permute-start.14 = (bf16[1,32,512]{2,1,0:T(8,128)(2,1)S(1)}, bf16[1,32,512]{2,1,0:T(8,128)(2,1)S(1)}, u32[]{:S(2)}, u32[]{:S(2)}) collective-permute-start(bf16[1,32,512]{2,1,0:T(8,128)(2,1)S(1)} %get-tuple-element.55), channel_id=1, source_target_pairs={{0,1},{1,0},{2,3},{3,2},{4,5},{5,4},{6,7},{7,6},{8,9},{9,8},{10,11... | collective-permute-start | bytes 98312 | tf_op jit(solution)/shard_map/ppermute | solution.py:24
  73.1 2.7 %collective-permute-done.15 = bf16[1,32,512]{2,1,0:T(8,128)(2,1)S(1)} collective-permute-done((bf16[1,32,512]{2,1,0:T(8,128)(2,1)S(1)}, bf16[1,32,512]{2,1,0:T(8,128)(2,1)S(1)}, u32[]{:S(2)}, u32[]{:S(2)}) %collective-permute-start.15) | collective-permute-done | bytes 32800 | tf_op jit(solution)/shard_map/ppermute | solution.py:24
  75.9 1.9 %collective-permute-done.16 = bf16[1,32,512]{2,1,0:T(8,128)(2,1)S(1)} collective-permute-done((bf16[1,32,512]{2,1,0:T(8,128)(2,1)S(1)}, bf16[1,32,512]{2,1,0:T(8,128)(2,1)S(1)}, u32[]{:S(2)}, u32[]{:S(2)}) %collective-permute-start.16) | collective-permute-done | bytes 32800 | tf_op jit(solution)/shard_map/ppermute | solution.py:24
  77.8 2.4 %head_products.1.refs_0_ = bf16[8,2048]{1,0:T(8,128)(2,1)S(1)} custom-call(bf16[32,512]{1,0:T(8,128)(2,1)S(1)} %bitcast.33, bf16[32,512]{1,0:T(8,128)(2,1)S(1)} %bitcast.34, bf16[32,512]{1,0:T(8,128)(2,1)S(1)} %bitcast.35, bf16[32,512]{1,0:T(8,128)(2,1)S(1)} %bitcast.36, bf16[16,128,128]{2,1,0:T(8,128)(2,1)S(1)} %copy-done.3, ...), custom_call_target="tpu_custom_call" | custom-call | tf_op jit(solution)/shard_map/head_products/pallas_call | solution.py:360
  82.1 2.0 %collective-permute-done.20.refs_2_ = bf16[8,2048]{1,0:T(8,128)(2,1)S(1)} collective-permute-done((bf16[8,2048]{1,0:T(8,128)(2,1)S(1)}, bf16[8,2048]{1,0:T(8,128)(2,1)S(1)}, u32[]{:S(2)}, u32[]{:S(2)}) %collective-permute-start.20) | collective-permute-done | bytes 32800 | tf_op jit(solution)/shard_map/ppermute | solution.py:24
  85.0 2.0 %copy-done = bf16[2048,896]{1,0:T(8,128)(2,1)S(1)} copy-done((bf16[2048,896]{1,0:T(8,128)(2,1)S(1)}, bf16[2048,896]{1,0:T(8,128)(2,1)}, u32[]{:S(2)}) %copy-start) | copy-done | bytes 3670040
  87.0 2.1 %output_product.1 = bf16[32,896]{1,0:T(8,128)(2,1)S(1)} custom-call(bf16[32,32]{1,0:T(8,128)(2,1)S(1)} %fusion.4.order_ref, bf16[8,2048]{1,0:T(8,128)(2,1)S(1)} %head_products.1.refs_0_, bf16[8,2048]{1,0:T(8,128)(2,1)S(1)} %collective-permute-done.19.refs_1_, bf16[8,2048]{1,0:T(8,128)(2,1)S(1)} %collective-permute-done.20.refs_2_, ...), custom_call_target="tpu_custom_call" | custom-call | tf_op jit(solution)/shard_map/output_product/pallas_call | solution.py:401
  90.7 2.9 %collective-permute-start.24 = (bf16[32,896]{1,0:T(8,128)(2,1)S(1)}, bf16[32,896]{1,0:T(8,128)(2,1)S(1)}, u32[]{:S(2)}, u32[]{:S(2)}) collective-permute-start(bf16[32,896]{1,0:T(8,128)(2,1)S(1)} %output_product.1), channel_id=1, source_target_pairs={{0,3},{1,2},{2,1},{3,0},{4,7},{5,6},{6,5},{7,4},{8,11},{9,10},{10,... | collective-permute-start | bytes 172040 | tf_op jit(solution)/shard_map/ppermute | solution.py:24
  95.4 1.8 %collective-permute-done.23 = bf16[32,896]{1,0:T(8,128)(2,1)S(1)} collective-permute-done((bf16[32,896]{1,0:T(8,128)(2,1)S(1)}, bf16[32,896]{1,0:T(8,128)(2,1)S(1)}, u32[]{:S(2)}, u32[]{:S(2)}) %collective-permute-start.23) | collective-permute-done | bytes 57376 | tf_op jit(solution)/shard_map/ppermute | solution.py:24
  99.3 2.8 %collective-permute-done.26.refs_2_ = bf16[4,8,896]{2,1,0:T(8,128)(2,1)S(1)} collective-permute-done((bf16[4,8,896]{2,1,0:T(8,128)(2,1)S(1)}, bf16[4,8,896]{2,1,0:T(8,128)(2,1)S(1)}, u32[]{:S(2)}, u32[]{:S(2)}) %collective-permute-start.26) | collective-permute-done | bytes 57376 | tf_op jit(solution)/shard_map/ppermute | solution.py:24
  103.4 8.2 %run_experts.1 = (bf16[4,8,896]{2,1,0:T(8,128)(2,1)S(1)}, bf16[4,8,896]{2,1,0:T(8,128)(2,1)S(1)}, bf16[4,8,896]{2,1,0:T(8,128)(2,1)S(1)}, bf16[4,8,896]{2,1,0:T(8,128)(2,1)S(1)}, bf16[4,8,896]{2,1,0:T(8,128)(2,1)S(1)}) custom-call(bf16[4,8,896]{2,1,0:T(8,128)(2,1)S(1)} %fusion.refs_0_, bf16[4,8,896]{2,1,0:T(8,128)(2,1)S(1)} %collective-permute-done.25.refs_1_, ...), custom_call_target="tpu_custom_call" | custom-call | tf_op jit(solution)/shard_map/run_experts/pallas_call | solution.py:476
  113.5 2.8 %collective-permute-done.32.refs_2_ = bf16[4,8,896]{2,1,0:T(8,128)(2,1)S(1)} collective-permute-done((bf16[4,8,896]{2,1,0:T(8,128)(2,1)S(1)}, bf16[4,8,896]{2,1,0:T(8,128)(2,1)S(1)}, u32[]{:S(2)}, u32[]{:S(2)}) %collective-permute-start.32) | collective-permute-done | bytes 57376 | tf_op jit(solution)/shard_map/ppermute | solution.py:24
  122.9 2.6 %collective-permute-done.36 = bf16[8,896]{1,0:T(8,128)(2,1)S(1)} collective-permute-done((bf16[8,896]{1,0:T(8,128)(2,1)S(1)}, bf16[8,896]{1,0:T(8,128)(2,1)S(1)}, u32[]{:S(2)}, u32[]{:S(2)}) %collective-permute-start.36) | collective-permute-done | bytes 14368 | tf_op jit(solution)/shard_map/ppermute | solution.py:24
  (131 shorter events, 56.0 us)
Async XLA Ops:
  1.1 34.0 %collective-permute-start.4 = (bf16[576,112]{1,0:T(8,128)(2,1)S(1)}, bf16[576,112]{1,0:T(8,128)(2,1)S(1)}, u32[]{:S(2)}, u32[]{:S(2)}) collective-permute-start(bf16[576,112]{1,0:T(8,128)(2,1)S(1)} %dynamic-slice_bitcast_fusion.refs_1_.refs_3_), channel_id=1, source_target_pairs={{0,1},{1,0},{2,3},{3,2},{4,5},{5,4},{6,7},{7,6},{8,9},{9,8},{10,11... | collective-permute-start | bytes 387080 | tf_op jit(solution)/shard_map/ppermute | solution.py:24
  4.2 31.4 %collective-permute-start.6 = (bf16[576,112]{1,0:T(8,128)(2,1)S(1)}, bf16[576,112]{1,0:T(8,128)(2,1)S(1)}, u32[]{:S(2)}, u32[]{:S(2)}) collective-permute-start(bf16[576,112]{1,0:T(8,128)(2,1)S(1)} %dynamic-slice_bitcast_fusion.refs_1_.refs_3_), channel_id=1, source_target_pairs={{0,2},{1,3},{2,0},{3,1},{4,6},{5,7},{6,4},{7,5},{8,10},{9,11},{10,... | collective-permute-start | bytes 387080 | tf_op jit(solution)/shard_map/ppermute | solution.py:24
  8.4 20.3 %collective-permute-start = (bf16[4,128,224]{2,1,0:T(8,128)(2,1)S(1)}, bf16[4,128,224]{2,1,0:T(8,128)(2,1)S(1)}, u32[]{:S(2)}, u32[]{:S(2)}) collective-permute-start(bf16[4,128,224]{2,1,0:T(8,128)(2,1)S(1)} %get-tuple-element.40), channel_id=1, source_target_pairs={{0,4},{4,0},{8,12},{12,8},{1,5},{5,1},{9,13},{13,9},{2,6},{6,2},{1... | collective-permute-start | bytes 688136 | tf_op jit(solution)/shard_map/ppermute | solution.py:24
  8.5 21.0 %collective-permute-start.1 = (bf16[4,128,224]{2,1,0:T(8,128)(2,1)S(1)}, bf16[4,128,224]{2,1,0:T(8,128)(2,1)S(1)}, u32[]{:S(2)}, u32[]{:S(2)}) collective-permute-start(bf16[4,128,224]{2,1,0:T(8,128)(2,1)S(1)} %get-tuple-element.41), channel_id=1, source_target_pairs={{0,8},{4,12},{8,0},{12,4},{1,9},{5,13},{9,1},{13,5},{2,10},{6,14},... | collective-permute-start | bytes 688136 | tf_op jit(solution)/shard_map/ppermute | solution.py:24
  10.1 21.9 %collective-permute-start.2 = (bf16[4,128,224]{2,1,0:T(8,128)(2,1)S(1)}, bf16[4,128,224]{2,1,0:T(8,128)(2,1)S(1)}, u32[]{:S(2)}, u32[]{:S(2)}) collective-permute-start(bf16[4,128,224]{2,1,0:T(8,128)(2,1)S(1)} %get-tuple-element.42), channel_id=1, source_target_pairs={{0,12},{4,8},{8,4},{12,0},{1,13},{5,9},{9,5},{13,1},{2,14},{6,10},... | collective-permute-start | bytes 688136 | tf_op jit(solution)/shard_map/ppermute | solution.py:24
  29.4 8.0 %collective-permute-start.8 = (bf16[576,112]{1,0:T(8,128)(2,1)S(1)}, bf16[576,112]{1,0:T(8,128)(2,1)S(1)}, u32[]{:S(2)}, u32[]{:S(2)}) collective-permute-start(bf16[576,112]{1,0:T(8,128)(2,1)S(1)} %dynamic-slice_bitcast_fusion.refs_1_.refs_3_), channel_id=1, source_target_pairs={{0,3},{1,2},{2,1},{3,0},{4,7},{5,6},{6,5},{7,4},{8,11},{9,10},{10,... | collective-permute-start | bytes 387080 | tf_op jit(solution)/shard_map/ppermute | solution.py:24
  30.2 17.7 %collective-permute-start.3 = (bf16[576,112]{1,0:T(8,128)(2,1)S(1)}, bf16[576,112]{1,0:T(8,128)(2,1)S(1)}, u32[]{:S(2)}, u32[]{:S(2)}) collective-permute-start(bf16[576,112]{1,0:T(8,128)(2,1)S(1)} %dynamic-slice_bitcast_fusion.refs_1_.refs_3_), channel_id=1, source_target_pairs={{0,16},{16,0},{1,17},{17,1},{2,18},{18,2},{3,19},{19,3},{4,20},{20... | collective-permute-start | bytes 387080 | tf_op jit(solution)/shard_map/ppermute | solution.py:24
  32.6 15.7 %collective-permute-start.13 = (bf16[16,128,128]{2,1,0:T(8,128)(2,1)}, bf16[16,128,128]{2,1,0:T(8,128)(2,1)S(1)}, u32[]{:S(2)}, u32[]{:S(2)}) collective-permute-start(bf16[16,128,128]{2,1,0:T(8,128)(2,1)} %refs_4_.1), channel_id=1, source_target_pairs={{0,8},{4,12},{8,0},{12,4},{1,9},{5,13},{9,1},{13,5},{2,10},{6,14},... | collective-permute-start | bytes 1572872 | tf_op jit(solution)/shard_map/ppermute | solution.py:24
  35.1 13.4 %collective-permute-start.5 = (bf16[576,112]{1,0:T(8,128)(2,1)S(1)}, bf16[576,112]{1,0:T(8,128)(2,1)S(1)}, u32[]{:S(2)}, u32[]{:S(2)}) collective-permute-start(bf16[576,112]{1,0:T(8,128)(2,1)S(1)} %collective-permute-done.4.refs_3_.refs_5_), channel_id=1, source_target_pairs={{0,16},{16,0},{1,17},{17,1},{2,18},{18,2},{3,19},{19,3},{4,20},{20... | collective-permute-start | bytes 387080 | tf_op jit(solution)/shard_map/ppermute | solution.py:24
  35.6 12.9 %collective-permute-start.7 = (bf16[576,112]{1,0:T(8,128)(2,1)S(1)}, bf16[576,112]{1,0:T(8,128)(2,1)S(1)}, u32[]{:S(2)}, u32[]{:S(2)}) collective-permute-start(bf16[576,112]{1,0:T(8,128)(2,1)S(1)} %collective-permute-done.6.refs_5_.refs_7_), channel_id=1, source_target_pairs={{0,16},{16,0},{1,17},{17,1},{2,18},{18,2},{3,19},{19,3},{4,20},{20... | collective-permute-start | bytes 387080 | tf_op jit(solution)/shard_map/ppermute | solution.py:24
  37.5 11.0 %collective-permute-start.9 = (bf16[576,112]{1,0:T(8,128)(2,1)S(1)}, bf16[576,112]{1,0:T(8,128)(2,1)S(1)}, u32[]{:S(2)}, u32[]{:S(2)}) collective-permute-start(bf16[576,112]{1,0:T(8,128)(2,1)S(1)} %collective-permute-done.8.refs_7_.refs_9_), channel_id=1, source_target_pairs={{0,16},{16,0},{1,17},{17,1},{2,18},{18,2},{3,19},{19,3},{4,20},{20... | collective-permute-start | bytes 387080 | tf_op jit(solution)/shard_map/ppermute | solution.py:24
  43.8 15.5 %all-to-all-start = ((bf16[16,40,144]{2,1,0:T(8,128)(2,1)}), bf16[16,40,144]{2,1,0:T(8,128)(2,1)S(1)}, u32[]{:S(2)}, u32[]{:S(2)}) async-start(bf16[16,40,144]{2,1,0:T(8,128)(2,1)} %absorb_queries.1), calls=%async_computation | async-start | bytes 655360 | tf_op jit(solution)/shard_map/all_to_all | solution.py:571
  47.9 25.2 %collective-permute-start.17 = (bf16[16,128,128]{2,1,0:T(8,128)(2,1)}, bf16[16,128,128]{2,1,0:T(8,128)(2,1)S(1)}, u32[]{:S(2)}, u32[]{:S(2)}) collective-permute-start(bf16[16,128,128]{2,1,0:T(8,128)(2,1)} %refs_4_.1), channel_id=1, source_target_pairs={{0,4},{4,0},{8,12},{12,8},{1,5},{5,1},{9,13},{13,9},{2,6},{6,2},{1... | collective-permute-start | bytes 1572872 | tf_op jit(solution)/shard_map/ppermute | solution.py:24
  48.4 29.4 %collective-permute-start.18 = (bf16[16,128,128]{2,1,0:T(8,128)(2,1)S(1)}, bf16[16,128,128]{2,1,0:T(8,128)(2,1)}, u32[]{:S(2)}, u32[]{:S(2)}) collective-permute-start(bf16[16,128,128]{2,1,0:T(8,128)(2,1)S(1)} %collective-permute-done.13.refs_6_), channel_id=1, source_target_pairs={{0,4},{4,0},{8,12},{12,8},{1,5},{5,1},{9,13},{13,9},{2,6},{6,2},{1... | collective-permute-start | bytes 1572872 | tf_op jit(solution)/shard_map/ppermute | solution.py:24
  52.9 6.5 %collective-permute-start.10 = (bf16[128,576]{1,0:T(8,128)(2,1)}, bf16[128,576]{1,0:T(8,128)(2,1)}, u32[]{:S(2)}, u32[]{:S(2)}) collective-permute-start(bf16[128,576]{1,0:T(8,128)(2,1)} %get-tuple-element.48), channel_id=1, source_target_pairs={{0,4},{4,0},{8,12},{12,8},{1,5},{5,1},{9,13},{13,9},{2,6},{6,2},{1... | collective-permute-start | bytes 442376 | tf_op jit(solution)/shard_map/ppermute | solution.py:24
  53.3 7.8 %collective-permute-start.11 = (bf16[128,576]{1,0:T(8,128)(2,1)}, bf16[128,576]{1,0:T(8,128)(2,1)}, u32[]{:S(2)}, u32[]{:S(2)}) collective-permute-start(bf16[128,576]{1,0:T(8,128)(2,1)} %get-tuple-element.49), channel_id=1, source_target_pairs={{0,8},{4,12},{8,0},{12,4},{1,9},{5,13},{9,1},{13,5},{2,10},{6,14},... | collective-permute-start | bytes 442376 | tf_op jit(solution)/shard_map/ppermute | solution.py:24
  55.0 8.8 %collective-permute-start.12 = (bf16[128,576]{1,0:T(8,128)(2,1)}, bf16[128,576]{1,0:T(8,128)(2,1)}, u32[]{:S(2)}, u32[]{:S(2)}) collective-permute-start(bf16[128,576]{1,0:T(8,128)(2,1)} %get-tuple-element.50), channel_id=1, source_target_pairs={{0,12},{4,8},{8,4},{12,0},{1,13},{5,9},{9,5},{13,1},{2,14},{6,10},... | collective-permute-start | bytes 442376 | tf_op jit(solution)/shard_map/ppermute | solution.py:24
  70.4 5.4 %collective-permute-start.15 = (bf16[1,32,512]{2,1,0:T(8,128)(2,1)S(1)}, bf16[1,32,512]{2,1,0:T(8,128)(2,1)S(1)}, u32[]{:S(2)}, u32[]{:S(2)}) collective-permute-start(bf16[1,32,512]{2,1,0:T(8,128)(2,1)S(1)} %get-tuple-element.56), channel_id=1, source_target_pairs={{0,2},{1,3},{2,0},{3,1},{4,6},{5,7},{6,4},{7,5},{8,10},{9,11},{10,... | collective-permute-start | bytes 98312 | tf_op jit(solution)/shard_map/ppermute | solution.py:24
  72.1 5.7 %collective-permute-start.16 = (bf16[1,32,512]{2,1,0:T(8,128)(2,1)S(1)}, bf16[1,32,512]{2,1,0:T(8,128)(2,1)S(1)}, u32[]{:S(2)}, u32[]{:S(2)}) collective-permute-start(bf16[1,32,512]{2,1,0:T(8,128)(2,1)S(1)} %get-tuple-element.57), channel_id=1, source_target_pairs={{0,3},{1,2},{2,1},{3,0},{4,7},{5,6},{6,5},{7,4},{8,11},{9,10},{10,... | collective-permute-start | bytes 98312 | tf_op jit(solution)/shard_map/ppermute | solution.py:24
  89.1 5.4 %collective-permute-start.22 = (bf16[32,896]{1,0:T(8,128)(2,1)S(1)}, bf16[32,896]{1,0:T(8,128)(2,1)S(1)}, u32[]{:S(2)}, u32[]{:S(2)}) collective-permute-start(bf16[32,896]{1,0:T(8,128)(2,1)S(1)} %output_product.1), channel_id=1, source_target_pairs={{0,1},{1,0},{2,3},{3,2},{4,5},{5,4},{6,7},{7,6},{8,9},{9,8},{10,11... | collective-permute-start | bytes 172040 | tf_op jit(solution)/shard_map/ppermute | solution.py:24
  89.2 8.0 %collective-permute-start.23 = (bf16[32,896]{1,0:T(8,128)(2,1)S(1)}, bf16[32,896]{1,0:T(8,128)(2,1)S(1)}, u32[]{:S(2)}, u32[]{:S(2)}) collective-permute-start(bf16[32,896]{1,0:T(8,128)(2,1)S(1)} %output_product.1), channel_id=1, source_target_pairs={{0,2},{1,3},{2,0},{3,1},{4,6},{5,7},{6,4},{7,5},{8,10},{9,11},{10,... | collective-permute-start | bytes 172040 | tf_op jit(solution)/shard_map/ppermute | solution.py:24
  90.7 6.6 %collective-permute-start.24 = (bf16[32,896]{1,0:T(8,128)(2,1)S(1)}, bf16[32,896]{1,0:T(8,128)(2,1)S(1)}, u32[]{:S(2)}, u32[]{:S(2)}) collective-permute-start(bf16[32,896]{1,0:T(8,128)(2,1)S(1)} %output_product.1), channel_id=1, source_target_pairs={{0,3},{1,2},{2,1},{3,0},{4,7},{5,6},{6,5},{7,4},{8,11},{9,10},{10,... | collective-permute-start | bytes 172040 | tf_op jit(solution)/shard_map/ppermute | solution.py:24
  93.6 5.7 %collective-permute-start.29 = (bf16[8,3616]{1,0:T(8,128)(2,1)}, bf16[8,3616]{1,0:T(8,128)(2,1)S(1)}, u32[]{:S(2)}, u32[]{:S(2)}) collective-permute-start(bf16[8,3616]{1,0:T(8,128)(2,1)} %concatenate.15.refs_4_), channel_id=1, source_target_pairs={{0,8},{4,12},{8,0},{12,4},{1,9},{5,13},{9,1},{13,5},{2,10},{6,14},... | collective-permute-start | bytes 173576 | tf_op jit(solution)/shard_map/ppermute | solution.py:24
  120.0 5.5 %collective-permute-start.36 = (bf16[8,896]{1,0:T(8,128)(2,1)S(1)}, bf16[8,896]{1,0:T(8,128)(2,1)S(1)}, u32[]{:S(2)}, u32[]{:S(2)}) collective-permute-start(bf16[8,896]{1,0:T(8,128)(2,1)S(1)} %get-tuple-element.68), channel_id=1, source_target_pairs={{0,3},{1,2},{2,1},{3,0},{4,7},{5,6},{6,5},{7,4},{8,11},{9,10},{10,... | collective-permute-start | bytes 43016 | tf_op jit(solution)/shard_map/ppermute | solution.py:24
  (30 other events, 203.0 us)

commit v5 on v4

v5 whole, which is shorter than its diff:
```python
import functools
import math

import jax
import jax.numpy as jnp
import numpy as np
from jax import lax
from jax.experimental import pallas as pl
from jax.experimental.pallas import tpu as pltpu
from jax.sharding import PartitionSpec as P

epsilon = 1e-06
masked_value = -1e30
route_scale = 2.5


def rotation(positions, width):
    halfway = width // 2
    frequency = 10000.0 ** (-2.0 * np.arange(halfway) / width)
    angles = np.arange(positions)[:, None] * frequency
    cosine = np.concatenate([np.cos(angles), np.cos(angles)], axis=1)
    sine = np.concatenate([-np.sin(angles), np.sin(angles)], axis=1)
    return jnp.asarray(cosine, jnp.float32), jnp.asarray(sine, jnp.float32)


def swap(block, axis, mask):
    size = lax.axis_size(axis)
    return lax.ppermute(block, axis, [(i, i ^ mask) for i in range(size)])


def deliver(blocks, axis):
    return [blocks[0]] + [swap(blocks[mask], axis, mask) for mask in range(1, len(blocks))]


def spread(block, axis):
    return [block] + [swap(block, axis, mask) for mask in range(1, lax.axis_size(axis))]


def params(*arrays, scale=1):
    held = sum(math.prod(array.shape) * array.dtype.itemsize for array in arrays)
    mebibytes = min(56, 4 + scale * held // 1024 // 1024)
    return pltpu.CompilerParams(vmem_limit_bytes=mebibytes * 1024 * 1024)


def fetch_kernel(count, *refs):
    sems = refs[2 * count]
    copies = [
        pltpu.make_async_copy(refs[index], refs[count + index], sems.at[index])
        for index in range(count)
    ]
    for copy in copies:
        copy.start()
    for copy in copies:
        copy.wait()


def fetch(*arrays):
    size = sum(array.size * array.dtype.itemsize for array in arrays)
    return pl.pallas_call(
        functools.partial(fetch_kernel, len(arrays)),
        out_shape=[pltpu.VMEM(array.shape, array.dtype) for array in arrays],
        in_specs=[pl.BlockSpec(memory_space=pltpu.HBM)] * len(arrays),
        out_specs=[pl.BlockSpec(memory_space=pltpu.VMEM)] * len(arrays),
        scratch_shapes=[pltpu.SemaphoreType.DMA((len(arrays),))],
        compiler_params=pltpu.CompilerParams(vmem_limit_bytes=1024 * 1024),
        cost_estimate=pl.CostEstimate(flops=0, bytes_accessed=2 * size, transcendentals=0),
        name="fetch",
    )(*[pltpu.with_memory_space_constraint(array, pltpu.HBM) for array in arrays])


def doubled(block, axis):
    held = {0: block}
    size = lax.axis_size(axis)
    masks = [1 << bit for bit in range(size.bit_length() - 1)]
    for mask in masks[1:] + masks[:1]:
        for other in list(held):
            held[other ^ mask] = swap(held[other], axis, mask)
    return [held[mask] for mask in range(size)]


def cut_kernel(sections, experts, piece, x_ref, *refs):
    out_refs, held = refs[:experts], refs[experts]
    rank = lax.axis_index("expert")
    for target in range(experts):
        for section in range(sections):
            at = (section * experts + target) * piece
            held[target, section] = x_ref[:, at : at + piece]
    for mask, ref in enumerate(out_refs):
        ref[...] = held[rank ^ mask]


def cut_columns(x, sections, experts):
    rows, width = x.shape
    piece = width // (sections * experts)
    block = jax.ShapeDtypeStruct((sections, rows, piece), x.dtype)
    return pl.pallas_call(
        functools.partial(cut_kernel, sections, experts, piece),
        out_shape=[block] * experts,
        scratch_shapes=[pltpu.VMEM((experts,) + block.shape, x.dtype)],
        compiler_params=params(x, scale=6),
        name="cut_columns",
    )(x)


def project_kernel(count, sections, groups, *refs):
    x_refs = refs[:count]
    w_refs = refs[count : count + sections * groups]
    out_refs = refs[count + sections * groups :]
    section_rank = lax.axis_index("section")
    group_rank = lax.axis_index("groups")
    rows = x_refs[0].shape[1]
    total = 0
    for mask in range(sections):
        held = [w_refs[mask * groups + other][...] for other in range(groups)]
        columns = []
        for group in range(groups):
            chosen = held[0]
            for other in range(1, groups):
                chosen = jnp.where((group_rank ^ other) == group, held[other], chosen)
            columns.append(chosen)
        weights = jnp.concatenate(columns, axis=1)
        x = jnp.concatenate([ref[section_rank ^ mask] for ref in x_refs], axis=0)
        total = total + lax.dot_general(
            x, weights, (((1,), (1,)), ((), ())), preferred_element_type=jnp.float32
        )
    for index, ref in enumerate(out_refs):
        ref[...] = total[index * rows : (index + 1) * rows].astype(ref.dtype)


def project(blocks, w_parts, sections, groups):
    out = jax.ShapeDtypeStruct((blocks[0].shape[1], w_parts[0].shape[0]), jnp.bfloat16)
    return pl.pallas_call(
        functools.partial(project_kernel, len(blocks), sections, groups),
        out_shape=[out] * len(blocks),
        compiler_params=params(*blocks, *w_parts, scale=6),
        name="project",
    )(*blocks, *w_parts)


def query_kernel(
    experts, sections, prompts, nope, *refs
):
    f32, bf16 = jnp.float32, jnp.bfloat16
    table_ref, query_refs = refs[0], refs[1 : 1 + experts]
    uk_ref, own_ref, gain_ref, wt_ref, out_ref, picked, ropes, made, normed, query_ref = refs[
        1 + experts :
    ]
    steps, sources, heads, wide = query_refs[0].shape
    rope = wide - nope
    chunk = uk_ref.shape[2]
    width = out_ref.shape[2]
    count = experts * sources
    block = prompts * steps * heads
    rank = lax.axis_index("expert")

    for mask, ref in enumerate(query_refs):
        query_ref[rank ^ mask] = ref[...]

    def pick(index, carry):
        owner = table_ref[index]
        for step in range(steps):
            value = query_ref[owner, step, index // sources].astype(f32)
            at = pl.ds(pl.multiple_of((index * steps + step) * heads, heads), heads)
            picked[at, :] = value[:, :nope]
            ropes[at, :] = value[:, nope:].astype(bf16)
        return carry

    if count <= 16:
        for index in range(count):
            pick(index, 0)
    else:
        lax.fori_loop(0, count, pick, 0)
    for head in range(heads):
        at = pl.ds(head, count * steps, stride=heads)
        value = jnp.dot(picked[at, :].astype(bf16), uk_ref[head], preferred_element_type=f32)
        if chunk < made.shape[1]:
            spare = jnp.zeros((count * steps, made.shape[1] - chunk), f32)
            value = jnp.concatenate([value, spare], axis=1)
        made[at, :] = value
    small = width - chunk
    pair = lax.broadcasted_iota(jnp.int32, (rope, small), 0)
    pair = pair == lax.broadcasted_iota(jnp.int32, (rope, small), 1) + rank * small
    turned = jnp.dot(
        ropes[...], jnp.where(pair, 1.0, 0.0).astype(bf16), preferred_element_type=f32
    )
    own = jnp.concatenate([own_ref[step] for step in range(steps)], axis=0).astype(f32)
    scale = lax.rsqrt(jnp.mean(own * own, axis=-1, keepdims=True) + epsilon)
    own = (own * scale * gain_ref[...][None].astype(f32)).astype(bf16)
    depth = wt_ref.shape[1]
    for section in range(sections):
        normed[section] = own[:, section * depth : (section + 1) * depth]
    fresh = lax.dot_general(
        normed[lax.axis_index("section")],
        wt_ref[...],
        (((1,), (1,)), ((), ())),
        preferred_element_type=f32,
    )
    for source in range(experts):
        lines = [
            fresh[step * sources + source :, part * width : (part + 1) * width][:1]
            for step in range(steps)
            for part in range(experts)
        ]
        lines = jnp.concatenate(lines, axis=0).astype(bf16)
        for section in range(sections):
            index = source * sections + section
            at = slice(index * block, (index + 1) * block)
            value = jnp.concatenate([made[at, :chunk], turned[at]], axis=1)
            out_ref[index, :block, :] = value.astype(bf16)
            out_ref[index, block:, :] = lines


def absorb_queries(table, queries, w_uk, own, gain, w_turned, prompts, sections):
    experts = len(queries)
    steps, sources, heads, wide = queries[0].shape
    _, nope, chunk = w_uk.shape
    width = chunk + (wide - nope) // experts
    rows = prompts * steps * heads + steps * experts
    count = experts * sources * steps * heads
    held = pl.BlockSpec(memory_space=pltpu.VMEM)
    return pl.pallas_call(
        functools.partial(query_kernel, experts, sections, prompts, nope),
        out_shape=jax.ShapeDtypeStruct((experts * sections, rows, width), jnp.bfloat16),
        in_specs=[pl.BlockSpec(memory_space=pltpu.SMEM)] + [held] * (experts + 4),
        out_specs=held,
        scratch_shapes=[
            pltpu.VMEM((count, nope), jnp.float32),
            pltpu.VMEM((count, wide - nope), jnp.bfloat16),
            pltpu.VMEM((count, max(chunk, 128)), jnp.float32),
            pltpu.VMEM(
                (sections, own.shape[0] * own.shape[1], w_turned.shape[1]), jnp.bfloat16
            ),
            pltpu.VMEM((experts,) + queries[0].shape, jnp.bfloat16),
        ],
        compiler_params=params(*queries, w_uk, own, w_turned, scale=4),
        name="absorb_queries",
    )(table, *queries, w_uk, own, gain, w_turned)


def turn(values, cosine, sine):
    half = values.shape[1] // 2
    other = jnp.concatenate([values[:, half:], values[:, :half]], axis=1)
    return values * cosine + other * sine


def scaled(values, gain):
    scale = lax.rsqrt(jnp.mean(values * values, axis=-1, keepdims=True) + epsilon)
    return values * scale * gain.astype(jnp.float32)


def gather_kernel(
    prompts, experts, sections, sources, heads, steps, latent, length_ref, owner_ref, gain_ref,
    cosine_ref, sine_ref, block_ref, query_ref, query_rope_ref, recent_ref, recent_rope_ref,
    cosine_held, sine_held
):
    f32, bf16 = jnp.float32, jnp.bfloat16
    rows = steps * heads
    chunk = latent // experts
    first = lax.axis_index("expert") * sources + lax.axis_index("section") * prompts
    gain = gain_ref[...][None]
    for prompt in range(prompts):
        length, owner = length_ref[first + prompt], owner_ref[first + prompt]
        for step in range(steps):
            at = slice(step * heads, (step + 1) * heads)
            cosine_held[at, :] = jnp.broadcast_to(
                cosine_ref[pl.ds(length + step, 1), :], (heads, cosine_ref.shape[1])
            )
            sine_held[at, :] = jnp.broadcast_to(
                sine_ref[pl.ds(length + step, 1), :], (heads, sine_ref.shape[1])
            )
        cosine, sine = cosine_held[...], sine_held[...]
        at = slice(prompt * rows, (prompt + 1) * rows)
        for section in range(sections):
            pieces = [block_ref[i * sections + section, at, :] for i in range(experts)]
            to = slice(section * rows, (section + 1) * rows)
            query_ref[prompt, to, :] = jnp.concatenate(
                [piece[:, :chunk] for piece in pieces], axis=1
            )
            rope = jnp.concatenate([piece[:, chunk:].astype(f32) for piece in pieces], axis=1)
            query_rope_ref[prompt, to, :] = turn(rope, cosine, sine).astype(bf16)
        lines = 0
        for section in range(sections):
            lines = lines + block_ref[
                owner * sections + section, prompts * rows :, :
            ].astype(f32)
        recent, recent_rope = [], []
        for step in range(steps):
            line = jnp.concatenate(
                [lines[step * experts + part :][:1] for part in range(experts)], axis=1
            )
            recent.append(scaled(line[:, :latent], gain))
            at = slice(step * heads, step * heads + 1)
            recent_rope.append(turn(line[:, latent:], cosine[at], sine[at]))
        spare = recent_ref.shape[1] - steps
        recent.append(jnp.zeros((spare, latent), f32))
        recent_rope.append(jnp.zeros((spare, recent_rope[0].shape[1]), f32))
        recent_ref[prompt] = jnp.concatenate(recent, axis=0).astype(bf16)
        recent_rope_ref[prompt] = jnp.concatenate(recent_rope, axis=0).astype(bf16)


def gather_queries(blocks, lengths, owners, kv_gain, table, prompts, sources, experts, sections,
                   steps, heads):
    latent = kv_gain.shape[0]
    rope = blocks.shape[2] * experts - latent
    rows = sections * steps * heads
    spare = steps + -steps % 16
    shape = lambda *sizes: jax.ShapeDtypeStruct((prompts,) + sizes, jnp.bfloat16)
    held = pl.BlockSpec(memory_space=pltpu.VMEM)
    return pl.pallas_call(
        functools.partial(
            gather_kernel, prompts, experts, sections, sources, heads, steps, latent
        ),
        out_shape=[shape(rows, latent), shape(rows, rope), shape(spare, latent), shape(spare, rope)],
        in_specs=[pl.BlockSpec(memory_space=pltpu.SMEM)] * 2 + [held] * 4,
        out_specs=[held] * 4,
        scratch_shapes=[pltpu.VMEM((steps * heads, rope), jnp.float32)] * 2,
        compiler_params=params(blocks, scale=4),
        name="gather_queries",
    )(lengths, owners, kv_gain, *table, blocks)


def attend_kernel(parts, sections, sources, heads, steps, score_scale, *refs):
    part_refs = refs[:parts]
    (length_ref, gain_ref, cosine_ref, sine_ref, query_ref, query_rope_ref, recent_ref,
     recent_rope_ref) = refs[parts : parts + 8]
    out_refs, held = refs[parts + 8 : -1], refs[-1]
    f32, bf16 = jnp.float32, jnp.bfloat16
    nt = (((1,), (1,)), ((), ()))
    prompts, _, latent = query_ref.shape
    rows = steps * heads
    section_rank = lax.axis_index("section")
    first = lax.axis_index("expert") * sources + section_rank * prompts
    positions = part_refs[0].shape[0] // prompts
    for prompt in range(prompts):
        at = slice(prompt * positions, (prompt + 1) * positions)
        projected = part_refs[0][at].astype(f32)
        for ref in part_refs[1:]:
            projected = projected + ref[at].astype(f32)
        keys = scaled(projected[:, :latent], gain_ref[...][None]).astype(bf16)
        key_rope = turn(
            projected[:, latent:], cosine_ref[:positions], sine_ref[:positions]
        ).astype(bf16)
        query, query_rope = query_ref[prompt], query_rope_ref[prompt]
        recent, recent_rope = recent_ref[prompt], recent_rope_ref[prompt]
        scores = lax.dot_general(query, keys, nt, preferred_element_type=f32)
        scores = scores + lax.dot_general(query_rope, key_rope, nt, preferred_element_type=f32)
        fresh = lax.dot_general(query, recent, nt, preferred_element_type=f32)
        fresh = fresh + lax.dot_general(query_rope, recent_rope, nt, preferred_element_type=f32)
        place = lax.broadcasted_iota(jnp.int32, scores.shape, 1)
        scores = jnp.where(
            place < length_ref[first + prompt], scores * score_scale, masked_value
        )
        row = lax.broadcasted_iota(jnp.int32, (rows, fresh.shape[1]), 0)
        place = lax.broadcasted_iota(jnp.int32, (rows, fresh.shape[1]), 1)
        seen = jnp.where(place < 1, 1.0, 0.0)
        for step in range(1, steps):
            seen = jnp.where((place <= step) & (row >= step * heads), 1.0, seen)
        seen = jnp.concatenate([seen] * sections, axis=0)
        fresh = jnp.where(seen > 0.5, fresh * score_scale, masked_value)
        most = jnp.maximum(
            jnp.max(scores, axis=-1, keepdims=True), jnp.max(fresh, axis=-1, keepdims=True)
        )
        scores = jnp.exp(scores - most)
        fresh = jnp.exp(fresh - most)
        total = jnp.sum(scores, axis=-1, keepdims=True) + jnp.sum(fresh, axis=-1, keepdims=True)
        scores = (scores / total).astype(bf16)
        fresh = (fresh / total).astype(bf16)
        mixed = jnp.dot(scores, keys, preferred_element_type=f32)
        mixed = mixed + jnp.dot(fresh, recent, preferred_element_type=f32)
        mixed = mixed.astype(bf16)
        for section in range(sections):
            held[section] = mixed[section * rows : (section + 1) * rows]
        for mask, ref in enumerate(out_refs):
            ref[prompt * rows : (prompt + 1) * rows, :] = held[section_rank ^ mask]


def attend(parts, lengths, kv_gain, table, gathered, sources, steps, sections, score_scale):
    prompts, rows, latent = gathered[0].shape
    out = (rows // sections, latent)
    held = pl.BlockSpec(memory_space=pltpu.VMEM)
    return pl.pallas_call(
        functools.partial(
            attend_kernel, len(parts), sections, sources, out[0] // steps, steps, score_scale
        ),
        out_shape=[jax.ShapeDtypeStruct((prompts * out[0], latent), jnp.bfloat16)] * sections,
        in_specs=[held] * len(parts) + [pl.BlockSpec(memory_space=pltpu.SMEM)] + [held] * 7,
        out_specs=[held] * sections,
        scratch_shapes=[pltpu.VMEM((sections,) + out, jnp.bfloat16)],
        compiler_params=params(*parts, *gathered, scale=6),
        name="attend",
    )(*parts, lengths, kv_gain, *table, *gathered)


def value_kernel(experts, sections, heads, steps, sources, *refs):
    owner_ref = refs[0]
    latent_refs, uv_refs = refs[1 : 1 + sections], refs[1 + sections : 1 + sections + experts]
    out_ref, held = refs[1 + sections + experts :]
    f32, bf16 = jnp.float32, jnp.bfloat16
    chunk = uv_refs[0].shape[2]
    rows = latent_refs[0].shape[0]
    for mask, ref in enumerate(latent_refs):
        for index in range(experts):
            held[index, mask * rows : (mask + 1) * rows, :chunk] = ref[
                :, index * chunk : (index + 1) * chunk
            ].astype(f32)
    rank = lax.axis_index("expert")
    values = []
    for head in range(heads):
        at = pl.ds(head, sections * rows // heads, stride=heads)
        total = 0
        for mask, ref in enumerate(uv_refs):
            total = total + lax.dot_general(
                held[rank ^ mask, at, :][:, :chunk].astype(bf16),
                ref[head],
                (((1,), (1,)), ((), ())),
                preferred_element_type=f32,
            )
        values.append(total.astype(bf16))
    values = jnp.concatenate(values, axis=1)
    prompts = sources // sections
    section_rank = lax.axis_index("section")
    size = sources * steps
    to = lax.broadcasted_iota(jnp.int32, (size, size), 0)
    row = lax.broadcasted_iota(jnp.int32, (size, size), 1)
    order = jnp.zeros((size, size), f32)
    for mask in range(sections):
        for prompt in range(prompts):
            owner = owner_ref[
                rank * sources + (section_rank ^ mask) * prompts + prompt
            ]
            for step in range(steps):
                index = (mask * prompts + prompt) * steps + step
                order = jnp.where((row == index) & (to == owner * steps + step), 1.0, order)
    out_ref[...] = jnp.dot(order.astype(bf16), values, preferred_element_type=f32).astype(bf16)


def head_products(owners, latents, uv_parts, steps, sources):
    rows, width = latents[0].shape
    heads, value, _ = uv_parts[0].shape
    held = pl.BlockSpec(memory_space=pltpu.VMEM)
    total = rows * len(latents)
    return pl.pallas_call(
        functools.partial(
            value_kernel, len(uv_parts), len(latents), heads, steps, sources
        ),
        out_shape=jax.ShapeDtypeStruct((total // heads, heads * value), jnp.bfloat16),
        in_specs=[pl.BlockSpec(memory_space=pltpu.SMEM)]
        + [held] * (len(latents) + len(uv_parts)),
        out_specs=held,
        scratch_shapes=[
            pltpu.VMEM((len(uv_parts), total, max(width // len(uv_parts), 128)), jnp.float32)
        ],
        compiler_params=params(*latents, *uv_parts, scale=4),
        name="head_products",
    )(owners, *latents, *uv_parts)


def output_kernel(experts, *refs):
    value_refs = refs[:experts]
    weight_ref, out_ref = refs[experts:]
    values = jnp.concatenate([ref[...] for ref in value_refs], axis=0)
    rows = values.shape[0]
    to = lax.broadcasted_iota(jnp.int32, (rows, rows), 0)
    row = lax.broadcasted_iota(jnp.int32, (rows, rows), 1)
    source = (to & (experts - 1)) ^ lax.axis_index("expert")
    rest = lax.shift_right_logical(to, experts.bit_length() - 1)
    order = jnp.where(row == source * (rows // experts) + rest, 1.0, 0.0).astype(jnp.bfloat16)
    values = jnp.dot(order, values, preferred_element_type=jnp.float32).astype(jnp.bfloat16)
    out_ref[...] = jnp.dot(
        values, weight_ref[...], preferred_element_type=jnp.float32
    ).astype(out_ref.dtype)


def output_product(values, weight):
    rows = sum(value.shape[0] for value in values)
    held = pl.BlockSpec(memory_space=pltpu.VMEM)
    return pl.pallas_call(
        functools.partial(output_kernel, len(values)),
        out_shape=jax.ShapeDtypeStruct((rows, weight.shape[1]), jnp.bfloat16),
        in_specs=[held] * (len(values) + 1),
        out_specs=held,
        compiler_params=params(*values, scale=8),
        name="output_product",
    )(*values, weight)


def expert_kernel(experts, sections, picks, *refs):
    attended_refs, own_refs = refs[:experts], refs[experts : 2 * experts]
    gain_ref, gate_ref, up_ref, down_ref, out_ref, near_ref, columns = refs[2 * experts :]
    f32, bf16 = jnp.float32, jnp.bfloat16
    count = gate_ref.shape[0]
    rank, section_rank = lax.axis_index("expert"), lax.axis_index("section")
    width = gain_ref.shape[0]
    steps, sources, _ = own_refs[0].shape
    block = steps * sources
    for mask, ref in enumerate(attended_refs):
        columns[rank ^ mask] = ref[...]
    attended, hidden, route = [], [], []
    for mask, ref in enumerate(own_refs):
        attended.append(
            jnp.concatenate([columns[i, rank ^ mask] for i in range(experts)], axis=1).astype(f32)
        )
        own = jnp.concatenate([ref[step] for step in range(steps)], axis=0).astype(f32)
        hidden.append(own[:, :width])
        route.append(own[:, width:])
    near = attended[0]
    mixed = jnp.concatenate(hidden, axis=0) + jnp.concatenate(attended, axis=0)
    route = jnp.concatenate(route, axis=0)
    named = route[:, :picks]
    weights = route[:, picks : 2 * picks] + route[:, 2 * picks :]
    weights = route_scale * weights / jnp.sum(weights, axis=-1, keepdims=True)
    scale = lax.rsqrt(jnp.mean(mixed * mixed, axis=-1, keepdims=True) + epsilon)
    rows_in = (mixed * scale * gain_ref[...][None].astype(f32)).astype(bf16)
    column = width // sections
    total = 0
    for x in range(count):
        mine = (rank * count + x).astype(f32)
        weight = jnp.sum(jnp.where(named == mine, weights, 0.0), axis=-1, keepdims=True)
        gate = jnp.dot(rows_in, gate_ref[x], preferred_element_type=f32)
        up = jnp.dot(rows_in, up_ref[x], preferred_element_type=f32)
        inner = gate / (1.0 + jnp.exp(-gate)) * up * weight
        total = total + jnp.dot(inner.astype(bf16), down_ref[x], preferred_element_type=f32)
    for section in range(sections):
        at = slice(section * column, (section + 1) * column)
        near_ref[section] = near[:, at].astype(bf16)
        for mask in range(experts):
            out_ref[(rank ^ mask) * sections + section] = total[
                mask * block : (mask + 1) * block, at
            ].astype(bf16)


def run_experts(attended, own, gain, w_gate, w_up, w_down, picks, sections):
    experts = len(own)
    width = gain.shape[0]
    block = (own[0].shape[0] * own[0].shape[1], width // sections)
    held = pl.BlockSpec(memory_space=pltpu.VMEM)
    return pl.pallas_call(
        functools.partial(expert_kernel, experts, sections, picks),
        out_shape=[
            jax.ShapeDtypeStruct((experts * sections,) + block, jnp.bfloat16),
            jax.ShapeDtypeStruct((sections,) + block, jnp.bfloat16),
        ],
        in_specs=[held] * (2 * experts + 4),
        out_specs=[held] * 2,
        scratch_shapes=[pltpu.VMEM((experts,) + attended[0].shape, jnp.bfloat16)],
        compiler_params=params(*attended, *own, scale=16),
        name="run_experts",
    )(*attended, *own, gain, w_gate, w_up, w_down)


def finish_kernel(block_ref, near_ref, base_ref, out_ref):
    f32 = jnp.float32
    steps, sources, _ = out_ref.shape
    total = near_ref[lax.axis_index("section")].astype(f32)
    for index in range(block_ref.shape[0]):
        total = total + block_ref[index].astype(f32)
    for step in range(steps):
        value = base_ref[step].astype(f32) + total[step * sources : (step + 1) * sources]
        out_ref[step] = value.astype(out_ref.dtype)


def finish(blocks, near, base):
    held = pl.BlockSpec(memory_space=pltpu.VMEM)
    return pl.pallas_call(
        finish_kernel,
        out_shape=jax.ShapeDtypeStruct(base.shape, base.dtype),
        in_specs=[held] * 3,
        out_specs=held,
        compiler_params=params(blocks, near, base, scale=4),
        name="finish",
    )(blocks, near, base)


def local(
    prompts,
    owners,
    lengths,
    residual,
    queries,
    expert_ids,
    route_scores,
    attn_gain,
    w_dkv,
    kv_gain,
    w_uk,
    w_uv,
    w_o,
    moe_gain,
    w_gate,
    w_up,
    w_down,
):
    bf16, f32 = jnp.bfloat16, jnp.float32
    expert_rank = lax.axis_index("expert")
    section_rank = lax.axis_index("section")
    group_rank = lax.axis_index("groups")
    experts = lax.axis_size("expert")
    sections = lax.axis_size("section")
    groups = lax.axis_size("groups")
    prompt_count, full_length, width = prompts.shape
    steps, tokens_here, heads, _ = queries.shape
    depth = w_dkv.shape[0]
    piece = depth // (groups * experts)
    latent = kv_gain.shape[0]
    cache_width = w_dkv.shape[1]
    rows = prompt_count * full_length
    own_rows = steps * tokens_here

    w_turned = w_dkv.T

    def w_piece(group):
        return lax.dynamic_slice_in_dim(
            w_turned, (expert_rank * groups + group) * piece, piece, 1
        )

    halves = spread(w_piece(group_rank), "section")
    queries_all = spread(queries, "expert")
    cut = list(cut_columns(prompts.reshape(rows, width), sections, experts))
    cut = deliver(cut, "expert")
    queries_all[0], *rest = lax.optimization_barrier((queries_all[0], *cut[1:], *halves[1:]))
    cut = cut[:1] + rest[: experts - 1]
    halves = halves[:1] + rest[experts - 1 :]
    w_parts = halves[:1] + [w_piece(group_rank ^ other) for other in range(1, groups)]
    for half in halves[1:]:
        w_parts += spread(half, "groups")

    blocks = absorb_queries(
        owners, queries_all, w_uk, residual, attn_gain, w_turned, prompt_count, sections
    )
    blocks = lax.all_to_all(blocks, ("expert", "section"), 0, 0, tiled=True)

    high = route_scores.astype(bf16)
    low = (route_scores - high.astype(f32)).astype(bf16)
    packed = jnp.concatenate([residual, expert_ids.astype(bf16), high, low], axis=2)
    w_uv, packed, cut[1] = lax.optimization_barrier((w_uv, packed, cut[1]))
    uv_parts = doubled(w_uv, "expert")
    packed = spread(packed, "expert")

    away = list(project(cut[1:], w_parts, sections, groups))
    near = list(project(cut[:1], w_parts, sections, groups))
    parts = deliver(near + away, "expert")
    table = rotation(full_length + steps + -(full_length + steps) % 8, cache_width - latent)
    gathered = list(gather_queries(
        blocks, lengths, owners, kv_gain, table, prompt_count, tokens_here, experts, sections,
        steps, heads
    ))
    gathered[0], *rest = lax.optimization_barrier((gathered[0], *uv_parts, *packed))
    uv_parts, packed = rest[:experts], rest[experts:]
    out_latent = attend(
        parts, lengths, kv_gain, table, gathered, tokens_here, steps, sections,
        queries.shape[-1] ** (-0.5),
    )

    out_latent = deliver(out_latent, "section")
    head_values = head_products(owners, out_latent, uv_parts, steps, tokens_here)
    head_values = spread(head_values, "expert")

    (w_o,) = fetch(w_o)
    (w_gate,) = fetch(w_gate)
    (w_up,) = fetch(w_up)
    (w_down,) = fetch(w_down)
    attended = output_product(head_values, w_o)
    attended = sum(part.astype(f32) for part in spread(attended, "section")).astype(bf16)
    attended = attended.reshape(experts, own_rows, -1)
    blocks, near = run_experts(
        spread(attended, "expert"),
        packed,
        moe_gain,
        w_gate,
        w_up,
        w_down,
        expert_ids.shape[2],
        sections,
    )
    blocks = lax.all_to_all(blocks, ("expert", "section"), 0, 0, tiled=True)
    column = width // sections
    base = lax.dynamic_slice_in_dim(residual, section_rank * column, column, 2)
    return finish(blocks, near, base)


def solution(mesh):
    placed = (
        P(("groups", "expert", "section"), None, None),
        P("groups"),
        P("groups"),
        P(None, ("groups", "expert"), None),
        P(None, ("groups", "expert"), "section", None),
        P(None, ("groups", "expert"), None),
        P(None, ("groups", "expert"), None),
        P(),
        P("section", None),
        P(),
        P("section", None, "expert"),
        P("section", None, "expert"),
        P("section", "expert"),
        P(),
        P("expert", None, "section"),
        P("expert", None, "section"),
        P("expert", "section", None),
    )
    return jax.shard_map(
        local,
        mesh=mesh,
        in_specs=placed,
        out_specs=P(None, ("groups", "expert"), "section"),
        check_vma=False,
    )
```

time: 127 us -> 144 us (1.13)
  waiting for transfers between devices: 24.1 us -> 54.4 us
  blocking collectives: 9.65 us -> 0 us
  Pallas kernels: 20.5 us -> 27 us
  other arithmetic: 7.41 us -> 1.49 us
  local copies, waits for them, and re-layouts: 22.2 us -> 17.2 us
    ppermute x37 -> x33, waiting for transfers between devices: 24.1 us -> 45.9 us  [swap(): return lax.ppermute(block, axis, [(i, i ^ mask) for i in range(size)])]
    all_gather x1 -> x0, blocking collectives: 9.65 us -> none  [local(): queries_all = lax.all_gather(queries, 'expert', axis=0)]
    all_to_all x1 -> x2, waiting for transfers between devices: 0.01 us -> 8.49 us  [local(): blocks = lax.all_to_all(blocks, ('expert', 'section'), 0, 0, tiled=True)]
    pallas_call x3 -> x8, Pallas kernels: 11.5 us -> 19.8 us  [the longest x4 11.4 us: fetch(): pl.pallas_call(functools.partial(fetch_kernel, len(arrays)), out_shape=[p...]
    all_to_all x1 -> x2, starting transfers between devices: 4.02 us -> 10.2 us  [local(): blocks = lax.all_to_all(blocks, ('expert', 'section'), 0, 0, tiled=True)]
    ppermute x37 -> x33, starting transfers between devices: 38 us -> 32.5 us  [swap(): return lax.ppermute(block, axis, [(i, i ^ mask) for i in range(size)])]
    reshape x4 -> x0, local copies, waits for them, and re-layouts: 2.93 us -> none  [the longest x1 0.84 us: local(): own = residual.reshape(own_rows, width)]
    concatenate x2 -> x0, other arithmetic: 2.53 us -> none  [the longest x1 1.66 us: attend(): cosine = jnp.concatenate([cosine, cosine], axis=-1)]
  transfers between devices with their start and end apart: 38 -> 35, of which waited for: 14 -> 15; matrix products, arithmetic and copies ran while one was open for 11% -> 2% of each run, Pallas kernels for 6% -> 12%
where the time goes in v5:
time: 144 us; the launch traced here: 143 us
  waiting for transfers between devices  54.4 us (38%)
  starting transfers between devices  42.7 us (30%)
  Pallas kernels  27 us (19%)
  local copies, waits for them, and re-layouts  17.2 us (12%)
  other arithmetic  1.49 us (1%)
    ppermute x33, waiting for transfers between devices, swap(): return lax.ppermute(block, axis, [(i, i ^ mask) for i in range(size)])  45.9 us
    ppermute x33, starting transfers between devices, swap(): return lax.ppermute(block, axis, [(i, i ^ mask) for i in range(size)])  32.5 us
    unnamed x56, local copies, waits for them, and re-layouts  14.3 us
    pallas_call x4, Pallas kernels, fetch(): pl.pallas_call(functools.partial(fetch_kernel, len(arrays)), out_shape=[p...  11.4 us
    all_to_all x2, starting transfers between devices, local(): blocks = lax.all_to_all(blocks, ('expert', 'section'), 0, 0, tiled=True)  10.2 us
    all_to_all x2, waiting for transfers between devices, local(): blocks = lax.all_to_all(blocks, ('expert', 'section'), 0, 0, tiled=True)  8.49 us
    pallas_call x1, Pallas kernels, run_experts(): pl.pallas_call(functools.partial(expert_kernel, experts, sections, picks)...  5.04 us
  transfers between devices with their start and end apart: 35, of which 15 were waited for; matrix products, arithmetic and copies ran while one was open for 2% of the time, Pallas kernels for 12%

profile of v5, /device:TPU:0, one launch (start us, length us, event | category | flops | bytes accessed | tf_op | source)
XLA Modules:
  0.0 143.2 jit_solution(16746650524226977043)
XLA Ops:
  1.3 3.1 %collective-permute-start.3 = (bf16[576,112]{1,0:T(8,128)(2,1)S(1)}, bf16[576,112]{1,0:T(8,128)(2,1)S(1)}, u32[]{:S(2)}, u32[]{:S(2)}) collective-permute-start(bf16[576,112]{1,0:T(8,128)(2,1)S(1)} %get-tuple-element.80.refs_1_.refs_3_), channel_id=1, source_target_pairs={{0,1},{1,0},{2,3},{3,2},{4,5},{5,4},{6,7},{7,6},{8,9},{9,8},{10,11... | collective-permute-start | bytes 387080 | tf_op jit(solution)/shard_map/ppermute | solution.py:28
  8.7 2.6 %collective-permute-start.4 = (bf16[576,112]{1,0:T(8,128)(2,1)S(1)}, bf16[576,112]{1,0:T(8,128)(2,1)S(1)}, u32[]{:S(2)}, u32[]{:S(2)}) collective-permute-start(bf16[576,112]{1,0:T(8,128)(2,1)S(1)} %get-tuple-element.80.refs_1_.refs_3_), channel_id=1, source_target_pairs={{0,2},{1,3},{2,0},{3,1},{4,6},{5,7},{6,4},{7,5},{8,10},{9,11},{10,... | collective-permute-start | bytes 387080 | tf_op jit(solution)/shard_map/ppermute | solution.py:28
  13.7 8.1 %collective-permute-done.4.refs_5_.refs_7_ = bf16[576,112]{1,0:T(8,128)(2,1)S(1)} collective-permute-done((bf16[576,112]{1,0:T(8,128)(2,1)S(1)}, bf16[576,112]{1,0:T(8,128)(2,1)S(1)}, u32[]{:S(2)}, u32[]{:S(2)}) %collective-permute-start.4) | collective-permute-done | bytes 129056 | tf_op jit(solution)/shard_map/ppermute | solution.py:28
  24.8 12.5 %collective-permute-done.16.refs_7_ = bf16[16,128,128]{2,1,0:T(8,128)(2,1)S(1)} collective-permute-done((bf16[16,128,128]{2,1,0:T(8,128)(2,1)}, bf16[16,128,128]{2,1,0:T(8,128)(2,1)S(1)}, u32[]{:S(2)}, u32[]{:S(2)}) %collective-permute-start.16) | collective-permute-done | bytes 524320 | tf_op jit(solution)/shard_map/ppermute | solution.py:28
  39.3 2.9 %collective-permute-done.13.refs_3_ = bf16[2,4,16,192]{3,2,1,0:T(8,128)(2,1)S(1)} collective-permute-done((bf16[2,4,16,192]{3,2,1,0:T(8,128)(2,1)}, bf16[2,4,16,192]{3,2,1,0:T(8,128)(2,1)S(1)}, u32[]{:S(2)}, u32[]{:S(2)}) %collective-permute-start.13) | collective-permute-done | bytes 49184 | tf_op jit(solution)/shard_map/ppermute | solution.py:28
  49.1 2.0 %absorb_queries.1 = bf16[16,40,144]{2,1,0:T(8,128)(2,1)} custom-call(s32[16]{0:T(128)S(1)} %copy-done.24, bf16[2,4,16,192]{3,2,1,0:T(8,128)(2,1)S(1)} %copy-done.15, bf16[2,4,16,192]{3,2,1,0:T(8,128)(2,1)S(1)} %collective-permute-done.12.refs_2_, bf16[2,4,16,192]{3,2,1,0:T(8,128)(2,1)S(1)} %collective-permute-done.13.refs_3_, ...), custom_call_target="tpu_custom_call" | custom-call | tf_op jit(solution)/shard_map/absorb_queries/pallas_call | solution.py:221
  51.1 5.9 %all-to-all-start = ((bf16[16,40,144]{2,1,0:T(8,128)(2,1)}), bf16[16,40,144]{2,1,0:T(8,128)(2,1)S(1)}, u32[]{:S(2)}, u32[]{:S(2)}) async-start(bf16[16,40,144]{2,1,0:T(8,128)(2,1)} %absorb_queries.1), calls=%async_computation | async-start | bytes 655360 | tf_op jit(solution)/shard_map/all_to_all | solution.py:630
  60.6 3.1 %collective-permute-done.6.refs_4_.refs_6_ = bf16[576,112]{1,0:T(8,128)(2,1)S(1)} collective-permute-done((bf16[576,112]{1,0:T(8,128)(2,1)S(1)}, bf16[576,112]{1,0:T(8,128)(2,1)S(1)}, u32[]{:S(2)}, u32[]{:S(2)}) %collective-permute-start.6) | collective-permute-done | bytes 129056 | tf_op jit(solution)/shard_map/ppermute | solution.py:28
  63.8 3.2 %collective-permute-done.7.refs_6_.refs_8_ = bf16[576,112]{1,0:T(8,128)(2,1)S(1)} collective-permute-done((bf16[576,112]{1,0:T(8,128)(2,1)S(1)}, bf16[576,112]{1,0:T(8,128)(2,1)S(1)}, u32[]{:S(2)}, u32[]{:S(2)}) %collective-permute-start.7) | collective-permute-done | bytes 129056 | tf_op jit(solution)/shard_map/ppermute | solution.py:28
  66.9 1.9 %collective-permute-start.19 = (bf16[2,4,3608]{2,1,0:T(4,128)(2,1)S(1)}, bf16[2,4,3608]{2,1,0:T(4,128)(2,1)S(1)}, u32[]{:S(2)}, u32[]{:S(2)}) collective-permute-start(bf16[2,4,3608]{2,1,0:T(4,128)(2,1)S(1)} %concatenate.3.refs_4_), channel_id=1, source_target_pairs={{0,8},{4,12},{8,0},{12,4},{1,9},{5,13},{9,1},{13,5},{2,10},{6,14},... | collective-permute-start | bytes 173192 | tf_op jit(solution)/shard_map/ppermute | solution.py:28
  82.3 3.7 %collective-permute-done.11.refs_3_ = bf16[128,576]{1,0:T(8,128)(2,1)} collective-permute-done((bf16[128,576]{1,0:T(8,128)(2,1)}, bf16[128,576]{1,0:T(8,128)(2,1)}, u32[]{:S(2)}, u32[]{:S(2)}) %collective-permute-start.11) | collective-permute-done | bytes 147488 | tf_op jit(solution)/shard_map/ppermute | solution.py:28
  86.0 1.9 %attend.1 = (bf16[32,512]{1,0:T(8,128)(2,1)S(1)}, bf16[32,512]{1,0:T(8,128)(2,1)S(1)}, bf16[32,512]{1,0:T(8,128)(2,1)S(1)}, bf16[32,512]{1,0:T(8,128)(2,1)S(1)}) custom-call(bf16[128,576]{1,0:T(8,128)(2,1)S(1)} %project.2.refs_0_, bf16[128,576]{1,0:T(8,128)(2,1)} %collective-permute-done.9.refs_1_, bf16[128,576]{1,0:T(8,128)(2,1)} %collective-permute-done.10.refs_2_, ...), custom_call_target="tpu_custom_call" | custom-call | tf_op jit(solution)/shard_map/attend/pallas_call | solution.py:381
  89.5 2.4 %collective-permute-start.22 = (bf16[32,512]{1,0:T(8,128)(2,1)S(1)}, bf16[32,512]{1,0:T(8,128)(2,1)S(1)}, u32[]{:S(2)}, u32[]{:S(2)}) collective-permute-start(bf16[32,512]{1,0:T(8,128)(2,1)S(1)} %get-tuple-element.65), channel_id=1, source_target_pairs={{0,2},{1,3},{2,0},{3,1},{4,6},{5,7},{6,4},{7,5},{8,10},{9,11},{10,... | collective-permute-start | bytes 98312 | tf_op jit(solution)/shard_map/ppermute | solution.py:28
  92.4 2.4 %collective-permute-done.22.refs_3_ = bf16[32,512]{1,0:T(8,128)(2,1)S(1)} collective-permute-done((bf16[32,512]{1,0:T(8,128)(2,1)S(1)}, bf16[32,512]{1,0:T(8,128)(2,1)S(1)}, u32[]{:S(2)}, u32[]{:S(2)}) %collective-permute-start.22) | collective-permute-done | bytes 32800 | tf_op jit(solution)/shard_map/ppermute | solution.py:28
  94.8 2.7 %collective-permute-done.23.refs_4_ = bf16[32,512]{1,0:T(8,128)(2,1)S(1)} collective-permute-done((bf16[32,512]{1,0:T(8,128)(2,1)S(1)}, bf16[32,512]{1,0:T(8,128)(2,1)S(1)}, u32[]{:S(2)}, u32[]{:S(2)}) %collective-permute-start.23) | collective-permute-done | bytes 32800 | tf_op jit(solution)/shard_map/ppermute | solution.py:28
  101.3 2.0 %fetch.4.refs_4_ = bf16[2048,896]{1,0:T(8,128)(2,1)S(1)} custom-call(bf16[2048,896]{1,0:T(8,128)(2,1)} %refs_0_.8), custom_call_target="tpu_custom_call" | custom-call | bytes 7340032 | tf_op jit(solution)/shard_map/fetch/pallas_call | solution.py:59
  105.5 3.3 %collective-permute-start.29 = (bf16[32,896]{1,0:T(8,128)(2,1)S(1)}, bf16[32,896]{1,0:T(8,128)(2,1)S(1)}, u32[]{:S(2)}, u32[]{:S(2)}) collective-permute-start(bf16[32,896]{1,0:T(8,128)(2,1)S(1)} %output_product.1), channel_id=1, source_target_pairs={{0,3},{1,2},{2,1},{3,0},{4,7},{5,6},{6,5},{7,4},{8,11},{9,10},{10,... | collective-permute-start | bytes 172040 | tf_op jit(solution)/shard_map/ppermute | solution.py:28
  109.5 3.0 %collective-permute-done.28 = bf16[32,896]{1,0:T(8,128)(2,1)S(1)} collective-permute-done((bf16[32,896]{1,0:T(8,128)(2,1)S(1)}, bf16[32,896]{1,0:T(8,128)(2,1)S(1)}, u32[]{:S(2)}, u32[]{:S(2)}) %collective-permute-start.28) | collective-permute-done | bytes 57376 | tf_op jit(solution)/shard_map/ppermute | solution.py:28
  114.5 3.1 %fetch.5.refs_9_ = bf16[4,3584,256]{2,1,0:T(8,128)(2,1)S(1)} custom-call(bf16[4,3584,256]{2,1,0:T(8,128)(2,1)} %refs_0_.9), custom_call_target="tpu_custom_call" | custom-call | bytes 14680064 | tf_op jit(solution)/shard_map/fetch/pallas_call | solution.py:59
  117.6 3.1 %fetch.6.refs_10_ = bf16[4,3584,256]{2,1,0:T(8,128)(2,1)S(1)} custom-call(bf16[4,3584,256]{2,1,0:T(8,128)(2,1)} %refs_0_.10), custom_call_target="tpu_custom_call" | custom-call | bytes 14680064 | tf_op jit(solution)/shard_map/fetch/pallas_call | solution.py:59
  120.7 3.1 %fetch.7.refs_11_ = bf16[4,256,3584]{2,1,0:T(8,128)(2,1)S(1)} custom-call(bf16[4,256,3584]{2,1,0:T(8,128)(2,1)} %refs_0_.11), custom_call_target="tpu_custom_call" | custom-call | bytes 14680064 | tf_op jit(solution)/shard_map/fetch/pallas_call | solution.py:59
  124.0 5.0 %run_experts.1 = (bf16[16,8,896]{2,1,0:T(8,128)(2,1)}, bf16[4,8,896]{2,1,0:T(8,128)(2,1)S(1)}) custom-call(bf16[4,8,896]{2,1,0:T(8,128)(2,1)S(1)} %fusion.refs_0_, bf16[4,8,896]{2,1,0:T(8,128)(2,1)S(1)} %collective-permute-done.30.refs_1_, bf16[4,8,896]{2,1,0:T(8,128)(2,1)S(1)} %collective-permute-done.31.refs_2_, ...), custom_call_target="tpu_custom_call" | custom-call | tf_op jit(solution)/shard_map/run_experts/pallas_call | solution.py:537
  129.0 4.3 %all-to-all-start.1 = ((bf16[16,8,896]{2,1,0:T(8,128)(2,1)}), bf16[16,8,896]{2,1,0:T(8,128)(2,1)S(1)}, u32[]{:S(2)}, u32[]{:S(2)}) async-start(bf16[16,8,896]{2,1,0:T(8,128)(2,1)} %get-tuple-element.75), calls=%async_computation.1 | async-start | bytes 458752 | tf_op jit(solution)/shard_map/all_to_all | solution.py:675
  134.1 8.5 %all-to-all-done.1.block_ref = bf16[16,8,896]{2,1,0:T(8,128)(2,1)S(1)} async-done(((bf16[16,8,896]{2,1,0:T(8,128)(2,1)}), bf16[16,8,896]{2,1,0:T(8,128)(2,1)S(1)}, u32[]{:S(2)}, u32[]{:S(2)}) %all-to-all-start.1) | async-done | bytes 229408 | tf_op jit(solution)/shard_map/all_to_all | solution.py:675
  (122 shorter events, 48.8 us)
Async XLA Ops:
  1.3 10.6 %collective-permute-start.3 = (bf16[576,112]{1,0:T(8,128)(2,1)S(1)}, bf16[576,112]{1,0:T(8,128)(2,1)S(1)}, u32[]{:S(2)}, u32[]{:S(2)}) collective-permute-start(bf16[576,112]{1,0:T(8,128)(2,1)S(1)} %get-tuple-element.80.refs_1_.refs_3_), channel_id=1, source_target_pairs={{0,1},{1,0},{2,3},{3,2},{4,5},{5,4},{6,7},{7,6},{8,9},{9,8},{10,11... | collective-permute-start | bytes 387080 | tf_op jit(solution)/shard_map/ppermute | solution.py:28
  6.8 15.0 %collective-permute-start = (bf16[4,128,224]{2,1,0:T(8,128)(2,1)S(1)}, bf16[4,128,224]{2,1,0:T(8,128)(2,1)S(1)}, u32[]{:S(2)}, u32[]{:S(2)}) collective-permute-start(bf16[4,128,224]{2,1,0:T(8,128)(2,1)S(1)} %get-tuple-element.42), channel_id=1, source_target_pairs={{0,4},{4,0},{8,12},{12,8},{1,5},{5,1},{9,13},{13,9},{2,6},{6,2},{1... | collective-permute-start | bytes 688136 | tf_op jit(solution)/shard_map/ppermute | solution.py:28
  6.8 15.0 %collective-permute-start.1 = (bf16[4,128,224]{2,1,0:T(8,128)(2,1)S(1)}, bf16[4,128,224]{2,1,0:T(8,128)(2,1)S(1)}, u32[]{:S(2)}, u32[]{:S(2)}) collective-permute-start(bf16[4,128,224]{2,1,0:T(8,128)(2,1)S(1)} %get-tuple-element.43), channel_id=1, source_target_pairs={{0,8},{4,12},{8,0},{12,4},{1,9},{5,13},{9,1},{13,5},{2,10},{6,14},... | collective-permute-start | bytes 688136 | tf_op jit(solution)/shard_map/ppermute | solution.py:28
  8.3 14.3 %collective-permute-start.2 = (bf16[4,128,224]{2,1,0:T(8,128)(2,1)S(1)}, bf16[4,128,224]{2,1,0:T(8,128)(2,1)S(1)}, u32[]{:S(2)}, u32[]{:S(2)}) collective-permute-start(bf16[4,128,224]{2,1,0:T(8,128)(2,1)S(1)} %get-tuple-element.44), channel_id=1, source_target_pairs={{0,12},{4,8},{8,4},{12,0},{1,13},{5,9},{9,5},{13,1},{2,14},{6,10},... | collective-permute-start | bytes 688136 | tf_op jit(solution)/shard_map/ppermute | solution.py:28
  8.7 13.1 %collective-permute-start.4 = (bf16[576,112]{1,0:T(8,128)(2,1)S(1)}, bf16[576,112]{1,0:T(8,128)(2,1)S(1)}, u32[]{:S(2)}, u32[]{:S(2)}) collective-permute-start(bf16[576,112]{1,0:T(8,128)(2,1)S(1)} %get-tuple-element.80.refs_1_.refs_3_), channel_id=1, source_target_pairs={{0,2},{1,3},{2,0},{3,1},{4,6},{5,7},{6,4},{7,5},{8,10},{9,11},{10,... | collective-permute-start | bytes 387080 | tf_op jit(solution)/shard_map/ppermute | solution.py:28
  11.9 9.9 %collective-permute-start.5 = (bf16[576,112]{1,0:T(8,128)(2,1)S(1)}, bf16[576,112]{1,0:T(8,128)(2,1)S(1)}, u32[]{:S(2)}, u32[]{:S(2)}) collective-permute-start(bf16[576,112]{1,0:T(8,128)(2,1)S(1)} %get-tuple-element.80.refs_1_.refs_3_), channel_id=1, source_target_pairs={{0,3},{1,2},{2,1},{3,0},{4,7},{5,6},{6,5},{7,4},{8,11},{9,10},{10,... | collective-permute-start | bytes 387080 | tf_op jit(solution)/shard_map/ppermute | solution.py:28
  23.3 14.0 %collective-permute-start.16 = (bf16[16,128,128]{2,1,0:T(8,128)(2,1)}, bf16[16,128,128]{2,1,0:T(8,128)(2,1)S(1)}, u32[]{:S(2)}, u32[]{:S(2)}) collective-permute-start(bf16[16,128,128]{2,1,0:T(8,128)(2,1)} %refs_5_.4), channel_id=1, source_target_pairs={{0,8},{4,12},{8,0},{12,4},{1,9},{5,13},{9,1},{13,5},{2,10},{6,14},... | collective-permute-start | bytes 1572872 | tf_op jit(solution)/shard_map/ppermute | solution.py:28
  24.8 56.5 %collective-permute-start.15 = (bf16[16,128,128]{2,1,0:T(8,128)(2,1)}, bf16[16,128,128]{2,1,0:T(8,128)(2,1)S(1)}, u32[]{:S(2)}, u32[]{:S(2)}) collective-permute-start(bf16[16,128,128]{2,1,0:T(8,128)(2,1)} %refs_5_.4), channel_id=1, source_target_pairs={{0,4},{4,0},{8,12},{12,8},{1,5},{5,1},{9,13},{13,9},{2,6},{6,2},{1... | collective-permute-start | bytes 1572872 | tf_op jit(solution)/shard_map/ppermute | solution.py:28
  37.3 44.0 %collective-permute-start.17 = (bf16[16,128,128]{2,1,0:T(8,128)(2,1)S(1)}, bf16[16,128,128]{2,1,0:T(8,128)(2,1)S(1)}, u32[]{:S(2)}, u32[]{:S(2)}) collective-permute-start(bf16[16,128,128]{2,1,0:T(8,128)(2,1)S(1)} %collective-permute-done.16.refs_7_), channel_id=1, source_target_pairs={{0,4},{4,0},{8,12},{12,8},{1,5},{5,1},{9,13},{13,9},{2,6},{6,2},{1... | collective-permute-start | bytes 1572872 | tf_op jit(solution)/shard_map/ppermute | solution.py:28
  51.1 29.3 %all-to-all-start = ((bf16[16,40,144]{2,1,0:T(8,128)(2,1)}), bf16[16,40,144]{2,1,0:T(8,128)(2,1)S(1)}, u32[]{:S(2)}, u32[]{:S(2)}) async-start(bf16[16,40,144]{2,1,0:T(8,128)(2,1)} %absorb_queries.1), calls=%async_computation | async-start | bytes 655360 | tf_op jit(solution)/shard_map/all_to_all | solution.py:630
  58.6 8.3 %collective-permute-start.7 = (bf16[576,112]{1,0:T(8,128)(2,1)S(1)}, bf16[576,112]{1,0:T(8,128)(2,1)S(1)}, u32[]{:S(2)}, u32[]{:S(2)}) collective-permute-start(bf16[576,112]{1,0:T(8,128)(2,1)S(1)} %collective-permute-done.4.refs_5_.refs_7_), channel_id=1, source_target_pairs={{0,16},{16,0},{1,17},{17,1},{2,18},{18,2},{3,19},{19,3},{4,20},{20... | collective-permute-start | bytes 387080 | tf_op jit(solution)/shard_map/ppermute | solution.py:28
  59.1 10.4 %collective-permute-start.8 = (bf16[576,112]{1,0:T(8,128)(2,1)S(1)}, bf16[576,112]{1,0:T(8,128)(2,1)S(1)}, u32[]{:S(2)}, u32[]{:S(2)}) collective-permute-start(bf16[576,112]{1,0:T(8,128)(2,1)S(1)} %collective-permute-done.5.refs_7_.refs_9_), channel_id=1, source_target_pairs={{0,16},{16,0},{1,17},{17,1},{2,18},{18,2},{3,19},{19,3},{4,20},{20... | collective-permute-start | bytes 387080 | tf_op jit(solution)/shard_map/ppermute | solution.py:28
  63.7 10.8 %collective-permute-start.18 = (bf16[2,4,3608]{2,1,0:T(4,128)(2,1)S(1)}, bf16[2,4,3608]{2,1,0:T(4,128)(2,1)S(1)}, u32[]{:S(2)}, u32[]{:S(2)}) collective-permute-start(bf16[2,4,3608]{2,1,0:T(4,128)(2,1)S(1)} %concatenate.3.refs_4_), channel_id=1, source_target_pairs={{0,4},{4,0},{8,12},{12,8},{1,5},{5,1},{9,13},{13,9},{2,6},{6,2},{1... | collective-permute-start | bytes 173192 | tf_op jit(solution)/shard_map/ppermute | solution.py:28
  66.9 9.3 %collective-permute-start.19 = (bf16[2,4,3608]{2,1,0:T(4,128)(2,1)S(1)}, bf16[2,4,3608]{2,1,0:T(4,128)(2,1)S(1)}, u32[]{:S(2)}, u32[]{:S(2)}) collective-permute-start(bf16[2,4,3608]{2,1,0:T(4,128)(2,1)S(1)} %concatenate.3.refs_4_), channel_id=1, source_target_pairs={{0,8},{4,12},{8,0},{12,4},{1,9},{5,13},{9,1},{13,5},{2,10},{6,14},... | collective-permute-start | bytes 173192 | tf_op jit(solution)/shard_map/ppermute | solution.py:28
  69.5 8.8 %collective-permute-start.20 = (bf16[2,4,3608]{2,1,0:T(4,128)(2,1)S(1)}, bf16[2,4,3608]{2,1,0:T(4,128)(2,1)S(1)}, u32[]{:S(2)}, u32[]{:S(2)}) collective-permute-start(bf16[2,4,3608]{2,1,0:T(4,128)(2,1)S(1)} %concatenate.3.refs_4_), channel_id=1, source_target_pairs={{0,12},{4,8},{8,4},{12,0},{1,13},{5,9},{9,5},{13,1},{2,14},{6,10},... | collective-permute-start | bytes 173192 | tf_op jit(solution)/shard_map/ppermute | solution.py:28
  75.1 7.2 %collective-permute-start.10 = (bf16[128,576]{1,0:T(8,128)(2,1)}, bf16[128,576]{1,0:T(8,128)(2,1)}, u32[]{:S(2)}, u32[]{:S(2)}) collective-permute-start(bf16[128,576]{1,0:T(8,128)(2,1)} %get-tuple-element.53), channel_id=1, source_target_pairs={{0,8},{4,12},{8,0},{12,4},{1,9},{5,13},{9,1},{13,5},{2,10},{6,14},... | collective-permute-start | bytes 442376 | tf_op jit(solution)/shard_map/ppermute | solution.py:28
  76.8 9.2 %collective-permute-start.11 = (bf16[128,576]{1,0:T(8,128)(2,1)}, bf16[128,576]{1,0:T(8,128)(2,1)}, u32[]{:S(2)}, u32[]{:S(2)}) collective-permute-start(bf16[128,576]{1,0:T(8,128)(2,1)} %get-tuple-element.54), channel_id=1, source_target_pairs={{0,12},{4,8},{8,4},{12,0},{1,13},{5,9},{9,5},{13,1},{2,14},{6,10},... | collective-permute-start | bytes 442376 | tf_op jit(solution)/shard_map/ppermute | solution.py:28
  78.9 7.1 %collective-permute-start.9 = (bf16[128,576]{1,0:T(8,128)(2,1)}, bf16[128,576]{1,0:T(8,128)(2,1)}, u32[]{:S(2)}, u32[]{:S(2)}) collective-permute-start(bf16[128,576]{1,0:T(8,128)(2,1)} %get-tuple-element.52), channel_id=1, source_target_pairs={{0,4},{4,0},{8,12},{12,8},{1,5},{5,1},{9,13},{13,9},{2,6},{6,2},{1... | collective-permute-start | bytes 442376 | tf_op jit(solution)/shard_map/ppermute | solution.py:28
  104.5 8.0 %collective-permute-start.28 = (bf16[32,896]{1,0:T(8,128)(2,1)S(1)}, bf16[32,896]{1,0:T(8,128)(2,1)S(1)}, u32[]{:S(2)}, u32[]{:S(2)}) collective-permute-start(bf16[32,896]{1,0:T(8,128)(2,1)S(1)} %output_product.1), channel_id=1, source_target_pairs={{0,2},{1,3},{2,0},{3,1},{4,6},{5,7},{6,4},{7,5},{8,10},{9,11},{10,... | collective-permute-start | bytes 172040 | tf_op jit(solution)/shard_map/ppermute | solution.py:28
  105.5 7.0 %collective-permute-start.29 = (bf16[32,896]{1,0:T(8,128)(2,1)S(1)}, bf16[32,896]{1,0:T(8,128)(2,1)S(1)}, u32[]{:S(2)}, u32[]{:S(2)}) collective-permute-start(bf16[32,896]{1,0:T(8,128)(2,1)S(1)} %output_product.1), channel_id=1, source_target_pairs={{0,3},{1,2},{2,1},{3,0},{4,7},{5,6},{6,5},{7,4},{8,11},{9,10},{10,... | collective-permute-start | bytes 172040 | tf_op jit(solution)/shard_map/ppermute | solution.py:28
  112.6 11.3 %collective-permute-start.30 = (bf16[4,8,896]{2,1,0:T(8,128)(2,1)S(1)}, bf16[4,8,896]{2,1,0:T(8,128)(2,1)S(1)}, u32[]{:S(2)}, u32[]{:S(2)}) collective-permute-start(bf16[4,8,896]{2,1,0:T(8,128)(2,1)S(1)} %fusion.refs_0_), channel_id=1, source_target_pairs={{0,4},{4,0},{8,12},{12,8},{1,5},{5,1},{9,13},{13,9},{2,6},{6,2},{1... | collective-permute-start | bytes 172040 | tf_op jit(solution)/shard_map/ppermute | solution.py:28
  112.6 11.3 %collective-permute-start.31 = (bf16[4,8,896]{2,1,0:T(8,128)(2,1)S(1)}, bf16[4,8,896]{2,1,0:T(8,128)(2,1)S(1)}, u32[]{:S(2)}, u32[]{:S(2)}) collective-permute-start(bf16[4,8,896]{2,1,0:T(8,128)(2,1)S(1)} %fusion.refs_0_), channel_id=1, source_target_pairs={{0,8},{4,12},{8,0},{12,4},{1,9},{5,13},{9,1},{13,5},{2,10},{6,14},... | collective-permute-start | bytes 172040 | tf_op jit(solution)/shard_map/ppermute | solution.py:28
  113.9 10.0 %collective-permute-start.32 = (bf16[4,8,896]{2,1,0:T(8,128)(2,1)S(1)}, bf16[4,8,896]{2,1,0:T(8,128)(2,1)S(1)}, u32[]{:S(2)}, u32[]{:S(2)}) collective-permute-start(bf16[4,8,896]{2,1,0:T(8,128)(2,1)S(1)} %fusion.refs_0_), channel_id=1, source_target_pairs={{0,12},{4,8},{8,4},{12,0},{1,13},{5,9},{9,5},{13,1},{2,14},{6,10},... | collective-permute-start | bytes 172040 | tf_op jit(solution)/shard_map/ppermute | solution.py:28
  129.0 13.6 %all-to-all-start.1 = ((bf16[16,8,896]{2,1,0:T(8,128)(2,1)}), bf16[16,8,896]{2,1,0:T(8,128)(2,1)S(1)}, u32[]{:S(2)}, u32[]{:S(2)}) async-start(bf16[16,8,896]{2,1,0:T(8,128)(2,1)} %get-tuple-element.75), calls=%async_computation.1 | async-start | bytes 458752 | tf_op jit(solution)/shard_map/all_to_all | solution.py:675
  (39 other events, 601.1 us)

commit v6 on v5

--- a/solution.py
+++ b/solution.py
@@ -42,10 +42,14 @@
     return pltpu.CompilerParams(vmem_limit_bytes=mebibytes * 1024 * 1024)
 
 
+def at_home(*arrays):
+    return [pltpu.with_memory_space_constraint(array, pltpu.HBM) for array in arrays]
+
+
 def fetch_kernel(count, *refs):
-    sems = refs[2 * count]
+    out_refs, sems = refs[-1 - count : -1], refs[-1]
     copies = [
-        pltpu.make_async_copy(refs[index], refs[count + index], sems.at[index])
+        pltpu.make_async_copy(refs[index], out_refs[index], sems.at[index])
         for index in range(count)
     ]
     for copy in copies:
@@ -54,18 +58,19 @@
         copy.wait()
 
 
-def fetch(*arrays):
+def fetch(arrays, after):
     size = sum(array.size * array.dtype.itemsize for array in arrays)
     return pl.pallas_call(
         functools.partial(fetch_kernel, len(arrays)),
         out_shape=[pltpu.VMEM(array.shape, array.dtype) for array in arrays],
-        in_specs=[pl.BlockSpec(memory_space=pltpu.HBM)] * len(arrays),
+        in_specs=[pl.BlockSpec(memory_space=pltpu.HBM)] * len(arrays)
+        + [pl.BlockSpec(memory_space=pl.ANY)] * len(after),
         out_specs=[pl.BlockSpec(memory_space=pltpu.VMEM)] * len(arrays),
         scratch_shapes=[pltpu.SemaphoreType.DMA((len(arrays),))],
         compiler_params=pltpu.CompilerParams(vmem_limit_bytes=1024 * 1024),
         cost_estimate=pl.CostEstimate(flops=0, bytes_accessed=2 * size, transcendentals=0),
         name="fetch",
-    )(*[pltpu.with_memory_space_constraint(array, pltpu.HBM) for array in arrays])
+    )(*at_home(*arrays), *after)
 
 
 def doubled(block, axis):
@@ -99,7 +104,7 @@
         scratch_shapes=[pltpu.VMEM((experts,) + block.shape, x.dtype)],
         compiler_params=params(x, scale=6),
         name="cut_columns",
-    )(x)
+    )(*at_home(x))
 
 
 def project_kernel(count, sections, groups, *refs):
@@ -142,9 +147,9 @@
 ):
     f32, bf16 = jnp.float32, jnp.bfloat16
     table_ref, query_refs = refs[0], refs[1 : 1 + experts]
-    uk_ref, own_ref, gain_ref, wt_ref, out_ref, picked, ropes, made, normed, query_ref = refs[
-        1 + experts :
-    ]
+    uk_ref, own_ref, gain_ref, wt_ref = refs[1 + experts : 5 + experts]
+    out_ref, token_ref, picked, ropes, made, normed, query_ref = refs[-7:]
+    token_ref[...] = jnp.zeros_like(token_ref)
     steps, sources, heads, wide = query_refs[0].shape
     rope = wide - nope
     chunk = uk_ref.shape[2]
@@ -210,7 +215,7 @@
             out_ref[index, block:, :] = lines
 
 
-def absorb_queries(table, queries, w_uk, own, gain, w_turned, prompts, sections):
+def absorb_queries(table, queries, w_uk, own, gain, w_turned, prompts, sections, after):
     experts = len(queries)
     steps, sources, heads, wide = queries[0].shape
     _, nope, chunk = w_uk.shape
@@ -220,9 +225,14 @@
     held = pl.BlockSpec(memory_space=pltpu.VMEM)
     return pl.pallas_call(
         functools.partial(query_kernel, experts, sections, prompts, nope),
-        out_shape=jax.ShapeDtypeStruct((experts * sections, rows, width), jnp.bfloat16),
-        in_specs=[pl.BlockSpec(memory_space=pltpu.SMEM)] + [held] * (experts + 4),
-        out_specs=held,
+        out_shape=[
+            jax.ShapeDtypeStruct((experts * sections, rows, width), jnp.bfloat16),
+            jax.ShapeDtypeStruct((8, 128), jnp.bfloat16),
+        ],
+        in_specs=[pl.BlockSpec(memory_space=pltpu.SMEM)]
+        + [held] * (experts + 4)
+        + [pl.BlockSpec(memory_space=pl.ANY)] * len(after),
+        out_specs=[held] * 2,
         scratch_shapes=[
             pltpu.VMEM((count, nope), jnp.float32),
             pltpu.VMEM((count, wide - nope), jnp.bfloat16),
@@ -234,7 +244,7 @@
         ],
         compiler_params=params(*queries, w_uk, own, w_turned, scale=4),
         name="absorb_queries",
-    )(table, *queries, w_uk, own, gain, w_turned)
+    )(table, *queries, *at_home(w_uk, own, gain, w_turned), *after)
 
 
 def turn(values, cosine, sine):
@@ -316,14 +326,14 @@
         scratch_shapes=[pltpu.VMEM((steps * heads, rope), jnp.float32)] * 2,
         compiler_params=params(blocks, scale=4),
         name="gather_queries",
-    )(lengths, owners, kv_gain, *table, blocks)
+    )(lengths, owners, *at_home(kv_gain, *table), blocks)
 
 
 def attend_kernel(parts, sections, sources, heads, steps, score_scale, *refs):
     part_refs = refs[:parts]
     (length_ref, gain_ref, cosine_ref, sine_ref, query_ref, query_rope_ref, recent_ref,
      recent_rope_ref) = refs[parts : parts + 8]
-    out_refs, held = refs[parts + 8 : -1], refs[-1]
+    out_refs, held = refs[-1 - sections : -1], refs[-1]
     f32, bf16 = jnp.float32, jnp.bfloat16
     nt = (((1,), (1,)), ((), ()))
     prompts, _, latent = query_ref.shape
@@ -374,7 +384,9 @@
             ref[prompt * rows : (prompt + 1) * rows, :] = held[section_rank ^ mask]
 
 
-def attend(parts, lengths, kv_gain, table, gathered, sources, steps, sections, score_scale):
+def attend(
+    parts, lengths, kv_gain, table, gathered, sources, steps, sections, score_scale, after
+):
     prompts, rows, latent = gathered[0].shape
     out = (rows // sections, latent)
     held = pl.BlockSpec(memory_space=pltpu.VMEM)
@@ -383,12 +395,15 @@
             attend_kernel, len(parts), sections, sources, out[0] // steps, steps, score_scale
         ),
         out_shape=[jax.ShapeDtypeStruct((prompts * out[0], latent), jnp.bfloat16)] * sections,
-        in_specs=[held] * len(parts) + [pl.BlockSpec(memory_space=pltpu.SMEM)] + [held] * 7,
+        in_specs=[held] * len(parts)
+        + [pl.BlockSpec(memory_space=pltpu.SMEM)]
+        + [held] * 7
+        + [pl.BlockSpec(memory_space=pl.ANY)] * len(after),
         out_specs=[held] * sections,
         scratch_shapes=[pltpu.VMEM((sections,) + out, jnp.bfloat16)],
         compiler_params=params(*parts, *gathered, scale=6),
         name="attend",
-    )(*parts, lengths, kv_gain, *table, *gathered)
+    )(*parts, lengths, *at_home(kv_gain, *table), *gathered, *after)
 
 
 def value_kernel(experts, sections, heads, steps, sources, *refs):
@@ -545,7 +560,7 @@
         scratch_shapes=[pltpu.VMEM((experts,) + attended[0].shape, jnp.bfloat16)],
         compiler_params=params(*attended, *own, scale=16),
         name="run_experts",
-    )(*attended, *own, gain, w_gate, w_up, w_down)
+    )(*attended, *own, *at_home(gain), w_gate, w_up, w_down)
 
 
 def finish_kernel(block_ref, near_ref, base_ref, out_ref):
@@ -617,22 +632,21 @@
     queries_all = spread(queries, "expert")
     cut = list(cut_columns(prompts.reshape(rows, width), sections, experts))
     cut = deliver(cut, "expert")
-    queries_all[0], *rest = lax.optimization_barrier((queries_all[0], *cut[1:], *halves[1:]))
-    cut = cut[:1] + rest[: experts - 1]
-    halves = halves[:1] + rest[experts - 1 :]
     w_parts = halves[:1] + [w_piece(group_rank ^ other) for other in range(1, groups)]
     for half in halves[1:]:
         w_parts += spread(half, "groups")
-
-    blocks = absorb_queries(
-        owners, queries_all, w_uk, residual, attn_gain, w_turned, prompt_count, sections
+    w_gate, w_up, w_down = fetch([w_gate, w_up, w_down], queries_all[1:])
+
+    blocks, token = absorb_queries(
+        owners, queries_all, w_uk, residual, attn_gain, w_turned, prompt_count, sections,
+        cut[1:] + halves[1:] + w_parts[groups : groups + 2] + [w_gate],
     )
     blocks = lax.all_to_all(blocks, ("expert", "section"), 0, 0, tiled=True)
 
     high = route_scores.astype(bf16)
     low = (route_scores - high.astype(f32)).astype(bf16)
     packed = jnp.concatenate([residual, expert_ids.astype(bf16), high, low], axis=2)
-    w_uv, packed, cut[1] = lax.optimization_barrier((w_uv, packed, cut[1]))
+    w_uv, token = lax.optimization_barrier((w_uv, token))
     uv_parts = doubled(w_uv, "expert")
     packed = spread(packed, "expert")
 
@@ -644,21 +658,16 @@
         blocks, lengths, owners, kv_gain, table, prompt_count, tokens_here, experts, sections,
         steps, heads
     ))
-    gathered[0], *rest = lax.optimization_barrier((gathered[0], *uv_parts, *packed))
-    uv_parts, packed = rest[:experts], rest[experts:]
     out_latent = attend(
         parts, lengths, kv_gain, table, gathered, tokens_here, steps, sections,
-        queries.shape[-1] ** (-0.5),
+        queries.shape[-1] ** (-0.5), packed + [uv_parts[2], token],
     )
 
     out_latent = deliver(out_latent, "section")
     head_values = head_products(owners, out_latent, uv_parts, steps, tokens_here)
     head_values = spread(head_values, "expert")
 
-    (w_o,) = fetch(w_o)
-    (w_gate,) = fetch(w_gate)
-    (w_up,) = fetch(w_up)
-    (w_down,) = fetch(w_down)
+    (w_o,) = fetch([w_o], [])
     attended = output_product(head_values, w_o)
     attended = sum(part.astype(f32) for part in spread(attended, "section")).astype(bf16)
     attended = attended.reshape(experts, own_rows, -1)

time: 144 us -> 129 us (0.90)
  waiting for transfers between devices: 54.4 us -> 39.7 us
  other arithmetic: 1.49 us -> 0.04 us
    ppermute x33, waiting for transfers between devices: 45.9 us -> 30.6 us  [swap(): return lax.ppermute(block, axis, [(i, i ^ mask) for i in range(size)])]
    pallas_call x4 -> x2, Pallas kernels: 11.4 us -> 9.33 us  [fetch(): pl.pallas_call(functools.partial(fetch_kernel, len(arrays)), out_shape=[p...]
    ppermute x33, starting transfers between devices: 32.5 us -> 34.2 us  [swap(): return lax.ppermute(block, axis, [(i, i ^ mask) for i in range(size)])]
    unnamed x56 -> x40, local copies, waits for them, and re-layouts: 14.3 us -> 15.1 us
  transfers between devices with their start and end apart: 35 -> 35, of which waited for: 15 -> 16; matrix products, arithmetic and copies ran while one was open for 2% -> 2% of each run, Pallas kernels for 12% -> 13%
where the time goes in v6:
time: 129 us
  starting transfers between devices  43 us (33%)
  waiting for transfers between devices  39.7 us (31%)
  Pallas kernels  28.3 us (22%)
  local copies, waits for them, and re-layouts  17.2 us (13%)
    ppermute x33, starting transfers between devices, swap(): return lax.ppermute(block, axis, [(i, i ^ mask) for i in range(size)])  34.2 us
    ppermute x33, waiting for transfers between devices, swap(): return lax.ppermute(block, axis, [(i, i ^ mask) for i in range(size)])  30.6 us
    unnamed x40, local copies, waits for them, and re-layouts  15.1 us
    pallas_call x2, Pallas kernels, fetch(): pl.pallas_call(functools.partial(fetch_kernel, len(arrays)), out_shape=[p...  9.33 us
    all_to_all x2, waiting for transfers between devices, local(): blocks = lax.all_to_all(blocks, ('expert', 'section'), 0, 0, tiled=True)  9.16 us
    all_to_all x2, starting transfers between devices, local(): blocks = lax.all_to_all(blocks, ('expert', 'section'), 0, 0, tiled=True)  8.78 us
    pallas_call x1, Pallas kernels, run_experts(): pl.pallas_call(functools.partial(expert_kernel, experts, sections, picks)...  5.75 us
  transfers between devices with their start and end apart: 35, of which 16 were waited for; matrix products, arithmetic and copies ran while one was open for 2% of the time, Pallas kernels for 13%

profile of v6, /device:TPU:0, one launch (start us, length us, event | category | flops | bytes accessed | tf_op | source)
XLA Modules:
  0.0 128.6 jit_solution(8954165292545303560)
XLA Ops:
  0.5 2.5 %collective-permute-start.13 = (bf16[2,4,16,192]{3,2,1,0:T(8,128)(2,1)}, bf16[2,4,16,192]{3,2,1,0:T(8,128)(2,1)S(1)}, u32[]{:S(2)}, u32[]{:S(2)}) collective-permute-start(bf16[2,4,16,192]{3,2,1,0:T(8,128)(2,1)} %refs_1_.3), channel_id=1, source_target_pairs={{0,8},{4,12},{8,0},{12,4},{1,9},{5,13},{9,1},{13,5},{2,10},{6,14},... | collective-permute-start | bytes 147464 | tf_op jit(solution)/shard_map/ppermute | solution.py:28
  6.3 2.6 %collective-permute-start.2 = (bf16[576,112]{1,0:T(8,128)(2,1)S(1)}, bf16[576,112]{1,0:T(8,128)(2,1)S(1)}, u32[]{:S(2)}, u32[]{:S(2)}) collective-permute-start(bf16[576,112]{1,0:T(8,128)(2,1)S(1)} %get-tuple-element.56.refs_1_.refs_3_), channel_id=1, source_target_pairs={{0,2},{1,3},{2,0},{3,1},{4,6},{5,7},{6,4},{7,5},{8,10},{9,11},{10,... | collective-permute-start | bytes 387080 | tf_op jit(solution)/shard_map/ppermute | solution.py:28
  13.4 2.8 %collective-permute-start.4 = (bf16[576,112]{1,0:T(8,128)(2,1)S(1)}, bf16[576,112]{1,0:T(8,128)(2,1)S(1)}, u32[]{:S(2)}, u32[]{:S(2)}) collective-permute-start(bf16[576,112]{1,0:T(8,128)(2,1)S(1)} %get-tuple-element.56.refs_1_.refs_3_), channel_id=1, source_target_pairs={{0,3},{1,2},{2,1},{3,0},{4,7},{5,6},{6,5},{7,4},{8,11},{9,10},{10,... | collective-permute-start | bytes 387080 | tf_op jit(solution)/shard_map/ppermute | solution.py:28
  17.7 7.3 %fetch.2 = (bf16[4,3584,256]{2,1,0:T(8,128)(2,1)S(1)}, bf16[4,3584,256]{2,1,0:T(8,128)(2,1)S(1)}, bf16[4,256,3584]{2,1,0:T(8,128)(2,1)S(1)}) custom-call(bf16[4,3584,256]{2,1,0:T(8,128)(2,1)} %refs_0_.4, bf16[4,3584,256]{2,1,0:T(8,128)(2,1)} %refs_1_.2, bf16[4,256,3584]{2,1,0:T(8,128)(2,1)} %refs_2_.1, ...), custom_call_target="tpu_custom_call" | custom-call | bytes 44040192 | tf_op jit(solution)/shard_map/fetch/pallas_call | solution.py:63
  25.0 2.9 %copy-done.1 = bf16[4,3584,256]{2,1,0:T(8,128)(2,1)} copy-done((bf16[4,3584,256]{2,1,0:T(8,128)(2,1)}, bf16[4,3584,256]{2,1,0:T(8,128)(2,1)S(1)}, u32[]{:S(2)}) %copy-start.1) | copy-done | bytes 7340056
  27.9 2.9 %copy-done.3 = bf16[4,256,3584]{2,1,0:T(8,128)(2,1)} copy-done((bf16[4,256,3584]{2,1,0:T(8,128)(2,1)}, bf16[4,256,3584]{2,1,0:T(8,128)(2,1)S(1)}, u32[]{:S(2)}) %copy-start.3) | copy-done | bytes 7340056
  30.9 2.2 %absorb_queries.1 = (bf16[16,40,144]{2,1,0:T(8,128)(2,1)S(1)}, bf16[8,128]{1,0:T(8,128)(2,1)S(1)}) custom-call(s32[16]{0:T(128)S(1)} %copy-done.13, bf16[2,4,16,192]{3,2,1,0:T(8,128)(2,1)S(1)} %copy-done.12, bf16[2,4,16,192]{3,2,1,0:T(8,128)(2,1)S(1)} %collective-permute-done.12.refs_3_.refs_2_, ...), custom_call_target="tpu_custom_call" | custom-call | tf_op jit(solution)/shard_map/absorb_queries/pallas_call | solution.py:226
  33.2 3.0 %copy-done = bf16[4,3584,256]{2,1,0:T(8,128)(2,1)} copy-done((bf16[4,3584,256]{2,1,0:T(8,128)(2,1)}, bf16[4,3584,256]{2,1,0:T(8,128)(2,1)S(1)}, u32[]{:S(2)}) %copy-start) | copy-done | bytes 7340056
  38.3 11.2 %collective-permute-done.18.refs_16_.refs_7_ = bf16[16,128,128]{2,1,0:T(8,128)(2,1)S(1)} collective-permute-done((bf16[16,128,128]{2,1,0:T(8,128)(2,1)S(1)}, bf16[16,128,128]{2,1,0:T(8,128)(2,1)S(1)}, u32[]{:S(2)}, u32[]{:S(2)}) %collective-permute-start.18) | collective-permute-done | bytes 524320 | tf_op jit(solution)/shard_map/ppermute | solution.py:28
  51.6 4.7 %all-to-all-start = ((bf16[16,40,144]{2,1,0:T(8,128)(2,1)}), bf16[16,40,144]{2,1,0:T(8,128)(2,1)S(1)}, u32[]{:S(2)}, u32[]{:S(2)}) async-start(bf16[16,40,144]{2,1,0:T(8,128)(2,1)} %copy-done.6), calls=%async_computation | async-start | bytes 655360 | tf_op jit(solution)/shard_map/all_to_all | solution.py:644
  69.1 3.4 %collective-permute-done.11.refs_3_ = bf16[128,576]{1,0:T(8,128)(2,1)S(1)} collective-permute-done((bf16[128,576]{1,0:T(8,128)(2,1)}, bf16[128,576]{1,0:T(8,128)(2,1)S(1)}, u32[]{:S(2)}, u32[]{:S(2)}) %collective-permute-start.11) | collective-permute-done | bytes 147488 | tf_op jit(solution)/shard_map/ppermute | solution.py:28
  73.4 2.0 %attend.1 = (bf16[32,512]{1,0:T(8,128)(2,1)S(1)}, bf16[32,512]{1,0:T(8,128)(2,1)S(1)}, bf16[32,512]{1,0:T(8,128)(2,1)S(1)}, bf16[32,512]{1,0:T(8,128)(2,1)S(1)}) custom-call(bf16[128,576]{1,0:T(8,128)(2,1)S(1)} %project.2.refs_0_, bf16[128,576]{1,0:T(8,128)(2,1)} %collective-permute-done.9.refs_1_, bf16[128,576]{1,0:T(8,128)(2,1)S(1)} %collective-permute-done.10.refs_2_, ...), custom_call_target="tpu_custom_call" | custom-call | tf_op jit(solution)/shard_map/attend/pallas_call | solution.py:393
  76.6 2.3 %collective-permute-start.20 = (bf16[32,512]{1,0:T(8,128)(2,1)S(1)}, bf16[32,512]{1,0:T(8,128)(2,1)S(1)}, u32[]{:S(2)}, u32[]{:S(2)}) collective-permute-start(bf16[32,512]{1,0:T(8,128)(2,1)S(1)} %get-tuple-element.47), channel_id=1, source_target_pairs={{0,2},{1,3},{2,0},{3,1},{4,6},{5,7},{6,4},{7,5},{8,10},{9,11},{10,... | collective-permute-start | bytes 98312 | tf_op jit(solution)/shard_map/ppermute | solution.py:28
  79.8 2.1 %collective-permute-done.20.refs_3_ = bf16[32,512]{1,0:T(8,128)(2,1)S(1)} collective-permute-done((bf16[32,512]{1,0:T(8,128)(2,1)S(1)}, bf16[32,512]{1,0:T(8,128)(2,1)S(1)}, u32[]{:S(2)}, u32[]{:S(2)}) %collective-permute-start.20) | collective-permute-done | bytes 32800 | tf_op jit(solution)/shard_map/ppermute | solution.py:28
  81.9 2.7 %collective-permute-done.21.refs_4_ = bf16[32,512]{1,0:T(8,128)(2,1)S(1)} collective-permute-done((bf16[32,512]{1,0:T(8,128)(2,1)S(1)}, bf16[32,512]{1,0:T(8,128)(2,1)S(1)}, u32[]{:S(2)}, u32[]{:S(2)}) %collective-permute-start.21) | collective-permute-done | bytes 32800 | tf_op jit(solution)/shard_map/ppermute | solution.py:28
  84.6 2.5 %head_products.1.refs_0_ = bf16[8,2048]{1,0:T(8,128)(2,1)S(1)} custom-call(s32[16]{0:T(128)S(1)} %copy-done.13, bf16[32,512]{1,0:T(8,128)(2,1)S(1)} %get-tuple-element.45.refs_1_, bf16[32,512]{1,0:T(8,128)(2,1)S(1)} %collective-permute-done.19.refs_2_, bf16[32,512]{1,0:T(8,128)(2,1)S(1)} %collective-permute-done.20.refs_3_, ...), custom_call_target="tpu_custom_call" | custom-call | tf_op jit(solution)/shard_map/head_products/pallas_call | solution.py:457
  89.0 2.0 %fetch.3.refs_4_ = bf16[2048,896]{1,0:T(8,128)(2,1)S(1)} custom-call(bf16[2048,896]{1,0:T(8,128)(2,1)} %refs_0_.7), custom_call_target="tpu_custom_call" | custom-call | bytes 7340032 | tf_op jit(solution)/shard_map/fetch/pallas_call | solution.py:63
  93.9 2.8 %collective-permute-start.29 = (bf16[32,896]{1,0:T(8,128)(2,1)S(1)}, bf16[32,896]{1,0:T(8,128)(2,1)S(1)}, u32[]{:S(2)}, u32[]{:S(2)}) collective-permute-start(bf16[32,896]{1,0:T(8,128)(2,1)S(1)} %output_product.1), channel_id=1, source_target_pairs={{0,3},{1,2},{2,1},{3,0},{4,7},{5,6},{6,5},{7,4},{8,11},{9,10},{10,... | collective-permute-start | bytes 172040 | tf_op jit(solution)/shard_map/ppermute | solution.py:28
  97.3 3.0 %collective-permute-done.28 = bf16[32,896]{1,0:T(8,128)(2,1)S(1)} collective-permute-done((bf16[32,896]{1,0:T(8,128)(2,1)S(1)}, bf16[32,896]{1,0:T(8,128)(2,1)S(1)}, u32[]{:S(2)}, u32[]{:S(2)}) %collective-permute-start.28) | collective-permute-done | bytes 57376 | tf_op jit(solution)/shard_map/ppermute | solution.py:28
  102.3 2.7 %collective-permute-done.31.refs_2_ = bf16[4,8,896]{2,1,0:T(8,128)(2,1)S(1)} collective-permute-done((bf16[4,8,896]{2,1,0:T(8,128)(2,1)S(1)}, bf16[4,8,896]{2,1,0:T(8,128)(2,1)S(1)}, u32[]{:S(2)}, u32[]{:S(2)}) %collective-permute-start.31) | collective-permute-done | bytes 57376 | tf_op jit(solution)/shard_map/ppermute | solution.py:28
  105.8 3.1 %copy-done.4 = bf16[4,256,3584]{2,1,0:T(8,128)(2,1)S(1)} copy-done((bf16[4,256,3584]{2,1,0:T(8,128)(2,1)S(1)}, bf16[4,256,3584]{2,1,0:T(8,128)(2,1)}, u32[]{:S(2)}) %copy-start.4) | copy-done | bytes 7340056
  108.9 5.7 %run_experts.1 = (bf16[16,8,896]{2,1,0:T(8,128)(2,1)}, bf16[4,8,896]{2,1,0:T(8,128)(2,1)S(1)}) custom-call(bf16[4,8,896]{2,1,0:T(8,128)(2,1)S(1)} %fusion.refs_0_, bf16[4,8,896]{2,1,0:T(8,128)(2,1)S(1)} %collective-permute-done.30.refs_1_, bf16[4,8,896]{2,1,0:T(8,128)(2,1)S(1)} %collective-permute-done.31.refs_2_, ...), custom_call_target="tpu_custom_call" | custom-call | tf_op jit(solution)/shard_map/run_experts/pallas_call | solution.py:552
  114.6 4.1 %all-to-all-start.1 = ((bf16[16,8,896]{2,1,0:T(8,128)(2,1)}), bf16[16,8,896]{2,1,0:T(8,128)(2,1)S(1)}, u32[]{:S(2)}, u32[]{:S(2)}) async-start(bf16[16,8,896]{2,1,0:T(8,128)(2,1)} %get-tuple-element.51), calls=%async_computation.1 | async-start | bytes 458752 | tf_op jit(solution)/shard_map/all_to_all | solution.py:684
  119.5 8.5 %all-to-all-done.1.block_ref = bf16[16,8,896]{2,1,0:T(8,128)(2,1)S(1)} async-done(((bf16[16,8,896]{2,1,0:T(8,128)(2,1)}), bf16[16,8,896]{2,1,0:T(8,128)(2,1)S(1)}, u32[]{:S(2)}, u32[]{:S(2)}) %all-to-all-start.1) | async-done | bytes 229408 | tf_op jit(solution)/shard_map/all_to_all | solution.py:684
  (105 shorter events, 39.3 us)
Async XLA Ops:
  0.0 10.5 %collective-permute-start.12 = (bf16[2,4,16,192]{3,2,1,0:T(8,128)(2,1)}, bf16[2,4,16,192]{3,2,1,0:T(8,128)(2,1)S(1)}, u32[]{:S(2)}, u32[]{:S(2)}) collective-permute-start(bf16[2,4,16,192]{3,2,1,0:T(8,128)(2,1)} %refs_1_.3), channel_id=1, source_target_pairs={{0,4},{4,0},{8,12},{12,8},{1,5},{5,1},{9,13},{13,9},{2,6},{6,2},{1... | collective-permute-start | bytes 147464 | tf_op jit(solution)/shard_map/ppermute | solution.py:28
  0.5 10.2 %collective-permute-start.13 = (bf16[2,4,16,192]{3,2,1,0:T(8,128)(2,1)}, bf16[2,4,16,192]{3,2,1,0:T(8,128)(2,1)S(1)}, u32[]{:S(2)}, u32[]{:S(2)}) collective-permute-start(bf16[2,4,16,192]{3,2,1,0:T(8,128)(2,1)} %refs_1_.3), channel_id=1, source_target_pairs={{0,8},{4,12},{8,0},{12,4},{1,9},{5,13},{9,1},{13,5},{2,10},{6,14},... | collective-permute-start | bytes 147464 | tf_op jit(solution)/shard_map/ppermute | solution.py:28
  2.9 9.1 %collective-permute-start.14 = (bf16[2,4,16,192]{3,2,1,0:T(8,128)(2,1)}, bf16[2,4,16,192]{3,2,1,0:T(8,128)(2,1)S(1)}, u32[]{:S(2)}, u32[]{:S(2)}) collective-permute-start(bf16[2,4,16,192]{3,2,1,0:T(8,128)(2,1)} %refs_1_.3), channel_id=1, source_target_pairs={{0,12},{4,8},{8,4},{12,0},{1,13},{5,9},{9,5},{13,1},{2,14},{6,10},... | collective-permute-start | bytes 147464 | tf_op jit(solution)/shard_map/ppermute | solution.py:28
  4.4 9.0 %collective-permute-start = (bf16[576,112]{1,0:T(8,128)(2,1)S(1)}, bf16[576,112]{1,0:T(8,128)(2,1)S(1)}, u32[]{:S(2)}, u32[]{:S(2)}) collective-permute-start(bf16[576,112]{1,0:T(8,128)(2,1)S(1)} %get-tuple-element.56.refs_1_.refs_3_), channel_id=1, source_target_pairs={{0,1},{1,0},{2,3},{3,2},{4,5},{5,4},{6,7},{7,6},{8,9},{9,8},{10,11... | collective-permute-start | bytes 387080 | tf_op jit(solution)/shard_map/ppermute | solution.py:28
  6.3 9.9 %collective-permute-start.2 = (bf16[576,112]{1,0:T(8,128)(2,1)S(1)}, bf16[576,112]{1,0:T(8,128)(2,1)S(1)}, u32[]{:S(2)}, u32[]{:S(2)}) collective-permute-start(bf16[576,112]{1,0:T(8,128)(2,1)S(1)} %get-tuple-element.56.refs_1_.refs_3_), channel_id=1, source_target_pairs={{0,2},{1,3},{2,0},{3,1},{4,6},{5,7},{6,4},{7,5},{8,10},{9,11},{10,... | collective-permute-start | bytes 387080 | tf_op jit(solution)/shard_map/ppermute | solution.py:28
  10.6 20.3 %collective-permute-start.6 = (bf16[4,128,224]{2,1,0:T(8,128)(2,1)S(1)}, bf16[4,128,224]{2,1,0:T(8,128)(2,1)S(1)}, u32[]{:S(2)}, u32[]{:S(2)}) collective-permute-start(bf16[4,128,224]{2,1,0:T(8,128)(2,1)S(1)} %get-tuple-element.30), channel_id=1, source_target_pairs={{0,4},{4,0},{8,12},{12,8},{1,5},{5,1},{9,13},{13,9},{2,6},{6,2},{1... | collective-permute-start | bytes 688136 | tf_op jit(solution)/shard_map/ppermute | solution.py:28
  10.6 20.2 %collective-permute-start.7 = (bf16[4,128,224]{2,1,0:T(8,128)(2,1)S(1)}, bf16[4,128,224]{2,1,0:T(8,128)(2,1)S(1)}, u32[]{:S(2)}, u32[]{:S(2)}) collective-permute-start(bf16[4,128,224]{2,1,0:T(8,128)(2,1)S(1)} %get-tuple-element.31), channel_id=1, source_target_pairs={{0,8},{4,12},{8,0},{12,4},{1,9},{5,13},{9,1},{13,5},{2,10},{6,14},... | collective-permute-start | bytes 688136 | tf_op jit(solution)/shard_map/ppermute | solution.py:28
  12.1 18.8 %collective-permute-start.8 = (bf16[4,128,224]{2,1,0:T(8,128)(2,1)S(1)}, bf16[4,128,224]{2,1,0:T(8,128)(2,1)S(1)}, u32[]{:S(2)}, u32[]{:S(2)}) collective-permute-start(bf16[4,128,224]{2,1,0:T(8,128)(2,1)S(1)} %get-tuple-element.32), channel_id=1, source_target_pairs={{0,12},{4,8},{8,4},{12,0},{1,13},{5,9},{9,5},{13,1},{2,14},{6,10},... | collective-permute-start | bytes 688136 | tf_op jit(solution)/shard_map/ppermute | solution.py:28
  13.4 17.5 %collective-permute-start.4 = (bf16[576,112]{1,0:T(8,128)(2,1)S(1)}, bf16[576,112]{1,0:T(8,128)(2,1)S(1)}, u32[]{:S(2)}, u32[]{:S(2)}) collective-permute-start(bf16[576,112]{1,0:T(8,128)(2,1)S(1)} %get-tuple-element.56.refs_1_.refs_3_), channel_id=1, source_target_pairs={{0,3},{1,2},{2,1},{3,0},{4,7},{5,6},{6,5},{7,4},{8,11},{9,10},{10,... | collective-permute-start | bytes 387080 | tf_op jit(solution)/shard_map/ppermute | solution.py:28
  16.1 14.7 %collective-permute-start.1 = (bf16[576,112]{1,0:T(8,128)(2,1)S(1)}, bf16[576,112]{1,0:T(8,128)(2,1)S(1)}, u32[]{:S(2)}, u32[]{:S(2)}) collective-permute-start(bf16[576,112]{1,0:T(8,128)(2,1)S(1)} %collective-permute-done.refs_3_.refs_5_.refs_12_.refs_15_), channel_id=1, source_target_pairs={{0,16},{16,0},{1,17},{17,1},{2,18},{18,2},{3,19},{19,3},{4,20},{20... | collective-permute-start | bytes 387080 | tf_op jit(solution)/shard_map/ppermute | solution.py:28
  36.9 12.6 %collective-permute-start.18 = (bf16[16,128,128]{2,1,0:T(8,128)(2,1)S(1)}, bf16[16,128,128]{2,1,0:T(8,128)(2,1)S(1)}, u32[]{:S(2)}, u32[]{:S(2)}) collective-permute-start(bf16[16,128,128]{2,1,0:T(8,128)(2,1)S(1)} %copy-done.5), channel_id=1, source_target_pairs={{0,8},{4,12},{8,0},{12,4},{1,9},{5,13},{9,1},{13,5},{2,10},{6,14},... | collective-permute-start | bytes 1572872 | tf_op jit(solution)/shard_map/ppermute | solution.py:28
  38.3 41.5 %collective-permute-start.22 = (bf16[16,128,128]{2,1,0:T(8,128)(2,1)S(1)}, bf16[16,128,128]{2,1,0:T(8,128)(2,1)}, u32[]{:S(2)}, u32[]{:S(2)}) collective-permute-start(bf16[16,128,128]{2,1,0:T(8,128)(2,1)S(1)} %copy-done.5), channel_id=1, source_target_pairs={{0,4},{4,0},{8,12},{12,8},{1,5},{5,1},{9,13},{13,9},{2,6},{6,2},{1... | collective-permute-start | bytes 1572872 | tf_op jit(solution)/shard_map/ppermute | solution.py:28
  49.5 35.2 %collective-permute-start.23 = (bf16[16,128,128]{2,1,0:T(8,128)(2,1)S(1)}, bf16[16,128,128]{2,1,0:T(8,128)(2,1)}, u32[]{:S(2)}, u32[]{:S(2)}) collective-permute-start(bf16[16,128,128]{2,1,0:T(8,128)(2,1)S(1)} %collective-permute-done.18.refs_16_.refs_7_), channel_id=1, source_target_pairs={{0,4},{4,0},{8,12},{12,8},{1,5},{5,1},{9,13},{13,9},{2,6},{6,2},{1... | collective-permute-start | bytes 1572872 | tf_op jit(solution)/shard_map/ppermute | solution.py:28
  49.5 7.4 %collective-permute-start.3 = (bf16[576,112]{1,0:T(8,128)(2,1)S(1)}, bf16[576,112]{1,0:T(8,128)(2,1)S(1)}, u32[]{:S(2)}, u32[]{:S(2)}) collective-permute-start(bf16[576,112]{1,0:T(8,128)(2,1)S(1)} %collective-permute-done.2.refs_5_.refs_7_.refs_13_), channel_id=1, source_target_pairs={{0,16},{16,0},{1,17},{17,1},{2,18},{18,2},{3,19},{19,3},{4,20},{20... | collective-permute-start | bytes 387080 | tf_op jit(solution)/shard_map/ppermute | solution.py:28
  50.1 8.8 %collective-permute-start.5 = (bf16[576,112]{1,0:T(8,128)(2,1)S(1)}, bf16[576,112]{1,0:T(8,128)(2,1)S(1)}, u32[]{:S(2)}, u32[]{:S(2)}) collective-permute-start(bf16[576,112]{1,0:T(8,128)(2,1)S(1)} %collective-permute-done.4.refs_7_.refs_9_.refs_14_), channel_id=1, source_target_pairs={{0,16},{16,0},{1,17},{17,1},{2,18},{18,2},{3,19},{19,3},{4,20},{20... | collective-permute-start | bytes 387080 | tf_op jit(solution)/shard_map/ppermute | solution.py:28
  51.6 16.2 %all-to-all-start = ((bf16[16,40,144]{2,1,0:T(8,128)(2,1)}), bf16[16,40,144]{2,1,0:T(8,128)(2,1)S(1)}, u32[]{:S(2)}, u32[]{:S(2)}) async-start(bf16[16,40,144]{2,1,0:T(8,128)(2,1)} %copy-done.6), calls=%async_computation | async-start | bytes 655360 | tf_op jit(solution)/shard_map/all_to_all | solution.py:644
  56.9 6.6 %collective-permute-start.16 = (bf16[2,4,3608]{2,1,0:T(4,128)(2,1)S(1)}, bf16[2,4,3608]{2,1,0:T(4,128)(2,1)S(1)}, u32[]{:S(2)}, u32[]{:S(2)}) collective-permute-start(bf16[2,4,3608]{2,1,0:T(4,128)(2,1)S(1)} %concatenate.3.refs_12_.refs_4_), channel_id=1, source_target_pairs={{0,8},{4,12},{8,0},{12,4},{1,9},{5,13},{9,1},{13,5},{2,10},{6,14},... | collective-permute-start | bytes 173192 | tf_op jit(solution)/shard_map/ppermute | solution.py:28
  61.3 7.8 %collective-permute-start.10 = (bf16[128,576]{1,0:T(8,128)(2,1)}, bf16[128,576]{1,0:T(8,128)(2,1)S(1)}, u32[]{:S(2)}, u32[]{:S(2)}) collective-permute-start(bf16[128,576]{1,0:T(8,128)(2,1)} %get-tuple-element.34), channel_id=1, source_target_pairs={{0,8},{4,12},{8,0},{12,4},{1,9},{5,13},{9,1},{13,5},{2,10},{6,14},... | collective-permute-start | bytes 442376 | tf_op jit(solution)/shard_map/ppermute | solution.py:28
  63.5 9.1 %collective-permute-start.11 = (bf16[128,576]{1,0:T(8,128)(2,1)}, bf16[128,576]{1,0:T(8,128)(2,1)S(1)}, u32[]{:S(2)}, u32[]{:S(2)}) collective-permute-start(bf16[128,576]{1,0:T(8,128)(2,1)} %get-tuple-element.35), channel_id=1, source_target_pairs={{0,12},{4,8},{8,4},{12,0},{1,13},{5,9},{9,5},{13,1},{2,14},{6,10},... | collective-permute-start | bytes 442376 | tf_op jit(solution)/shard_map/ppermute | solution.py:28
  65.0 7.5 %collective-permute-start.9 = (bf16[128,576]{1,0:T(8,128)(2,1)}, bf16[128,576]{1,0:T(8,128)(2,1)}, u32[]{:S(2)}, u32[]{:S(2)}) collective-permute-start(bf16[128,576]{1,0:T(8,128)(2,1)} %get-tuple-element.33), channel_id=1, source_target_pairs={{0,4},{4,0},{8,12},{12,8},{1,5},{5,1},{9,13},{13,9},{2,6},{6,2},{1... | collective-permute-start | bytes 442376 | tf_op jit(solution)/shard_map/ppermute | solution.py:28
  78.9 5.7 %collective-permute-start.21 = (bf16[32,512]{1,0:T(8,128)(2,1)S(1)}, bf16[32,512]{1,0:T(8,128)(2,1)S(1)}, u32[]{:S(2)}, u32[]{:S(2)}) collective-permute-start(bf16[32,512]{1,0:T(8,128)(2,1)S(1)} %get-tuple-element.48), channel_id=1, source_target_pairs={{0,3},{1,2},{2,1},{3,0},{4,7},{5,6},{6,5},{7,4},{8,11},{9,10},{10,... | collective-permute-start | bytes 98312 | tf_op jit(solution)/shard_map/ppermute | solution.py:28
  92.3 8.0 %collective-permute-start.28 = (bf16[32,896]{1,0:T(8,128)(2,1)S(1)}, bf16[32,896]{1,0:T(8,128)(2,1)S(1)}, u32[]{:S(2)}, u32[]{:S(2)}) collective-permute-start(bf16[32,896]{1,0:T(8,128)(2,1)S(1)} %output_product.1), channel_id=1, source_target_pairs={{0,2},{1,3},{2,0},{3,1},{4,6},{5,7},{6,4},{7,5},{8,10},{9,11},{10,... | collective-permute-start | bytes 172040 | tf_op jit(solution)/shard_map/ppermute | solution.py:28
  93.9 6.4 %collective-permute-start.29 = (bf16[32,896]{1,0:T(8,128)(2,1)S(1)}, bf16[32,896]{1,0:T(8,128)(2,1)S(1)}, u32[]{:S(2)}, u32[]{:S(2)}) collective-permute-start(bf16[32,896]{1,0:T(8,128)(2,1)S(1)} %output_product.1), channel_id=1, source_target_pairs={{0,3},{1,2},{2,1},{3,0},{4,7},{5,6},{6,5},{7,4},{8,11},{9,10},{10,... | collective-permute-start | bytes 172040 | tf_op jit(solution)/shard_map/ppermute | solution.py:28
  114.6 13.3 %all-to-all-start.1 = ((bf16[16,8,896]{2,1,0:T(8,128)(2,1)}), bf16[16,8,896]{2,1,0:T(8,128)(2,1)S(1)}, u32[]{:S(2)}, u32[]{:S(2)}) async-start(bf16[16,8,896]{2,1,0:T(8,128)(2,1)} %get-tuple-element.51), calls=%async_computation.1 | async-start | bytes 458752 | tf_op jit(solution)/shard_map/all_to_all | solution.py:684
  (31 other events, 343.3 us)

commit v7 on v6

--- a/solution.py
+++ b/solution.py
@@ -73,84 +73,104 @@
     )(*at_home(*arrays), *after)
 
 
-def doubled(block, axis):
-    held = {0: block}
-    size = lax.axis_size(axis)
-    masks = [1 << bit for bit in range(size.bit_length() - 1)]
-    for mask in masks[1:] + masks[:1]:
+def doubled(held, axis, masks):
+    held = dict(held)
+    for mask in masks:
         for other in list(held):
             held[other ^ mask] = swap(held[other], axis, mask)
-    return [held[mask] for mask in range(size)]
-
-
-def cut_kernel(sections, experts, piece, x_ref, *refs):
-    out_refs, held = refs[:experts], refs[experts]
+    return held
+
+
+def cut_kernel(sections, experts, piece, x_ref, query_ref, *refs):
+    out_refs, held = refs[-1 - experts : -1], refs[-1]
     rank = lax.axis_index("expert")
+    steps, sources, heads, wide = query_ref.shape
+    rows = x_ref.shape[0]
     for target in range(experts):
         for section in range(sections):
             at = (section * experts + target) * piece
-            held[target, section] = x_ref[:, at : at + piece]
+            held[target, section * rows : (section + 1) * rows] = x_ref[:, at : at + piece]
     for mask, ref in enumerate(out_refs):
-        ref[...] = held[rank ^ mask]
-
-
-def cut_columns(x, sections, experts):
+        ref[: sections * rows, :piece] = held[rank ^ mask]
+        for step in range(steps):
+            for source in range(sources):
+                at = sections * rows + (step * sources + source) * heads
+                ref[at : at + heads, :wide] = query_ref[step, source]
+
+
+def cut_columns(x, queries, sections, experts, after):
     rows, width = x.shape
     piece = width // (sections * experts)
-    block = jax.ShapeDtypeStruct((sections, rows, piece), x.dtype)
+    steps, sources, heads, wide = queries.shape
+    block = jax.ShapeDtypeStruct(
+        (sections * rows + steps * sources * heads, max(piece, wide)), x.dtype
+    )
     return pl.pallas_call(
         functools.partial(cut_kernel, sections, experts, piece),
         out_shape=[block] * experts,
-        scratch_shapes=[pltpu.VMEM((experts,) + block.shape, x.dtype)],
-        compiler_params=params(x, scale=6),
+        in_specs=[pl.BlockSpec(memory_space=pltpu.VMEM)] * 2
+        + [pl.BlockSpec(memory_space=pl.ANY)] * len(after),
+        scratch_shapes=[pltpu.VMEM((experts, sections * rows, piece), x.dtype)],
+        compiler_params=params(x, block, scale=6),
         name="cut_columns",
-    )(*at_home(x))
-
-
-def project_kernel(count, sections, groups, *refs):
-    x_refs = refs[:count]
-    w_refs = refs[count : count + sections * groups]
-    out_refs = refs[count + sections * groups :]
-    section_rank = lax.axis_index("section")
-    group_rank = lax.axis_index("groups")
-    rows = x_refs[0].shape[1]
+    )(*at_home(x, queries), *after)
+
+
+def project_kernel(count, first, rows, experts, sections, *refs):
+    x_refs, (own_ref, *w_refs) = refs[:count], refs[count : count + 1 + sections]
+    out_refs, columns = refs[-1 - count : -1], refs[-1]
+    section_rank, rank = lax.axis_index("section"), lax.axis_index("expert")
+    width, piece = w_refs[0].shape
+    steps = own_ref.shape[0]
     total = 0
     for mask in range(sections):
-        held = [w_refs[mask * groups + other][...] for other in range(groups)]
-        columns = []
-        for group in range(groups):
-            chosen = held[0]
-            for other in range(1, groups):
-                chosen = jnp.where((group_rank ^ other) == group, held[other], chosen)
-            columns.append(chosen)
-        weights = jnp.concatenate(columns, axis=1)
-        x = jnp.concatenate([ref[section_rank ^ mask] for ref in x_refs], axis=0)
+        at = pl.ds(pl.multiple_of((section_rank ^ mask) * rows, rows), rows)
+        x = jnp.concatenate([ref[at, :piece] for ref in x_refs], axis=0)
         total = total + lax.dot_general(
-            x, weights, (((1,), (1,)), ((), ())), preferred_element_type=jnp.float32
+            x, w_refs[mask][...], (((1,), (1,)), ((), ())), preferred_element_type=jnp.float32
         )
+    own = jnp.concatenate([own_ref[step] for step in range(steps)], axis=0).astype(jnp.float32)
+    block = own.shape[0]
+    column = columns.shape[2]
+    for target in range(experts):
+        columns[target] = own[:, target * column : (target + 1) * column]
     for index, ref in enumerate(out_refs):
-        ref[...] = total[index * rows : (index + 1) * rows].astype(ref.dtype)
-
-
-def project(blocks, w_parts, sections, groups):
-    out = jax.ShapeDtypeStruct((blocks[0].shape[1], w_parts[0].shape[0]), jnp.bfloat16)
-    return pl.pallas_call(
-        functools.partial(project_kernel, len(blocks), sections, groups),
+        ref[:rows, :] = total[index * rows : (index + 1) * rows].astype(ref.dtype)
+        value = columns[rank ^ (first + index)]
+        for line, at in enumerate(range(0, column, width)):
+            end = min(at + width, column)
+            to = rows + line * block
+            ref[to : to + block, : end - at] = value[:, at:end].astype(ref.dtype)
+
+
+def project(blocks, own, w_parts, first, rows, experts, after):
+    width = w_parts[0].shape[0]
+    column = own.shape[2] // experts
+    block = own.shape[0] * own.shape[1]
+    out = jax.ShapeDtypeStruct((rows + block * -(-column // width), width), jnp.bfloat16)
+    held = pl.BlockSpec(memory_space=pltpu.VMEM)
+    return pl.pallas_call(
+        functools.partial(
+            project_kernel, len(blocks), first, rows, experts, len(w_parts)
+        ),
         out_shape=[out] * len(blocks),
+        in_specs=[held] * (len(blocks) + 1 + len(w_parts))
+        + [pl.BlockSpec(memory_space=pl.ANY)] * len(after),
+        scratch_shapes=[pltpu.VMEM((experts, block, column), jnp.float32)],
         compiler_params=params(*blocks, *w_parts, scale=6),
         name="project",
-    )(*blocks, *w_parts)
+    )(*blocks, *at_home(own), *w_parts, *after)
 
 
 def query_kernel(
-    experts, sections, prompts, nope, *refs
+    experts, sections, prompts, nope, shape, *refs
 ):
     f32, bf16 = jnp.float32, jnp.bfloat16
     table_ref, query_refs = refs[0], refs[1 : 1 + experts]
     uk_ref, own_ref, gain_ref, wt_ref = refs[1 + experts : 5 + experts]
     out_ref, token_ref, picked, ropes, made, normed, query_ref = refs[-7:]
     token_ref[...] = jnp.zeros_like(token_ref)
-    steps, sources, heads, wide = query_refs[0].shape
+    steps, sources, heads, wide = shape
     rope = wide - nope
     chunk = uk_ref.shape[2]
     width = out_ref.shape[2]
@@ -159,7 +179,10 @@
     rank = lax.axis_index("expert")
 
     for mask, ref in enumerate(query_refs):
-        query_ref[rank ^ mask] = ref[...]
+        for step in range(steps):
+            for source in range(sources):
+                at = ref.shape[0] - (steps * sources - step * sources - source) * heads
+                query_ref[rank ^ mask, step, source] = ref[at : at + heads, :wide]
 
     def pick(index, carry):
         owner = table_ref[index]
@@ -215,16 +238,16 @@
             out_ref[index, block:, :] = lines
 
 
-def absorb_queries(table, queries, w_uk, own, gain, w_turned, prompts, sections, after):
+def absorb_queries(table, queries, shape, w_uk, own, gain, w_turned, prompts, sections, after):
     experts = len(queries)
-    steps, sources, heads, wide = queries[0].shape
+    steps, sources, heads, wide = shape
     _, nope, chunk = w_uk.shape
     width = chunk + (wide - nope) // experts
     rows = prompts * steps * heads + steps * experts
     count = experts * sources * steps * heads
     held = pl.BlockSpec(memory_space=pltpu.VMEM)
     return pl.pallas_call(
-        functools.partial(query_kernel, experts, sections, prompts, nope),
+        functools.partial(query_kernel, experts, sections, prompts, nope, shape),
         out_shape=[
             jax.ShapeDtypeStruct((experts * sections, rows, width), jnp.bfloat16),
             jax.ShapeDtypeStruct((8, 128), jnp.bfloat16),
@@ -240,11 +263,11 @@
             pltpu.VMEM(
                 (sections, own.shape[0] * own.shape[1], w_turned.shape[1]), jnp.bfloat16
             ),
-            pltpu.VMEM((experts,) + queries[0].shape, jnp.bfloat16),
+            pltpu.VMEM((experts,) + shape, jnp.bfloat16),
         ],
         compiler_params=params(*queries, w_uk, own, w_turned, scale=4),
         name="absorb_queries",
-    )(table, *queries, *at_home(w_uk, own, gain, w_turned), *after)
+    )(*at_home(table), *queries, *at_home(w_uk, own, gain, w_turned), *after)
 
 
 def turn(values, cosine, sine):
@@ -326,21 +349,21 @@
         scratch_shapes=[pltpu.VMEM((steps * heads, rope), jnp.float32)] * 2,
         compiler_params=params(blocks, scale=4),
         name="gather_queries",
-    )(lengths, owners, *at_home(kv_gain, *table), blocks)
-
-
-def attend_kernel(parts, sections, sources, heads, steps, score_scale, *refs):
+    )(*at_home(lengths, owners, kv_gain, *table), blocks)
+
+
+def attend_kernel(parts, positions, sections, sources, heads, steps, score_scale, *refs):
     part_refs = refs[:parts]
     (length_ref, gain_ref, cosine_ref, sine_ref, query_ref, query_rope_ref, recent_ref,
      recent_rope_ref) = refs[parts : parts + 8]
-    out_refs, held = refs[-1 - sections : -1], refs[-1]
+    out_refs, token_ref, held = refs[-2 - sections : -2], refs[-2], refs[-1]
+    token_ref[...] = jnp.zeros_like(token_ref)
     f32, bf16 = jnp.float32, jnp.bfloat16
     nt = (((1,), (1,)), ((), ()))
     prompts, _, latent = query_ref.shape
     rows = steps * heads
     section_rank = lax.axis_index("section")
     first = lax.axis_index("expert") * sources + section_rank * prompts
-    positions = part_refs[0].shape[0] // prompts
     for prompt in range(prompts):
         at = slice(prompt * positions, (prompt + 1) * positions)
         projected = part_refs[0][at].astype(f32)
@@ -385,31 +408,33 @@
 
 
 def attend(
-    parts, lengths, kv_gain, table, gathered, sources, steps, sections, score_scale, after
+    parts, positions, lengths, kv_gain, table, gathered, sources, steps, sections, score_scale
 ):
     prompts, rows, latent = gathered[0].shape
     out = (rows // sections, latent)
     held = pl.BlockSpec(memory_space=pltpu.VMEM)
     return pl.pallas_call(
         functools.partial(
-            attend_kernel, len(parts), sections, sources, out[0] // steps, steps, score_scale
+            attend_kernel, len(parts), positions, sections, sources, out[0] // steps, steps,
+            score_scale
         ),
-        out_shape=[jax.ShapeDtypeStruct((prompts * out[0], latent), jnp.bfloat16)] * sections,
+        out_shape=[jax.ShapeDtypeStruct((prompts * out[0], latent), jnp.bfloat16)] * sections
+        + [jax.ShapeDtypeStruct((8, 128), jnp.bfloat16)],
         in_specs=[held] * len(parts)
         + [pl.BlockSpec(memory_space=pltpu.SMEM)]
-        + [held] * 7
-        + [pl.BlockSpec(memory_space=pl.ANY)] * len(after),
-        out_specs=[held] * sections,
+        + [held] * 7,
+        out_specs=[held] * (sections + 1),
         scratch_shapes=[pltpu.VMEM((sections,) + out, jnp.bfloat16)],
         compiler_params=params(*parts, *gathered, scale=6),
         name="attend",
-    )(*parts, lengths, *at_home(kv_gain, *table), *gathered, *after)
+    )(*parts, *at_home(lengths, kv_gain, *table), *gathered)
 
 
 def value_kernel(experts, sections, heads, steps, sources, *refs):
     owner_ref = refs[0]
     latent_refs, uv_refs = refs[1 : 1 + sections], refs[1 + sections : 1 + sections + experts]
-    out_ref, held = refs[1 + sections + experts :]
+    route_ref = refs[1 + sections + experts]
+    out_ref, held = refs[-2:]
     f32, bf16 = jnp.float32, jnp.bfloat16
     chunk = uv_refs[0].shape[2]
     rows = latent_refs[0].shape[0]
@@ -446,10 +471,14 @@
             for step in range(steps):
                 index = (mask * prompts + prompt) * steps + step
                 order = jnp.where((row == index) & (to == owner * steps + step), 1.0, order)
-    out_ref[...] = jnp.dot(order.astype(bf16), values, preferred_element_type=f32).astype(bf16)
-
-
-def head_products(owners, latents, uv_parts, steps, sources):
+    width = values.shape[1]
+    out_ref[:, :width] = jnp.dot(
+        order.astype(bf16), values, preferred_element_type=f32
+    ).astype(bf16)
+    out_ref[:, width:] = route_ref[...]
+
+
+def head_products(owners, latents, uv_parts, route, steps, sources, after):
     rows, width = latents[0].shape
     heads, value, _ = uv_parts[0].shape
     held = pl.BlockSpec(memory_space=pltpu.VMEM)
@@ -458,22 +487,26 @@
         functools.partial(
             value_kernel, len(uv_parts), len(latents), heads, steps, sources
         ),
-        out_shape=jax.ShapeDtypeStruct((total // heads, heads * value), jnp.bfloat16),
+        out_shape=jax.ShapeDtypeStruct(
+            (total // heads, heads * value + route.shape[1]), jnp.bfloat16
+        ),
         in_specs=[pl.BlockSpec(memory_space=pltpu.SMEM)]
-        + [held] * (len(latents) + len(uv_parts)),
+        + [held] * (len(latents) + len(uv_parts) + 1)
+        + [pl.BlockSpec(memory_space=pl.ANY)] * len(after),
         out_specs=held,
         scratch_shapes=[
             pltpu.VMEM((len(uv_parts), total, max(width // len(uv_parts), 128)), jnp.float32)
         ],
         compiler_params=params(*latents, *uv_parts, scale=4),
         name="head_products",
-    )(owners, *latents, *uv_parts)
+    )(*at_home(owners), *latents, *uv_parts, route, *after)
 
 
 def output_kernel(experts, *refs):
     value_refs = refs[:experts]
     weight_ref, out_ref = refs[experts:]
-    values = jnp.concatenate([ref[...] for ref in value_refs], axis=0)
+    depth = weight_ref.shape[0]
+    values = jnp.concatenate([ref[:, :depth] for ref in value_refs], axis=0)
     rows = values.shape[0]
     to = lax.broadcasted_iota(jnp.int32, (rows, rows), 0)
     row = lax.broadcasted_iota(jnp.int32, (rows, rows), 1)
@@ -499,30 +532,65 @@
     )(*values, weight)
 
 
+def mix_kernel(count, owners, rows, *refs):
+    part_refs, own_refs = refs[:count], refs[count : count + owners]
+    out_ref, held = refs[-2:]
+    f32 = jnp.float32
+    total = part_refs[0][...].astype(f32)
+    for ref in part_refs[1:]:
+        total = total + ref[...].astype(f32)
+    block, column = held.shape[1:]
+    for owner in range(owners):
+        held[owner] = total[owner * block : (owner + 1) * block]
+    rank = lax.axis_index("expert")
+    for mask, ref in enumerate(own_refs):
+        lines = []
+        for line, at in enumerate(range(0, column, ref.shape[1])):
+            end = min(at + ref.shape[1], column)
+            to = rows + line * block
+            lines.append(ref[to : to + block, : end - at].astype(f32))
+        lines = lines[0] if len(lines) == 1 else jnp.concatenate(lines, axis=1)
+        out_ref[rank ^ mask] = (held[rank ^ mask] + lines).astype(out_ref.dtype)
+
+
+def mix(parts, owns, rows, after):
+    total, width = parts[0].shape
+    owners = len(owns)
+    held = pl.BlockSpec(memory_space=pltpu.VMEM)
+    shape = (owners, total // owners, width)
+    return pl.pallas_call(
+        functools.partial(mix_kernel, len(parts), owners, rows),
+        out_shape=jax.ShapeDtypeStruct(shape, parts[0].dtype),
+        in_specs=[held] * (len(parts) + owners)
+        + [pl.BlockSpec(memory_space=pl.ANY)] * len(after),
+        out_specs=held,
+        scratch_shapes=[pltpu.VMEM(shape, jnp.float32)],
+        compiler_params=params(*parts, *owns, scale=4),
+        name="mix",
+    )(*parts, *owns, *after)
+
+
 def expert_kernel(experts, sections, picks, *refs):
-    attended_refs, own_refs = refs[:experts], refs[experts : 2 * experts]
+    mixed_refs, route_refs = refs[:experts], refs[experts : 2 * experts]
     gain_ref, gate_ref, up_ref, down_ref, out_ref, near_ref, columns = refs[2 * experts :]
     f32, bf16 = jnp.float32, jnp.bfloat16
     count = gate_ref.shape[0]
-    rank, section_rank = lax.axis_index("expert"), lax.axis_index("section")
+    rank = lax.axis_index("expert")
     width = gain_ref.shape[0]
-    steps, sources, _ = own_refs[0].shape
-    block = steps * sources
-    for mask, ref in enumerate(attended_refs):
+    block = mixed_refs[0].shape[1]
+    for mask, ref in enumerate(mixed_refs):
         columns[rank ^ mask] = ref[...]
-    attended, hidden, route = [], [], []
-    for mask, ref in enumerate(own_refs):
-        attended.append(
+    mixed, route = [], []
+    for mask, ref in enumerate(route_refs):
+        mixed.append(
             jnp.concatenate([columns[i, rank ^ mask] for i in range(experts)], axis=1).astype(f32)
         )
-        own = jnp.concatenate([ref[step] for step in range(steps)], axis=0).astype(f32)
-        hidden.append(own[:, :width])
-        route.append(own[:, width:])
-    near = attended[0]
-    mixed = jnp.concatenate(hidden, axis=0) + jnp.concatenate(attended, axis=0)
+        route.append(ref[:, ref.shape[1] - 128 :].astype(f32))
+    near = mixed[0]
+    mixed = jnp.concatenate(mixed, axis=0)
     route = jnp.concatenate(route, axis=0)
     named = route[:, :picks]
-    weights = route[:, picks : 2 * picks] + route[:, 2 * picks :]
+    weights = route[:, picks : 2 * picks] + route[:, 2 * picks : 3 * picks]
     weights = route_scale * weights / jnp.sum(weights, axis=-1, keepdims=True)
     scale = lax.rsqrt(jnp.mean(mixed * mixed, axis=-1, keepdims=True) + epsilon)
     rows_in = (mixed * scale * gain_ref[...][None].astype(f32)).astype(bf16)
@@ -544,10 +612,9 @@
             ].astype(bf16)
 
 
-def run_experts(attended, own, gain, w_gate, w_up, w_down, picks, sections):
-    experts = len(own)
-    width = gain.shape[0]
-    block = (own[0].shape[0] * own[0].shape[1], width // sections)
+def run_experts(mixed, routes, gain, w_gate, w_up, w_down, picks, sections):
+    experts = len(mixed)
+    block = (mixed[0].shape[1], gain.shape[0] // sections)
     held = pl.BlockSpec(memory_space=pltpu.VMEM)
     return pl.pallas_call(
         functools.partial(expert_kernel, experts, sections, picks),
@@ -557,33 +624,33 @@
         ],
         in_specs=[held] * (2 * experts + 4),
         out_specs=[held] * 2,
-        scratch_shapes=[pltpu.VMEM((experts,) + attended[0].shape, jnp.bfloat16)],
-        compiler_params=params(*attended, *own, scale=16),
+        scratch_shapes=[pltpu.VMEM((experts,) + mixed[0].shape, jnp.bfloat16)],
+        compiler_params=params(*mixed, scale=32),
         name="run_experts",
-    )(*attended, *own, *at_home(gain), w_gate, w_up, w_down)
-
-
-def finish_kernel(block_ref, near_ref, base_ref, out_ref):
+    )(*mixed, *routes, *at_home(gain), w_gate, w_up, w_down)
+
+
+def finish_kernel(block_ref, near_ref, out_ref):
     f32 = jnp.float32
     steps, sources, _ = out_ref.shape
     total = near_ref[lax.axis_index("section")].astype(f32)
     for index in range(block_ref.shape[0]):
         total = total + block_ref[index].astype(f32)
     for step in range(steps):
-        value = base_ref[step].astype(f32) + total[step * sources : (step + 1) * sources]
-        out_ref[step] = value.astype(out_ref.dtype)
-
-
-def finish(blocks, near, base):
-    held = pl.BlockSpec(memory_space=pltpu.VMEM)
+        out_ref[step] = total[step * sources : (step + 1) * sources].astype(out_ref.dtype)
+
+
+def finish(blocks, near, steps):
+    held = pl.BlockSpec(memory_space=pltpu.VMEM)
+    _, rows, column = near.shape
     return pl.pallas_call(
         finish_kernel,
-        out_shape=jax.ShapeDtypeStruct(base.shape, base.dtype),
-        in_specs=[held] * 3,
+        out_shape=jax.ShapeDtypeStruct((steps, rows // steps, column), near.dtype),
+        in_specs=[held] * 2,
         out_specs=held,
-        compiler_params=params(blocks, near, base, scale=4),
+        compiler_params=params(blocks, near, scale=4),
         name="finish",
-    )(blocks, near, base)
+    )(blocks, near)
 
 
 def local(
@@ -608,72 +675,70 @@
     bf16, f32 = jnp.bfloat16, jnp.float32
     expert_rank = lax.axis_index("expert")
     section_rank = lax.axis_index("section")
-    group_rank = lax.axis_index("groups")
     experts = lax.axis_size("expert")
     sections = lax.axis_size("section")
-    groups = lax.axis_size("groups")
     prompt_count, full_length, width = prompts.shape
     steps, tokens_here, heads, _ = queries.shape
     depth = w_dkv.shape[0]
-    piece = depth // (groups * experts)
+    piece = depth // experts
     latent = kv_gain.shape[0]
     cache_width = w_dkv.shape[1]
     rows = prompt_count * full_length
     own_rows = steps * tokens_here
 
     w_turned = w_dkv.T
-
-    def w_piece(group):
-        return lax.dynamic_slice_in_dim(
-            w_turned, (expert_rank * groups + group) * piece, piece, 1
-        )
-
-    halves = spread(w_piece(group_rank), "section")
-    queries_all = spread(queries, "expert")
-    cut = list(cut_columns(prompts.reshape(rows, width), sections, experts))
+    w_piece = lax.dynamic_slice_in_dim(w_turned, expert_rank * piece, piece, 1)
+    masks = [1 << bit for bit in range(experts.bit_length() - 1)]
+    uv_parts = doubled({0: w_uv}, "expert", masks[1:])
+    w_parts = spread(w_piece, "section")
+    cut = cut_columns(
+        prompts.reshape(rows, width), queries, sections, experts,
+        [],
+    )
     cut = deliver(cut, "expert")
-    w_parts = halves[:1] + [w_piece(group_rank ^ other) for other in range(1, groups)]
-    for half in halves[1:]:
-        w_parts += spread(half, "groups")
-    w_gate, w_up, w_down = fetch([w_gate, w_up, w_down], queries_all[1:])
 
     blocks, token = absorb_queries(
-        owners, queries_all, w_uk, residual, attn_gain, w_turned, prompt_count, sections,
-        cut[1:] + halves[1:] + w_parts[groups : groups + 2] + [w_gate],
+        owners, cut, queries.shape, w_uk, residual, attn_gain, w_turned, prompt_count, sections,
+        [uv_parts[masks[-1]]],
     )
     blocks = lax.all_to_all(blocks, ("expert", "section"), 0, 0, tiled=True)
 
-    high = route_scores.astype(bf16)
-    low = (route_scores - high.astype(f32)).astype(bf16)
-    packed = jnp.concatenate([residual, expert_ids.astype(bf16), high, low], axis=2)
-    w_uv, token = lax.optimization_barrier((w_uv, token))
-    uv_parts = doubled(w_uv, "expert")
-    packed = spread(packed, "expert")
-
-    away = list(project(cut[1:], w_parts, sections, groups))
-    near = list(project(cut[:1], w_parts, sections, groups))
+    away = list(project(cut[1:], residual, w_parts, 1, rows, experts, [token]))
+    near = list(project(cut[:1], residual, w_parts, 0, rows, experts, away[:1]))
     parts = deliver(near + away, "expert")
     table = rotation(full_length + steps + -(full_length + steps) % 8, cache_width - latent)
     gathered = list(gather_queries(
         blocks, lengths, owners, kv_gain, table, prompt_count, tokens_here, experts, sections,
         steps, heads
     ))
-    out_latent = attend(
-        parts, lengths, kv_gain, table, gathered, tokens_here, steps, sections,
-        queries.shape[-1] ** (-0.5), packed + [uv_parts[2], token],
-    )
-
+    *out_latent, token = attend(
+        parts, full_length, lengths, kv_gain, table, gathered, tokens_here, steps, sections,
+        queries.shape[-1] ** (-0.5),
+    )
+
+    (w_gate,) = fetch([w_gate], [token])
+    order = sorted(uv_parts)
+    *uv_parts, token = lax.optimization_barrier((*[uv_parts[mask] for mask in order], token))
+    uv_parts = doubled(dict(zip(order, uv_parts)), "expert", masks[:1])
     out_latent = deliver(out_latent, "section")
-    head_values = head_products(owners, out_latent, uv_parts, steps, tokens_here)
+    high = route_scores.astype(bf16)
+    low = (route_scores - high.astype(f32)).astype(bf16)
+    route = jnp.concatenate([expert_ids.astype(bf16), high, low], axis=2).reshape(own_rows, -1)
+    route = jnp.pad(route, ((0, 0), (0, 128 - route.shape[1])))
+    head_values = head_products(
+        owners, out_latent, [uv_parts[mask] for mask in range(experts)], route, steps,
+        tokens_here, [w_gate, token],
+    )
     head_values = spread(head_values, "expert")
 
     (w_o,) = fetch([w_o], [])
     attended = output_product(head_values, w_o)
-    attended = sum(part.astype(f32) for part in spread(attended, "section")).astype(bf16)
-    attended = attended.reshape(experts, own_rows, -1)
+    (w_up,) = fetch([w_up], [attended])
+    mixed = mix(spread(attended, "section"), parts, rows, [w_up])
+    (w_down,) = fetch([w_down], [mixed])
     blocks, near = run_experts(
-        spread(attended, "expert"),
-        packed,
+        spread(mixed, "expert"),
+        head_values,
         moe_gain,
         w_gate,
         w_up,
@@ -682,9 +747,7 @@
         sections,
     )
     blocks = lax.all_to_all(blocks, ("expert", "section"), 0, 0, tiled=True)
-    column = width // sections
-    base = lax.dynamic_slice_in_dim(residual, section_rank * column, column, 2)
-    return finish(blocks, near, base)
+    return finish(blocks, near, steps)
 
 
 def solution(mesh):

time: 129 us -> 104 us (0.81)
  local copies, waits for them, and re-layouts: 17.2 us -> 1.9 us
  waiting for transfers between devices: 39.7 us -> 25.5 us
  blocking collectives: 0 us -> 12.1 us
  starting transfers between devices: 43 us -> 32.7 us
  Pallas kernels: 28.3 us -> 31 us
    unnamed x40 -> x8, local copies, waits for them, and re-layouts: 15.1 us -> 0.73 us
    all_to_all x0 -> x1, blocking collectives: none -> 12.1 us  [local(): blocks = lax.all_to_all(blocks, ('expert', 'section'), 0, 0, tiled=True)]
    ppermute x33 -> x24, waiting for transfers between devices: 30.6 us -> 19.9 us  [swap(): return lax.ppermute(block, axis, [(i, i ^ mask) for i in range(size)])]
    ppermute x33 -> x24, starting transfers between devices: 34.2 us -> 26 us  [swap(): return lax.ppermute(block, axis, [(i, i ^ mask) for i in range(size)])]
    all_to_all x2 -> x1, waiting for transfers between devices: 9.16 us -> 5.59 us  [local(): blocks = lax.all_to_all(blocks, ('expert', 'section'), 0, 0, tiled=True)]
    all_to_all x2 -> x1, starting transfers between devices: 8.78 us -> 6.62 us  [local(): blocks = lax.all_to_all(blocks, ('expert', 'section'), 0, 0, tiled=True)]
    pallas_call x2 -> x4, Pallas kernels: 9.33 us -> 11.4 us  [fetch(): pl.pallas_call(functools.partial(fetch_kernel, len(arrays)), out_shape=[p...]
    pallas_call x4 -> x5, Pallas kernels: 4.87 us -> 6.24 us  [the longest x2 3.7 us: project(): pl.pallas_call(functools.partial(project_kernel, len(blocks), first, rows...]
  transfers between devices with their start and end apart: 35 -> 25, of which waited for: 16 -> 8; matrix products, arithmetic and copies ran while one was open for 2% -> 1% of each run, Pallas kernels for 13% -> 20%
where the time goes in v7:
time: 104 us; the launch traced here: 103 us
  starting transfers between devices  32.7 us (31%)
  Pallas kernels  31 us (30%)
  waiting for transfers between devices  25.5 us (25%)
  blocking collectives  12.1 us (12%)
  local copies, waits for them, and re-layouts  1.9 us (2%)
    ppermute x24, starting transfers between devices, swap(): return lax.ppermute(block, axis, [(i, i ^ mask) for i in range(size)])  26 us
    ppermute x24, waiting for transfers between devices, swap(): return lax.ppermute(block, axis, [(i, i ^ mask) for i in range(size)])  19.9 us
    all_to_all x1, blocking collectives, local(): blocks = lax.all_to_all(blocks, ('expert', 'section'), 0, 0, tiled=True)  12.1 us
    pallas_call x4, Pallas kernels, fetch(): pl.pallas_call(functools.partial(fetch_kernel, len(arrays)), out_shape=[p...  11.4 us
    all_to_all x1, starting transfers between devices, local(): blocks = lax.all_to_all(blocks, ('expert', 'section'), 0, 0, tiled=True)  6.62 us
    all_to_all x1, waiting for transfers between devices, local(): blocks = lax.all_to_all(blocks, ('expert', 'section'), 0, 0, tiled=True)  5.59 us
    pallas_call x1, Pallas kernels, run_experts(): pl.pallas_call(functools.partial(expert_kernel, experts, sections, picks)...  4.98 us
    pallas_call x2, Pallas kernels, project(): pl.pallas_call(functools.partial(project_kernel, len(blocks), first, rows...  3.7 us
  transfers between devices with their start and end apart: 25, of which 8 were waited for; matrix products, arithmetic and copies ran while one was open for 1% of the time, Pallas kernels for 20%

profile of v7, /device:TPU:0, one launch (start us, length us, event | category | flops | bytes accessed | tf_op | source)
XLA Modules:
  0.0 103.4 jit_solution(3252937881684300834)
XLA Ops:
  0.0 2.9 %collective-permute-start.6 = (bf16[16,128,128]{2,1,0:T(8,128)(2,1)}, bf16[16,128,128]{2,1,0:T(8,128)(2,1)S(1)}, u32[]{:S(2)}, u32[]{:S(2)}) collective-permute-start(bf16[16,128,128]{2,1,0:T(8,128)(2,1)} %refs_5_.4), channel_id=1, source_target_pairs={{0,8},{4,12},{8,0},{12,4},{1,9},{5,13},{9,1},{13,5},{2,10},{6,14},... | collective-permute-start | bytes 1572872 | tf_op jit(solution)/shard_map/ppermute | solution.py:28
  2.9 2.4 %cut_columns.1 = (bf16[640,224]{1,0:T(8,128)(2,1)S(1)}, bf16[640,224]{1,0:T(8,128)(2,1)S(1)}, bf16[640,224]{1,0:T(8,128)(2,1)}, bf16[640,224]{1,0:T(8,128)(2,1)S(1)}) custom-call(bf16[128,3584]{1,0:T(8,128)(2,1)} %bitcast.6, bf16[2,4,16,192]{3,2,1,0:T(8,128)(2,1)} %query_ref.1), custom_call_target="tpu_custom_call" | custom-call | tf_op jit(solution)/shard_map/cut_columns/pallas_call | solution.py:108
  5.4 1.8 %collective-permute-start.5 = (bf16[640,224]{1,0:T(8,128)(2,1)S(1)}, bf16[640,224]{1,0:T(8,128)(2,1)S(1)}, u32[]{:S(2)}, u32[]{:S(2)}) collective-permute-start(bf16[640,224]{1,0:T(8,128)(2,1)S(1)} %get-tuple-element.31), channel_id=1, source_target_pairs={{0,12},{4,8},{8,4},{12,0},{1,13},{5,9},{9,5},{13,1},{2,14},{6,10},... | collective-permute-start | bytes 860168 | tf_op jit(solution)/shard_map/ppermute | solution.py:28
  8.4 3.7 %collective-permute-start.2 = (bf16[576,224]{1,0:T(8,128)(2,1)S(1)}, bf16[576,224]{1,0:T(8,128)(2,1)S(1)}, u32[]{:S(2)}, u32[]{:S(2)}) collective-permute-start(bf16[576,224]{1,0:T(8,128)(2,1)S(1)} %dynamic-slice_bitcast_fusion.refs_4_.refs_2_), channel_id=1, source_target_pairs={{0,3},{1,2},{2,1},{3,0},{4,7},{5,6},{6,5},{7,4},{8,11},{9,10},{10,... | collective-permute-start | bytes 774152 | tf_op jit(solution)/shard_map/ppermute | solution.py:28
  12.0 10.9 %collective-permute-done.4.refs_3_.refs_1_ = bf16[640,224]{1,0:T(8,128)(2,1)S(1)} collective-permute-done((bf16[640,224]{1,0:T(8,128)(2,1)}, bf16[640,224]{1,0:T(8,128)(2,1)S(1)}, u32[]{:S(2)}, u32[]{:S(2)}) %collective-permute-start.4) | collective-permute-done | bytes 286752 | tf_op jit(solution)/shard_map/ppermute | solution.py:28
  22.9 2.1 %collective-permute-start = (bf16[576,224]{1,0:T(8,128)(2,1)S(1)}, bf16[576,224]{1,0:T(8,128)(2,1)S(1)}, u32[]{:S(2)}, u32[]{:S(2)}) collective-permute-start(bf16[576,224]{1,0:T(8,128)(2,1)S(1)} %dynamic-slice_bitcast_fusion.refs_4_.refs_2_), channel_id=1, source_target_pairs={{0,1},{1,0},{2,3},{3,2},{4,5},{5,4},{6,7},{7,6},{8,9},{9,8},{10,11... | collective-permute-start | bytes 774152 | tf_op jit(solution)/shard_map/ppermute | solution.py:28
  25.1 3.3 %collective-permute-done.5.refs_4_.refs_2_ = bf16[640,224]{1,0:T(8,128)(2,1)S(1)} collective-permute-done((bf16[640,224]{1,0:T(8,128)(2,1)S(1)}, bf16[640,224]{1,0:T(8,128)(2,1)S(1)}, u32[]{:S(2)}, u32[]{:S(2)}) %collective-permute-start.5) | collective-permute-done | bytes 286752 | tf_op jit(solution)/shard_map/ppermute | solution.py:28
  28.4 2.2 %absorb_queries.1 = (bf16[16,40,144]{2,1,0:T(8,128)(2,1)S(1)}, bf16[8,128]{1,0:T(8,128)(2,1)S(1)}) custom-call(s32[16]{0:T(128)} %refs_0_.8, bf16[640,224]{1,0:T(8,128)(2,1)S(1)} %get-tuple-element.28.refs_1_.refs_0_, bf16[640,224]{1,0:T(8,128)(2,1)S(1)} %collective-permute-done.3.refs_2_.refs_0_, ...), custom_call_target="tpu_custom_call" | custom-call | tf_op jit(solution)/shard_map/absorb_queries/pallas_call | solution.py:249
  31.3 6.6 %all-to-all-start = ((bf16[16,40,144]{2,1,0:T(8,128)(2,1)}), bf16[16,40,144]{2,1,0:T(8,128)(2,1)S(1)}, u32[]{:S(2)}, u32[]{:S(2)}) async-start(bf16[16,40,144]{2,1,0:T(8,128)(2,1)} %copy-done.1), calls=%async_computation | async-start | bytes 655360 | tf_op jit(solution)/shard_map/all_to_all | solution.py:704
  37.9 2.4 %project.2 = (bf16[144,576]{1,0:T(8,128)(2,1)}, bf16[144,576]{1,0:T(8,128)(2,1)}, bf16[144,576]{1,0:T(8,128)(2,1)}) custom-call(bf16[640,224]{1,0:T(8,128)(2,1)S(1)} %collective-permute-done.3.refs_2_.refs_0_, bf16[640,224]{1,0:T(8,128)(2,1)S(1)} %collective-permute-done.4.refs_3_.refs_1_, bf16[640,224]{1,0:T(8,128)(2,1)S(1)} %collective-permute-done.5.refs_4_.refs_2_, ...), custom_call_target="tpu_custom_call" | custom-call | tf_op jit(solution)/shard_map/project/pallas_call | solution.py:152
  40.3 1.9 %collective-permute-start.8 = (bf16[144,576]{1,0:T(8,128)(2,1)}, bf16[144,576]{1,0:T(8,128)(2,1)S(1)}, u32[]{:S(2)}, u32[]{:S(2)}) collective-permute-start(bf16[144,576]{1,0:T(8,128)(2,1)} %get-tuple-element.34), channel_id=1, source_target_pairs={{0,8},{4,12},{8,0},{12,4},{1,9},{5,13},{9,1},{13,5},{2,10},{6,14},... | collective-permute-start | bytes 497672 | tf_op jit(solution)/shard_map/ppermute | solution.py:28
  43.8 5.6 %all-to-all-done.block_ref = bf16[16,40,144]{2,1,0:T(8,128)(2,1)S(1)} async-done(((bf16[16,40,144]{2,1,0:T(8,128)(2,1)}), bf16[16,40,144]{2,1,0:T(8,128)(2,1)S(1)}, u32[]{:S(2)}, u32[]{:S(2)}) %all-to-all-start) | async-done | bytes 184352 | tf_op jit(solution)/shard_map/all_to_all | solution.py:704
  50.6 2.5 %collective-permute-done.9.refs_3_.refs_7_ = bf16[144,576]{1,0:T(8,128)(2,1)S(1)} collective-permute-done((bf16[144,576]{1,0:T(8,128)(2,1)}, bf16[144,576]{1,0:T(8,128)(2,1)S(1)}, u32[]{:S(2)}, u32[]{:S(2)}) %collective-permute-start.9) | collective-permute-done | bytes 165920 | tf_op jit(solution)/shard_map/ppermute | solution.py:28
  53.1 1.8 %attend.1 = (bf16[32,512]{1,0:T(8,128)(2,1)S(1)}, bf16[32,512]{1,0:T(8,128)(2,1)S(1)}, bf16[32,512]{1,0:T(8,128)(2,1)S(1)}, bf16[32,512]{1,0:T(8,128)(2,1)S(1)}, bf16[8,128]{1,0:T(8,128)(2,1)S(1)}) custom-call(bf16[144,576]{1,0:T(8,128)(2,1)S(1)} %project.3.refs_0_.refs_4_, bf16[144,576]{1,0:T(8,128)(2,1)S(1)} %collective-permute-done.7.refs_1_.refs_5_, ...), custom_call_target="tpu_custom_call" | custom-call | tf_op jit(solution)/shard_map/attend/pallas_call | solution.py:416
  55.5 1.7 %collective-permute-start.10 = (bf16[32,512]{1,0:T(8,128)(2,1)S(1)}, bf16[32,512]{1,0:T(8,128)(2,1)S(1)}, u32[]{:S(2)}, u32[]{:S(2)}) collective-permute-start(bf16[32,512]{1,0:T(8,128)(2,1)S(1)} %get-tuple-element.42), channel_id=1, source_target_pairs={{0,1},{1,0},{2,3},{3,2},{4,5},{5,4},{6,7},{7,6},{8,9},{9,8},{10,11... | collective-permute-start | bytes 98312 | tf_op jit(solution)/shard_map/ppermute | solution.py:28
  57.2 1.9 %collective-permute-start.11 = (bf16[32,512]{1,0:T(8,128)(2,1)S(1)}, bf16[32,512]{1,0:T(8,128)(2,1)S(1)}, u32[]{:S(2)}, u32[]{:S(2)}) collective-permute-start(bf16[32,512]{1,0:T(8,128)(2,1)S(1)} %get-tuple-element.43), channel_id=1, source_target_pairs={{0,2},{1,3},{2,0},{3,1},{4,6},{5,7},{6,4},{7,5},{8,10},{9,11},{10,... | collective-permute-start | bytes 98312 | tf_op jit(solution)/shard_map/ppermute | solution.py:28
  60.0 3.2 %fetch.4.refs_10_.refs_9_ = bf16[4,3584,256]{2,1,0:T(8,128)(2,1)S(1)} custom-call(bf16[4,3584,256]{2,1,0:T(8,128)(2,1)} %refs_0_.7, bf16[8,128]{1,0:T(8,128)(2,1)S(1)} %get-tuple-element.48.refs_1_.refs_11_), custom_call_target="tpu_custom_call" | custom-call | bytes 14680064 | tf_op jit(solution)/shard_map/fetch/pallas_call | solution.py:63
  64.8 2.0 %head_products.1.refs_0_.refs_4_ = bf16[8,2176]{1,0:T(8,128)(2,1)S(1)} custom-call(s32[16]{0:T(128)} %refs_0_.8, bf16[32,512]{1,0:T(8,128)(2,1)S(1)} %get-tuple-element.41.refs_1_, bf16[32,512]{1,0:T(8,128)(2,1)S(1)} %collective-permute-done.10.refs_2_, bf16[32,512]{1,0:T(8,128)(2,1)S(1)} %collective-permute-done.11.refs_3_, ...), custom_call_target="tpu_custom_call" | custom-call | tf_op jit(solution)/shard_map/head_products/pallas_call | solution.py:486
  68.6 2.0 %fetch.5.refs_4_ = bf16[2048,896]{1,0:T(8,128)(2,1)S(1)} custom-call(bf16[2048,896]{1,0:T(8,128)(2,1)} %refs_0_.9), custom_call_target="tpu_custom_call" | custom-call | bytes 7340032 | tf_op jit(solution)/shard_map/fetch/pallas_call | solution.py:63
  73.3 3.0 %collective-permute-start.18 = (bf16[32,896]{1,0:T(8,128)(2,1)S(1)}, bf16[32,896]{1,0:T(8,128)(2,1)S(1)}, u32[]{:S(2)}, u32[]{:S(2)}) collective-permute-start(bf16[32,896]{1,0:T(8,128)(2,1)S(1)} %output_product.1.refs_1_.refs_0_), channel_id=1, source_target_pairs={{0,1},{1,0},{2,3},{3,2},{4,5},{5,4},{6,7},{7,6},{8,9},{9,8},{10,11... | collective-permute-start | bytes 172040 | tf_op jit(solution)/shard_map/ppermute | solution.py:28
  76.3 3.1 %fetch.6.refs_8_.refs_10_ = bf16[4,3584,256]{2,1,0:T(8,128)(2,1)S(1)} custom-call(bf16[4,3584,256]{2,1,0:T(8,128)(2,1)} %refs_0_.10, bf16[32,896]{1,0:T(8,128)(2,1)S(1)} %output_product.1.refs_1_.refs_0_), custom_call_target="tpu_custom_call" | custom-call | bytes 14680064 | tf_op jit(solution)/shard_map/fetch/pallas_call | solution.py:63
  82.1 3.1 %fetch.7.refs_11_ = bf16[4,256,3584]{2,1,0:T(8,128)(2,1)S(1)} custom-call(bf16[4,256,3584]{2,1,0:T(8,128)(2,1)} %refs_0_.11, bf16[4,8,896]{2,1,0:T(8,128)(2,1)S(1)} %mix.1.refs_1_.refs_0_), custom_call_target="tpu_custom_call" | custom-call | bytes 14680064 | tf_op jit(solution)/shard_map/fetch/pallas_call | solution.py:63
  85.7 5.0 %run_experts.1 = (bf16[16,8,896]{2,1,0:T(8,128)(2,1)S(1)}, bf16[4,8,896]{2,1,0:T(8,128)(2,1)S(1)}) custom-call(bf16[4,8,896]{2,1,0:T(8,128)(2,1)S(1)} %mix.1.refs_1_.refs_0_, bf16[4,8,896]{2,1,0:T(8,128)(2,1)S(1)} %collective-permute-done.21.refs_1_, bf16[4,8,896]{2,1,0:T(8,128)(2,1)S(1)} %collective-permute-done.22.refs_2_, ...), custom_call_target="tpu_custom_call" | custom-call | tf_op jit(solution)/shard_map/run_experts/pallas_call | solution.py:619
  90.7 12.1 %all_to_all.10.block_ref = bf16[16,8,896]{2,1,0:T(8,128)(2,1)S(1)} all-to-all(bf16[16,8,896]{2,1,0:T(8,128)(2,1)S(1)} %get-tuple-element.49), channel_id=1, replica_groups=mesh['groups'=2,'expert'=4,'section'=4] {'expert','section'}, dimensions={0} | all-to-all | bytes 458752 | tf_op jit(solution)/shard_map/all_to_all | solution.py:749
  (55 shorter events, 16.1 us)
Async XLA Ops:
  0.0 28.4 %collective-permute-start.6 = (bf16[16,128,128]{2,1,0:T(8,128)(2,1)}, bf16[16,128,128]{2,1,0:T(8,128)(2,1)S(1)}, u32[]{:S(2)}, u32[]{:S(2)}) collective-permute-start(bf16[16,128,128]{2,1,0:T(8,128)(2,1)} %refs_5_.4), channel_id=1, source_target_pairs={{0,8},{4,12},{8,0},{12,4},{1,9},{5,13},{9,1},{13,5},{2,10},{6,14},... | collective-permute-start | bytes 1572872 | tf_op jit(solution)/shard_map/ppermute | solution.py:28
  5.3 6.7 %collective-permute-start.3 = (bf16[640,224]{1,0:T(8,128)(2,1)S(1)}, bf16[640,224]{1,0:T(8,128)(2,1)S(1)}, u32[]{:S(2)}, u32[]{:S(2)}) collective-permute-start(bf16[640,224]{1,0:T(8,128)(2,1)S(1)} %get-tuple-element.29), channel_id=1, source_target_pairs={{0,4},{4,0},{8,12},{12,8},{1,5},{5,1},{9,13},{13,9},{2,6},{6,2},{1... | collective-permute-start | bytes 860168 | tf_op jit(solution)/shard_map/ppermute | solution.py:28
  5.3 17.6 %collective-permute-start.4 = (bf16[640,224]{1,0:T(8,128)(2,1)}, bf16[640,224]{1,0:T(8,128)(2,1)S(1)}, u32[]{:S(2)}, u32[]{:S(2)}) collective-permute-start(bf16[640,224]{1,0:T(8,128)(2,1)} %get-tuple-element.30), channel_id=1, source_target_pairs={{0,8},{4,12},{8,0},{12,4},{1,9},{5,13},{9,1},{13,5},{2,10},{6,14},... | collective-permute-start | bytes 860168 | tf_op jit(solution)/shard_map/ppermute | solution.py:28
  5.4 23.0 %collective-permute-start.5 = (bf16[640,224]{1,0:T(8,128)(2,1)S(1)}, bf16[640,224]{1,0:T(8,128)(2,1)S(1)}, u32[]{:S(2)}, u32[]{:S(2)}) collective-permute-start(bf16[640,224]{1,0:T(8,128)(2,1)S(1)} %get-tuple-element.31), channel_id=1, source_target_pairs={{0,12},{4,8},{8,4},{12,0},{1,13},{5,9},{9,5},{13,1},{2,14},{6,10},... | collective-permute-start | bytes 860168 | tf_op jit(solution)/shard_map/ppermute | solution.py:28
  8.4 29.5 %collective-permute-start.2 = (bf16[576,224]{1,0:T(8,128)(2,1)S(1)}, bf16[576,224]{1,0:T(8,128)(2,1)S(1)}, u32[]{:S(2)}, u32[]{:S(2)}) collective-permute-start(bf16[576,224]{1,0:T(8,128)(2,1)S(1)} %dynamic-slice_bitcast_fusion.refs_4_.refs_2_), channel_id=1, source_target_pairs={{0,3},{1,2},{2,1},{3,0},{4,7},{5,6},{6,5},{7,4},{8,11},{9,10},{10,... | collective-permute-start | bytes 774152 | tf_op jit(solution)/shard_map/ppermute | solution.py:28
  12.0 25.9 %collective-permute-start.1 = (bf16[576,224]{1,0:T(8,128)(2,1)S(1)}, bf16[576,224]{1,0:T(8,128)(2,1)S(1)}, u32[]{:S(2)}, u32[]{:S(2)}) collective-permute-start(bf16[576,224]{1,0:T(8,128)(2,1)S(1)} %dynamic-slice_bitcast_fusion.refs_4_.refs_2_), channel_id=1, source_target_pairs={{0,2},{1,3},{2,0},{3,1},{4,6},{5,7},{6,4},{7,5},{8,10},{9,11},{10,... | collective-permute-start | bytes 774152 | tf_op jit(solution)/shard_map/ppermute | solution.py:28
  22.9 15.0 %collective-permute-start = (bf16[576,224]{1,0:T(8,128)(2,1)S(1)}, bf16[576,224]{1,0:T(8,128)(2,1)S(1)}, u32[]{:S(2)}, u32[]{:S(2)}) collective-permute-start(bf16[576,224]{1,0:T(8,128)(2,1)S(1)} %dynamic-slice_bitcast_fusion.refs_4_.refs_2_), channel_id=1, source_target_pairs={{0,1},{1,0},{2,3},{3,2},{4,5},{5,4},{6,7},{7,6},{8,9},{9,8},{10,11... | collective-permute-start | bytes 774152 | tf_op jit(solution)/shard_map/ppermute | solution.py:28
  31.3 18.1 %all-to-all-start = ((bf16[16,40,144]{2,1,0:T(8,128)(2,1)}), bf16[16,40,144]{2,1,0:T(8,128)(2,1)S(1)}, u32[]{:S(2)}, u32[]{:S(2)}) async-start(bf16[16,40,144]{2,1,0:T(8,128)(2,1)} %copy-done.1), calls=%async_computation | async-start | bytes 655360 | tf_op jit(solution)/shard_map/all_to_all | solution.py:704
  40.3 10.2 %collective-permute-start.8 = (bf16[144,576]{1,0:T(8,128)(2,1)}, bf16[144,576]{1,0:T(8,128)(2,1)S(1)}, u32[]{:S(2)}, u32[]{:S(2)}) collective-permute-start(bf16[144,576]{1,0:T(8,128)(2,1)} %get-tuple-element.34), channel_id=1, source_target_pairs={{0,8},{4,12},{8,0},{12,4},{1,9},{5,13},{9,1},{13,5},{2,10},{6,14},... | collective-permute-start | bytes 497672 | tf_op jit(solution)/shard_map/ppermute | solution.py:28
  42.2 10.8 %collective-permute-start.9 = (bf16[144,576]{1,0:T(8,128)(2,1)}, bf16[144,576]{1,0:T(8,128)(2,1)S(1)}, u32[]{:S(2)}, u32[]{:S(2)}) collective-permute-start(bf16[144,576]{1,0:T(8,128)(2,1)} %get-tuple-element.35), channel_id=1, source_target_pairs={{0,12},{4,8},{8,4},{12,0},{1,13},{5,9},{9,5},{13,1},{2,14},{6,10},... | collective-permute-start | bytes 497672 | tf_op jit(solution)/shard_map/ppermute | solution.py:28
  42.2 10.8 %collective-permute-start.7 = (bf16[144,576]{1,0:T(8,128)(2,1)}, bf16[144,576]{1,0:T(8,128)(2,1)S(1)}, u32[]{:S(2)}, u32[]{:S(2)}) collective-permute-start(bf16[144,576]{1,0:T(8,128)(2,1)} %get-tuple-element.33.refs_6_), channel_id=1, source_target_pairs={{0,4},{4,0},{8,12},{12,8},{1,5},{5,1},{9,13},{13,9},{2,6},{6,2},{1... | collective-permute-start | bytes 497672 | tf_op jit(solution)/shard_map/ppermute | solution.py:28
  54.9 9.9 %collective-permute-start.13 = (bf16[16,128,128]{2,1,0:T(8,128)(2,1)}, bf16[16,128,128]{2,1,0:T(8,128)(2,1)S(1)}, u32[]{:S(2)}, u32[]{:S(2)}) collective-permute-start(bf16[16,128,128]{2,1,0:T(8,128)(2,1)} %refs_5_.4), channel_id=1, source_target_pairs={{0,4},{4,0},{8,12},{12,8},{1,5},{5,1},{9,13},{13,9},{2,6},{6,2},{1... | collective-permute-start | bytes 1572872 | tf_op jit(solution)/shard_map/ppermute | solution.py:28
  55.1 9.7 %collective-permute-start.14 = (bf16[16,128,128]{2,1,0:T(8,128)(2,1)S(1)}, bf16[16,128,128]{2,1,0:T(8,128)(2,1)S(1)}, u32[]{:S(2)}, u32[]{:S(2)}) collective-permute-start(bf16[16,128,128]{2,1,0:T(8,128)(2,1)S(1)} %collective-permute-done.6.refs_9_.refs_7_), channel_id=1, source_target_pairs={{0,4},{4,0},{8,12},{12,8},{1,5},{5,1},{9,13},{13,9},{2,6},{6,2},{1... | collective-permute-start | bytes 1572872 | tf_op jit(solution)/shard_map/ppermute | solution.py:28
  55.5 7.7 %collective-permute-start.10 = (bf16[32,512]{1,0:T(8,128)(2,1)S(1)}, bf16[32,512]{1,0:T(8,128)(2,1)S(1)}, u32[]{:S(2)}, u32[]{:S(2)}) collective-permute-start(bf16[32,512]{1,0:T(8,128)(2,1)S(1)} %get-tuple-element.42), channel_id=1, source_target_pairs={{0,1},{1,0},{2,3},{3,2},{4,5},{5,4},{6,7},{7,6},{8,9},{9,8},{10,11... | collective-permute-start | bytes 98312 | tf_op jit(solution)/shard_map/ppermute | solution.py:28
  57.2 6.0 %collective-permute-start.11 = (bf16[32,512]{1,0:T(8,128)(2,1)S(1)}, bf16[32,512]{1,0:T(8,128)(2,1)S(1)}, u32[]{:S(2)}, u32[]{:S(2)}) collective-permute-start(bf16[32,512]{1,0:T(8,128)(2,1)S(1)} %get-tuple-element.43), channel_id=1, source_target_pairs={{0,2},{1,3},{2,0},{3,1},{4,6},{5,7},{6,4},{7,5},{8,10},{9,11},{10,... | collective-permute-start | bytes 98312 | tf_op jit(solution)/shard_map/ppermute | solution.py:28
  59.0 5.7 %collective-permute-start.12 = (bf16[32,512]{1,0:T(8,128)(2,1)S(1)}, bf16[32,512]{1,0:T(8,128)(2,1)S(1)}, u32[]{:S(2)}, u32[]{:S(2)}) collective-permute-start(bf16[32,512]{1,0:T(8,128)(2,1)S(1)} %get-tuple-element.44), channel_id=1, source_target_pairs={{0,3},{1,2},{2,1},{3,0},{4,7},{5,6},{6,5},{7,4},{8,11},{9,10},{10,... | collective-permute-start | bytes 98312 | tf_op jit(solution)/shard_map/ppermute | solution.py:28
  66.7 3.9 %collective-permute-start.17 = (bf16[8,2176]{1,0:T(8,128)(2,1)S(1)}, bf16[8,2176]{1,0:T(8,128)(2,1)S(1)}, u32[]{:S(2)}, u32[]{:S(2)}) collective-permute-start(bf16[8,2176]{1,0:T(8,128)(2,1)S(1)} %head_products.1.refs_0_.refs_4_), channel_id=1, source_target_pairs={{0,12},{4,8},{8,4},{12,0},{1,13},{5,9},{9,5},{13,1},{2,14},{6,10},... | collective-permute-start | bytes 104456 | tf_op jit(solution)/shard_map/ppermute | solution.py:28
  66.7 4.3 %collective-permute-start.16 = (bf16[8,2176]{1,0:T(8,128)(2,1)S(1)}, bf16[8,2176]{1,0:T(8,128)(2,1)S(1)}, u32[]{:S(2)}, u32[]{:S(2)}) collective-permute-start(bf16[8,2176]{1,0:T(8,128)(2,1)S(1)} %head_products.1.refs_0_.refs_4_), channel_id=1, source_target_pairs={{0,8},{4,12},{8,0},{12,4},{1,9},{5,13},{9,1},{13,5},{2,10},{6,14},... | collective-permute-start | bytes 104456 | tf_op jit(solution)/shard_map/ppermute | solution.py:28
  71.8 7.6 %collective-permute-start.20 = (bf16[32,896]{1,0:T(8,128)(2,1)S(1)}, bf16[32,896]{1,0:T(8,128)(2,1)S(1)}, u32[]{:S(2)}, u32[]{:S(2)}) collective-permute-start(bf16[32,896]{1,0:T(8,128)(2,1)S(1)} %output_product.1.refs_1_.refs_0_), channel_id=1, source_target_pairs={{0,3},{1,2},{2,1},{3,0},{4,7},{5,6},{6,5},{7,4},{8,11},{9,10},{10,... | collective-permute-start | bytes 172040 | tf_op jit(solution)/shard_map/ppermute | solution.py:28
  73.3 6.8 %collective-permute-start.19 = (bf16[32,896]{1,0:T(8,128)(2,1)S(1)}, bf16[32,896]{1,0:T(8,128)(2,1)S(1)}, u32[]{:S(2)}, u32[]{:S(2)}) collective-permute-start(bf16[32,896]{1,0:T(8,128)(2,1)S(1)} %output_product.1.refs_1_.refs_0_), channel_id=1, source_target_pairs={{0,2},{1,3},{2,0},{3,1},{4,6},{5,7},{6,4},{7,5},{8,10},{9,11},{10,... | collective-permute-start | bytes 172040 | tf_op jit(solution)/shard_map/ppermute | solution.py:28
  73.3 6.8 %collective-permute-start.18 = (bf16[32,896]{1,0:T(8,128)(2,1)S(1)}, bf16[32,896]{1,0:T(8,128)(2,1)S(1)}, u32[]{:S(2)}, u32[]{:S(2)}) collective-permute-start(bf16[32,896]{1,0:T(8,128)(2,1)S(1)} %output_product.1.refs_1_.refs_0_), channel_id=1, source_target_pairs={{0,1},{1,0},{2,3},{3,2},{4,5},{5,4},{6,7},{7,6},{8,9},{9,8},{10,11... | collective-permute-start | bytes 172040 | tf_op jit(solution)/shard_map/ppermute | solution.py:28
  80.2 5.0 %collective-permute-start.23 = (bf16[4,8,896]{2,1,0:T(8,128)(2,1)S(1)}, bf16[4,8,896]{2,1,0:T(8,128)(2,1)S(1)}, u32[]{:S(2)}, u32[]{:S(2)}) collective-permute-start(bf16[4,8,896]{2,1,0:T(8,128)(2,1)S(1)} %mix.1.refs_1_.refs_0_), channel_id=1, source_target_pairs={{0,12},{4,8},{8,4},{12,0},{1,13},{5,9},{9,5},{13,1},{2,14},{6,10},... | collective-permute-start | bytes 172040 | tf_op jit(solution)/shard_map/ppermute | solution.py:28
  80.7 5.0 %collective-permute-start.22 = (bf16[4,8,896]{2,1,0:T(8,128)(2,1)S(1)}, bf16[4,8,896]{2,1,0:T(8,128)(2,1)S(1)}, u32[]{:S(2)}, u32[]{:S(2)}) collective-permute-start(bf16[4,8,896]{2,1,0:T(8,128)(2,1)S(1)} %mix.1.refs_1_.refs_0_), channel_id=1, source_target_pairs={{0,8},{4,12},{8,0},{12,4},{1,9},{5,13},{9,1},{13,5},{2,10},{6,14},... | collective-permute-start | bytes 172040 | tf_op jit(solution)/shard_map/ppermute | solution.py:28
  81.9 3.8 %collective-permute-start.21 = (bf16[4,8,896]{2,1,0:T(8,128)(2,1)S(1)}, bf16[4,8,896]{2,1,0:T(8,128)(2,1)S(1)}, u32[]{:S(2)}, u32[]{:S(2)}) collective-permute-start(bf16[4,8,896]{2,1,0:T(8,128)(2,1)S(1)} %mix.1.refs_1_.refs_0_), channel_id=1, source_target_pairs={{0,4},{4,0},{8,12},{12,8},{1,5},{5,1},{9,13},{13,9},{2,6},{6,2},{1... | collective-permute-start | bytes 172040 | tf_op jit(solution)/shard_map/ppermute | solution.py:28
  (5 other events, 119.7 us)

commit v8 on v7

--- a/solution.py
+++ b/solution.py
@@ -81,11 +81,14 @@
     return held
 
 
-def cut_kernel(sections, experts, piece, x_ref, query_ref, *refs):
-    out_refs, held = refs[-1 - experts : -1], refs[-1]
+def cut_kernel(sections, experts, piece, x_ref, query_ref, w_ref, *refs):
+    w_out_ref, *out_refs, w_held, held = refs
     rank = lax.axis_index("expert")
     steps, sources, heads, wide = query_ref.shape
     rows = x_ref.shape[0]
+    for target in range(experts):
+        w_held[target] = w_ref[:, target * piece : (target + 1) * piece]
+    w_out_ref[...] = w_held[rank]
     for target in range(experts):
         for section in range(sections):
             at = (section * experts + target) * piece
@@ -98,7 +101,7 @@
                 ref[at : at + heads, :wide] = query_ref[step, source]
 
 
-def cut_columns(x, queries, sections, experts, after):
+def cut_columns(x, queries, w_turned, sections, experts):
     rows, width = x.shape
     piece = width // (sections * experts)
     steps, sources, heads, wide = queries.shape
@@ -107,21 +110,21 @@
     )
     return pl.pallas_call(
         functools.partial(cut_kernel, sections, experts, piece),
-        out_shape=[block] * experts,
-        in_specs=[pl.BlockSpec(memory_space=pltpu.VMEM)] * 2
-        + [pl.BlockSpec(memory_space=pl.ANY)] * len(after),
-        scratch_shapes=[pltpu.VMEM((experts, sections * rows, piece), x.dtype)],
-        compiler_params=params(x, block, scale=6),
+        out_shape=[jax.ShapeDtypeStruct((w_turned.shape[0], piece), x.dtype)] + [block] * experts,
+        scratch_shapes=[
+            pltpu.VMEM((experts, w_turned.shape[0], piece), x.dtype),
+            pltpu.VMEM((experts, sections * rows, piece), x.dtype),
+        ],
+        compiler_params=params(x, block, w_turned, scale=6),
         name="cut_columns",
-    )(*at_home(x, queries), *after)
-
-
-def project_kernel(count, first, rows, experts, sections, *refs):
-    x_refs, (own_ref, *w_refs) = refs[:count], refs[count : count + 1 + sections]
-    out_refs, columns = refs[-1 - count : -1], refs[-1]
-    section_rank, rank = lax.axis_index("section"), lax.axis_index("expert")
-    width, piece = w_refs[0].shape
-    steps = own_ref.shape[0]
+    )(*at_home(x, queries, w_turned))
+
+
+def project_kernel(count, first, rows, *refs):
+    x_refs, rider_ref, w_refs, out_refs = refs[:count], refs[count], refs[count + 1 :], refs[-count:]
+    section_rank = lax.axis_index("section")
+    sections = lax.axis_size("section")
+    piece = w_refs[0].shape[1]
     total = 0
     for mask in range(sections):
         at = pl.ds(pl.multiple_of((section_rank ^ mask) * rows, rows), rows)
@@ -129,37 +132,22 @@
         total = total + lax.dot_general(
             x, w_refs[mask][...], (((1,), (1,)), ((), ())), preferred_element_type=jnp.float32
         )
-    own = jnp.concatenate([own_ref[step] for step in range(steps)], axis=0).astype(jnp.float32)
-    block = own.shape[0]
-    column = columns.shape[2]
-    for target in range(experts):
-        columns[target] = own[:, target * column : (target + 1) * column]
     for index, ref in enumerate(out_refs):
         ref[:rows, :] = total[index * rows : (index + 1) * rows].astype(ref.dtype)
-        value = columns[rank ^ (first + index)]
-        for line, at in enumerate(range(0, column, width)):
-            end = min(at + width, column)
-            to = rows + line * block
-            ref[to : to + block, : end - at] = value[:, at:end].astype(ref.dtype)
-
-
-def project(blocks, own, w_parts, first, rows, experts, after):
-    width = w_parts[0].shape[0]
-    column = own.shape[2] // experts
-    block = own.shape[0] * own.shape[1]
-    out = jax.ShapeDtypeStruct((rows + block * -(-column // width), width), jnp.bfloat16)
-    held = pl.BlockSpec(memory_space=pltpu.VMEM)
-    return pl.pallas_call(
-        functools.partial(
-            project_kernel, len(blocks), first, rows, experts, len(w_parts)
-        ),
+        ref[rows:, :] = rider_ref[first + index]
+
+
+def project(blocks, riders, w_parts, first, rows, after):
+    out = jax.ShapeDtypeStruct((rows + riders.shape[1], riders.shape[2]), jnp.bfloat16)
+    held = pl.BlockSpec(memory_space=pltpu.VMEM)
+    return pl.pallas_call(
+        functools.partial(project_kernel, len(blocks), first, rows),
         out_shape=[out] * len(blocks),
         in_specs=[held] * (len(blocks) + 1 + len(w_parts))
         + [pl.BlockSpec(memory_space=pl.ANY)] * len(after),
-        scratch_shapes=[pltpu.VMEM((experts, block, column), jnp.float32)],
         compiler_params=params(*blocks, *w_parts, scale=6),
         name="project",
-    )(*blocks, *at_home(own), *w_parts, *after)
+    )(*blocks, riders, *w_parts, *after)
 
 
 def query_kernel(
@@ -168,7 +156,7 @@
     f32, bf16 = jnp.float32, jnp.bfloat16
     table_ref, query_refs = refs[0], refs[1 : 1 + experts]
     uk_ref, own_ref, gain_ref, wt_ref = refs[1 + experts : 5 + experts]
-    out_ref, token_ref, picked, ropes, made, normed, query_ref = refs[-7:]
+    out_ref, rider_ref, token_ref, picked, ropes, made, normed, query_ref, columns = refs[-9:]
     token_ref[...] = jnp.zeros_like(token_ref)
     steps, sources, heads, wide = shape
     rope = wide - nope
@@ -212,6 +200,16 @@
         ropes[...], jnp.where(pair, 1.0, 0.0).astype(bf16), preferred_element_type=f32
     )
     own = jnp.concatenate([own_ref[step] for step in range(steps)], axis=0).astype(f32)
+    lines, column = columns.shape[1:]
+    for target in range(experts):
+        columns[target] = own[:, target * column : (target + 1) * column]
+    for mask in range(experts):
+        value = columns[rank ^ mask]
+        for line, at in enumerate(range(0, column, rider_ref.shape[2])):
+            end = min(at + rider_ref.shape[2], column)
+            rider_ref[mask, line * lines : (line + 1) * lines, : end - at] = value[
+                :, at:end
+            ].astype(bf16)
     scale = lax.rsqrt(jnp.mean(own * own, axis=-1, keepdims=True) + epsilon)
     own = (own * scale * gain_ref[...][None].astype(f32)).astype(bf16)
     depth = wt_ref.shape[1]
@@ -238,11 +236,13 @@
             out_ref[index, block:, :] = lines
 
 
-def absorb_queries(table, queries, shape, w_uk, own, gain, w_turned, prompts, sections, after):
+def absorb_queries(table, queries, shape, w_uk, own, gain, w_turned, prompts, sections):
     experts = len(queries)
     steps, sources, heads, wide = shape
     _, nope, chunk = w_uk.shape
     width = chunk + (wide - nope) // experts
+    block, column = own.shape[0] * own.shape[1], own.shape[2] // experts
+    cache_width = w_turned.shape[0]
     rows = prompts * steps * heads + steps * experts
     count = experts * sources * steps * heads
     held = pl.BlockSpec(memory_space=pltpu.VMEM)
@@ -250,12 +250,14 @@
         functools.partial(query_kernel, experts, sections, prompts, nope, shape),
         out_shape=[
             jax.ShapeDtypeStruct((experts * sections, rows, width), jnp.bfloat16),
+            jax.ShapeDtypeStruct(
+                (experts, block * -(-column // cache_width), cache_width), jnp.bfloat16
+            ),
             jax.ShapeDtypeStruct((8, 128), jnp.bfloat16),
         ],
         in_specs=[pl.BlockSpec(memory_space=pltpu.SMEM)]
-        + [held] * (experts + 4)
-        + [pl.BlockSpec(memory_space=pl.ANY)] * len(after),
-        out_specs=[held] * 2,
+        + [held] * (experts + 4),
+        out_specs=[held] * 3,
         scratch_shapes=[
             pltpu.VMEM((count, nope), jnp.float32),
             pltpu.VMEM((count, wide - nope), jnp.bfloat16),
@@ -264,10 +266,11 @@
                 (sections, own.shape[0] * own.shape[1], w_turned.shape[1]), jnp.bfloat16
             ),
             pltpu.VMEM((experts,) + shape, jnp.bfloat16),
+            pltpu.VMEM((experts, block, column), jnp.float32),
         ],
         compiler_params=params(*queries, w_uk, own, w_turned, scale=4),
         name="absorb_queries",
-    )(*at_home(table), *queries, *at_home(w_uk, own, gain, w_turned), *after)
+    )(*at_home(table), *queries, *at_home(w_uk, own, gain, w_turned))
 
 
 def turn(values, cosine, sine):
@@ -679,32 +682,28 @@
     sections = lax.axis_size("section")
     prompt_count, full_length, width = prompts.shape
     steps, tokens_here, heads, _ = queries.shape
-    depth = w_dkv.shape[0]
-    piece = depth // experts
     latent = kv_gain.shape[0]
     cache_width = w_dkv.shape[1]
     rows = prompt_count * full_length
     own_rows = steps * tokens_here
 
     w_turned = w_dkv.T
-    w_piece = lax.dynamic_slice_in_dim(w_turned, expert_rank * piece, piece, 1)
+    w_piece, *cut = cut_columns(
+        prompts.reshape(rows, width), queries, w_turned, sections, experts
+    )
+    w_parts = spread(w_piece, "section")
+    cut = deliver(cut, "expert")
+
+    blocks, riders, token = absorb_queries(
+        owners, cut, queries.shape, w_uk, residual, attn_gain, w_turned, prompt_count, sections
+    )
+    blocks = lax.all_to_all(blocks, ("expert", "section"), 0, 0, tiled=True)
+    w_uv, token = lax.optimization_barrier((w_uv, token))
     masks = [1 << bit for bit in range(experts.bit_length() - 1)]
     uv_parts = doubled({0: w_uv}, "expert", masks[1:])
-    w_parts = spread(w_piece, "section")
-    cut = cut_columns(
-        prompts.reshape(rows, width), queries, sections, experts,
-        [],
-    )
-    cut = deliver(cut, "expert")
-
-    blocks, token = absorb_queries(
-        owners, cut, queries.shape, w_uk, residual, attn_gain, w_turned, prompt_count, sections,
-        [uv_parts[masks[-1]]],
-    )
-    blocks = lax.all_to_all(blocks, ("expert", "section"), 0, 0, tiled=True)
-
-    away = list(project(cut[1:], residual, w_parts, 1, rows, experts, [token]))
-    near = list(project(cut[:1], residual, w_parts, 0, rows, experts, away[:1]))
+
+    away = list(project(cut[1:], riders, w_parts, 1, rows, [token]))
+    near = list(project(cut[:1], riders, w_parts, 0, rows, away[:1]))
     parts = deliver(near + away, "expert")
     table = rotation(full_length + steps + -(full_length + steps) % 8, cache_width - latent)
     gathered = list(gather_queries(

time: 104 us -> 120 us (1.15)
  waiting for transfers between devices: 25.5 us -> 45.3 us
  starting transfers between devices: 32.7 us -> 30.7 us
    ppermute x24, waiting for transfers between devices: 19.9 us -> 45.3 us  [swap(): return lax.ppermute(block, axis, [(i, i ^ mask) for i in range(size)])]
    all_to_all x1, waiting for transfers between devices: 5.59 us -> 0.01 us  [local(): blocks = lax.all_to_all(blocks, ('expert', 'section'), 0, 0, tiled=True)]
    pallas_call x2, Pallas kernels: 3.7 us -> 2.02 us  [project(): pl.pallas_call(functools.partial(project_kernel, len(blocks), first, rows...]
    all_to_all x1, starting transfers between devices: 6.62 us -> 4.98 us  [local(): blocks = lax.all_to_all(blocks, ('expert', 'section'), 0, 0, tiled=True)]
  transfers between devices with their start and end apart: 25 -> 25, of which waited for: 8 -> 10; matrix products, arithmetic and copies ran while one was open for 1% -> 0% of each run, Pallas kernels for 20% -> 14%
where the time goes in v8:
time: 120 us
  waiting for transfers between devices  45.3 us (38%)
  starting transfers between devices  30.7 us (26%)
  Pallas kernels  29.8 us (25%)
  blocking collectives  12.7 us (11%)
    ppermute x24, waiting for transfers between devices, swap(): return lax.ppermute(block, axis, [(i, i ^ mask) for i in range(size)])  45.3 us
    ppermute x24, starting transfers between devices, swap(): return lax.ppermute(block, axis, [(i, i ^ mask) for i in range(size)])  25.7 us
    all_to_all x1, blocking collectives, local(): blocks = lax.all_to_all(blocks, ('expert', 'section'), 0, 0, tiled=True)  12.7 us
    pallas_call x4, Pallas kernels, fetch(): pl.pallas_call(functools.partial(fetch_kernel, len(arrays)), out_shape=[p...  11.3 us
    all_to_all x1, starting transfers between devices, local(): blocks = lax.all_to_all(blocks, ('expert', 'section'), 0, 0, tiled=True)  4.98 us
    pallas_call x1, Pallas kernels, run_experts(): pl.pallas_call(functools.partial(expert_kernel, experts, sections, picks)...  4.96 us
    pallas_call x1, Pallas kernels, cut_columns(): pl.pallas_call(functools.partial(cut_kernel, sections, experts, piece), o...  2.5 us
  transfers between devices with their start and end apart: 25, of which 10 were waited for; matrix products, arithmetic and copies ran while one was open for 0% of the time, Pallas kernels for 14%

profile of v8, /device:TPU:0, one launch (start us, length us, event | category | flops | bytes accessed | tf_op | source)
XLA Modules:
  0.0 119.5 jit_solution(6982232678332061958)
XLA Ops:
  0.0 2.5 %cut_columns.1 = (bf16[576,224]{1,0:T(8,128)(2,1)S(1)}, bf16[640,224]{1,0:T(8,128)(2,1)S(1)}, bf16[640,224]{1,0:T(8,128)(2,1)S(1)}, bf16[640,224]{1,0:T(8,128)(2,1)S(1)}, bf16[640,224]{1,0:T(8,128)(2,1)S(1)}) custom-call(bf16[128,3584]{1,0:T(8,128)(2,1)} %bitcast.5, bf16[2,4,16,192]{3,2,1,0:T(8,128)(2,1)} %query_ref.1, bf16[576,896]{1,0:T(8,128)(2,1)} %bitcast.3), custom_call_target="tpu_custom_call" | custom-call | tf_op jit(solution)/shard_map/cut_columns/pallas_call | solution.py:111
  3.0 2.6 %collective-permute-start.1 = (bf16[640,224]{1,0:T(8,128)(2,1)S(1)}, bf16[640,224]{1,0:T(8,128)(2,1)S(1)}, u32[]{:S(2)}, u32[]{:S(2)}) collective-permute-start(bf16[640,224]{1,0:T(8,128)(2,1)S(1)} %get-tuple-element.34), channel_id=1, source_target_pairs={{0,8},{4,12},{8,0},{12,4},{1,9},{5,13},{9,1},{13,5},{2,10},{6,14},... | collective-permute-start | bytes 860168 | tf_op jit(solution)/shard_map/ppermute | solution.py:28
  5.7 8.5 %collective-permute-done.1.refs_3_.refs_1_ = bf16[640,224]{1,0:T(8,128)(2,1)S(1)} collective-permute-done((bf16[640,224]{1,0:T(8,128)(2,1)S(1)}, bf16[640,224]{1,0:T(8,128)(2,1)S(1)}, u32[]{:S(2)}, u32[]{:S(2)}) %collective-permute-start.1) | collective-permute-done | bytes 286752 | tf_op jit(solution)/shard_map/ppermute | solution.py:28
  14.2 6.5 %collective-permute-done.2.refs_4_.refs_2_ = bf16[640,224]{1,0:T(8,128)(2,1)S(1)} collective-permute-done((bf16[640,224]{1,0:T(8,128)(2,1)S(1)}, bf16[640,224]{1,0:T(8,128)(2,1)S(1)}, u32[]{:S(2)}, u32[]{:S(2)}) %collective-permute-start.2) | collective-permute-done | bytes 286752 | tf_op jit(solution)/shard_map/ppermute | solution.py:28
  20.7 2.2 %absorb_queries.1 = (bf16[16,40,144]{2,1,0:T(8,128)(2,1)S(1)}, bf16[4,16,576]{2,1,0:T(8,128)(2,1)S(1)}, bf16[8,128]{1,0:T(8,128)(2,1)S(1)}) custom-call(s32[16]{0:T(128)} %refs_0_.8, bf16[640,224]{1,0:T(8,128)(2,1)S(1)} %get-tuple-element.32.refs_1_.refs_0_, bf16[640,224]{1,0:T(8,128)(2,1)S(1)} %collective-permute-done.refs_2_.refs_0_, ...), custom_call_target="tpu_custom_call" | custom-call | tf_op jit(solution)/shard_map/absorb_queries/pallas_call | solution.py:249
  23.6 1.6 %collective-permute-start.12 = (bf16[16,128,128]{2,1,0:T(8,128)(2,1)}, bf16[16,128,128]{2,1,0:T(8,128)(2,1)}, u32[]{:S(2)}, u32[]{:S(2)}) collective-permute-start(bf16[16,128,128]{2,1,0:T(8,128)(2,1)} %refs_5_.4), channel_id=1, source_target_pairs={{0,8},{4,12},{8,0},{12,4},{1,9},{5,13},{9,1},{13,5},{2,10},{6,14},... | collective-permute-start | bytes 1572872 | tf_op jit(solution)/shard_map/ppermute | solution.py:28
  25.1 3.6 %collective-permute-start.5 = (bf16[576,224]{1,0:T(8,128)(2,1)S(1)}, bf16[576,224]{1,0:T(8,128)(2,1)S(1)}, u32[]{:S(2)}, u32[]{:S(2)}) collective-permute-start(bf16[576,224]{1,0:T(8,128)(2,1)S(1)} %get-tuple-element.37.refs_4_.refs_2_), channel_id=1, source_target_pairs={{0,3},{1,2},{2,1},{3,0},{4,7},{5,6},{6,5},{7,4},{8,11},{9,10},{10,... | collective-permute-start | bytes 774152 | tf_op jit(solution)/shard_map/ppermute | solution.py:28
  29.5 5.0 %all-to-all-start = ((bf16[16,40,144]{2,1,0:T(8,128)(2,1)}), bf16[16,40,144]{2,1,0:T(8,128)(2,1)S(1)}, u32[]{:S(2)}, u32[]{:S(2)}) async-start(bf16[16,40,144]{2,1,0:T(8,128)(2,1)} %copy-done.1), calls=%async_computation | async-start | bytes 655360 | tf_op jit(solution)/shard_map/all_to_all | solution.py:700
  34.5 2.4 %collective-permute-done.5.refs_7_.refs_5_ = bf16[576,224]{1,0:T(8,128)(2,1)S(1)} collective-permute-done((bf16[576,224]{1,0:T(8,128)(2,1)S(1)}, bf16[576,224]{1,0:T(8,128)(2,1)S(1)}, u32[]{:S(2)}, u32[]{:S(2)}) %collective-permute-start.5) | collective-permute-done | bytes 258080 | tf_op jit(solution)/shard_map/ppermute | solution.py:28
  37.0 21.5 %collective-permute-done.4.refs_6_.refs_4_ = bf16[576,224]{1,0:T(8,128)(2,1)S(1)} collective-permute-done((bf16[576,224]{1,0:T(8,128)(2,1)S(1)}, bf16[576,224]{1,0:T(8,128)(2,1)S(1)}, u32[]{:S(2)}, u32[]{:S(2)}) %collective-permute-start.4) | collective-permute-done | bytes 258080 | tf_op jit(solution)/shard_map/ppermute | solution.py:28
  60.5 1.6 %collective-permute-start.6 = (bf16[144,576]{1,0:T(8,128)(2,1)}, bf16[144,576]{1,0:T(8,128)(2,1)S(1)}, u32[]{:S(2)}, u32[]{:S(2)}) collective-permute-start(bf16[144,576]{1,0:T(8,128)(2,1)} %get-tuple-element.40.refs_6_), channel_id=1, source_target_pairs={{0,4},{4,0},{8,12},{12,8},{1,5},{5,1},{9,13},{13,9},{2,6},{6,2},{1... | collective-permute-start | bytes 497672 | tf_op jit(solution)/shard_map/ppermute | solution.py:28
  63.8 3.9 %collective-permute-done.7.refs_2_.refs_6_ = bf16[144,576]{1,0:T(8,128)(2,1)S(1)} collective-permute-done((bf16[144,576]{1,0:T(8,128)(2,1)}, bf16[144,576]{1,0:T(8,128)(2,1)S(1)}, u32[]{:S(2)}, u32[]{:S(2)}) %collective-permute-start.7) | collective-permute-done | bytes 165920 | tf_op jit(solution)/shard_map/ppermute | solution.py:28
  67.9 1.8 %attend.1 = (bf16[32,512]{1,0:T(8,128)(2,1)S(1)}, bf16[32,512]{1,0:T(8,128)(2,1)S(1)}, bf16[32,512]{1,0:T(8,128)(2,1)S(1)}, bf16[32,512]{1,0:T(8,128)(2,1)S(1)}, bf16[8,128]{1,0:T(8,128)(2,1)S(1)}) custom-call(bf16[144,576]{1,0:T(8,128)(2,1)S(1)} %project.3.refs_0_.refs_4_, bf16[144,576]{1,0:T(8,128)(2,1)S(1)} %collective-permute-done.6.refs_1_.refs_5_, ...), custom_call_target="tpu_custom_call" | custom-call | tf_op jit(solution)/shard_map/attend/pallas_call | solution.py:419
  69.7 1.7 %collective-permute-start.13 = (bf16[16,128,128]{2,1,0:T(8,128)(2,1)S(1)}, bf16[16,128,128]{2,1,0:T(8,128)(2,1)S(1)}, u32[]{:S(2)}, u32[]{:S(2)}) collective-permute-start(bf16[16,128,128]{2,1,0:T(8,128)(2,1)S(1)} %copy-done), channel_id=1, source_target_pairs={{0,4},{4,0},{8,12},{12,8},{1,5},{5,1},{9,13},{13,9},{2,6},{6,2},{1... | collective-permute-start | bytes 1572872 | tf_op jit(solution)/shard_map/ppermute | solution.py:28
  71.5 3.1 %collective-permute-start.10 = (bf16[32,512]{1,0:T(8,128)(2,1)S(1)}, bf16[32,512]{1,0:T(8,128)(2,1)S(1)}, u32[]{:S(2)}, u32[]{:S(2)}) collective-permute-start(bf16[32,512]{1,0:T(8,128)(2,1)S(1)} %get-tuple-element.50), channel_id=1, source_target_pairs={{0,2},{1,3},{2,0},{3,1},{4,6},{5,7},{6,4},{7,5},{8,10},{9,11},{10,... | collective-permute-start | bytes 98312 | tf_op jit(solution)/shard_map/ppermute | solution.py:28
  76.0 3.1 %fetch.4.refs_10_.refs_9_ = bf16[4,3584,256]{2,1,0:T(8,128)(2,1)S(1)} custom-call(bf16[4,3584,256]{2,1,0:T(8,128)(2,1)} %refs_0_.7, bf16[8,128]{1,0:T(8,128)(2,1)S(1)} %get-tuple-element.56.refs_1_.refs_11_), custom_call_target="tpu_custom_call" | custom-call | bytes 14680064 | tf_op jit(solution)/shard_map/fetch/pallas_call | solution.py:63
  80.3 2.4 %head_products.1.refs_0_.refs_4_ = bf16[8,2176]{1,0:T(8,128)(2,1)S(1)} custom-call(s32[16]{0:T(128)} %refs_0_.8, bf16[32,512]{1,0:T(8,128)(2,1)S(1)} %get-tuple-element.48.refs_1_, bf16[32,512]{1,0:T(8,128)(2,1)S(1)} %collective-permute-done.9.refs_2_, bf16[32,512]{1,0:T(8,128)(2,1)S(1)} %collective-permute-done.10.refs_3_, ...), custom_call_target="tpu_custom_call" | custom-call | tf_op jit(solution)/shard_map/head_products/pallas_call | solution.py:489
  84.6 2.0 %fetch.5.refs_4_ = bf16[2048,896]{1,0:T(8,128)(2,1)S(1)} custom-call(bf16[2048,896]{1,0:T(8,128)(2,1)} %refs_0_.9), custom_call_target="tpu_custom_call" | custom-call | bytes 7340032 | tf_op jit(solution)/shard_map/fetch/pallas_call | solution.py:63
  87.6 1.6 %collective-permute-start.20 = (bf16[32,896]{1,0:T(8,128)(2,1)S(1)}, bf16[32,896]{1,0:T(8,128)(2,1)S(1)}, u32[]{:S(2)}, u32[]{:S(2)}) collective-permute-start(bf16[32,896]{1,0:T(8,128)(2,1)S(1)} %output_product.1.refs_1_.refs_0_), channel_id=1, source_target_pairs={{0,3},{1,2},{2,1},{3,0},{4,7},{5,6},{6,5},{7,4},{8,11},{9,10},{10,... | collective-permute-start | bytes 172040 | tf_op jit(solution)/shard_map/ppermute | solution.py:28
  89.1 2.9 %collective-permute-start.18 = (bf16[32,896]{1,0:T(8,128)(2,1)S(1)}, bf16[32,896]{1,0:T(8,128)(2,1)S(1)}, u32[]{:S(2)}, u32[]{:S(2)}) collective-permute-start(bf16[32,896]{1,0:T(8,128)(2,1)S(1)} %output_product.1.refs_1_.refs_0_), channel_id=1, source_target_pairs={{0,1},{1,0},{2,3},{3,2},{4,5},{5,4},{6,7},{7,6},{8,9},{9,8},{10,11... | collective-permute-start | bytes 172040 | tf_op jit(solution)/shard_map/ppermute | solution.py:28
  92.0 3.1 %fetch.6.refs_8_.refs_10_ = bf16[4,3584,256]{2,1,0:T(8,128)(2,1)S(1)} custom-call(bf16[4,3584,256]{2,1,0:T(8,128)(2,1)} %refs_0_.10, bf16[32,896]{1,0:T(8,128)(2,1)S(1)} %output_product.1.refs_1_.refs_0_), custom_call_target="tpu_custom_call" | custom-call | bytes 14680064 | tf_op jit(solution)/shard_map/fetch/pallas_call | solution.py:63
  97.7 3.1 %fetch.7.refs_11_ = bf16[4,256,3584]{2,1,0:T(8,128)(2,1)S(1)} custom-call(bf16[4,256,3584]{2,1,0:T(8,128)(2,1)} %refs_0_.11, bf16[4,8,896]{2,1,0:T(8,128)(2,1)S(1)} %mix.1.refs_1_.refs_0_), custom_call_target="tpu_custom_call" | custom-call | bytes 14680064 | tf_op jit(solution)/shard_map/fetch/pallas_call | solution.py:63
  101.2 5.0 %run_experts.1 = (bf16[16,8,896]{2,1,0:T(8,128)(2,1)S(1)}, bf16[4,8,896]{2,1,0:T(8,128)(2,1)S(1)}) custom-call(bf16[4,8,896]{2,1,0:T(8,128)(2,1)S(1)} %mix.1.refs_1_.refs_0_, bf16[4,8,896]{2,1,0:T(8,128)(2,1)S(1)} %collective-permute-done.21.refs_1_, bf16[4,8,896]{2,1,0:T(8,128)(2,1)S(1)} %collective-permute-done.22.refs_2_, ...), custom_call_target="tpu_custom_call" | custom-call | tf_op jit(solution)/shard_map/run_experts/pallas_call | solution.py:622
  106.2 12.7 %all_to_all.10.block_ref = bf16[16,8,896]{2,1,0:T(8,128)(2,1)S(1)} all-to-all(bf16[16,8,896]{2,1,0:T(8,128)(2,1)S(1)} %get-tuple-element.57), channel_id=1, replica_groups=mesh['groups'=2,'expert'=4,'section'=4] {'expert','section'}, dimensions={0} | all-to-all | bytes 458752 | tf_op jit(solution)/shard_map/all_to_all | solution.py:748
  (54 shorter events, 15.3 us)
Async XLA Ops:
  3.0 11.1 %collective-permute-start.1 = (bf16[640,224]{1,0:T(8,128)(2,1)S(1)}, bf16[640,224]{1,0:T(8,128)(2,1)S(1)}, u32[]{:S(2)}, u32[]{:S(2)}) collective-permute-start(bf16[640,224]{1,0:T(8,128)(2,1)S(1)} %get-tuple-element.34), channel_id=1, source_target_pairs={{0,8},{4,12},{8,0},{12,4},{1,9},{5,13},{9,1},{13,5},{2,10},{6,14},... | collective-permute-start | bytes 860168 | tf_op jit(solution)/shard_map/ppermute | solution.py:28
  5.6 15.1 %collective-permute-start.2 = (bf16[640,224]{1,0:T(8,128)(2,1)S(1)}, bf16[640,224]{1,0:T(8,128)(2,1)S(1)}, u32[]{:S(2)}, u32[]{:S(2)}) collective-permute-start(bf16[640,224]{1,0:T(8,128)(2,1)S(1)} %get-tuple-element.35), channel_id=1, source_target_pairs={{0,12},{4,8},{8,4},{12,0},{1,13},{5,9},{9,5},{13,1},{2,14},{6,10},... | collective-permute-start | bytes 860168 | tf_op jit(solution)/shard_map/ppermute | solution.py:28
  23.6 46.1 %collective-permute-start.12 = (bf16[16,128,128]{2,1,0:T(8,128)(2,1)}, bf16[16,128,128]{2,1,0:T(8,128)(2,1)}, u32[]{:S(2)}, u32[]{:S(2)}) collective-permute-start(bf16[16,128,128]{2,1,0:T(8,128)(2,1)} %refs_5_.4), channel_id=1, source_target_pairs={{0,8},{4,12},{8,0},{12,4},{1,9},{5,13},{9,1},{13,5},{2,10},{6,14},... | collective-permute-start | bytes 1572872 | tf_op jit(solution)/shard_map/ppermute | solution.py:28
  25.1 11.8 %collective-permute-start.5 = (bf16[576,224]{1,0:T(8,128)(2,1)S(1)}, bf16[576,224]{1,0:T(8,128)(2,1)S(1)}, u32[]{:S(2)}, u32[]{:S(2)}) collective-permute-start(bf16[576,224]{1,0:T(8,128)(2,1)S(1)} %get-tuple-element.37.refs_4_.refs_2_), channel_id=1, source_target_pairs={{0,3},{1,2},{2,1},{3,0},{4,7},{5,6},{6,5},{7,4},{8,11},{9,10},{10,... | collective-permute-start | bytes 774152 | tf_op jit(solution)/shard_map/ppermute | solution.py:28
  28.7 29.7 %collective-permute-start.4 = (bf16[576,224]{1,0:T(8,128)(2,1)S(1)}, bf16[576,224]{1,0:T(8,128)(2,1)S(1)}, u32[]{:S(2)}, u32[]{:S(2)}) collective-permute-start(bf16[576,224]{1,0:T(8,128)(2,1)S(1)} %get-tuple-element.37.refs_4_.refs_2_), channel_id=1, source_target_pairs={{0,2},{1,3},{2,0},{3,1},{4,6},{5,7},{6,4},{7,5},{8,10},{9,11},{10,... | collective-permute-start | bytes 774152 | tf_op jit(solution)/shard_map/ppermute | solution.py:28
  28.7 29.7 %collective-permute-start.3 = (bf16[576,224]{1,0:T(8,128)(2,1)S(1)}, bf16[576,224]{1,0:T(8,128)(2,1)S(1)}, u32[]{:S(2)}, u32[]{:S(2)}) collective-permute-start(bf16[576,224]{1,0:T(8,128)(2,1)S(1)} %get-tuple-element.37.refs_4_.refs_2_), channel_id=1, source_target_pairs={{0,1},{1,0},{2,3},{3,2},{4,5},{5,4},{6,7},{7,6},{8,9},{9,8},{10,11... | collective-permute-start | bytes 774152 | tf_op jit(solution)/shard_map/ppermute | solution.py:28
  29.5 33.1 %all-to-all-start = ((bf16[16,40,144]{2,1,0:T(8,128)(2,1)}), bf16[16,40,144]{2,1,0:T(8,128)(2,1)S(1)}, u32[]{:S(2)}, u32[]{:S(2)}) async-start(bf16[16,40,144]{2,1,0:T(8,128)(2,1)} %copy-done.1), calls=%async_computation | async-start | bytes 655360 | tf_op jit(solution)/shard_map/all_to_all | solution.py:700
  60.0 7.7 %collective-permute-start.7 = (bf16[144,576]{1,0:T(8,128)(2,1)}, bf16[144,576]{1,0:T(8,128)(2,1)S(1)}, u32[]{:S(2)}, u32[]{:S(2)}) collective-permute-start(bf16[144,576]{1,0:T(8,128)(2,1)} %get-tuple-element.41), channel_id=1, source_target_pairs={{0,8},{4,12},{8,0},{12,4},{1,9},{5,13},{9,1},{13,5},{2,10},{6,14},... | collective-permute-start | bytes 497672 | tf_op jit(solution)/shard_map/ppermute | solution.py:28
  60.5 7.3 %collective-permute-start.8 = (bf16[144,576]{1,0:T(8,128)(2,1)}, bf16[144,576]{1,0:T(8,128)(2,1)S(1)}, u32[]{:S(2)}, u32[]{:S(2)}) collective-permute-start(bf16[144,576]{1,0:T(8,128)(2,1)} %get-tuple-element.42), channel_id=1, source_target_pairs={{0,12},{4,8},{8,4},{12,0},{1,13},{5,9},{9,5},{13,1},{2,14},{6,10},... | collective-permute-start | bytes 497672 | tf_op jit(solution)/shard_map/ppermute | solution.py:28
  60.5 7.3 %collective-permute-start.6 = (bf16[144,576]{1,0:T(8,128)(2,1)}, bf16[144,576]{1,0:T(8,128)(2,1)S(1)}, u32[]{:S(2)}, u32[]{:S(2)}) collective-permute-start(bf16[144,576]{1,0:T(8,128)(2,1)} %get-tuple-element.40.refs_6_), channel_id=1, source_target_pairs={{0,4},{4,0},{8,12},{12,8},{1,5},{5,1},{9,13},{13,9},{2,6},{6,2},{1... | collective-permute-start | bytes 497672 | tf_op jit(solution)/shard_map/ppermute | solution.py:28
  69.7 10.6 %collective-permute-start.13 = (bf16[16,128,128]{2,1,0:T(8,128)(2,1)S(1)}, bf16[16,128,128]{2,1,0:T(8,128)(2,1)S(1)}, u32[]{:S(2)}, u32[]{:S(2)}) collective-permute-start(bf16[16,128,128]{2,1,0:T(8,128)(2,1)S(1)} %copy-done), channel_id=1, source_target_pairs={{0,4},{4,0},{8,12},{12,8},{1,5},{5,1},{9,13},{13,9},{2,6},{6,2},{1... | collective-permute-start | bytes 1572872 | tf_op jit(solution)/shard_map/ppermute | solution.py:28
  71.4 9.0 %collective-permute-start.14 = (bf16[16,128,128]{2,1,0:T(8,128)(2,1)}, bf16[16,128,128]{2,1,0:T(8,128)(2,1)S(1)}, u32[]{:S(2)}, u32[]{:S(2)}) collective-permute-start(bf16[16,128,128]{2,1,0:T(8,128)(2,1)} %collective-permute-done.12.refs_7_), channel_id=1, source_target_pairs={{0,4},{4,0},{8,12},{12,8},{1,5},{5,1},{9,13},{13,9},{2,6},{6,2},{1... | collective-permute-start | bytes 1572872 | tf_op jit(solution)/shard_map/ppermute | solution.py:28
  71.5 7.6 %collective-permute-start.9 = (bf16[32,512]{1,0:T(8,128)(2,1)S(1)}, bf16[32,512]{1,0:T(8,128)(2,1)S(1)}, u32[]{:S(2)}, u32[]{:S(2)}) collective-permute-start(bf16[32,512]{1,0:T(8,128)(2,1)S(1)} %get-tuple-element.49), channel_id=1, source_target_pairs={{0,1},{1,0},{2,3},{3,2},{4,5},{5,4},{6,7},{7,6},{8,9},{9,8},{10,11... | collective-permute-start | bytes 98312 | tf_op jit(solution)/shard_map/ppermute | solution.py:28
  71.5 7.6 %collective-permute-start.10 = (bf16[32,512]{1,0:T(8,128)(2,1)S(1)}, bf16[32,512]{1,0:T(8,128)(2,1)S(1)}, u32[]{:S(2)}, u32[]{:S(2)}) collective-permute-start(bf16[32,512]{1,0:T(8,128)(2,1)S(1)} %get-tuple-element.50), channel_id=1, source_target_pairs={{0,2},{1,3},{2,0},{3,1},{4,6},{5,7},{6,4},{7,5},{8,10},{9,11},{10,... | collective-permute-start | bytes 98312 | tf_op jit(solution)/shard_map/ppermute | solution.py:28
  74.6 5.7 %collective-permute-start.11 = (bf16[32,512]{1,0:T(8,128)(2,1)S(1)}, bf16[32,512]{1,0:T(8,128)(2,1)S(1)}, u32[]{:S(2)}, u32[]{:S(2)}) collective-permute-start(bf16[32,512]{1,0:T(8,128)(2,1)S(1)} %get-tuple-element.51), channel_id=1, source_target_pairs={{0,3},{1,2},{2,1},{3,0},{4,7},{5,6},{6,5},{7,4},{8,11},{9,10},{10,... | collective-permute-start | bytes 98312 | tf_op jit(solution)/shard_map/ppermute | solution.py:28
  82.7 3.9 %collective-permute-start.17 = (bf16[8,2176]{1,0:T(8,128)(2,1)S(1)}, bf16[8,2176]{1,0:T(8,128)(2,1)S(1)}, u32[]{:S(2)}, u32[]{:S(2)}) collective-permute-start(bf16[8,2176]{1,0:T(8,128)(2,1)S(1)} %head_products.1.refs_0_.refs_4_), channel_id=1, source_target_pairs={{0,12},{4,8},{8,4},{12,0},{1,13},{5,9},{9,5},{13,1},{2,14},{6,10},... | collective-permute-start | bytes 104456 | tf_op jit(solution)/shard_map/ppermute | solution.py:28
  82.7 4.1 %collective-permute-start.16 = (bf16[8,2176]{1,0:T(8,128)(2,1)S(1)}, bf16[8,2176]{1,0:T(8,128)(2,1)S(1)}, u32[]{:S(2)}, u32[]{:S(2)}) collective-permute-start(bf16[8,2176]{1,0:T(8,128)(2,1)S(1)} %head_products.1.refs_0_.refs_4_), channel_id=1, source_target_pairs={{0,8},{4,12},{8,0},{12,4},{1,9},{5,13},{9,1},{13,5},{2,10},{6,14},... | collective-permute-start | bytes 104456 | tf_op jit(solution)/shard_map/ppermute | solution.py:28
  83.3 3.5 %collective-permute-start.15 = (bf16[8,2176]{1,0:T(8,128)(2,1)S(1)}, bf16[8,2176]{1,0:T(8,128)(2,1)S(1)}, u32[]{:S(2)}, u32[]{:S(2)}) collective-permute-start(bf16[8,2176]{1,0:T(8,128)(2,1)S(1)} %head_products.1.refs_0_.refs_4_), channel_id=1, source_target_pairs={{0,4},{4,0},{8,12},{12,8},{1,5},{5,1},{9,13},{13,9},{2,6},{6,2},{1... | collective-permute-start | bytes 104456 | tf_op jit(solution)/shard_map/ppermute | solution.py:28
  87.6 7.6 %collective-permute-start.20 = (bf16[32,896]{1,0:T(8,128)(2,1)S(1)}, bf16[32,896]{1,0:T(8,128)(2,1)S(1)}, u32[]{:S(2)}, u32[]{:S(2)}) collective-permute-start(bf16[32,896]{1,0:T(8,128)(2,1)S(1)} %output_product.1.refs_1_.refs_0_), channel_id=1, source_target_pairs={{0,3},{1,2},{2,1},{3,0},{4,7},{5,6},{6,5},{7,4},{8,11},{9,10},{10,... | collective-permute-start | bytes 172040 | tf_op jit(solution)/shard_map/ppermute | solution.py:28
  89.1 6.5 %collective-permute-start.19 = (bf16[32,896]{1,0:T(8,128)(2,1)S(1)}, bf16[32,896]{1,0:T(8,128)(2,1)S(1)}, u32[]{:S(2)}, u32[]{:S(2)}) collective-permute-start(bf16[32,896]{1,0:T(8,128)(2,1)S(1)} %output_product.1.refs_1_.refs_0_), channel_id=1, source_target_pairs={{0,2},{1,3},{2,0},{3,1},{4,6},{5,7},{6,4},{7,5},{8,10},{9,11},{10,... | collective-permute-start | bytes 172040 | tf_op jit(solution)/shard_map/ppermute | solution.py:28
  89.1 6.5 %collective-permute-start.18 = (bf16[32,896]{1,0:T(8,128)(2,1)S(1)}, bf16[32,896]{1,0:T(8,128)(2,1)S(1)}, u32[]{:S(2)}, u32[]{:S(2)}) collective-permute-start(bf16[32,896]{1,0:T(8,128)(2,1)S(1)} %output_product.1.refs_1_.refs_0_), channel_id=1, source_target_pairs={{0,1},{1,0},{2,3},{3,2},{4,5},{5,4},{6,7},{7,6},{8,9},{9,8},{10,11... | collective-permute-start | bytes 172040 | tf_op jit(solution)/shard_map/ppermute | solution.py:28
  95.7 5.0 %collective-permute-start.23 = (bf16[4,8,896]{2,1,0:T(8,128)(2,1)S(1)}, bf16[4,8,896]{2,1,0:T(8,128)(2,1)S(1)}, u32[]{:S(2)}, u32[]{:S(2)}) collective-permute-start(bf16[4,8,896]{2,1,0:T(8,128)(2,1)S(1)} %mix.1.refs_1_.refs_0_), channel_id=1, source_target_pairs={{0,12},{4,8},{8,4},{12,0},{1,13},{5,9},{9,5},{13,1},{2,14},{6,10},... | collective-permute-start | bytes 172040 | tf_op jit(solution)/shard_map/ppermute | solution.py:28
  96.3 4.9 %collective-permute-start.22 = (bf16[4,8,896]{2,1,0:T(8,128)(2,1)S(1)}, bf16[4,8,896]{2,1,0:T(8,128)(2,1)S(1)}, u32[]{:S(2)}, u32[]{:S(2)}) collective-permute-start(bf16[4,8,896]{2,1,0:T(8,128)(2,1)S(1)} %mix.1.refs_1_.refs_0_), channel_id=1, source_target_pairs={{0,8},{4,12},{8,0},{12,4},{1,9},{5,13},{9,1},{13,5},{2,10},{6,14},... | collective-permute-start | bytes 172040 | tf_op jit(solution)/shard_map/ppermute | solution.py:28
  97.4 3.8 %collective-permute-start.21 = (bf16[4,8,896]{2,1,0:T(8,128)(2,1)S(1)}, bf16[4,8,896]{2,1,0:T(8,128)(2,1)S(1)}, u32[]{:S(2)}, u32[]{:S(2)}) collective-permute-start(bf16[4,8,896]{2,1,0:T(8,128)(2,1)S(1)} %mix.1.refs_1_.refs_0_), channel_id=1, source_target_pairs={{0,4},{4,0},{8,12},{12,8},{1,5},{5,1},{9,13},{13,9},{2,6},{6,2},{1... | collective-permute-start | bytes 172040 | tf_op jit(solution)/shard_map/ppermute | solution.py:28
  (5 other events, 216.4 us)

commit v9 on v8

--- a/solution.py
+++ b/solution.py
@@ -81,7 +81,7 @@
     return held
 
 
-def cut_kernel(sections, experts, piece, x_ref, query_ref, w_ref, *refs):
+def cut_kernel(sections, experts, piece, x_ref, query_ref, w_ref, uv_ref, *refs):
     w_out_ref, *out_refs, w_held, held = refs
     rank = lax.axis_index("expert")
     steps, sources, heads, wide = query_ref.shape
@@ -99,25 +99,34 @@
             for source in range(sources):
                 at = sections * rows + (step * sources + source) * heads
                 ref[at : at + heads, :wide] = query_ref[step, source]
-
-
-def cut_columns(x, queries, w_turned, sections, experts):
+    ref = out_refs[experts // 2]
+    heads, value, chunk = uv_ref.shape
+    base = ref.shape[0] - heads // 2 * value
+    for head in range(heads):
+        at = base + head % (heads // 2) * value
+        to = head // (heads // 2) * chunk
+        ref[at : at + value, to : to + chunk] = uv_ref[head]
+
+
+def cut_columns(x, queries, w_turned, w_uv, sections, experts):
     rows, width = x.shape
     piece = width // (sections * experts)
     steps, sources, heads, wide = queries.shape
-    block = jax.ShapeDtypeStruct(
-        (sections * rows + steps * sources * heads, max(piece, wide)), x.dtype
-    )
+    uv_heads, value, chunk = w_uv.shape
+    lanes = max(piece, wide, 2 * chunk)
+    block = jax.ShapeDtypeStruct((sections * rows + steps * sources * heads, lanes), x.dtype)
+    tall = jax.ShapeDtypeStruct((block.shape[0] + uv_heads // 2 * value, lanes), x.dtype)
     return pl.pallas_call(
         functools.partial(cut_kernel, sections, experts, piece),
-        out_shape=[jax.ShapeDtypeStruct((w_turned.shape[0], piece), x.dtype)] + [block] * experts,
+        out_shape=[jax.ShapeDtypeStruct((w_turned.shape[0], piece), x.dtype)]
+        + [tall if mask == experts // 2 else block for mask in range(experts)],
         scratch_shapes=[
             pltpu.VMEM((experts, w_turned.shape[0], piece), x.dtype),
             pltpu.VMEM((experts, sections * rows, piece), x.dtype),
         ],
-        compiler_params=params(x, block, w_turned, scale=6),
+        compiler_params=params(x, block, w_turned, w_uv, scale=6),
         name="cut_columns",
-    )(*at_home(x, queries, w_turned))
+    )(*at_home(x, queries, w_turned, w_uv))
 
 
 def project_kernel(count, first, rows, *refs):
@@ -151,7 +160,7 @@
 
 
 def query_kernel(
-    experts, sections, prompts, nope, shape, *refs
+    experts, sections, prompts, nope, shape, base, *refs
 ):
     f32, bf16 = jnp.float32, jnp.bfloat16
     table_ref, query_refs = refs[0], refs[1 : 1 + experts]
@@ -169,7 +178,7 @@
     for mask, ref in enumerate(query_refs):
         for step in range(steps):
             for source in range(sources):
-                at = ref.shape[0] - (steps * sources - step * sources - source) * heads
+                at = base + (step * sources + source) * heads
                 query_ref[rank ^ mask, step, source] = ref[at : at + heads, :wide]
 
     def pick(index, carry):
@@ -236,7 +245,7 @@
             out_ref[index, block:, :] = lines
 
 
-def absorb_queries(table, queries, shape, w_uk, own, gain, w_turned, prompts, sections):
+def absorb_queries(table, queries, shape, w_uk, own, gain, w_turned, prompts, sections, after):
     experts = len(queries)
     steps, sources, heads, wide = shape
     _, nope, chunk = w_uk.shape
@@ -247,7 +256,10 @@
     count = experts * sources * steps * heads
     held = pl.BlockSpec(memory_space=pltpu.VMEM)
     return pl.pallas_call(
-        functools.partial(query_kernel, experts, sections, prompts, nope, shape),
+        functools.partial(
+            query_kernel, experts, sections, prompts, nope, shape,
+            queries[0].shape[0] - steps * sources * heads,
+        ),
         out_shape=[
             jax.ShapeDtypeStruct((experts * sections, rows, width), jnp.bfloat16),
             jax.ShapeDtypeStruct(
@@ -256,7 +268,8 @@
             jax.ShapeDtypeStruct((8, 128), jnp.bfloat16),
         ],
         in_specs=[pl.BlockSpec(memory_space=pltpu.SMEM)]
-        + [held] * (experts + 4),
+        + [held] * (experts + 4)
+        + [pl.BlockSpec(memory_space=pl.ANY)] * len(after),
         out_specs=[held] * 3,
         scratch_shapes=[
             pltpu.VMEM((count, nope), jnp.float32),
@@ -270,7 +283,7 @@
         ],
         compiler_params=params(*queries, w_uk, own, w_turned, scale=4),
         name="absorb_queries",
-    )(*at_home(table), *queries, *at_home(w_uk, own, gain, w_turned))
+    )(*at_home(table), *queries, *at_home(w_uk, own, gain, w_turned), *after)
 
 
 def turn(values, cosine, sine):
@@ -439,7 +452,7 @@
     route_ref = refs[1 + sections + experts]
     out_ref, held = refs[-2:]
     f32, bf16 = jnp.float32, jnp.bfloat16
-    chunk = uv_refs[0].shape[2]
+    value, chunk = uv_refs[0].shape[1:]
     rows = latent_refs[0].shape[0]
     for mask, ref in enumerate(latent_refs):
         for index in range(experts):
@@ -452,9 +465,15 @@
         at = pl.ds(head, sections * rows // heads, stride=heads)
         total = 0
         for mask, ref in enumerate(uv_refs):
+            if len(ref.shape) == 3:
+                weight = ref[head]
+            else:
+                low = ref.shape[0] - (heads // 2 - head % (heads // 2)) * value
+                side = head // (heads // 2) * chunk
+                weight = ref[low : low + value, side : side + chunk]
             total = total + lax.dot_general(
                 held[rank ^ mask, at, :][:, :chunk].astype(bf16),
-                ref[head],
+                weight,
                 (((1,), (1,)), ((), ())),
                 preferred_element_type=f32,
             )
@@ -689,19 +708,16 @@
 
     w_turned = w_dkv.T
     w_piece, *cut = cut_columns(
-        prompts.reshape(rows, width), queries, w_turned, sections, experts
+        prompts.reshape(rows, width), queries, w_turned, w_uv, sections, experts
     )
     w_parts = spread(w_piece, "section")
     cut = deliver(cut, "expert")
 
     blocks, riders, token = absorb_queries(
-        owners, cut, queries.shape, w_uk, residual, attn_gain, w_turned, prompt_count, sections
+        owners, cut, queries.shape, w_uk, residual, attn_gain, w_turned, prompt_count, sections,
+        w_parts[1:],
     )
     blocks = lax.all_to_all(blocks, ("expert", "section"), 0, 0, tiled=True)
-    w_uv, token = lax.optimization_barrier((w_uv, token))
-    masks = [1 << bit for bit in range(experts.bit_length() - 1)]
-    uv_parts = doubled({0: w_uv}, "expert", masks[1:])
-
     away = list(project(cut[1:], riders, w_parts, 1, rows, [token]))
     near = list(project(cut[:1], riders, w_parts, 0, rows, away[:1]))
     parts = deliver(near + away, "expert")
@@ -716,9 +732,9 @@
     )
 
     (w_gate,) = fetch([w_gate], [token])
-    order = sorted(uv_parts)
-    *uv_parts, token = lax.optimization_barrier((*[uv_parts[mask] for mask in order], token))
-    uv_parts = doubled(dict(zip(order, uv_parts)), "expert", masks[:1])
+    masks = [1 << bit for bit in range(experts.bit_length() - 1)]
+    uv_parts = {0: w_uv, masks[-1]: cut[masks[-1]]}
+    uv_parts = doubled(uv_parts, "expert", masks[1:-1] + masks[:1])
     out_latent = deliver(out_latent, "section")
     high = route_scores.astype(bf16)
     low = (route_scores - high.astype(f32)).astype(bf16)

time: 120 us -> 117 us (0.975)
  waiting for transfers between devices: 45.3 us -> 40.4 us
  starting transfers between devices: 30.7 us -> 32.3 us
    ppermute x24 -> x23, waiting for transfers between devices: 45.3 us -> 33.1 us  [swap(): return lax.ppermute(block, axis, [(i, i ^ mask) for i in range(size)])]
    all_to_all x1, waiting for transfers between devices: 0.01 us -> 7.3 us  [local(): blocks = lax.all_to_all(blocks, ('expert', 'section'), 0, 0, tiled=True)]
    ppermute x24 -> x23, starting transfers between devices: 25.7 us -> 27.6 us  [swap(): return lax.ppermute(block, axis, [(i, i ^ mask) for i in range(size)])]
  transfers between devices with their start and end apart: 25 -> 24, of which waited for: 10 -> 9; matrix products, arithmetic and copies ran while one was open for 0% -> 0% of each run, Pallas kernels for 14% -> 16%
where the time goes in v9:
time: 117 us; the launch traced here: 116 us
  waiting for transfers between devices  40.4 us (35%)
  starting transfers between devices  32.3 us (28%)
  Pallas kernels  30.3 us (26%)
  blocking collectives  12.3 us (11%)
    ppermute x23, waiting for transfers between devices, swap(): return lax.ppermute(block, axis, [(i, i ^ mask) for i in range(size)])  33.1 us
    ppermute x23, starting transfers between devices, swap(): return lax.ppermute(block, axis, [(i, i ^ mask) for i in range(size)])  27.6 us
    all_to_all x1, blocking collectives, local(): blocks = lax.all_to_all(blocks, ('expert', 'section'), 0, 0, tiled=True)  12.3 us
    pallas_call x4, Pallas kernels, fetch(): pl.pallas_call(functools.partial(fetch_kernel, len(arrays)), out_shape=[p...  11.4 us
    all_to_all x1, waiting for transfers between devices, local(): blocks = lax.all_to_all(blocks, ('expert', 'section'), 0, 0, tiled=True)  7.3 us
    pallas_call x1, Pallas kernels, run_experts(): pl.pallas_call(functools.partial(expert_kernel, experts, sections, picks)...  4.96 us
    all_to_all x1, starting transfers between devices, local(): blocks = lax.all_to_all(blocks, ('expert', 'section'), 0, 0, tiled=True)  4.69 us
    pallas_call x1, Pallas kernels, cut_columns(): pl.pallas_call(functools.partial(cut_kernel, sections, experts, piece), o...  2.7 us
  transfers between devices with their start and end apart: 24, of which 9 were waited for; matrix products, arithmetic and copies ran while one was open for 0% of the time, Pallas kernels for 16%

profile of v9, /device:TPU:0, one launch (start us, length us, event | category | flops | bytes accessed | tf_op | source)
XLA Modules:
  0.0 116.3 jit_solution(11327949908092547254)
XLA Ops:
  0.0 2.7 %cut_columns.1 = (bf16[576,224]{1,0:T(8,128)(2,1)S(1)}, bf16[640,256]{1,0:T(8,128)(2,1)S(1)}, bf16[640,256]{1,0:T(8,128)(2,1)S(1)}, bf16[1664,256]{1,0:T(8,128)(2,1)S(1)}, bf16[640,256]{1,0:T(8,128)(2,1)S(1)}) custom-call(bf16[128,3584]{1,0:T(8,128)(2,1)} %bitcast.5, bf16[2,4,16,192]{3,2,1,0:T(8,128)(2,1)} %query_ref.1, bf16[576,896]{1,0:T(8,128)(2,1)} %bitcast.3, ...), custom_call_target="tpu_custom_call" | custom-call | tf_op jit(solution)/shard_map/cut_columns/pallas_call | solution.py:119
  2.7 3.0 %collective-permute-start.1 = (bf16[1664,256]{1,0:T(8,128)(2,1)S(1)}, bf16[1664,256]{1,0:T(8,128)(2,1)S(1)}, u32[]{:S(2)}, u32[]{:S(2)}) collective-permute-start(bf16[1664,256]{1,0:T(8,128)(2,1)S(1)} %get-tuple-element.29), channel_id=1, source_target_pairs={{0,8},{4,12},{8,0},{12,4},{1,9},{5,13},{9,1},{13,5},{2,10},{6,14},... | collective-permute-start | bytes 2555912 | tf_op jit(solution)/shard_map/ppermute | solution.py:28
  5.7 3.6 %collective-permute-start.5 = (bf16[576,224]{1,0:T(8,128)(2,1)S(1)}, bf16[576,224]{1,0:T(8,128)(2,1)S(1)}, u32[]{:S(2)}, u32[]{:S(2)}) collective-permute-start(bf16[576,224]{1,0:T(8,128)(2,1)S(1)} %get-tuple-element.31.refs_4_.refs_2_), channel_id=1, source_target_pairs={{0,3},{1,2},{2,1},{3,0},{4,7},{5,6},{6,5},{7,4},{8,11},{9,10},{10,... | collective-permute-start | bytes 774152 | tf_op jit(solution)/shard_map/ppermute | solution.py:28
  9.3 15.4 %collective-permute-done.1.refs_3_.refs_1_.refs_7_ = bf16[1664,256]{1,0:T(8,128)(2,1)S(1)} collective-permute-done((bf16[1664,256]{1,0:T(8,128)(2,1)S(1)}, bf16[1664,256]{1,0:T(8,128)(2,1)S(1)}, u32[]{:S(2)}, u32[]{:S(2)}) %collective-permute-start.1) | collective-permute-done | bytes 852000 | tf_op jit(solution)/shard_map/ppermute | solution.py:28
  26.6 2.6 %collective-permute-start.4 = (bf16[576,224]{1,0:T(8,128)(2,1)S(1)}, bf16[576,224]{1,0:T(8,128)(2,1)S(1)}, u32[]{:S(2)}, u32[]{:S(2)}) collective-permute-start(bf16[576,224]{1,0:T(8,128)(2,1)S(1)} %get-tuple-element.31.refs_4_.refs_2_), channel_id=1, source_target_pairs={{0,2},{1,3},{2,0},{3,1},{4,6},{5,7},{6,4},{7,5},{8,10},{9,11},{10,... | collective-permute-start | bytes 774152 | tf_op jit(solution)/shard_map/ppermute | solution.py:28
  29.2 1.6 %collective-permute-start.3 = (bf16[576,224]{1,0:T(8,128)(2,1)S(1)}, bf16[576,224]{1,0:T(8,128)(2,1)S(1)}, u32[]{:S(2)}, u32[]{:S(2)}) collective-permute-start(bf16[576,224]{1,0:T(8,128)(2,1)S(1)} %get-tuple-element.31.refs_4_.refs_2_), channel_id=1, source_target_pairs={{0,1},{1,0},{2,3},{3,2},{4,5},{5,4},{6,7},{7,6},{8,9},{9,8},{10,11... | collective-permute-start | bytes 774152 | tf_op jit(solution)/shard_map/ppermute | solution.py:28
  30.7 12.6 %collective-permute-done.4.refs_10_.refs_6_.refs_4_ = bf16[576,224]{1,0:T(8,128)(2,1)S(1)} collective-permute-done((bf16[576,224]{1,0:T(8,128)(2,1)S(1)}, bf16[576,224]{1,0:T(8,128)(2,1)S(1)}, u32[]{:S(2)}, u32[]{:S(2)}) %collective-permute-start.4) | collective-permute-done | bytes 258080 | tf_op jit(solution)/shard_map/ppermute | solution.py:28
  43.5 2.2 %absorb_queries.1 = (bf16[16,40,144]{2,1,0:T(8,128)(2,1)S(1)}, bf16[4,16,576]{2,1,0:T(8,128)(2,1)S(1)}, bf16[8,128]{1,0:T(8,128)(2,1)S(1)}) custom-call(s32[16]{0:T(128)} %refs_0_.8, bf16[640,256]{1,0:T(8,128)(2,1)S(1)} %get-tuple-element.27.refs_1_.refs_0_, bf16[640,256]{1,0:T(8,128)(2,1)S(1)} %collective-permute-done.refs_2_.refs_0_, ...), custom_call_target="tpu_custom_call" | custom-call | tf_op jit(solution)/shard_map/absorb_queries/pallas_call | solution.py:258
  46.4 4.7 %all-to-all-start = ((bf16[16,40,144]{2,1,0:T(8,128)(2,1)}), bf16[16,40,144]{2,1,0:T(8,128)(2,1)S(1)}, u32[]{:S(2)}, u32[]{:S(2)}) async-start(bf16[16,40,144]{2,1,0:T(8,128)(2,1)} %copy-done.1), calls=%async_computation | async-start | bytes 655360 | tf_op jit(solution)/shard_map/all_to_all | solution.py:720
  52.6 1.9 %collective-permute-start.7 = (bf16[144,576]{1,0:T(8,128)(2,1)}, bf16[144,576]{1,0:T(8,128)(2,1)S(1)}, u32[]{:S(2)}, u32[]{:S(2)}) collective-permute-start(bf16[144,576]{1,0:T(8,128)(2,1)} %get-tuple-element.35), channel_id=1, source_target_pairs={{0,8},{4,12},{8,0},{12,4},{1,9},{5,13},{9,1},{13,5},{2,10},{6,14},... | collective-permute-start | bytes 497672 | tf_op jit(solution)/shard_map/ppermute | solution.py:28
  55.3 7.3 %all-to-all-done.block_ref = bf16[16,40,144]{2,1,0:T(8,128)(2,1)S(1)} async-done(((bf16[16,40,144]{2,1,0:T(8,128)(2,1)}), bf16[16,40,144]{2,1,0:T(8,128)(2,1)S(1)}, u32[]{:S(2)}, u32[]{:S(2)}) %all-to-all-start) | async-done | bytes 184352 | tf_op jit(solution)/shard_map/all_to_all | solution.py:720
  63.8 1.9 %collective-permute-done.8.refs_3_.refs_7_ = bf16[144,576]{1,0:T(8,128)(2,1)S(1)} collective-permute-done((bf16[144,576]{1,0:T(8,128)(2,1)}, bf16[144,576]{1,0:T(8,128)(2,1)S(1)}, u32[]{:S(2)}, u32[]{:S(2)}) %collective-permute-start.8) | collective-permute-done | bytes 165920 | tf_op jit(solution)/shard_map/ppermute | solution.py:28
  65.7 1.8 %attend.1 = (bf16[32,512]{1,0:T(8,128)(2,1)S(1)}, bf16[32,512]{1,0:T(8,128)(2,1)S(1)}, bf16[32,512]{1,0:T(8,128)(2,1)S(1)}, bf16[32,512]{1,0:T(8,128)(2,1)S(1)}, bf16[8,128]{1,0:T(8,128)(2,1)S(1)}) custom-call(bf16[144,576]{1,0:T(8,128)(2,1)S(1)} %project.3.refs_0_.refs_4_, bf16[144,576]{1,0:T(8,128)(2,1)S(1)} %collective-permute-done.6.refs_1_.refs_5_, ...), custom_call_target="tpu_custom_call" | custom-call | tf_op jit(solution)/shard_map/attend/pallas_call | solution.py:432
  67.5 2.1 %collective-permute-start.9 = (bf16[32,512]{1,0:T(8,128)(2,1)S(1)}, bf16[32,512]{1,0:T(8,128)(2,1)S(1)}, u32[]{:S(2)}, u32[]{:S(2)}) collective-permute-start(bf16[32,512]{1,0:T(8,128)(2,1)S(1)} %get-tuple-element.43), channel_id=1, source_target_pairs={{0,1},{1,0},{2,3},{3,2},{4,5},{5,4},{6,7},{7,6},{8,9},{9,8},{10,11... | collective-permute-start | bytes 98312 | tf_op jit(solution)/shard_map/ppermute | solution.py:28
  69.6 1.8 %collective-permute-start.10 = (bf16[32,512]{1,0:T(8,128)(2,1)S(1)}, bf16[32,512]{1,0:T(8,128)(2,1)S(1)}, u32[]{:S(2)}, u32[]{:S(2)}) collective-permute-start(bf16[32,512]{1,0:T(8,128)(2,1)S(1)} %get-tuple-element.44), channel_id=1, source_target_pairs={{0,2},{1,3},{2,0},{3,1},{4,6},{5,7},{6,4},{7,5},{8,10},{9,11},{10,... | collective-permute-start | bytes 98312 | tf_op jit(solution)/shard_map/ppermute | solution.py:28
  72.1 3.2 %fetch.4.refs_10_.refs_9_ = bf16[4,3584,256]{2,1,0:T(8,128)(2,1)S(1)} custom-call(bf16[4,3584,256]{2,1,0:T(8,128)(2,1)} %refs_0_.7, bf16[8,128]{1,0:T(8,128)(2,1)S(1)} %get-tuple-element.46.refs_1_.refs_11_), custom_call_target="tpu_custom_call" | custom-call | bytes 14680064 | tf_op jit(solution)/shard_map/fetch/pallas_call | solution.py:63
  75.3 1.8 %collective-permute-done.11.refs_4_ = bf16[32,512]{1,0:T(8,128)(2,1)S(1)} collective-permute-done((bf16[32,512]{1,0:T(8,128)(2,1)S(1)}, bf16[32,512]{1,0:T(8,128)(2,1)S(1)}, u32[]{:S(2)}, u32[]{:S(2)}) %collective-permute-start.11) | collective-permute-done | bytes 32800 | tf_op jit(solution)/shard_map/ppermute | solution.py:28
  77.1 2.6 %head_products.1.refs_0_.refs_4_ = bf16[8,2176]{1,0:T(8,128)(2,1)S(1)} custom-call(s32[16]{0:T(128)} %refs_0_.8, bf16[32,512]{1,0:T(8,128)(2,1)S(1)} %get-tuple-element.42.refs_1_, bf16[32,512]{1,0:T(8,128)(2,1)S(1)} %collective-permute-done.9.refs_2_, bf16[32,512]{1,0:T(8,128)(2,1)S(1)} %collective-permute-done.10.refs_3_, ...), custom_call_target="tpu_custom_call" | custom-call | tf_op jit(solution)/shard_map/head_products/pallas_call | solution.py:508
  81.7 2.0 %fetch.5.refs_4_ = bf16[2048,896]{1,0:T(8,128)(2,1)S(1)} custom-call(bf16[2048,896]{1,0:T(8,128)(2,1)} %refs_0_.9), custom_call_target="tpu_custom_call" | custom-call | bytes 7340032 | tf_op jit(solution)/shard_map/fetch/pallas_call | solution.py:63
  86.2 3.0 %collective-permute-start.17 = (bf16[32,896]{1,0:T(8,128)(2,1)S(1)}, bf16[32,896]{1,0:T(8,128)(2,1)S(1)}, u32[]{:S(2)}, u32[]{:S(2)}) collective-permute-start(bf16[32,896]{1,0:T(8,128)(2,1)S(1)} %output_product.1.refs_1_.refs_0_), channel_id=1, source_target_pairs={{0,1},{1,0},{2,3},{3,2},{4,5},{5,4},{6,7},{7,6},{8,9},{9,8},{10,11... | collective-permute-start | bytes 172040 | tf_op jit(solution)/shard_map/ppermute | solution.py:28
  89.1 3.1 %fetch.6.refs_8_.refs_10_ = bf16[4,3584,256]{2,1,0:T(8,128)(2,1)S(1)} custom-call(bf16[4,3584,256]{2,1,0:T(8,128)(2,1)} %refs_0_.10, bf16[32,896]{1,0:T(8,128)(2,1)S(1)} %output_product.1.refs_1_.refs_0_), custom_call_target="tpu_custom_call" | custom-call | bytes 14680064 | tf_op jit(solution)/shard_map/fetch/pallas_call | solution.py:63
  94.8 3.1 %fetch.7.refs_11_ = bf16[4,256,3584]{2,1,0:T(8,128)(2,1)S(1)} custom-call(bf16[4,256,3584]{2,1,0:T(8,128)(2,1)} %refs_0_.11, bf16[4,8,896]{2,1,0:T(8,128)(2,1)S(1)} %mix.1.refs_1_.refs_0_), custom_call_target="tpu_custom_call" | custom-call | bytes 14680064 | tf_op jit(solution)/shard_map/fetch/pallas_call | solution.py:63
  98.4 5.0 %run_experts.1 = (bf16[16,8,896]{2,1,0:T(8,128)(2,1)S(1)}, bf16[4,8,896]{2,1,0:T(8,128)(2,1)S(1)}) custom-call(bf16[4,8,896]{2,1,0:T(8,128)(2,1)S(1)} %mix.1.refs_1_.refs_0_, bf16[4,8,896]{2,1,0:T(8,128)(2,1)S(1)} %collective-permute-done.20.refs_1_, bf16[4,8,896]{2,1,0:T(8,128)(2,1)S(1)} %collective-permute-done.21.refs_2_, ...), custom_call_target="tpu_custom_call" | custom-call | tf_op jit(solution)/shard_map/run_experts/pallas_call | solution.py:641
  103.3 12.3 %all_to_all.10.block_ref = bf16[16,8,896]{2,1,0:T(8,128)(2,1)S(1)} all-to-all(bf16[16,8,896]{2,1,0:T(8,128)(2,1)S(1)} %get-tuple-element.47), channel_id=1, replica_groups=mesh['groups'=2,'expert'=4,'section'=4] {'expert','section'}, dimensions={0} | all-to-all | bytes 458752 | tf_op jit(solution)/shard_map/all_to_all | solution.py:764
  (52 shorter events, 14.9 us)
Async XLA Ops:
  2.7 22.0 %collective-permute-start.1 = (bf16[1664,256]{1,0:T(8,128)(2,1)S(1)}, bf16[1664,256]{1,0:T(8,128)(2,1)S(1)}, u32[]{:S(2)}, u32[]{:S(2)}) collective-permute-start(bf16[1664,256]{1,0:T(8,128)(2,1)S(1)} %get-tuple-element.29), channel_id=1, source_target_pairs={{0,8},{4,12},{8,0},{12,4},{1,9},{5,13},{9,1},{13,5},{2,10},{6,14},... | collective-permute-start | bytes 2555912 | tf_op jit(solution)/shard_map/ppermute | solution.py:28
  5.7 23.4 %collective-permute-start.5 = (bf16[576,224]{1,0:T(8,128)(2,1)S(1)}, bf16[576,224]{1,0:T(8,128)(2,1)S(1)}, u32[]{:S(2)}, u32[]{:S(2)}) collective-permute-start(bf16[576,224]{1,0:T(8,128)(2,1)S(1)} %get-tuple-element.31.refs_4_.refs_2_), channel_id=1, source_target_pairs={{0,3},{1,2},{2,1},{3,0},{4,7},{5,6},{6,5},{7,4},{8,11},{9,10},{10,... | collective-permute-start | bytes 774152 | tf_op jit(solution)/shard_map/ppermute | solution.py:28
  24.7 52.4 %collective-permute-start.13 = (bf16[1664,256]{1,0:T(8,128)(2,1)S(1)}, bf16[1664,256]{1,0:T(8,128)(2,1)}, u32[]{:S(2)}, u32[]{:S(2)}) collective-permute-start(bf16[1664,256]{1,0:T(8,128)(2,1)S(1)} %collective-permute-done.1.refs_3_.refs_1_.refs_7_), channel_id=1, source_target_pairs={{0,4},{4,0},{8,12},{12,8},{1,5},{5,1},{9,13},{13,9},{2,6},{6,2},{1... | collective-permute-start | bytes 2555912 | tf_op jit(solution)/shard_map/ppermute | solution.py:28
  24.7 18.8 %collective-permute-start = (bf16[640,256]{1,0:T(8,128)(2,1)S(1)}, bf16[640,256]{1,0:T(8,128)(2,1)S(1)}, u32[]{:S(2)}, u32[]{:S(2)}) collective-permute-start(bf16[640,256]{1,0:T(8,128)(2,1)S(1)} %get-tuple-element.28), channel_id=1, source_target_pairs={{0,4},{4,0},{8,12},{12,8},{1,5},{5,1},{9,13},{13,9},{2,6},{6,2},{1... | collective-permute-start | bytes 983048 | tf_op jit(solution)/shard_map/ppermute | solution.py:28
  25.2 18.3 %collective-permute-start.2 = (bf16[640,256]{1,0:T(8,128)(2,1)S(1)}, bf16[640,256]{1,0:T(8,128)(2,1)S(1)}, u32[]{:S(2)}, u32[]{:S(2)}) collective-permute-start(bf16[640,256]{1,0:T(8,128)(2,1)S(1)} %get-tuple-element.30), channel_id=1, source_target_pairs={{0,12},{4,8},{8,4},{12,0},{1,13},{5,9},{9,5},{13,1},{2,14},{6,10},... | collective-permute-start | bytes 983048 | tf_op jit(solution)/shard_map/ppermute | solution.py:28
  26.6 16.7 %collective-permute-start.4 = (bf16[576,224]{1,0:T(8,128)(2,1)S(1)}, bf16[576,224]{1,0:T(8,128)(2,1)S(1)}, u32[]{:S(2)}, u32[]{:S(2)}) collective-permute-start(bf16[576,224]{1,0:T(8,128)(2,1)S(1)} %get-tuple-element.31.refs_4_.refs_2_), channel_id=1, source_target_pairs={{0,2},{1,3},{2,0},{3,1},{4,6},{5,7},{6,4},{7,5},{8,10},{9,11},{10,... | collective-permute-start | bytes 774152 | tf_op jit(solution)/shard_map/ppermute | solution.py:28
  29.2 14.3 %collective-permute-start.3 = (bf16[576,224]{1,0:T(8,128)(2,1)S(1)}, bf16[576,224]{1,0:T(8,128)(2,1)S(1)}, u32[]{:S(2)}, u32[]{:S(2)}) collective-permute-start(bf16[576,224]{1,0:T(8,128)(2,1)S(1)} %get-tuple-element.31.refs_4_.refs_2_), channel_id=1, source_target_pairs={{0,1},{1,0},{2,3},{3,2},{4,5},{5,4},{6,7},{7,6},{8,9},{9,8},{10,11... | collective-permute-start | bytes 774152 | tf_op jit(solution)/shard_map/ppermute | solution.py:28
  43.3 32.0 %collective-permute-start.12 = (bf16[16,128,128]{2,1,0:T(8,128)(2,1)}, bf16[16,128,128]{2,1,0:T(8,128)(2,1)}, u32[]{:S(2)}, u32[]{:S(2)}) collective-permute-start(bf16[16,128,128]{2,1,0:T(8,128)(2,1)} %refs_5_.5), channel_id=1, source_target_pairs={{0,4},{4,0},{8,12},{12,8},{1,5},{5,1},{9,13},{13,9},{2,6},{6,2},{1... | collective-permute-start | bytes 1572872 | tf_op jit(solution)/shard_map/ppermute | solution.py:28
  46.4 16.2 %all-to-all-start = ((bf16[16,40,144]{2,1,0:T(8,128)(2,1)}), bf16[16,40,144]{2,1,0:T(8,128)(2,1)S(1)}, u32[]{:S(2)}, u32[]{:S(2)}) async-start(bf16[16,40,144]{2,1,0:T(8,128)(2,1)} %copy-done.1), calls=%async_computation | async-start | bytes 655360 | tf_op jit(solution)/shard_map/all_to_all | solution.py:720
  52.6 11.1 %collective-permute-start.7 = (bf16[144,576]{1,0:T(8,128)(2,1)}, bf16[144,576]{1,0:T(8,128)(2,1)S(1)}, u32[]{:S(2)}, u32[]{:S(2)}) collective-permute-start(bf16[144,576]{1,0:T(8,128)(2,1)} %get-tuple-element.35), channel_id=1, source_target_pairs={{0,8},{4,12},{8,0},{12,4},{1,9},{5,13},{9,1},{13,5},{2,10},{6,14},... | collective-permute-start | bytes 497672 | tf_op jit(solution)/shard_map/ppermute | solution.py:28
  54.6 11.1 %collective-permute-start.8 = (bf16[144,576]{1,0:T(8,128)(2,1)}, bf16[144,576]{1,0:T(8,128)(2,1)S(1)}, u32[]{:S(2)}, u32[]{:S(2)}) collective-permute-start(bf16[144,576]{1,0:T(8,128)(2,1)} %get-tuple-element.36), channel_id=1, source_target_pairs={{0,12},{4,8},{8,4},{12,0},{1,13},{5,9},{9,5},{13,1},{2,14},{6,10},... | collective-permute-start | bytes 497672 | tf_op jit(solution)/shard_map/ppermute | solution.py:28
  54.6 11.1 %collective-permute-start.6 = (bf16[144,576]{1,0:T(8,128)(2,1)}, bf16[144,576]{1,0:T(8,128)(2,1)S(1)}, u32[]{:S(2)}, u32[]{:S(2)}) collective-permute-start(bf16[144,576]{1,0:T(8,128)(2,1)} %get-tuple-element.34.refs_6_), channel_id=1, source_target_pairs={{0,4},{4,0},{8,12},{12,8},{1,5},{5,1},{9,13},{13,9},{2,6},{6,2},{1... | collective-permute-start | bytes 497672 | tf_op jit(solution)/shard_map/ppermute | solution.py:28
  67.5 7.8 %collective-permute-start.9 = (bf16[32,512]{1,0:T(8,128)(2,1)S(1)}, bf16[32,512]{1,0:T(8,128)(2,1)S(1)}, u32[]{:S(2)}, u32[]{:S(2)}) collective-permute-start(bf16[32,512]{1,0:T(8,128)(2,1)S(1)} %get-tuple-element.43), channel_id=1, source_target_pairs={{0,1},{1,0},{2,3},{3,2},{4,5},{5,4},{6,7},{7,6},{8,9},{9,8},{10,11... | collective-permute-start | bytes 98312 | tf_op jit(solution)/shard_map/ppermute | solution.py:28
  69.6 5.7 %collective-permute-start.10 = (bf16[32,512]{1,0:T(8,128)(2,1)S(1)}, bf16[32,512]{1,0:T(8,128)(2,1)S(1)}, u32[]{:S(2)}, u32[]{:S(2)}) collective-permute-start(bf16[32,512]{1,0:T(8,128)(2,1)S(1)} %get-tuple-element.44), channel_id=1, source_target_pairs={{0,2},{1,3},{2,0},{3,1},{4,6},{5,7},{6,4},{7,5},{8,10},{9,11},{10,... | collective-permute-start | bytes 98312 | tf_op jit(solution)/shard_map/ppermute | solution.py:28
  71.4 5.7 %collective-permute-start.11 = (bf16[32,512]{1,0:T(8,128)(2,1)S(1)}, bf16[32,512]{1,0:T(8,128)(2,1)S(1)}, u32[]{:S(2)}, u32[]{:S(2)}) collective-permute-start(bf16[32,512]{1,0:T(8,128)(2,1)S(1)} %get-tuple-element.45), channel_id=1, source_target_pairs={{0,3},{1,2},{2,1},{3,0},{4,7},{5,6},{6,5},{7,4},{8,11},{9,10},{10,... | collective-permute-start | bytes 98312 | tf_op jit(solution)/shard_map/ppermute | solution.py:28
  79.8 3.9 %collective-permute-start.16 = (bf16[8,2176]{1,0:T(8,128)(2,1)S(1)}, bf16[8,2176]{1,0:T(8,128)(2,1)S(1)}, u32[]{:S(2)}, u32[]{:S(2)}) collective-permute-start(bf16[8,2176]{1,0:T(8,128)(2,1)S(1)} %head_products.1.refs_0_.refs_4_), channel_id=1, source_target_pairs={{0,12},{4,8},{8,4},{12,0},{1,13},{5,9},{9,5},{13,1},{2,14},{6,10},... | collective-permute-start | bytes 104456 | tf_op jit(solution)/shard_map/ppermute | solution.py:28
  79.8 4.2 %collective-permute-start.15 = (bf16[8,2176]{1,0:T(8,128)(2,1)S(1)}, bf16[8,2176]{1,0:T(8,128)(2,1)S(1)}, u32[]{:S(2)}, u32[]{:S(2)}) collective-permute-start(bf16[8,2176]{1,0:T(8,128)(2,1)S(1)} %head_products.1.refs_0_.refs_4_), channel_id=1, source_target_pairs={{0,8},{4,12},{8,0},{12,4},{1,9},{5,13},{9,1},{13,5},{2,10},{6,14},... | collective-permute-start | bytes 104456 | tf_op jit(solution)/shard_map/ppermute | solution.py:28
  80.5 3.4 %collective-permute-start.14 = (bf16[8,2176]{1,0:T(8,128)(2,1)S(1)}, bf16[8,2176]{1,0:T(8,128)(2,1)S(1)}, u32[]{:S(2)}, u32[]{:S(2)}) collective-permute-start(bf16[8,2176]{1,0:T(8,128)(2,1)S(1)} %head_products.1.refs_0_.refs_4_), channel_id=1, source_target_pairs={{0,4},{4,0},{8,12},{12,8},{1,5},{5,1},{9,13},{13,9},{2,6},{6,2},{1... | collective-permute-start | bytes 104456 | tf_op jit(solution)/shard_map/ppermute | solution.py:28
  84.7 7.6 %collective-permute-start.19 = (bf16[32,896]{1,0:T(8,128)(2,1)S(1)}, bf16[32,896]{1,0:T(8,128)(2,1)S(1)}, u32[]{:S(2)}, u32[]{:S(2)}) collective-permute-start(bf16[32,896]{1,0:T(8,128)(2,1)S(1)} %output_product.1.refs_1_.refs_0_), channel_id=1, source_target_pairs={{0,3},{1,2},{2,1},{3,0},{4,7},{5,6},{6,5},{7,4},{8,11},{9,10},{10,... | collective-permute-start | bytes 172040 | tf_op jit(solution)/shard_map/ppermute | solution.py:28
  86.2 6.5 %collective-permute-start.18 = (bf16[32,896]{1,0:T(8,128)(2,1)S(1)}, bf16[32,896]{1,0:T(8,128)(2,1)S(1)}, u32[]{:S(2)}, u32[]{:S(2)}) collective-permute-start(bf16[32,896]{1,0:T(8,128)(2,1)S(1)} %output_product.1.refs_1_.refs_0_), channel_id=1, source_target_pairs={{0,2},{1,3},{2,0},{3,1},{4,6},{5,7},{6,4},{7,5},{8,10},{9,11},{10,... | collective-permute-start | bytes 172040 | tf_op jit(solution)/shard_map/ppermute | solution.py:28
  86.2 6.5 %collective-permute-start.17 = (bf16[32,896]{1,0:T(8,128)(2,1)S(1)}, bf16[32,896]{1,0:T(8,128)(2,1)S(1)}, u32[]{:S(2)}, u32[]{:S(2)}) collective-permute-start(bf16[32,896]{1,0:T(8,128)(2,1)S(1)} %output_product.1.refs_1_.refs_0_), channel_id=1, source_target_pairs={{0,1},{1,0},{2,3},{3,2},{4,5},{5,4},{6,7},{7,6},{8,9},{9,8},{10,11... | collective-permute-start | bytes 172040 | tf_op jit(solution)/shard_map/ppermute | solution.py:28
  92.8 5.0 %collective-permute-start.22 = (bf16[4,8,896]{2,1,0:T(8,128)(2,1)S(1)}, bf16[4,8,896]{2,1,0:T(8,128)(2,1)S(1)}, u32[]{:S(2)}, u32[]{:S(2)}) collective-permute-start(bf16[4,8,896]{2,1,0:T(8,128)(2,1)S(1)} %mix.1.refs_1_.refs_0_), channel_id=1, source_target_pairs={{0,12},{4,8},{8,4},{12,0},{1,13},{5,9},{9,5},{13,1},{2,14},{6,10},... | collective-permute-start | bytes 172040 | tf_op jit(solution)/shard_map/ppermute | solution.py:28
  93.4 4.9 %collective-permute-start.21 = (bf16[4,8,896]{2,1,0:T(8,128)(2,1)S(1)}, bf16[4,8,896]{2,1,0:T(8,128)(2,1)S(1)}, u32[]{:S(2)}, u32[]{:S(2)}) collective-permute-start(bf16[4,8,896]{2,1,0:T(8,128)(2,1)S(1)} %mix.1.refs_1_.refs_0_), channel_id=1, source_target_pairs={{0,8},{4,12},{8,0},{12,4},{1,9},{5,13},{9,1},{13,5},{2,10},{6,14},... | collective-permute-start | bytes 172040 | tf_op jit(solution)/shard_map/ppermute | solution.py:28
  94.5 3.8 %collective-permute-start.20 = (bf16[4,8,896]{2,1,0:T(8,128)(2,1)S(1)}, bf16[4,8,896]{2,1,0:T(8,128)(2,1)S(1)}, u32[]{:S(2)}, u32[]{:S(2)}) collective-permute-start(bf16[4,8,896]{2,1,0:T(8,128)(2,1)S(1)} %mix.1.refs_1_.refs_0_), channel_id=1, source_target_pairs={{0,4},{4,0},{8,12},{12,8},{1,5},{5,1},{9,13},{13,9},{2,6},{6,2},{1... | collective-permute-start | bytes 172040 | tf_op jit(solution)/shard_map/ppermute | solution.py:28
  (4 other events, 111.7 us)

commit v10 on v9

--- a/solution.py
+++ b/solution.py
@@ -715,7 +715,7 @@
 
     blocks, riders, token = absorb_queries(
         owners, cut, queries.shape, w_uk, residual, attn_gain, w_turned, prompt_count, sections,
-        w_parts[1:],
+        w_parts[2:],
     )
     blocks = lax.all_to_all(blocks, ("expert", "section"), 0, 0, tiled=True)
     away = list(project(cut[1:], riders, w_parts, 1, rows, [token]))
@@ -733,7 +733,8 @@
 
     (w_gate,) = fetch([w_gate], [token])
     masks = [1 << bit for bit in range(experts.bit_length() - 1)]
-    uv_parts = {0: w_uv, masks[-1]: cut[masks[-1]]}
+    near_uv, far_uv, token = lax.optimization_barrier((w_uv, cut[masks[-1]], token))
+    uv_parts = {0: near_uv, masks[-1]: far_uv}
     uv_parts = doubled(uv_parts, "expert", masks[1:-1] + masks[:1])
     out_latent = deliver(out_latent, "section")
     high = route_scores.astype(bf16)

time: 117 us -> 108 us (0.923)
  waiting for transfers between devices: 40.4 us -> 23.5 us
  starting transfers between devices: 32.3 us -> 38.4 us
  Pallas kernels: 30.3 us -> 32 us
    ppermute x23, waiting for transfers between devices: 33.1 us -> 18.3 us  [swap(): return lax.ppermute(block, axis, [(i, i ^ mask) for i in range(size)])]
    ppermute x23, starting transfers between devices: 27.6 us -> 34.5 us  [swap(): return lax.ppermute(block, axis, [(i, i ^ mask) for i in range(size)])]
    pallas_call x2, Pallas kernels: 2 us -> 4.13 us  [project(): pl.pallas_call(functools.partial(project_kernel, len(blocks), first, rows...]
    all_to_all x1, waiting for transfers between devices: 7.3 us -> 5.19 us  [local(): blocks = lax.all_to_all(blocks, ('expert', 'section'), 0, 0, tiled=True)]
  transfers between devices with their start and end apart: 24 -> 24, of which waited for: 9 -> 8; matrix products, arithmetic and copies ran while one was open for 0% -> 0% of each run, Pallas kernels for 16% -> 18%
where the time goes in v10:
time: 108 us; the launch traced here: 107 us
  starting transfers between devices  38.4 us (36%)
  Pallas kernels  32 us (30%)
  waiting for transfers between devices  23.5 us (22%)
  blocking collectives  12 us (11%)
    ppermute x23, starting transfers between devices, swap(): return lax.ppermute(block, axis, [(i, i ^ mask) for i in range(size)])  34.5 us
    ppermute x23, waiting for transfers between devices, swap(): return lax.ppermute(block, axis, [(i, i ^ mask) for i in range(size)])  18.3 us
    all_to_all x1, blocking collectives, local(): blocks = lax.all_to_all(blocks, ('expert', 'section'), 0, 0, tiled=True)  12 us
    pallas_call x4, Pallas kernels, fetch(): pl.pallas_call(functools.partial(fetch_kernel, len(arrays)), out_shape=[p...  11.3 us
    all_to_all x1, waiting for transfers between devices, local(): blocks = lax.all_to_all(blocks, ('expert', 'section'), 0, 0, tiled=True)  5.19 us
    pallas_call x1, Pallas kernels, run_experts(): pl.pallas_call(functools.partial(expert_kernel, experts, sections, picks)...  4.96 us
    pallas_call x2, Pallas kernels, project(): pl.pallas_call(functools.partial(project_kernel, len(blocks), first, rows...  4.13 us
    all_to_all x1, starting transfers between devices, local(): blocks = lax.all_to_all(blocks, ('expert', 'section'), 0, 0, tiled=True)  3.86 us
  transfers between devices with their start and end apart: 24, of which 8 were waited for; matrix products, arithmetic and copies ran while one was open for 0% of the time, Pallas kernels for 18%

profile of v10, /device:TPU:0, one launch (start us, length us, event | category | flops | bytes accessed | tf_op | source)
XLA Modules:
  0.0 107.0 jit_solution(12768454540387063584)
XLA Ops:
  0.0 3.0 %cut_columns.1 = (bf16[576,224]{1,0:T(8,128)(2,1)}, bf16[640,256]{1,0:T(8,128)(2,1)S(1)}, bf16[640,256]{1,0:T(8,128)(2,1)S(1)}, bf16[1664,256]{1,0:T(8,128)(2,1)S(1)}, bf16[640,256]{1,0:T(8,128)(2,1)S(1)}) custom-call(bf16[128,3584]{1,0:T(8,128)(2,1)} %bitcast.5, bf16[2,4,16,192]{3,2,1,0:T(8,128)(2,1)} %query_ref.1, bf16[576,896]{1,0:T(8,128)(2,1)} %bitcast.3, ...), custom_call_target="tpu_custom_call" | custom-call | tf_op jit(solution)/shard_map/cut_columns/pallas_call | solution.py:119
  3.0 2.9 %collective-permute-start.1 = (bf16[1664,256]{1,0:T(8,128)(2,1)S(1)}, bf16[1664,256]{1,0:T(8,128)(2,1)S(1)}, u32[]{:S(2)}, u32[]{:S(2)}) collective-permute-start(bf16[1664,256]{1,0:T(8,128)(2,1)S(1)} %get-tuple-element.32), channel_id=1, source_target_pairs={{0,8},{4,12},{8,0},{12,4},{1,9},{5,13},{9,1},{13,5},{2,10},{6,14},... | collective-permute-start | bytes 2555912 | tf_op jit(solution)/shard_map/ppermute | solution.py:28
  6.0 3.6 %collective-permute-start.4 = (bf16[576,224]{1,0:T(8,128)(2,1)}, bf16[576,224]{1,0:T(8,128)(2,1)S(1)}, u32[]{:S(2)}, u32[]{:S(2)}) collective-permute-start(bf16[576,224]{1,0:T(8,128)(2,1)} %get-tuple-element.34.refs_4_.refs_2_), channel_id=1, source_target_pairs={{0,3},{1,2},{2,1},{3,0},{4,7},{5,6},{6,5},{7,4},{8,11},{9,10},{10,... | collective-permute-start | bytes 774152 | tf_op jit(solution)/shard_map/ppermute | solution.py:28
  10.2 7.7 %collective-permute-done.4.refs_10_.refs_7_.refs_5_ = bf16[576,224]{1,0:T(8,128)(2,1)S(1)} collective-permute-done((bf16[576,224]{1,0:T(8,128)(2,1)}, bf16[576,224]{1,0:T(8,128)(2,1)S(1)}, u32[]{:S(2)}, u32[]{:S(2)}) %collective-permute-start.4) | collective-permute-done | bytes 258080 | tf_op jit(solution)/shard_map/ppermute | solution.py:28
  18.0 11.9 %collective-permute-start.5 = (bf16[576,224]{1,0:T(8,128)(2,1)}, bf16[576,224]{1,0:T(8,128)(2,1)}, u32[]{:S(2)}, u32[]{:S(2)}) collective-permute-start(bf16[576,224]{1,0:T(8,128)(2,1)} %get-tuple-element.34.refs_4_.refs_2_), channel_id=1, source_target_pairs={{0,1},{1,0},{2,3},{3,2},{4,5},{5,4},{6,7},{7,6},{8,9},{9,8},{10,11... | collective-permute-start | bytes 774152 | tf_op jit(solution)/shard_map/ppermute | solution.py:28
  29.9 4.9 %collective-permute-done.3.refs_9_.refs_6_.refs_4_ = bf16[576,224]{1,0:T(8,128)(2,1)S(1)} collective-permute-done((bf16[576,224]{1,0:T(8,128)(2,1)}, bf16[576,224]{1,0:T(8,128)(2,1)S(1)}, u32[]{:S(2)}, u32[]{:S(2)}) %collective-permute-start.3) | collective-permute-done | bytes 258080 | tf_op jit(solution)/shard_map/ppermute | solution.py:28
  34.8 2.2 %absorb_queries.1 = (bf16[16,40,144]{2,1,0:T(8,128)(2,1)S(1)}, bf16[4,16,576]{2,1,0:T(8,128)(2,1)S(1)}, bf16[8,128]{1,0:T(8,128)(2,1)S(1)}) custom-call(s32[16]{0:T(128)} %refs_0_.8, bf16[640,256]{1,0:T(8,128)(2,1)S(1)} %get-tuple-element.30.refs_1_.refs_0_, bf16[640,256]{1,0:T(8,128)(2,1)S(1)} %collective-permute-done.refs_2_.refs_0_, ...), custom_call_target="tpu_custom_call" | custom-call | tf_op jit(solution)/shard_map/absorb_queries/pallas_call | solution.py:258
  37.7 3.9 %all-to-all-start = ((bf16[16,40,144]{2,1,0:T(8,128)(2,1)}), bf16[16,40,144]{2,1,0:T(8,128)(2,1)S(1)}, u32[]{:S(2)}, u32[]{:S(2)}) async-start(bf16[16,40,144]{2,1,0:T(8,128)(2,1)} %copy-done.1), calls=%async_computation | async-start | bytes 655360 | tf_op jit(solution)/shard_map/all_to_all | solution.py:720
  41.6 2.6 %project.2 = (bf16[144,576]{1,0:T(8,128)(2,1)}, bf16[144,576]{1,0:T(8,128)(2,1)}, bf16[144,576]{1,0:T(8,128)(2,1)}) custom-call(bf16[640,256]{1,0:T(8,128)(2,1)S(1)} %collective-permute-done.refs_2_.refs_0_, bf16[1664,256]{1,0:T(8,128)(2,1)S(1)} %collective-permute-done.1.refs_3_.refs_1_.refs_7_, ...), custom_call_target="tpu_custom_call" | custom-call | tf_op jit(solution)/shard_map/project/pallas_call | solution.py:152
  44.1 1.9 %collective-permute-start.7 = (bf16[144,576]{1,0:T(8,128)(2,1)}, bf16[144,576]{1,0:T(8,128)(2,1)S(1)}, u32[]{:S(2)}, u32[]{:S(2)}) collective-permute-start(bf16[144,576]{1,0:T(8,128)(2,1)} %get-tuple-element.38), channel_id=1, source_target_pairs={{0,8},{4,12},{8,0},{12,4},{1,9},{5,13},{9,1},{13,5},{2,10},{6,14},... | collective-permute-start | bytes 497672 | tf_op jit(solution)/shard_map/ppermute | solution.py:28
  46.3 1.6 %project.3.refs_0_.refs_4_ = bf16[144,576]{1,0:T(8,128)(2,1)S(1)} custom-call(bf16[640,256]{1,0:T(8,128)(2,1)S(1)} %get-tuple-element.30.refs_1_.refs_0_, bf16[4,16,576]{2,1,0:T(8,128)(2,1)S(1)} %get-tuple-element.35.refs_3_.refs_1_, bf16[576,224]{1,0:T(8,128)(2,1)} %get-tuple-element.34.refs_4_.refs_2_, ...), custom_call_target="tpu_custom_call" | custom-call | tf_op jit(solution)/shard_map/project/pallas_call | solution.py:152
  47.8 5.2 %all-to-all-done.block_ref = bf16[16,40,144]{2,1,0:T(8,128)(2,1)S(1)} async-done(((bf16[16,40,144]{2,1,0:T(8,128)(2,1)}), bf16[16,40,144]{2,1,0:T(8,128)(2,1)S(1)}, u32[]{:S(2)}, u32[]{:S(2)}) %all-to-all-start) | async-done | bytes 184352 | tf_op jit(solution)/shard_map/all_to_all | solution.py:720
  54.2 2.7 %collective-permute-done.8.refs_3_.refs_7_ = bf16[144,576]{1,0:T(8,128)(2,1)S(1)} collective-permute-done((bf16[144,576]{1,0:T(8,128)(2,1)}, bf16[144,576]{1,0:T(8,128)(2,1)S(1)}, u32[]{:S(2)}, u32[]{:S(2)}) %collective-permute-start.8) | collective-permute-done | bytes 165920 | tf_op jit(solution)/shard_map/ppermute | solution.py:28
  56.9 1.8 %attend.1 = (bf16[32,512]{1,0:T(8,128)(2,1)S(1)}, bf16[32,512]{1,0:T(8,128)(2,1)S(1)}, bf16[32,512]{1,0:T(8,128)(2,1)S(1)}, bf16[32,512]{1,0:T(8,128)(2,1)S(1)}, bf16[8,128]{1,0:T(8,128)(2,1)S(1)}) custom-call(bf16[144,576]{1,0:T(8,128)(2,1)S(1)} %project.3.refs_0_.refs_4_, bf16[144,576]{1,0:T(8,128)(2,1)S(1)} %collective-permute-done.6.refs_1_.refs_5_, ...), custom_call_target="tpu_custom_call" | custom-call | tf_op jit(solution)/shard_map/attend/pallas_call | solution.py:432
  59.3 1.5 %collective-permute-start.9 = (bf16[32,512]{1,0:T(8,128)(2,1)S(1)}, bf16[32,512]{1,0:T(8,128)(2,1)S(1)}, u32[]{:S(2)}, u32[]{:S(2)}) collective-permute-start(bf16[32,512]{1,0:T(8,128)(2,1)S(1)} %get-tuple-element.46), channel_id=1, source_target_pairs={{0,1},{1,0},{2,3},{3,2},{4,5},{5,4},{6,7},{7,6},{8,9},{9,8},{10,11... | collective-permute-start | bytes 98312 | tf_op jit(solution)/shard_map/ppermute | solution.py:28
  60.7 1.9 %collective-permute-start.10 = (bf16[32,512]{1,0:T(8,128)(2,1)S(1)}, bf16[32,512]{1,0:T(8,128)(2,1)S(1)}, u32[]{:S(2)}, u32[]{:S(2)}) collective-permute-start(bf16[32,512]{1,0:T(8,128)(2,1)S(1)} %get-tuple-element.47), channel_id=1, source_target_pairs={{0,2},{1,3},{2,0},{3,1},{4,6},{5,7},{6,4},{7,5},{8,10},{9,11},{10,... | collective-permute-start | bytes 98312 | tf_op jit(solution)/shard_map/ppermute | solution.py:28
  63.8 3.1 %fetch.4.refs_10_.refs_9_ = bf16[4,3584,256]{2,1,0:T(8,128)(2,1)S(1)} custom-call(bf16[4,3584,256]{2,1,0:T(8,128)(2,1)} %refs_0_.7, bf16[8,128]{1,0:T(8,128)(2,1)S(1)} %get-tuple-element.52.refs_1_.refs_11_), custom_call_target="tpu_custom_call" | custom-call | bytes 14680064 | tf_op jit(solution)/shard_map/fetch/pallas_call | solution.py:63
  68.4 2.0 %head_products.1.refs_0_.refs_4_ = bf16[8,2176]{1,0:T(8,128)(2,1)S(1)} custom-call(s32[16]{0:T(128)} %refs_0_.8, bf16[32,512]{1,0:T(8,128)(2,1)S(1)} %get-tuple-element.45.refs_1_, bf16[32,512]{1,0:T(8,128)(2,1)S(1)} %collective-permute-done.9.refs_2_, bf16[32,512]{1,0:T(8,128)(2,1)S(1)} %collective-permute-done.10.refs_3_, ...), custom_call_target="tpu_custom_call" | custom-call | tf_op jit(solution)/shard_map/head_products/pallas_call | solution.py:508
  72.2 2.0 %fetch.5.refs_4_ = bf16[2048,896]{1,0:T(8,128)(2,1)S(1)} custom-call(bf16[2048,896]{1,0:T(8,128)(2,1)} %refs_0_.9), custom_call_target="tpu_custom_call" | custom-call | bytes 7340032 | tf_op jit(solution)/shard_map/fetch/pallas_call | solution.py:63
  76.9 3.0 %collective-permute-start.17 = (bf16[32,896]{1,0:T(8,128)(2,1)S(1)}, bf16[32,896]{1,0:T(8,128)(2,1)S(1)}, u32[]{:S(2)}, u32[]{:S(2)}) collective-permute-start(bf16[32,896]{1,0:T(8,128)(2,1)S(1)} %output_product.1.refs_1_.refs_0_), channel_id=1, source_target_pairs={{0,1},{1,0},{2,3},{3,2},{4,5},{5,4},{6,7},{7,6},{8,9},{9,8},{10,11... | collective-permute-start | bytes 172040 | tf_op jit(solution)/shard_map/ppermute | solution.py:28
  79.9 3.1 %fetch.6.refs_8_.refs_10_ = bf16[4,3584,256]{2,1,0:T(8,128)(2,1)S(1)} custom-call(bf16[4,3584,256]{2,1,0:T(8,128)(2,1)} %refs_0_.10, bf16[32,896]{1,0:T(8,128)(2,1)S(1)} %output_product.1.refs_1_.refs_0_), custom_call_target="tpu_custom_call" | custom-call | bytes 14680064 | tf_op jit(solution)/shard_map/fetch/pallas_call | solution.py:63
  85.7 3.1 %fetch.7.refs_11_ = bf16[4,256,3584]{2,1,0:T(8,128)(2,1)S(1)} custom-call(bf16[4,256,3584]{2,1,0:T(8,128)(2,1)} %refs_0_.11, bf16[4,8,896]{2,1,0:T(8,128)(2,1)S(1)} %mix.1.refs_1_.refs_0_), custom_call_target="tpu_custom_call" | custom-call | bytes 14680064 | tf_op jit(solution)/shard_map/fetch/pallas_call | solution.py:63
  89.3 5.0 %run_experts.1 = (bf16[16,8,896]{2,1,0:T(8,128)(2,1)S(1)}, bf16[4,8,896]{2,1,0:T(8,128)(2,1)S(1)}) custom-call(bf16[4,8,896]{2,1,0:T(8,128)(2,1)S(1)} %mix.1.refs_1_.refs_0_, bf16[4,8,896]{2,1,0:T(8,128)(2,1)S(1)} %collective-permute-done.20.refs_1_, bf16[4,8,896]{2,1,0:T(8,128)(2,1)S(1)} %collective-permute-done.21.refs_2_, ...), custom_call_target="tpu_custom_call" | custom-call | tf_op jit(solution)/shard_map/run_experts/pallas_call | solution.py:641
  94.3 12.0 %all_to_all.10.block_ref = bf16[16,8,896]{2,1,0:T(8,128)(2,1)S(1)} all-to-all(bf16[16,8,896]{2,1,0:T(8,128)(2,1)S(1)} %get-tuple-element.53), channel_id=1, replica_groups=mesh['groups'=2,'expert'=4,'section'=4] {'expert','section'}, dimensions={0} | all-to-all | bytes 458752 | tf_op jit(solution)/shard_map/all_to_all | solution.py:765
  (52 shorter events, 14.2 us)
Async XLA Ops:
  3.0 31.7 %collective-permute-start.1 = (bf16[1664,256]{1,0:T(8,128)(2,1)S(1)}, bf16[1664,256]{1,0:T(8,128)(2,1)S(1)}, u32[]{:S(2)}, u32[]{:S(2)}) collective-permute-start(bf16[1664,256]{1,0:T(8,128)(2,1)S(1)} %get-tuple-element.32), channel_id=1, source_target_pairs={{0,8},{4,12},{8,0},{12,4},{1,9},{5,13},{9,1},{13,5},{2,10},{6,14},... | collective-permute-start | bytes 2555912 | tf_op jit(solution)/shard_map/ppermute | solution.py:28
  6.0 12.0 %collective-permute-start.4 = (bf16[576,224]{1,0:T(8,128)(2,1)}, bf16[576,224]{1,0:T(8,128)(2,1)S(1)}, u32[]{:S(2)}, u32[]{:S(2)}) collective-permute-start(bf16[576,224]{1,0:T(8,128)(2,1)} %get-tuple-element.34.refs_4_.refs_2_), channel_id=1, source_target_pairs={{0,3},{1,2},{2,1},{3,0},{4,7},{5,6},{6,5},{7,4},{8,11},{9,10},{10,... | collective-permute-start | bytes 774152 | tf_op jit(solution)/shard_map/ppermute | solution.py:28
  9.6 25.2 %collective-permute-start = (bf16[640,256]{1,0:T(8,128)(2,1)S(1)}, bf16[640,256]{1,0:T(8,128)(2,1)S(1)}, u32[]{:S(2)}, u32[]{:S(2)}) collective-permute-start(bf16[640,256]{1,0:T(8,128)(2,1)S(1)} %get-tuple-element.31), channel_id=1, source_target_pairs={{0,4},{4,0},{8,12},{12,8},{1,5},{5,1},{9,13},{13,9},{2,6},{6,2},{1... | collective-permute-start | bytes 983048 | tf_op jit(solution)/shard_map/ppermute | solution.py:28
  9.6 25.2 %collective-permute-start.2 = (bf16[640,256]{1,0:T(8,128)(2,1)S(1)}, bf16[640,256]{1,0:T(8,128)(2,1)S(1)}, u32[]{:S(2)}, u32[]{:S(2)}) collective-permute-start(bf16[640,256]{1,0:T(8,128)(2,1)S(1)} %get-tuple-element.33), channel_id=1, source_target_pairs={{0,12},{4,8},{8,4},{12,0},{1,13},{5,9},{9,5},{13,1},{2,14},{6,10},... | collective-permute-start | bytes 983048 | tf_op jit(solution)/shard_map/ppermute | solution.py:28
  10.2 24.5 %collective-permute-start.3 = (bf16[576,224]{1,0:T(8,128)(2,1)}, bf16[576,224]{1,0:T(8,128)(2,1)S(1)}, u32[]{:S(2)}, u32[]{:S(2)}) collective-permute-start(bf16[576,224]{1,0:T(8,128)(2,1)} %get-tuple-element.34.refs_4_.refs_2_), channel_id=1, source_target_pairs={{0,2},{1,3},{2,0},{3,1},{4,6},{5,7},{6,4},{7,5},{8,10},{9,11},{10,... | collective-permute-start | bytes 774152 | tf_op jit(solution)/shard_map/ppermute | solution.py:28
  18.0 23.6 %collective-permute-start.5 = (bf16[576,224]{1,0:T(8,128)(2,1)}, bf16[576,224]{1,0:T(8,128)(2,1)}, u32[]{:S(2)}, u32[]{:S(2)}) collective-permute-start(bf16[576,224]{1,0:T(8,128)(2,1)} %get-tuple-element.34.refs_4_.refs_2_), channel_id=1, source_target_pairs={{0,1},{1,0},{2,3},{3,2},{4,5},{5,4},{6,7},{7,6},{8,9},{9,8},{10,11... | collective-permute-start | bytes 774152 | tf_op jit(solution)/shard_map/ppermute | solution.py:28
  37.7 15.3 %all-to-all-start = ((bf16[16,40,144]{2,1,0:T(8,128)(2,1)}), bf16[16,40,144]{2,1,0:T(8,128)(2,1)S(1)}, u32[]{:S(2)}, u32[]{:S(2)}) async-start(bf16[16,40,144]{2,1,0:T(8,128)(2,1)} %copy-done.1), calls=%async_computation | async-start | bytes 655360 | tf_op jit(solution)/shard_map/all_to_all | solution.py:720
  44.1 10.1 %collective-permute-start.7 = (bf16[144,576]{1,0:T(8,128)(2,1)}, bf16[144,576]{1,0:T(8,128)(2,1)S(1)}, u32[]{:S(2)}, u32[]{:S(2)}) collective-permute-start(bf16[144,576]{1,0:T(8,128)(2,1)} %get-tuple-element.38), channel_id=1, source_target_pairs={{0,8},{4,12},{8,0},{12,4},{1,9},{5,13},{9,1},{13,5},{2,10},{6,14},... | collective-permute-start | bytes 497672 | tf_op jit(solution)/shard_map/ppermute | solution.py:28
  46.1 10.8 %collective-permute-start.8 = (bf16[144,576]{1,0:T(8,128)(2,1)}, bf16[144,576]{1,0:T(8,128)(2,1)S(1)}, u32[]{:S(2)}, u32[]{:S(2)}) collective-permute-start(bf16[144,576]{1,0:T(8,128)(2,1)} %get-tuple-element.39), channel_id=1, source_target_pairs={{0,12},{4,8},{8,4},{12,0},{1,13},{5,9},{9,5},{13,1},{2,14},{6,10},... | collective-permute-start | bytes 497672 | tf_op jit(solution)/shard_map/ppermute | solution.py:28
  46.1 10.8 %collective-permute-start.6 = (bf16[144,576]{1,0:T(8,128)(2,1)}, bf16[144,576]{1,0:T(8,128)(2,1)S(1)}, u32[]{:S(2)}, u32[]{:S(2)}) collective-permute-start(bf16[144,576]{1,0:T(8,128)(2,1)} %get-tuple-element.37.refs_6_), channel_id=1, source_target_pairs={{0,4},{4,0},{8,12},{12,8},{1,5},{5,1},{9,13},{13,9},{2,6},{6,2},{1... | collective-permute-start | bytes 497672 | tf_op jit(solution)/shard_map/ppermute | solution.py:28
  58.7 9.7 %collective-permute-start.13 = (bf16[1664,256]{1,0:T(8,128)(2,1)S(1)}, bf16[1664,256]{1,0:T(8,128)(2,1)S(1)}, u32[]{:S(2)}, u32[]{:S(2)}) collective-permute-start(bf16[1664,256]{1,0:T(8,128)(2,1)S(1)} %collective-permute-done.1.refs_3_.refs_1_.refs_7_), channel_id=1, source_target_pairs={{0,4},{4,0},{8,12},{12,8},{1,5},{5,1},{9,13},{13,9},{2,6},{6,2},{1... | collective-permute-start | bytes 2555912 | tf_op jit(solution)/shard_map/ppermute | solution.py:28
  58.8 9.6 %collective-permute-start.12 = (bf16[16,128,128]{2,1,0:T(8,128)(2,1)S(1)}, bf16[16,128,128]{2,1,0:T(8,128)(2,1)S(1)}, u32[]{:S(2)}, u32[]{:S(2)}) collective-permute-start(bf16[16,128,128]{2,1,0:T(8,128)(2,1)S(1)} %copy-done), channel_id=1, source_target_pairs={{0,4},{4,0},{8,12},{12,8},{1,5},{5,1},{9,13},{13,9},{2,6},{6,2},{1... | collective-permute-start | bytes 1572872 | tf_op jit(solution)/shard_map/ppermute | solution.py:28
  59.3 7.6 %collective-permute-start.9 = (bf16[32,512]{1,0:T(8,128)(2,1)S(1)}, bf16[32,512]{1,0:T(8,128)(2,1)S(1)}, u32[]{:S(2)}, u32[]{:S(2)}) collective-permute-start(bf16[32,512]{1,0:T(8,128)(2,1)S(1)} %get-tuple-element.46), channel_id=1, source_target_pairs={{0,1},{1,0},{2,3},{3,2},{4,5},{5,4},{6,7},{7,6},{8,9},{9,8},{10,11... | collective-permute-start | bytes 98312 | tf_op jit(solution)/shard_map/ppermute | solution.py:28
  60.7 6.2 %collective-permute-start.10 = (bf16[32,512]{1,0:T(8,128)(2,1)S(1)}, bf16[32,512]{1,0:T(8,128)(2,1)S(1)}, u32[]{:S(2)}, u32[]{:S(2)}) collective-permute-start(bf16[32,512]{1,0:T(8,128)(2,1)S(1)} %get-tuple-element.47), channel_id=1, source_target_pairs={{0,2},{1,3},{2,0},{3,1},{4,6},{5,7},{6,4},{7,5},{8,10},{9,11},{10,... | collective-permute-start | bytes 98312 | tf_op jit(solution)/shard_map/ppermute | solution.py:28
  62.7 5.7 %collective-permute-start.11 = (bf16[32,512]{1,0:T(8,128)(2,1)S(1)}, bf16[32,512]{1,0:T(8,128)(2,1)S(1)}, u32[]{:S(2)}, u32[]{:S(2)}) collective-permute-start(bf16[32,512]{1,0:T(8,128)(2,1)S(1)} %get-tuple-element.48), channel_id=1, source_target_pairs={{0,3},{1,2},{2,1},{3,0},{4,7},{5,6},{6,5},{7,4},{8,11},{9,10},{10,... | collective-permute-start | bytes 98312 | tf_op jit(solution)/shard_map/ppermute | solution.py:28
  70.4 3.9 %collective-permute-start.16 = (bf16[8,2176]{1,0:T(8,128)(2,1)S(1)}, bf16[8,2176]{1,0:T(8,128)(2,1)S(1)}, u32[]{:S(2)}, u32[]{:S(2)}) collective-permute-start(bf16[8,2176]{1,0:T(8,128)(2,1)S(1)} %head_products.1.refs_0_.refs_4_), channel_id=1, source_target_pairs={{0,12},{4,8},{8,4},{12,0},{1,13},{5,9},{9,5},{13,1},{2,14},{6,10},... | collective-permute-start | bytes 104456 | tf_op jit(solution)/shard_map/ppermute | solution.py:28
  70.4 4.3 %collective-permute-start.15 = (bf16[8,2176]{1,0:T(8,128)(2,1)S(1)}, bf16[8,2176]{1,0:T(8,128)(2,1)S(1)}, u32[]{:S(2)}, u32[]{:S(2)}) collective-permute-start(bf16[8,2176]{1,0:T(8,128)(2,1)S(1)} %head_products.1.refs_0_.refs_4_), channel_id=1, source_target_pairs={{0,8},{4,12},{8,0},{12,4},{1,9},{5,13},{9,1},{13,5},{2,10},{6,14},... | collective-permute-start | bytes 104456 | tf_op jit(solution)/shard_map/ppermute | solution.py:28
  71.4 3.3 %collective-permute-start.14 = (bf16[8,2176]{1,0:T(8,128)(2,1)S(1)}, bf16[8,2176]{1,0:T(8,128)(2,1)S(1)}, u32[]{:S(2)}, u32[]{:S(2)}) collective-permute-start(bf16[8,2176]{1,0:T(8,128)(2,1)S(1)} %head_products.1.refs_0_.refs_4_), channel_id=1, source_target_pairs={{0,4},{4,0},{8,12},{12,8},{1,5},{5,1},{9,13},{13,9},{2,6},{6,2},{1... | collective-permute-start | bytes 104456 | tf_op jit(solution)/shard_map/ppermute | solution.py:28
  75.4 7.6 %collective-permute-start.19 = (bf16[32,896]{1,0:T(8,128)(2,1)S(1)}, bf16[32,896]{1,0:T(8,128)(2,1)S(1)}, u32[]{:S(2)}, u32[]{:S(2)}) collective-permute-start(bf16[32,896]{1,0:T(8,128)(2,1)S(1)} %output_product.1.refs_1_.refs_0_), channel_id=1, source_target_pairs={{0,3},{1,2},{2,1},{3,0},{4,7},{5,6},{6,5},{7,4},{8,11},{9,10},{10,... | collective-permute-start | bytes 172040 | tf_op jit(solution)/shard_map/ppermute | solution.py:28
  76.8 6.8 %collective-permute-start.18 = (bf16[32,896]{1,0:T(8,128)(2,1)S(1)}, bf16[32,896]{1,0:T(8,128)(2,1)S(1)}, u32[]{:S(2)}, u32[]{:S(2)}) collective-permute-start(bf16[32,896]{1,0:T(8,128)(2,1)S(1)} %output_product.1.refs_1_.refs_0_), channel_id=1, source_target_pairs={{0,2},{1,3},{2,0},{3,1},{4,6},{5,7},{6,4},{7,5},{8,10},{9,11},{10,... | collective-permute-start | bytes 172040 | tf_op jit(solution)/shard_map/ppermute | solution.py:28
  76.9 6.8 %collective-permute-start.17 = (bf16[32,896]{1,0:T(8,128)(2,1)S(1)}, bf16[32,896]{1,0:T(8,128)(2,1)S(1)}, u32[]{:S(2)}, u32[]{:S(2)}) collective-permute-start(bf16[32,896]{1,0:T(8,128)(2,1)S(1)} %output_product.1.refs_1_.refs_0_), channel_id=1, source_target_pairs={{0,1},{1,0},{2,3},{3,2},{4,5},{5,4},{6,7},{7,6},{8,9},{9,8},{10,11... | collective-permute-start | bytes 172040 | tf_op jit(solution)/shard_map/ppermute | solution.py:28
  83.8 5.0 %collective-permute-start.22 = (bf16[4,8,896]{2,1,0:T(8,128)(2,1)S(1)}, bf16[4,8,896]{2,1,0:T(8,128)(2,1)S(1)}, u32[]{:S(2)}, u32[]{:S(2)}) collective-permute-start(bf16[4,8,896]{2,1,0:T(8,128)(2,1)S(1)} %mix.1.refs_1_.refs_0_), channel_id=1, source_target_pairs={{0,12},{4,8},{8,4},{12,0},{1,13},{5,9},{9,5},{13,1},{2,14},{6,10},... | collective-permute-start | bytes 172040 | tf_op jit(solution)/shard_map/ppermute | solution.py:28
  84.3 5.0 %collective-permute-start.21 = (bf16[4,8,896]{2,1,0:T(8,128)(2,1)S(1)}, bf16[4,8,896]{2,1,0:T(8,128)(2,1)S(1)}, u32[]{:S(2)}, u32[]{:S(2)}) collective-permute-start(bf16[4,8,896]{2,1,0:T(8,128)(2,1)S(1)} %mix.1.refs_1_.refs_0_), channel_id=1, source_target_pairs={{0,8},{4,12},{8,0},{12,4},{1,9},{5,13},{9,1},{13,5},{2,10},{6,14},... | collective-permute-start | bytes 172040 | tf_op jit(solution)/shard_map/ppermute | solution.py:28
  85.5 3.8 %collective-permute-start.20 = (bf16[4,8,896]{2,1,0:T(8,128)(2,1)S(1)}, bf16[4,8,896]{2,1,0:T(8,128)(2,1)S(1)}, u32[]{:S(2)}, u32[]{:S(2)}) collective-permute-start(bf16[4,8,896]{2,1,0:T(8,128)(2,1)S(1)} %mix.1.refs_1_.refs_0_), channel_id=1, source_target_pairs={{0,4},{4,0},{8,12},{12,8},{1,5},{5,1},{9,13},{13,9},{2,6},{6,2},{1... | collective-permute-start | bytes 172040 | tf_op jit(solution)/shard_map/ppermute | solution.py:28
  (4 other events, 178.0 us)

commit v11 on v8

--- a/solution.py
+++ b/solution.py
@@ -81,14 +81,11 @@
     return held
 
 
-def cut_kernel(sections, experts, piece, x_ref, query_ref, w_ref, *refs):
-    w_out_ref, *out_refs, w_held, held = refs
+def cut_kernel(sections, experts, piece, x_ref, query_ref, *refs):
+    out_refs, held = refs[-1 - experts : -1], refs[-1]
     rank = lax.axis_index("expert")
     steps, sources, heads, wide = query_ref.shape
     rows = x_ref.shape[0]
-    for target in range(experts):
-        w_held[target] = w_ref[:, target * piece : (target + 1) * piece]
-    w_out_ref[...] = w_held[rank]
     for target in range(experts):
         for section in range(sections):
             at = (section * experts + target) * piece
@@ -101,7 +98,7 @@
                 ref[at : at + heads, :wide] = query_ref[step, source]
 
 
-def cut_columns(x, queries, w_turned, sections, experts):
+def cut_columns(x, queries, sections, experts, after):
     rows, width = x.shape
     piece = width // (sections * experts)
     steps, sources, heads, wide = queries.shape
@@ -110,14 +107,13 @@
     )
     return pl.pallas_call(
         functools.partial(cut_kernel, sections, experts, piece),
-        out_shape=[jax.ShapeDtypeStruct((w_turned.shape[0], piece), x.dtype)] + [block] * experts,
-        scratch_shapes=[
-            pltpu.VMEM((experts, w_turned.shape[0], piece), x.dtype),
-            pltpu.VMEM((experts, sections * rows, piece), x.dtype),
-        ],
-        compiler_params=params(x, block, w_turned, scale=6),
+        out_shape=[block] * experts,
+        in_specs=[pl.BlockSpec(memory_space=pltpu.VMEM)] * 2
+        + [pl.BlockSpec(memory_space=pl.ANY)] * len(after),
+        scratch_shapes=[pltpu.VMEM((experts, sections * rows, piece), x.dtype)],
+        compiler_params=params(x, block, scale=6),
         name="cut_columns",
-    )(*at_home(x, queries, w_turned))
+    )(*at_home(x, queries), *after)
 
 
 def project_kernel(count, first, rows, *refs):
@@ -178,7 +174,7 @@
             value = query_ref[owner, step, index // sources].astype(f32)
             at = pl.ds(pl.multiple_of((index * steps + step) * heads, heads), heads)
             picked[at, :] = value[:, :nope]
-            ropes[at, :] = value[:, nope:].astype(bf16)
+            ropes[at, :rope] = value[:, nope:]
         return carry
 
     if count <= 16:
@@ -193,12 +189,22 @@
             spare = jnp.zeros((count * steps, made.shape[1] - chunk), f32)
             value = jnp.concatenate([value, spare], axis=1)
         made[at, :] = value
-    small = width - chunk
-    pair = lax.broadcasted_iota(jnp.int32, (rope, small), 0)
-    pair = pair == lax.broadcasted_iota(jnp.int32, (rope, small), 1) + rank * small
-    turned = jnp.dot(
-        ropes[...], jnp.where(pair, 1.0, 0.0).astype(bf16), preferred_element_type=f32
-    )
+    small = (rope + experts - 1) // experts
+    lanes = rope if width != chunk else width
+    groups = width // small if width == chunk else 1
+    source_lane = lax.broadcasted_iota(jnp.int32, (rope, lanes), 0)
+    lane = lax.broadcasted_iota(jnp.int32, (rope, lanes), 1)
+    turned = 0
+    for group in range(groups):
+        pair = (source_lane == lane - group * small + rank * small) & (
+            (lane >= group * small) & (lane < (group + 1) * small)
+        )
+        at = pl.ds(group, count * steps * heads // groups, stride=groups)
+        turned = turned + jnp.dot(
+            ropes[at, :][:, :rope].astype(bf16),
+            jnp.where(pair, 1.0, 0.0).astype(bf16),
+            preferred_element_type=f32,
+        )
     own = jnp.concatenate([own_ref[step] for step in range(steps)], axis=0).astype(f32)
     lines, column = columns.shape[1:]
     for target in range(experts):
@@ -222,28 +228,57 @@
         preferred_element_type=f32,
     )
     for source in range(experts):
-        lines = [
-            fresh[step * sources + source :, part * width : (part + 1) * width][:1]
-            for step in range(steps)
-            for part in range(experts)
-        ]
+        picks = [step * sources + source for step in range(steps)]
+        if width == chunk:
+            latent = width * experts
+            lines = [
+                fresh[pick:, part * width : (part + 1) * width][:1]
+                for pick in picks
+                for part in range(experts)
+            ]
+            lines.append(
+                jnp.concatenate([fresh[pick:, latent:][:1] for pick in picks], axis=1)
+            )
+        else:
+            lines = [
+                fresh[pick:, part * width : (part + 1) * width][:1]
+                for pick in picks
+                for part in range(experts)
+            ]
         lines = jnp.concatenate(lines, axis=0).astype(bf16)
         for section in range(sections):
             index = source * sections + section
             at = slice(index * block, (index + 1) * block)
-            value = jnp.concatenate([made[at, :chunk], turned[at]], axis=1)
-            out_ref[index, :block, :] = value.astype(bf16)
-            out_ref[index, block:, :] = lines
-
-
-def absorb_queries(table, queries, shape, w_uk, own, gain, w_turned, prompts, sections):
+            if width == chunk:
+                few = block // groups
+                out_ref[index, :block, :] = made[at, :chunk].astype(bf16)
+                tail = [turned[index * few : (index + 1) * few].astype(bf16), lines]
+                spare = out_ref.shape[1] - block - few - lines.shape[0]
+                if spare:
+                    tail.append(jnp.zeros((spare, width), bf16))
+                out_ref[index, block:, :] = jnp.concatenate(tail, axis=0)
+            else:
+                value = jnp.concatenate([made[at, :chunk], turned[at, :small]], axis=1)
+                out_ref[index, :block, :] = value.astype(bf16)
+                out_ref[index, block:, :] = lines
+
+
+def block_shape(prompts, steps, heads, experts, chunk, rope):
+    rows = prompts * steps * heads
+    small = rope // experts
+    if chunk == 128 and small * 8 == chunk and steps * rope == chunk:
+        rows = rows + rows // 8 + steps * experts + 1
+        return rows + -rows % 16, chunk
+    return rows + steps * experts, chunk + small
+
+
+def absorb_queries(table, queries, shape, w_uk, own, gain, w_turned, prompts, sections, after):
     experts = len(queries)
     steps, sources, heads, wide = shape
     _, nope, chunk = w_uk.shape
-    width = chunk + (wide - nope) // experts
+    rows, width = block_shape(prompts, steps, heads, experts, chunk, wide - nope)
     block, column = own.shape[0] * own.shape[1], own.shape[2] // experts
     cache_width = w_turned.shape[0]
-    rows = prompts * steps * heads + steps * experts
     count = experts * sources * steps * heads
     held = pl.BlockSpec(memory_space=pltpu.VMEM)
     return pl.pallas_call(
@@ -256,11 +291,12 @@
             jax.ShapeDtypeStruct((8, 128), jnp.bfloat16),
         ],
         in_specs=[pl.BlockSpec(memory_space=pltpu.SMEM)]
-        + [held] * (experts + 4),
+        + [held] * (experts + 4)
+        + [pl.BlockSpec(memory_space=pl.ANY)] * len(after),
         out_specs=[held] * 3,
         scratch_shapes=[
             pltpu.VMEM((count, nope), jnp.float32),
-            pltpu.VMEM((count, wide - nope), jnp.bfloat16),
+            pltpu.VMEM((count, max(wide - nope, 128)), jnp.float32),
             pltpu.VMEM((count, max(chunk, 128)), jnp.float32),
             pltpu.VMEM(
                 (sections, own.shape[0] * own.shape[1], w_turned.shape[1]), jnp.bfloat16
@@ -270,7 +306,7 @@
         ],
         compiler_params=params(*queries, w_uk, own, w_turned, scale=4),
         name="absorb_queries",
-    )(*at_home(table), *queries, *at_home(w_uk, own, gain, w_turned))
+    )(*at_home(table), *queries, *at_home(w_uk, own, gain, w_turned), *after)
 
 
 def turn(values, cosine, sine):
@@ -287,11 +323,13 @@
 def gather_kernel(
     prompts, experts, sections, sources, heads, steps, latent, length_ref, owner_ref, gain_ref,
     cosine_ref, sine_ref, block_ref, query_ref, query_rope_ref, recent_ref, recent_rope_ref,
-    cosine_held, sine_held
+    cosine_held, sine_held, ropes_held
 ):
     f32, bf16 = jnp.float32, jnp.bfloat16
     rows = steps * heads
     chunk = latent // experts
+    whole = block_ref.shape[2] == chunk
+    extra = prompts * rows // 8 if whole else 0
     first = lax.axis_index("expert") * sources + lax.axis_index("section") * prompts
     gain = gain_ref[...][None]
     for prompt in range(prompts):
@@ -305,6 +343,32 @@
                 sine_ref[pl.ds(length + step, 1), :], (heads, sine_ref.shape[1])
             )
         cosine, sine = cosine_held[...], sine_held[...]
+        if whole:
+            few = rows // 8
+            small = cosine.shape[1] // experts
+            low = prompts * rows + prompt * few
+            tail = jnp.concatenate(
+                [
+                    jnp.concatenate(
+                        [block_ref[i * sections + section, low : low + few, :]
+                         for i in range(experts)],
+                        axis=1,
+                    )
+                    for section in range(sections)
+                ],
+                axis=0,
+            )
+            shape = (experts * chunk, experts * small)
+            source_lane = lax.broadcasted_iota(jnp.int32, shape, 0)
+            lane = lax.broadcasted_iota(jnp.int32, shape, 1)
+            bits = small.bit_length() - 1
+            lane = lax.shift_right_logical(lane, bits) * chunk + (lane & (small - 1))
+            for group in range(8):
+                pair = jnp.where(source_lane == lane + group * small, 1.0, 0.0).astype(bf16)
+                value = jnp.dot(tail, pair, preferred_element_type=f32)
+                pad = ropes_held.shape[1] - value.shape[1]
+                value = jnp.concatenate([value, jnp.zeros((value.shape[0], pad), f32)], axis=1)
+                ropes_held[pl.ds(group, sections * few, stride=8), :] = value
         at = slice(prompt * rows, (prompt + 1) * rows)
         for section in range(sections):
             pieces = [block_ref[i * sections + section, at, :] for i in range(experts)]
@@ -312,18 +376,27 @@
             query_ref[prompt, to, :] = jnp.concatenate(
                 [piece[:, :chunk] for piece in pieces], axis=1
             )
-            rope = jnp.concatenate([piece[:, chunk:].astype(f32) for piece in pieces], axis=1)
+            if whole:
+                rope = ropes_held[to, : cosine.shape[1]]
+            else:
+                rope = jnp.concatenate(
+                    [piece[:, chunk:].astype(f32) for piece in pieces], axis=1
+                )
             query_rope_ref[prompt, to, :] = turn(rope, cosine, sine).astype(bf16)
         lines = 0
         for section in range(sections):
             lines = lines + block_ref[
-                owner * sections + section, prompts * rows :, :
+                owner * sections + section, prompts * rows + extra :, :
             ].astype(f32)
         recent, recent_rope = [], []
         for step in range(steps):
-            line = jnp.concatenate(
-                [lines[step * experts + part :][:1] for part in range(experts)], axis=1
-            )
+            parts = [lines[step * experts + part :][:1] for part in range(experts)]
+            if whole:
+                end = cosine.shape[1]
+                parts.append(
+                    lines[steps * experts :][:1, step * end : (step + 1) * end]
+                )
+            line = jnp.concatenate(parts, axis=1)
             recent.append(scaled(line[:, :latent], gain))
             at = slice(step * heads, step * heads + 1)
             recent_rope.append(turn(line[:, latent:], cosine[at], sine[at]))
@@ -337,7 +410,7 @@
 def gather_queries(blocks, lengths, owners, kv_gain, table, prompts, sources, experts, sections,
                    steps, heads):
     latent = kv_gain.shape[0]
-    rope = blocks.shape[2] * experts - latent
+    rope = table[0].shape[1]
     rows = sections * steps * heads
     spare = steps + -steps % 16
     shape = lambda *sizes: jax.ShapeDtypeStruct((prompts,) + sizes, jnp.bfloat16)
@@ -349,7 +422,8 @@
         out_shape=[shape(rows, latent), shape(rows, rope), shape(spare, latent), shape(spare, rope)],
         in_specs=[pl.BlockSpec(memory_space=pltpu.SMEM)] * 2 + [held] * 4,
         out_specs=[held] * 4,
-        scratch_shapes=[pltpu.VMEM((steps * heads, rope), jnp.float32)] * 2,
+        scratch_shapes=[pltpu.VMEM((steps * heads, rope), jnp.float32)] * 2
+        + [pltpu.VMEM((rows, 128), jnp.float32)],
         compiler_params=params(blocks, scale=4),
         name="gather_queries",
     )(*at_home(lengths, owners, kv_gain, *table), blocks)
@@ -682,25 +756,29 @@
     sections = lax.axis_size("section")
     prompt_count, full_length, width = prompts.shape
     steps, tokens_here, heads, _ = queries.shape
+    depth = w_dkv.shape[0]
+    piece = depth // experts
     latent = kv_gain.shape[0]
     cache_width = w_dkv.shape[1]
     rows = prompt_count * full_length
     own_rows = steps * tokens_here
 
     w_turned = w_dkv.T
-    w_piece, *cut = cut_columns(
-        prompts.reshape(rows, width), queries, w_turned, sections, experts
+    w_piece = lax.dynamic_slice_in_dim(w_turned, expert_rank * piece, piece, 1)
+    masks = [1 << bit for bit in range(experts.bit_length() - 1)]
+    uv_parts = doubled({0: w_uv}, "expert", masks[1:])
+    w_parts = spread(w_piece, "section")
+    cut = cut_columns(
+        prompts.reshape(rows, width), queries, sections, experts,
+        [],
     )
-    w_parts = spread(w_piece, "section")
     cut = deliver(cut, "expert")
 
     blocks, riders, token = absorb_queries(
-        owners, cut, queries.shape, w_uk, residual, attn_gain, w_turned, prompt_count, sections
+        owners, cut, queries.shape, w_uk, residual, attn_gain, w_turned, prompt_count, sections,
+        [uv_parts[masks[-1]]],
     )
     blocks = lax.all_to_all(blocks, ("expert", "section"), 0, 0, tiled=True)
-    w_uv, token = lax.optimization_barrier((w_uv, token))
-    masks = [1 << bit for bit in range(experts.bit_length() - 1)]
-    uv_parts = doubled({0: w_uv}, "expert", masks[1:])
 
     away = list(project(cut[1:], riders, w_parts, 1, rows, [token]))
     near = list(project(cut[:1], riders, w_parts, 0, rows, away[:1]))

time: 120 us -> 102 us (0.85)
  waiting for transfers between devices: 45.3 us -> 25 us
  starting transfers between devices: 30.7 us -> 32.7 us
    ppermute x24, waiting for transfers between devices: 45.3 us -> 21.1 us  [swap(): return lax.ppermute(block, axis, [(i, i ^ mask) for i in range(size)])]
    all_to_all x1, waiting for transfers between devices: 0.01 us -> 3.94 us  [local(): blocks = lax.all_to_all(blocks, ('expert', 'section'), 0, 0, tiled=True)]
    all_to_all x1, starting transfers between devices: 4.98 us -> 6.62 us  [local(): blocks = lax.all_to_all(blocks, ('expert', 'section'), 0, 0, tiled=True)]
  transfers between devices with their start and end apart: 25 -> 25, of which waited for: 10 -> 9; matrix products, arithmetic and copies ran while one was open for 0% -> 1% of each run, Pallas kernels for 14% -> 19%
where the time goes in v11:
time: 102 us
  starting transfers between devices  32.7 us (32%)
  Pallas kernels  29.5 us (29%)
  waiting for transfers between devices  25 us (25%)
  blocking collectives  12.4 us (12%)
  local copies, waits for them, and re-layouts  1.84 us (2%)
    ppermute x24, starting transfers between devices, swap(): return lax.ppermute(block, axis, [(i, i ^ mask) for i in range(size)])  26 us
    ppermute x24, waiting for transfers between devices, swap(): return lax.ppermute(block, axis, [(i, i ^ mask) for i in range(size)])  21.1 us
    all_to_all x1, blocking collectives, local(): blocks = lax.all_to_all(blocks, ('expert', 'section'), 0, 0, tiled=True)  12.4 us
    pallas_call x4, Pallas kernels, fetch(): pl.pallas_call(functools.partial(fetch_kernel, len(arrays)), out_shape=[p...  11.4 us
    all_to_all x1, starting transfers between devices, local(): blocks = lax.all_to_all(blocks, ('expert', 'section'), 0, 0, tiled=True)  6.62 us
    pallas_call x1, Pallas kernels, run_experts(): pl.pallas_call(functools.partial(expert_kernel, experts, sections, picks)...  4.98 us
    all_to_all x1, waiting for transfers between devices, local(): blocks = lax.all_to_all(blocks, ('expert', 'section'), 0, 0, tiled=True)  3.94 us
    pallas_call x1, Pallas kernels, cut_columns(): pl.pallas_call(functools.partial(cut_kernel, sections, experts, piece), o...  2.39 us
  transfers between devices with their start and end apart: 25, of which 9 were waited for; matrix products, arithmetic and copies ran while one was open for 1% of the time, Pallas kernels for 19%

profile of v11, /device:TPU:0, one launch (start us, length us, event | category | flops | bytes accessed | tf_op | source)
XLA Modules:
  0.0 101.7 jit_solution(5448161366136161409)
XLA Ops:
  0.0 2.9 %collective-permute-start.3 = (bf16[16,128,128]{2,1,0:T(8,128)(2,1)}, bf16[16,128,128]{2,1,0:T(8,128)(2,1)S(1)}, u32[]{:S(2)}, u32[]{:S(2)}) collective-permute-start(bf16[16,128,128]{2,1,0:T(8,128)(2,1)} %refs_5_.4), channel_id=1, source_target_pairs={{0,8},{4,12},{8,0},{12,4},{1,9},{5,13},{9,1},{13,5},{2,10},{6,14},... | collective-permute-start | bytes 1572872 | tf_op jit(solution)/shard_map/ppermute | solution.py:28
  2.9 2.4 %cut_columns.1 = (bf16[640,224]{1,0:T(8,128)(2,1)S(1)}, bf16[640,224]{1,0:T(8,128)(2,1)S(1)}, bf16[640,224]{1,0:T(8,128)(2,1)}, bf16[640,224]{1,0:T(8,128)(2,1)S(1)}) custom-call(bf16[128,3584]{1,0:T(8,128)(2,1)} %bitcast.6, bf16[2,4,16,192]{3,2,1,0:T(8,128)(2,1)} %query_ref.1), custom_call_target="tpu_custom_call" | custom-call | tf_op jit(solution)/shard_map/cut_columns/pallas_call | solution.py:108
  5.4 1.8 %collective-permute-start.2 = (bf16[640,224]{1,0:T(8,128)(2,1)S(1)}, bf16[640,224]{1,0:T(8,128)(2,1)S(1)}, u32[]{:S(2)}, u32[]{:S(2)}) collective-permute-start(bf16[640,224]{1,0:T(8,128)(2,1)S(1)} %get-tuple-element.32), channel_id=1, source_target_pairs={{0,12},{4,8},{8,4},{12,0},{1,13},{5,9},{9,5},{13,1},{2,14},{6,10},... | collective-permute-start | bytes 860168 | tf_op jit(solution)/shard_map/ppermute | solution.py:28
  8.4 3.7 %collective-permute-start.6 = (bf16[576,224]{1,0:T(8,128)(2,1)S(1)}, bf16[576,224]{1,0:T(8,128)(2,1)S(1)}, u32[]{:S(2)}, u32[]{:S(2)}) collective-permute-start(bf16[576,224]{1,0:T(8,128)(2,1)S(1)} %dynamic-slice_bitcast_fusion.refs_4_.refs_2_), channel_id=1, source_target_pairs={{0,3},{1,2},{2,1},{3,0},{4,7},{5,6},{6,5},{7,4},{8,11},{9,10},{10,... | collective-permute-start | bytes 774152 | tf_op jit(solution)/shard_map/ppermute | solution.py:28
  12.0 10.9 %collective-permute-done.1.refs_3_.refs_1_ = bf16[640,224]{1,0:T(8,128)(2,1)S(1)} collective-permute-done((bf16[640,224]{1,0:T(8,128)(2,1)}, bf16[640,224]{1,0:T(8,128)(2,1)S(1)}, u32[]{:S(2)}, u32[]{:S(2)}) %collective-permute-start.1) | collective-permute-done | bytes 286752 | tf_op jit(solution)/shard_map/ppermute | solution.py:28
  22.9 2.1 %collective-permute-start.4 = (bf16[576,224]{1,0:T(8,128)(2,1)S(1)}, bf16[576,224]{1,0:T(8,128)(2,1)S(1)}, u32[]{:S(2)}, u32[]{:S(2)}) collective-permute-start(bf16[576,224]{1,0:T(8,128)(2,1)S(1)} %dynamic-slice_bitcast_fusion.refs_4_.refs_2_), channel_id=1, source_target_pairs={{0,1},{1,0},{2,3},{3,2},{4,5},{5,4},{6,7},{7,6},{8,9},{9,8},{10,11... | collective-permute-start | bytes 774152 | tf_op jit(solution)/shard_map/ppermute | solution.py:28
  25.1 3.3 %collective-permute-done.2.refs_4_.refs_2_ = bf16[640,224]{1,0:T(8,128)(2,1)S(1)} collective-permute-done((bf16[640,224]{1,0:T(8,128)(2,1)S(1)}, bf16[640,224]{1,0:T(8,128)(2,1)S(1)}, u32[]{:S(2)}, u32[]{:S(2)}) %collective-permute-start.2) | collective-permute-done | bytes 286752 | tf_op jit(solution)/shard_map/ppermute | solution.py:28
  28.4 2.2 %absorb_queries.1 = (bf16[16,48,128]{2,1,0:T(8,128)(2,1)S(1)}, bf16[4,16,576]{2,1,0:T(8,128)(2,1)S(1)}, bf16[8,128]{1,0:T(8,128)(2,1)S(1)}) custom-call(s32[16]{0:T(128)} %refs_0_.8, bf16[640,224]{1,0:T(8,128)(2,1)S(1)} %get-tuple-element.29.refs_1_.refs_0_, bf16[640,224]{1,0:T(8,128)(2,1)S(1)} %collective-permute-done.refs_2_.refs_0_, ...), custom_call_target="tpu_custom_call" | custom-call | tf_op jit(solution)/shard_map/absorb_queries/pallas_call | solution.py:284
  31.3 6.6 %all-to-all-start = ((bf16[16,48,128]{2,1,0:T(8,128)(2,1)}), bf16[16,48,128]{2,1,0:T(8,128)(2,1)S(1)}, u32[]{:S(2)}, u32[]{:S(2)}) async-start(bf16[16,48,128]{2,1,0:T(8,128)(2,1)} %copy-done.1), calls=%async_computation | async-start | bytes 393216 | tf_op jit(solution)/shard_map/all_to_all | solution.py:781
  37.9 1.5 %project.2 = (bf16[144,576]{1,0:T(8,128)(2,1)}, bf16[144,576]{1,0:T(8,128)(2,1)}, bf16[144,576]{1,0:T(8,128)(2,1)}) custom-call(bf16[640,224]{1,0:T(8,128)(2,1)S(1)} %collective-permute-done.refs_2_.refs_0_, bf16[640,224]{1,0:T(8,128)(2,1)S(1)} %collective-permute-done.1.refs_3_.refs_1_, bf16[640,224]{1,0:T(8,128)(2,1)S(1)} %collective-permute-done.2.refs_4_.refs_2_, ...), custom_call_target="tpu_custom_call" | custom-call | tf_op jit(solution)/shard_map/project/pallas_call | solution.py:139
  39.4 1.9 %collective-permute-start.8 = (bf16[144,576]{1,0:T(8,128)(2,1)}, bf16[144,576]{1,0:T(8,128)(2,1)S(1)}, u32[]{:S(2)}, u32[]{:S(2)}) collective-permute-start(bf16[144,576]{1,0:T(8,128)(2,1)} %get-tuple-element.36), channel_id=1, source_target_pairs={{0,8},{4,12},{8,0},{12,4},{1,9},{5,13},{9,1},{13,5},{2,10},{6,14},... | collective-permute-start | bytes 497672 | tf_op jit(solution)/shard_map/ppermute | solution.py:28
  42.1 3.9 %all-to-all-done.block_ref = bf16[16,48,128]{2,1,0:T(8,128)(2,1)S(1)} async-done(((bf16[16,48,128]{2,1,0:T(8,128)(2,1)}), bf16[16,48,128]{2,1,0:T(8,128)(2,1)S(1)}, u32[]{:S(2)}, u32[]{:S(2)}) %all-to-all-start) | async-done | bytes 196640 | tf_op jit(solution)/shard_map/all_to_all | solution.py:781
  48.1 3.5 %collective-permute-done.9.refs_3_.refs_7_ = bf16[144,576]{1,0:T(8,128)(2,1)S(1)} collective-permute-done((bf16[144,576]{1,0:T(8,128)(2,1)}, bf16[144,576]{1,0:T(8,128)(2,1)S(1)}, u32[]{:S(2)}, u32[]{:S(2)}) %collective-permute-start.9) | collective-permute-done | bytes 165920 | tf_op jit(solution)/shard_map/ppermute | solution.py:28
  51.6 1.8 %attend.1 = (bf16[32,512]{1,0:T(8,128)(2,1)S(1)}, bf16[32,512]{1,0:T(8,128)(2,1)S(1)}, bf16[32,512]{1,0:T(8,128)(2,1)S(1)}, bf16[32,512]{1,0:T(8,128)(2,1)S(1)}, bf16[8,128]{1,0:T(8,128)(2,1)S(1)}) custom-call(bf16[144,576]{1,0:T(8,128)(2,1)S(1)} %project.3.refs_0_.refs_4_, bf16[144,576]{1,0:T(8,128)(2,1)S(1)} %collective-permute-done.7.refs_1_.refs_5_, ...), custom_call_target="tpu_custom_call" | custom-call | tf_op jit(solution)/shard_map/attend/pallas_call | solution.py:493
  55.3 2.1 %collective-permute-start.11 = (bf16[32,512]{1,0:T(8,128)(2,1)S(1)}, bf16[32,512]{1,0:T(8,128)(2,1)S(1)}, u32[]{:S(2)}, u32[]{:S(2)}) collective-permute-start(bf16[32,512]{1,0:T(8,128)(2,1)S(1)} %get-tuple-element.45), channel_id=1, source_target_pairs={{0,2},{1,3},{2,0},{3,1},{4,6},{5,7},{6,4},{7,5},{8,10},{9,11},{10,... | collective-permute-start | bytes 98312 | tf_op jit(solution)/shard_map/ppermute | solution.py:28
  58.5 3.2 %fetch.4.refs_10_.refs_9_ = bf16[4,3584,256]{2,1,0:T(8,128)(2,1)S(1)} custom-call(bf16[4,3584,256]{2,1,0:T(8,128)(2,1)} %refs_0_.7, bf16[8,128]{1,0:T(8,128)(2,1)S(1)} %get-tuple-element.50.refs_1_.refs_11_), custom_call_target="tpu_custom_call" | custom-call | bytes 14680064 | tf_op jit(solution)/shard_map/fetch/pallas_call | solution.py:63
  63.2 2.0 %head_products.1.refs_0_.refs_4_ = bf16[8,2176]{1,0:T(8,128)(2,1)S(1)} custom-call(s32[16]{0:T(128)} %refs_0_.8, bf16[32,512]{1,0:T(8,128)(2,1)S(1)} %get-tuple-element.43.refs_1_, bf16[32,512]{1,0:T(8,128)(2,1)S(1)} %collective-permute-done.10.refs_2_, bf16[32,512]{1,0:T(8,128)(2,1)S(1)} %collective-permute-done.11.refs_3_, ...), custom_call_target="tpu_custom_call" | custom-call | tf_op jit(solution)/shard_map/head_products/pallas_call | solution.py:563
  67.0 2.0 %fetch.5.refs_4_ = bf16[2048,896]{1,0:T(8,128)(2,1)S(1)} custom-call(bf16[2048,896]{1,0:T(8,128)(2,1)} %refs_0_.9), custom_call_target="tpu_custom_call" | custom-call | bytes 7340032 | tf_op jit(solution)/shard_map/fetch/pallas_call | solution.py:63
  70.0 1.5 %collective-permute-start.20 = (bf16[32,896]{1,0:T(8,128)(2,1)S(1)}, bf16[32,896]{1,0:T(8,128)(2,1)S(1)}, u32[]{:S(2)}, u32[]{:S(2)}) collective-permute-start(bf16[32,896]{1,0:T(8,128)(2,1)S(1)} %output_product.1.refs_1_.refs_0_), channel_id=1, source_target_pairs={{0,3},{1,2},{2,1},{3,0},{4,7},{5,6},{6,5},{7,4},{8,11},{9,10},{10,... | collective-permute-start | bytes 172040 | tf_op jit(solution)/shard_map/ppermute | solution.py:28
  71.5 3.0 %collective-permute-start.18 = (bf16[32,896]{1,0:T(8,128)(2,1)S(1)}, bf16[32,896]{1,0:T(8,128)(2,1)S(1)}, u32[]{:S(2)}, u32[]{:S(2)}) collective-permute-start(bf16[32,896]{1,0:T(8,128)(2,1)S(1)} %output_product.1.refs_1_.refs_0_), channel_id=1, source_target_pairs={{0,1},{1,0},{2,3},{3,2},{4,5},{5,4},{6,7},{7,6},{8,9},{9,8},{10,11... | collective-permute-start | bytes 172040 | tf_op jit(solution)/shard_map/ppermute | solution.py:28
  74.5 3.1 %fetch.6.refs_8_.refs_10_ = bf16[4,3584,256]{2,1,0:T(8,128)(2,1)S(1)} custom-call(bf16[4,3584,256]{2,1,0:T(8,128)(2,1)} %refs_0_.10, bf16[32,896]{1,0:T(8,128)(2,1)S(1)} %output_product.1.refs_1_.refs_0_), custom_call_target="tpu_custom_call" | custom-call | bytes 14680064 | tf_op jit(solution)/shard_map/fetch/pallas_call | solution.py:63
  80.1 3.1 %fetch.7.refs_11_ = bf16[4,256,3584]{2,1,0:T(8,128)(2,1)S(1)} custom-call(bf16[4,256,3584]{2,1,0:T(8,128)(2,1)} %refs_0_.11, bf16[4,8,896]{2,1,0:T(8,128)(2,1)S(1)} %mix.1.refs_1_.refs_0_), custom_call_target="tpu_custom_call" | custom-call | bytes 14680064 | tf_op jit(solution)/shard_map/fetch/pallas_call | solution.py:63
  83.7 5.0 %run_experts.1 = (bf16[16,8,896]{2,1,0:T(8,128)(2,1)S(1)}, bf16[4,8,896]{2,1,0:T(8,128)(2,1)S(1)}) custom-call(bf16[4,8,896]{2,1,0:T(8,128)(2,1)S(1)} %mix.1.refs_1_.refs_0_, bf16[4,8,896]{2,1,0:T(8,128)(2,1)S(1)} %collective-permute-done.21.refs_1_, bf16[4,8,896]{2,1,0:T(8,128)(2,1)S(1)} %collective-permute-done.22.refs_2_, ...), custom_call_target="tpu_custom_call" | custom-call | tf_op jit(solution)/shard_map/run_experts/pallas_call | solution.py:696
  88.7 12.4 %all_to_all.10.block_ref = bf16[16,8,896]{2,1,0:T(8,128)(2,1)S(1)} all-to-all(bf16[16,8,896]{2,1,0:T(8,128)(2,1)S(1)} %get-tuple-element.51), channel_id=1, replica_groups=mesh['groups'=2,'expert'=4,'section'=4] {'expert','section'}, dimensions={0} | all-to-all | bytes 458752 | tf_op jit(solution)/shard_map/all_to_all | solution.py:826
  (55 shorter events, 15.6 us)
Async XLA Ops:
  0.0 28.4 %collective-permute-start.3 = (bf16[16,128,128]{2,1,0:T(8,128)(2,1)}, bf16[16,128,128]{2,1,0:T(8,128)(2,1)S(1)}, u32[]{:S(2)}, u32[]{:S(2)}) collective-permute-start(bf16[16,128,128]{2,1,0:T(8,128)(2,1)} %refs_5_.4), channel_id=1, source_target_pairs={{0,8},{4,12},{8,0},{12,4},{1,9},{5,13},{9,1},{13,5},{2,10},{6,14},... | collective-permute-start | bytes 1572872 | tf_op jit(solution)/shard_map/ppermute | solution.py:28
  5.3 6.7 %collective-permute-start = (bf16[640,224]{1,0:T(8,128)(2,1)S(1)}, bf16[640,224]{1,0:T(8,128)(2,1)S(1)}, u32[]{:S(2)}, u32[]{:S(2)}) collective-permute-start(bf16[640,224]{1,0:T(8,128)(2,1)S(1)} %get-tuple-element.30), channel_id=1, source_target_pairs={{0,4},{4,0},{8,12},{12,8},{1,5},{5,1},{9,13},{13,9},{2,6},{6,2},{1... | collective-permute-start | bytes 860168 | tf_op jit(solution)/shard_map/ppermute | solution.py:28
  5.3 17.6 %collective-permute-start.1 = (bf16[640,224]{1,0:T(8,128)(2,1)}, bf16[640,224]{1,0:T(8,128)(2,1)S(1)}, u32[]{:S(2)}, u32[]{:S(2)}) collective-permute-start(bf16[640,224]{1,0:T(8,128)(2,1)} %get-tuple-element.31), channel_id=1, source_target_pairs={{0,8},{4,12},{8,0},{12,4},{1,9},{5,13},{9,1},{13,5},{2,10},{6,14},... | collective-permute-start | bytes 860168 | tf_op jit(solution)/shard_map/ppermute | solution.py:28
  5.4 23.0 %collective-permute-start.2 = (bf16[640,224]{1,0:T(8,128)(2,1)S(1)}, bf16[640,224]{1,0:T(8,128)(2,1)S(1)}, u32[]{:S(2)}, u32[]{:S(2)}) collective-permute-start(bf16[640,224]{1,0:T(8,128)(2,1)S(1)} %get-tuple-element.32), channel_id=1, source_target_pairs={{0,12},{4,8},{8,4},{12,0},{1,13},{5,9},{9,5},{13,1},{2,14},{6,10},... | collective-permute-start | bytes 860168 | tf_op jit(solution)/shard_map/ppermute | solution.py:28
  8.4 29.5 %collective-permute-start.6 = (bf16[576,224]{1,0:T(8,128)(2,1)S(1)}, bf16[576,224]{1,0:T(8,128)(2,1)S(1)}, u32[]{:S(2)}, u32[]{:S(2)}) collective-permute-start(bf16[576,224]{1,0:T(8,128)(2,1)S(1)} %dynamic-slice_bitcast_fusion.refs_4_.refs_2_), channel_id=1, source_target_pairs={{0,3},{1,2},{2,1},{3,0},{4,7},{5,6},{6,5},{7,4},{8,11},{9,10},{10,... | collective-permute-start | bytes 774152 | tf_op jit(solution)/shard_map/ppermute | solution.py:28
  12.0 25.9 %collective-permute-start.5 = (bf16[576,224]{1,0:T(8,128)(2,1)S(1)}, bf16[576,224]{1,0:T(8,128)(2,1)S(1)}, u32[]{:S(2)}, u32[]{:S(2)}) collective-permute-start(bf16[576,224]{1,0:T(8,128)(2,1)S(1)} %dynamic-slice_bitcast_fusion.refs_4_.refs_2_), channel_id=1, source_target_pairs={{0,2},{1,3},{2,0},{3,1},{4,6},{5,7},{6,4},{7,5},{8,10},{9,11},{10,... | collective-permute-start | bytes 774152 | tf_op jit(solution)/shard_map/ppermute | solution.py:28
  22.9 15.0 %collective-permute-start.4 = (bf16[576,224]{1,0:T(8,128)(2,1)S(1)}, bf16[576,224]{1,0:T(8,128)(2,1)S(1)}, u32[]{:S(2)}, u32[]{:S(2)}) collective-permute-start(bf16[576,224]{1,0:T(8,128)(2,1)S(1)} %dynamic-slice_bitcast_fusion.refs_4_.refs_2_), channel_id=1, source_target_pairs={{0,1},{1,0},{2,3},{3,2},{4,5},{5,4},{6,7},{7,6},{8,9},{9,8},{10,11... | collective-permute-start | bytes 774152 | tf_op jit(solution)/shard_map/ppermute | solution.py:28
  31.3 14.8 %all-to-all-start = ((bf16[16,48,128]{2,1,0:T(8,128)(2,1)}), bf16[16,48,128]{2,1,0:T(8,128)(2,1)S(1)}, u32[]{:S(2)}, u32[]{:S(2)}) async-start(bf16[16,48,128]{2,1,0:T(8,128)(2,1)} %copy-done.1), calls=%async_computation | async-start | bytes 393216 | tf_op jit(solution)/shard_map/all_to_all | solution.py:781
  39.4 8.6 %collective-permute-start.8 = (bf16[144,576]{1,0:T(8,128)(2,1)}, bf16[144,576]{1,0:T(8,128)(2,1)S(1)}, u32[]{:S(2)}, u32[]{:S(2)}) collective-permute-start(bf16[144,576]{1,0:T(8,128)(2,1)} %get-tuple-element.36), channel_id=1, source_target_pairs={{0,8},{4,12},{8,0},{12,4},{1,9},{5,13},{9,1},{13,5},{2,10},{6,14},... | collective-permute-start | bytes 497672 | tf_op jit(solution)/shard_map/ppermute | solution.py:28
  41.4 10.2 %collective-permute-start.9 = (bf16[144,576]{1,0:T(8,128)(2,1)}, bf16[144,576]{1,0:T(8,128)(2,1)S(1)}, u32[]{:S(2)}, u32[]{:S(2)}) collective-permute-start(bf16[144,576]{1,0:T(8,128)(2,1)} %get-tuple-element.37), channel_id=1, source_target_pairs={{0,12},{4,8},{8,4},{12,0},{1,13},{5,9},{9,5},{13,1},{2,14},{6,10},... | collective-permute-start | bytes 497672 | tf_op jit(solution)/shard_map/ppermute | solution.py:28
  41.4 10.2 %collective-permute-start.7 = (bf16[144,576]{1,0:T(8,128)(2,1)}, bf16[144,576]{1,0:T(8,128)(2,1)S(1)}, u32[]{:S(2)}, u32[]{:S(2)}) collective-permute-start(bf16[144,576]{1,0:T(8,128)(2,1)} %get-tuple-element.35.refs_6_), channel_id=1, source_target_pairs={{0,4},{4,0},{8,12},{12,8},{1,5},{5,1},{9,13},{13,9},{2,6},{6,2},{1... | collective-permute-start | bytes 497672 | tf_op jit(solution)/shard_map/ppermute | solution.py:28
  53.4 9.8 %collective-permute-start.13 = (bf16[16,128,128]{2,1,0:T(8,128)(2,1)}, bf16[16,128,128]{2,1,0:T(8,128)(2,1)S(1)}, u32[]{:S(2)}, u32[]{:S(2)}) collective-permute-start(bf16[16,128,128]{2,1,0:T(8,128)(2,1)} %refs_5_.4), channel_id=1, source_target_pairs={{0,4},{4,0},{8,12},{12,8},{1,5},{5,1},{9,13},{13,9},{2,6},{6,2},{1... | collective-permute-start | bytes 1572872 | tf_op jit(solution)/shard_map/ppermute | solution.py:28
  53.6 9.6 %collective-permute-start.14 = (bf16[16,128,128]{2,1,0:T(8,128)(2,1)S(1)}, bf16[16,128,128]{2,1,0:T(8,128)(2,1)S(1)}, u32[]{:S(2)}, u32[]{:S(2)}) collective-permute-start(bf16[16,128,128]{2,1,0:T(8,128)(2,1)S(1)} %collective-permute-done.3.refs_9_.refs_7_), channel_id=1, source_target_pairs={{0,4},{4,0},{8,12},{12,8},{1,5},{5,1},{9,13},{13,9},{2,6},{6,2},{1... | collective-permute-start | bytes 1572872 | tf_op jit(solution)/shard_map/ppermute | solution.py:28
  54.0 7.7 %collective-permute-start.10 = (bf16[32,512]{1,0:T(8,128)(2,1)S(1)}, bf16[32,512]{1,0:T(8,128)(2,1)S(1)}, u32[]{:S(2)}, u32[]{:S(2)}) collective-permute-start(bf16[32,512]{1,0:T(8,128)(2,1)S(1)} %get-tuple-element.44), channel_id=1, source_target_pairs={{0,1},{1,0},{2,3},{3,2},{4,5},{5,4},{6,7},{7,6},{8,9},{9,8},{10,11... | collective-permute-start | bytes 98312 | tf_op jit(solution)/shard_map/ppermute | solution.py:28
  55.3 6.4 %collective-permute-start.11 = (bf16[32,512]{1,0:T(8,128)(2,1)S(1)}, bf16[32,512]{1,0:T(8,128)(2,1)S(1)}, u32[]{:S(2)}, u32[]{:S(2)}) collective-permute-start(bf16[32,512]{1,0:T(8,128)(2,1)S(1)} %get-tuple-element.45), channel_id=1, source_target_pairs={{0,2},{1,3},{2,0},{3,1},{4,6},{5,7},{6,4},{7,5},{8,10},{9,11},{10,... | collective-permute-start | bytes 98312 | tf_op jit(solution)/shard_map/ppermute | solution.py:28
  57.5 5.7 %collective-permute-start.12 = (bf16[32,512]{1,0:T(8,128)(2,1)S(1)}, bf16[32,512]{1,0:T(8,128)(2,1)S(1)}, u32[]{:S(2)}, u32[]{:S(2)}) collective-permute-start(bf16[32,512]{1,0:T(8,128)(2,1)S(1)} %get-tuple-element.46), channel_id=1, source_target_pairs={{0,3},{1,2},{2,1},{3,0},{4,7},{5,6},{6,5},{7,4},{8,11},{9,10},{10,... | collective-permute-start | bytes 98312 | tf_op jit(solution)/shard_map/ppermute | solution.py:28
  65.2 3.9 %collective-permute-start.17 = (bf16[8,2176]{1,0:T(8,128)(2,1)S(1)}, bf16[8,2176]{1,0:T(8,128)(2,1)S(1)}, u32[]{:S(2)}, u32[]{:S(2)}) collective-permute-start(bf16[8,2176]{1,0:T(8,128)(2,1)S(1)} %head_products.1.refs_0_.refs_4_), channel_id=1, source_target_pairs={{0,12},{4,8},{8,4},{12,0},{1,13},{5,9},{9,5},{13,1},{2,14},{6,10},... | collective-permute-start | bytes 104456 | tf_op jit(solution)/shard_map/ppermute | solution.py:28
  65.2 4.1 %collective-permute-start.16 = (bf16[8,2176]{1,0:T(8,128)(2,1)S(1)}, bf16[8,2176]{1,0:T(8,128)(2,1)S(1)}, u32[]{:S(2)}, u32[]{:S(2)}) collective-permute-start(bf16[8,2176]{1,0:T(8,128)(2,1)S(1)} %head_products.1.refs_0_.refs_4_), channel_id=1, source_target_pairs={{0,8},{4,12},{8,0},{12,4},{1,9},{5,13},{9,1},{13,5},{2,10},{6,14},... | collective-permute-start | bytes 104456 | tf_op jit(solution)/shard_map/ppermute | solution.py:28
  70.0 7.6 %collective-permute-start.20 = (bf16[32,896]{1,0:T(8,128)(2,1)S(1)}, bf16[32,896]{1,0:T(8,128)(2,1)S(1)}, u32[]{:S(2)}, u32[]{:S(2)}) collective-permute-start(bf16[32,896]{1,0:T(8,128)(2,1)S(1)} %output_product.1.refs_1_.refs_0_), channel_id=1, source_target_pairs={{0,3},{1,2},{2,1},{3,0},{4,7},{5,6},{6,5},{7,4},{8,11},{9,10},{10,... | collective-permute-start | bytes 172040 | tf_op jit(solution)/shard_map/ppermute | solution.py:28
  71.5 6.6 %collective-permute-start.19 = (bf16[32,896]{1,0:T(8,128)(2,1)S(1)}, bf16[32,896]{1,0:T(8,128)(2,1)S(1)}, u32[]{:S(2)}, u32[]{:S(2)}) collective-permute-start(bf16[32,896]{1,0:T(8,128)(2,1)S(1)} %output_product.1.refs_1_.refs_0_), channel_id=1, source_target_pairs={{0,2},{1,3},{2,0},{3,1},{4,6},{5,7},{6,4},{7,5},{8,10},{9,11},{10,... | collective-permute-start | bytes 172040 | tf_op jit(solution)/shard_map/ppermute | solution.py:28
  71.5 6.6 %collective-permute-start.18 = (bf16[32,896]{1,0:T(8,128)(2,1)S(1)}, bf16[32,896]{1,0:T(8,128)(2,1)S(1)}, u32[]{:S(2)}, u32[]{:S(2)}) collective-permute-start(bf16[32,896]{1,0:T(8,128)(2,1)S(1)} %output_product.1.refs_1_.refs_0_), channel_id=1, source_target_pairs={{0,1},{1,0},{2,3},{3,2},{4,5},{5,4},{6,7},{7,6},{8,9},{9,8},{10,11... | collective-permute-start | bytes 172040 | tf_op jit(solution)/shard_map/ppermute | solution.py:28
  78.2 5.0 %collective-permute-start.23 = (bf16[4,8,896]{2,1,0:T(8,128)(2,1)S(1)}, bf16[4,8,896]{2,1,0:T(8,128)(2,1)S(1)}, u32[]{:S(2)}, u32[]{:S(2)}) collective-permute-start(bf16[4,8,896]{2,1,0:T(8,128)(2,1)S(1)} %mix.1.refs_1_.refs_0_), channel_id=1, source_target_pairs={{0,12},{4,8},{8,4},{12,0},{1,13},{5,9},{9,5},{13,1},{2,14},{6,10},... | collective-permute-start | bytes 172040 | tf_op jit(solution)/shard_map/ppermute | solution.py:28
  78.8 4.9 %collective-permute-start.22 = (bf16[4,8,896]{2,1,0:T(8,128)(2,1)S(1)}, bf16[4,8,896]{2,1,0:T(8,128)(2,1)S(1)}, u32[]{:S(2)}, u32[]{:S(2)}) collective-permute-start(bf16[4,8,896]{2,1,0:T(8,128)(2,1)S(1)} %mix.1.refs_1_.refs_0_), channel_id=1, source_target_pairs={{0,8},{4,12},{8,0},{12,4},{1,9},{5,13},{9,1},{13,5},{2,10},{6,14},... | collective-permute-start | bytes 172040 | tf_op jit(solution)/shard_map/ppermute | solution.py:28
  79.9 3.8 %collective-permute-start.21 = (bf16[4,8,896]{2,1,0:T(8,128)(2,1)S(1)}, bf16[4,8,896]{2,1,0:T(8,128)(2,1)S(1)}, u32[]{:S(2)}, u32[]{:S(2)}) collective-permute-start(bf16[4,8,896]{2,1,0:T(8,128)(2,1)S(1)} %mix.1.refs_1_.refs_0_), channel_id=1, source_target_pairs={{0,4},{4,0},{8,12},{12,8},{1,5},{5,1},{9,13},{13,9},{2,6},{6,2},{1... | collective-permute-start | bytes 172040 | tf_op jit(solution)/shard_map/ppermute | solution.py:28
  (5 other events, 116.7 us)

commit v12 on v11

--- a/solution.py
+++ b/solution.py
@@ -81,8 +81,10 @@
     return held
 
 
-def cut_kernel(sections, experts, piece, x_ref, query_ref, *refs):
+def cut_kernel(sections, experts, piece, x_ref, query_ref, uv_ref, half_ref, *refs):
     out_refs, held = refs[-1 - experts : -1], refs[-1]
+    share = half_ref.shape[0]
+    half_ref[...] = uv_ref[pl.ds(lax.axis_index("groups") * share, share)]
     rank = lax.axis_index("expert")
     steps, sources, heads, wide = query_ref.shape
     rows = x_ref.shape[0]
@@ -98,7 +100,7 @@
                 ref[at : at + heads, :wide] = query_ref[step, source]
 
 
-def cut_columns(x, queries, sections, experts, after):
+def cut_columns(x, queries, w_uv, sections, experts, groups):
     rows, width = x.shape
     piece = width // (sections * experts)
     steps, sources, heads, wide = queries.shape
@@ -107,13 +109,14 @@
     )
     return pl.pallas_call(
         functools.partial(cut_kernel, sections, experts, piece),
-        out_shape=[block] * experts,
-        in_specs=[pl.BlockSpec(memory_space=pltpu.VMEM)] * 2
-        + [pl.BlockSpec(memory_space=pl.ANY)] * len(after),
+        out_shape=[
+            jax.ShapeDtypeStruct((w_uv.shape[0] // groups,) + w_uv.shape[1:], w_uv.dtype)
+        ]
+        + [block] * experts,
         scratch_shapes=[pltpu.VMEM((experts, sections * rows, piece), x.dtype)],
-        compiler_params=params(x, block, scale=6),
+        compiler_params=params(x, block, w_uv, scale=6),
         name="cut_columns",
-    )(*at_home(x, queries), *after)
+    )(*at_home(x, queries, w_uv))
 
 
 def project_kernel(count, first, rows, *refs):
@@ -507,13 +510,21 @@
     )(*parts, *at_home(lengths, kv_gain, *table), *gathered)
 
 
-def value_kernel(experts, sections, heads, steps, sources, *refs):
-    owner_ref = refs[0]
-    latent_refs, uv_refs = refs[1 : 1 + sections], refs[1 + sections : 1 + sections + experts]
-    route_ref = refs[1 + sections + experts]
+def value_kernel(experts, sections, heads, steps, sources, count, *refs):
+    owner_ref, latent_refs, uv_refs = refs[0], refs[1 : 1 + sections], refs[1 + sections :]
+    route_ref = uv_refs[count]
+    uv_refs = list(uv_refs[:count])
     out_ref, held = refs[-2:]
+    group_rank, groups = lax.axis_index("groups"), lax.axis_size("groups")
+    weights = []
+    while uv_refs:
+        if uv_refs[0].shape[0] == heads:
+            weights.append(uv_refs[:1])
+        else:
+            weights.append(uv_refs[:groups])
+        uv_refs = uv_refs[len(weights[-1]) :]
     f32, bf16 = jnp.float32, jnp.bfloat16
-    chunk = uv_refs[0].shape[2]
+    chunk = weights[0][0].shape[2]
     rows = latent_refs[0].shape[0]
     for mask, ref in enumerate(latent_refs):
         for index in range(experts):
@@ -525,10 +536,15 @@
     for head in range(heads):
         at = pl.ds(head, sections * rows // heads, stride=heads)
         total = 0
-        for mask, ref in enumerate(uv_refs):
+        for mask, shares in enumerate(weights):
+            size = shares[0].shape[0]
+            weight = shares[0][head % size]
+            for other in range(1, len(shares)):
+                mine = (group_rank ^ other) == head // size
+                weight = jnp.where(mine, shares[other][head % size], weight)
             total = total + lax.dot_general(
                 held[rank ^ mask, at, :][:, :chunk].astype(bf16),
-                ref[head],
+                weight,
                 (((1,), (1,)), ((), ())),
                 preferred_element_type=f32,
             )
@@ -557,12 +573,14 @@
 
 def head_products(owners, latents, uv_parts, route, steps, sources, after):
     rows, width = latents[0].shape
-    heads, value, _ = uv_parts[0].shape
+    heads, value, _ = uv_parts[0][0].shape
+    experts = len(uv_parts)
+    uv_parts = [share for part in uv_parts for share in part]
     held = pl.BlockSpec(memory_space=pltpu.VMEM)
     total = rows * len(latents)
     return pl.pallas_call(
         functools.partial(
-            value_kernel, len(uv_parts), len(latents), heads, steps, sources
+            value_kernel, experts, len(latents), heads, steps, sources, len(uv_parts)
         ),
         out_shape=jax.ShapeDtypeStruct(
             (total // heads, heads * value + route.shape[1]), jnp.bfloat16
@@ -572,7 +590,7 @@
         + [pl.BlockSpec(memory_space=pl.ANY)] * len(after),
         out_specs=held,
         scratch_shapes=[
-            pltpu.VMEM((len(uv_parts), total, max(width // len(uv_parts), 128)), jnp.float32)
+            pltpu.VMEM((experts, total, max(width // experts, 128)), jnp.float32)
         ],
         compiler_params=params(*latents, *uv_parts, scale=4),
         name="head_products",
@@ -754,6 +772,7 @@
     section_rank = lax.axis_index("section")
     experts = lax.axis_size("expert")
     sections = lax.axis_size("section")
+    groups = lax.axis_size("groups")
     prompt_count, full_length, width = prompts.shape
     steps, tokens_here, heads, _ = queries.shape
     depth = w_dkv.shape[0]
@@ -766,17 +785,17 @@
     w_turned = w_dkv.T
     w_piece = lax.dynamic_slice_in_dim(w_turned, expert_rank * piece, piece, 1)
     masks = [1 << bit for bit in range(experts.bit_length() - 1)]
-    uv_parts = doubled({0: w_uv}, "expert", masks[1:])
+    far = masks[-1]
     w_parts = spread(w_piece, "section")
-    cut = cut_columns(
-        prompts.reshape(rows, width), queries, sections, experts,
-        [],
+    uv_share, *cut = cut_columns(
+        prompts.reshape(rows, width), queries, w_uv, sections, experts, groups
     )
+    uv_share = swap(uv_share, "expert", far)
     cut = deliver(cut, "expert")
 
     blocks, riders, token = absorb_queries(
         owners, cut, queries.shape, w_uk, residual, attn_gain, w_turned, prompt_count, sections,
-        [uv_parts[masks[-1]]],
+        [uv_share],
     )
     blocks = lax.all_to_all(blocks, ("expert", "section"), 0, 0, tiled=True)
 
@@ -794,9 +813,13 @@
     )
 
     (w_gate,) = fetch([w_gate], [token])
-    order = sorted(uv_parts)
-    *uv_parts, token = lax.optimization_barrier((*[uv_parts[mask] for mask in order], token))
-    uv_parts = doubled(dict(zip(order, uv_parts)), "expert", masks[:1])
+    uv_shares = spread(uv_share, "groups")
+    *uv_shares, uv_own, token = lax.optimization_barrier((*uv_shares, w_uv, token))
+    later = masks[1:-1] + masks[:1]
+    held = [doubled({far: share}, "expert", later) for share in uv_shares]
+    uv_parts = {mask: [share[mask] for share in held] for mask in held[0]}
+    for mask, part in doubled({0: uv_own}, "expert", later).items():
+        uv_parts[mask] = [part]
     out_latent = deliver(out_latent, "section")
     high = route_scores.astype(bf16)
     low = (route_scores - high.astype(f32)).astype(bf16)

time: 102 us -> 104 us (1.020)
  waiting for transfers between devices: 25 us -> 18.9 us
  starting transfers between devices: 32.7 us -> 36.9 us
  other arithmetic: 0.09 us -> 1.53 us
  local copies, waits for them, and re-layouts: 1.84 us -> 3.1 us
    ppermute x24 -> x26, starting transfers between devices: 26 us -> 31 us  [swap(): return lax.ppermute(block, axis, [(i, i ^ mask) for i in range(size)])]
    ppermute x24 -> x26, waiting for transfers between devices: 21.1 us -> 17.6 us  [swap(): return lax.ppermute(block, axis, [(i, i ^ mask) for i in range(size)])]
    all_to_all x1, waiting for transfers between devices: 3.94 us -> 1.29 us  [local(): blocks = lax.all_to_all(blocks, ('expert', 'section'), 0, 0, tiled=True)]
    unnamed x8, local copies, waits for them, and re-layouts: 0.68 us -> 1.94 us
  transfers between devices with their start and end apart: 25 -> 27, of which waited for: 9 -> 11; matrix products, arithmetic and copies ran while one was open for 1% -> 3% of each run, Pallas kernels for 19% -> 18%
where the time goes in v12:
time: 104 us; the launch traced here: 103 us
  starting transfers between devices  36.9 us (35%)
  Pallas kernels  30.2 us (29%)
  waiting for transfers between devices  18.9 us (18%)
  blocking collectives  12.3 us (12%)
  local copies, waits for them, and re-layouts  3.1 us (3%)
  other arithmetic  1.53 us (1%)
    ppermute x26, starting transfers between devices, swap(): return lax.ppermute(block, axis, [(i, i ^ mask) for i in range(size)])  31 us
    ppermute x26, waiting for transfers between devices, swap(): return lax.ppermute(block, axis, [(i, i ^ mask) for i in range(size)])  17.6 us
    all_to_all x1, blocking collectives, local(): blocks = lax.all_to_all(blocks, ('expert', 'section'), 0, 0, tiled=True)  12.3 us
    pallas_call x4, Pallas kernels, fetch(): pl.pallas_call(functools.partial(fetch_kernel, len(arrays)), out_shape=[p...  11.3 us
    all_to_all x1, starting transfers between devices, local(): blocks = lax.all_to_all(blocks, ('expert', 'section'), 0, 0, tiled=True)  5.96 us
    pallas_call x1, Pallas kernels, run_experts(): pl.pallas_call(functools.partial(expert_kernel, experts, sections, picks)...  4.98 us
    pallas_call x1, Pallas kernels, cut_columns(): pl.pallas_call(functools.partial(cut_kernel, sections, experts, piece), o...  2.82 us
    pallas_call x1, Pallas kernels, head_products(): pl.pallas_call(functools.partial(value_kernel, experts, len(latents), hea...  2.27 us
  transfers between devices with their start and end apart: 27, of which 11 were waited for; matrix products, arithmetic and copies ran while one was open for 3% of the time, Pallas kernels for 18%

profile of v12, /device:TPU:0, one launch (start us, length us, event | category | flops | bytes accessed | tf_op | source)
XLA Modules:
  0.0 103.2 jit_solution(13504995859642405826)
XLA Ops:
  0.0 2.8 %cut_columns.1 = (bf16[8,128,128]{2,1,0:T(8,128)(2,1)S(1)}, bf16[640,224]{1,0:T(8,128)(2,1)S(1)}, bf16[640,224]{1,0:T(8,128)(2,1)}, bf16[640,224]{1,0:T(8,128)(2,1)}, bf16[640,224]{1,0:T(8,128)(2,1)}) custom-call(bf16[128,3584]{1,0:T(8,128)(2,1)} %bitcast.6, bf16[2,4,16,192]{3,2,1,0:T(8,128)(2,1)} %query_ref.1, bf16[16,128,128]{2,1,0:T(8,128)(2,1)} %refs_5_.4), custom_call_target="tpu_custom_call" | custom-call | tf_op jit(solution)/shard_map/cut_columns/pallas_call | solution.py:110
  3.3 2.5 %collective-permute-start.3 = (bf16[8,128,128]{2,1,0:T(8,128)(2,1)S(1)}, bf16[8,128,128]{2,1,0:T(8,128)(2,1)S(1)}, u32[]{:S(2)}, u32[]{:S(2)}) collective-permute-start(bf16[8,128,128]{2,1,0:T(8,128)(2,1)S(1)} %get-tuple-element.35), channel_id=1, source_target_pairs={{0,8},{4,12},{8,0},{12,4},{1,9},{5,13},{9,1},{13,5},{2,10},{6,14},... | collective-permute-start | bytes 786440 | tf_op jit(solution)/shard_map/ppermute | solution.py:28
  8.5 3.7 %collective-permute-start.6 = (bf16[576,224]{1,0:T(8,128)(2,1)S(1)}, bf16[576,224]{1,0:T(8,128)(2,1)S(1)}, u32[]{:S(2)}, u32[]{:S(2)}) collective-permute-start(bf16[576,224]{1,0:T(8,128)(2,1)S(1)} %dynamic-slice_bitcast_fusion.refs_4_.refs_2_), channel_id=1, source_target_pairs={{0,3},{1,2},{2,1},{3,0},{4,7},{5,6},{6,5},{7,4},{8,11},{9,10},{10,... | collective-permute-start | bytes 774152 | tf_op jit(solution)/shard_map/ppermute | solution.py:28
  12.9 3.0 %collective-permute-start.5 = (bf16[576,224]{1,0:T(8,128)(2,1)S(1)}, bf16[576,224]{1,0:T(8,128)(2,1)S(1)}, u32[]{:S(2)}, u32[]{:S(2)}) collective-permute-start(bf16[576,224]{1,0:T(8,128)(2,1)S(1)} %dynamic-slice_bitcast_fusion.refs_4_.refs_2_), channel_id=1, source_target_pairs={{0,2},{1,3},{2,0},{3,1},{4,6},{5,7},{6,4},{7,5},{8,10},{9,11},{10,... | collective-permute-start | bytes 774152 | tf_op jit(solution)/shard_map/ppermute | solution.py:28
  16.0 1.6 %collective-permute-start.4 = (bf16[576,224]{1,0:T(8,128)(2,1)S(1)}, bf16[576,224]{1,0:T(8,128)(2,1)S(1)}, u32[]{:S(2)}, u32[]{:S(2)}) collective-permute-start(bf16[576,224]{1,0:T(8,128)(2,1)S(1)} %dynamic-slice_bitcast_fusion.refs_4_.refs_2_), channel_id=1, source_target_pairs={{0,1},{1,0},{2,3},{3,2},{4,5},{5,4},{6,7},{7,6},{8,9},{9,8},{10,11... | collective-permute-start | bytes 774152 | tf_op jit(solution)/shard_map/ppermute | solution.py:28
  17.6 2.4 %collective-permute-done.1.refs_3_.refs_1_ = bf16[640,224]{1,0:T(8,128)(2,1)S(1)} collective-permute-done((bf16[640,224]{1,0:T(8,128)(2,1)}, bf16[640,224]{1,0:T(8,128)(2,1)S(1)}, u32[]{:S(2)}, u32[]{:S(2)}) %collective-permute-start.1) | collective-permute-done | bytes 286752 | tf_op jit(solution)/shard_map/ppermute | solution.py:28
  19.9 6.7 %collective-permute-done.2.refs_4_.refs_2_ = bf16[640,224]{1,0:T(8,128)(2,1)S(1)} collective-permute-done((bf16[640,224]{1,0:T(8,128)(2,1)}, bf16[640,224]{1,0:T(8,128)(2,1)S(1)}, u32[]{:S(2)}, u32[]{:S(2)}) %collective-permute-start.2) | collective-permute-done | bytes 286752 | tf_op jit(solution)/shard_map/ppermute | solution.py:28
  26.6 2.2 %absorb_queries.1 = (bf16[16,48,128]{2,1,0:T(8,128)(2,1)S(1)}, bf16[4,16,576]{2,1,0:T(8,128)(2,1)S(1)}, bf16[8,128]{1,0:T(8,128)(2,1)S(1)}) custom-call(s32[16]{0:T(128)} %refs_0_.8, bf16[640,224]{1,0:T(8,128)(2,1)S(1)} %get-tuple-element.31.refs_1_.refs_0_, bf16[640,224]{1,0:T(8,128)(2,1)S(1)} %collective-permute-done.refs_2_.refs_0_, ...), custom_call_target="tpu_custom_call" | custom-call | tf_op jit(solution)/shard_map/absorb_queries/pallas_call | solution.py:287
  30.1 6.0 %all-to-all-start = ((bf16[16,48,128]{2,1,0:T(8,128)(2,1)}), bf16[16,48,128]{2,1,0:T(8,128)(2,1)S(1)}, u32[]{:S(2)}, u32[]{:S(2)}) async-start(bf16[16,48,128]{2,1,0:T(8,128)(2,1)} %copy-done.1), calls=%async_computation | async-start | bytes 393216 | tf_op jit(solution)/shard_map/all_to_all | solution.py:800
  36.0 1.6 %collective-permute-start.13 = (bf16[8,128,128]{2,1,0:T(8,128)(2,1)S(1)}, bf16[8,128,128]{2,1,0:T(8,128)(2,1)}, u32[]{:S(2)}, u32[]{:S(2)}) collective-permute-start(bf16[8,128,128]{2,1,0:T(8,128)(2,1)S(1)} %collective-permute-done.3.refs_9_.refs_7_), channel_id=1, source_target_pairs={{0,16},{16,0},{1,17},{17,1},{2,18},{18,2},{3,19},{19,3},{4,20},{20... | collective-permute-start | bytes 786440 | tf_op jit(solution)/shard_map/ppermute | solution.py:28
  45.5 2.7 %collective-permute-done.8.refs_2_.refs_6_ = bf16[144,576]{1,0:T(8,128)(2,1)S(1)} collective-permute-done((bf16[144,576]{1,0:T(8,128)(2,1)}, bf16[144,576]{1,0:T(8,128)(2,1)S(1)}, u32[]{:S(2)}, u32[]{:S(2)}) %collective-permute-start.8) | collective-permute-done | bytes 165920 | tf_op jit(solution)/shard_map/ppermute | solution.py:28
  48.2 2.0 %collective-permute-done.9.refs_3_.refs_7_ = bf16[144,576]{1,0:T(8,128)(2,1)S(1)} collective-permute-done((bf16[144,576]{1,0:T(8,128)(2,1)}, bf16[144,576]{1,0:T(8,128)(2,1)S(1)}, u32[]{:S(2)}, u32[]{:S(2)}) %collective-permute-start.9) | collective-permute-done | bytes 165920 | tf_op jit(solution)/shard_map/ppermute | solution.py:28
  50.2 1.8 %attend.1 = (bf16[32,512]{1,0:T(8,128)(2,1)S(1)}, bf16[32,512]{1,0:T(8,128)(2,1)S(1)}, bf16[32,512]{1,0:T(8,128)(2,1)S(1)}, bf16[32,512]{1,0:T(8,128)(2,1)S(1)}, bf16[8,128]{1,0:T(8,128)(2,1)S(1)}) custom-call(bf16[144,576]{1,0:T(8,128)(2,1)S(1)} %project.3.refs_0_.refs_4_, bf16[144,576]{1,0:T(8,128)(2,1)S(1)} %collective-permute-done.7.refs_1_.refs_5_, ...), custom_call_target="tpu_custom_call" | custom-call | tf_op jit(solution)/shard_map/attend/pallas_call | solution.py:496
  56.3 2.0 %collective-permute-start.11 = (bf16[32,512]{1,0:T(8,128)(2,1)S(1)}, bf16[32,512]{1,0:T(8,128)(2,1)S(1)}, u32[]{:S(2)}, u32[]{:S(2)}) collective-permute-start(bf16[32,512]{1,0:T(8,128)(2,1)S(1)} %get-tuple-element.48), channel_id=1, source_target_pairs={{0,2},{1,3},{2,0},{3,1},{4,6},{5,7},{6,4},{7,5},{8,10},{9,11},{10,... | collective-permute-start | bytes 98312 | tf_op jit(solution)/shard_map/ppermute | solution.py:28
  59.8 3.1 %fetch.4.refs_12_.refs_9_ = bf16[4,3584,256]{2,1,0:T(8,128)(2,1)S(1)} custom-call(bf16[4,3584,256]{2,1,0:T(8,128)(2,1)} %refs_0_.7, bf16[8,128]{1,0:T(8,128)(2,1)S(1)} %get-tuple-element.54.refs_1_.refs_13_), custom_call_target="tpu_custom_call" | custom-call | bytes 14680064 | tf_op jit(solution)/shard_map/fetch/pallas_call | solution.py:63
  64.0 2.3 %head_products.1.refs_0_.refs_4_ = bf16[8,2176]{1,0:T(8,128)(2,1)S(1)} custom-call(s32[16]{0:T(128)} %refs_0_.8, bf16[32,512]{1,0:T(8,128)(2,1)S(1)} %get-tuple-element.46.refs_1_, bf16[32,512]{1,0:T(8,128)(2,1)S(1)} %collective-permute-done.10.refs_2_, bf16[32,512]{1,0:T(8,128)(2,1)S(1)} %collective-permute-done.11.refs_3_, ...), custom_call_target="tpu_custom_call" | custom-call | tf_op jit(solution)/shard_map/head_products/pallas_call | solution.py:581
  66.3 1.5 %collective-permute-start.18 = (bf16[8,2176]{1,0:T(8,128)(2,1)S(1)}, bf16[8,2176]{1,0:T(8,128)(2,1)S(1)}, u32[]{:S(2)}, u32[]{:S(2)}) collective-permute-start(bf16[8,2176]{1,0:T(8,128)(2,1)S(1)} %head_products.1.refs_0_.refs_4_), channel_id=1, source_target_pairs={{0,8},{4,12},{8,0},{12,4},{1,9},{5,13},{9,1},{13,5},{2,10},{6,14},... | collective-permute-start | bytes 104456 | tf_op jit(solution)/shard_map/ppermute | solution.py:28
  68.2 2.0 %fetch.5.refs_4_ = bf16[2048,896]{1,0:T(8,128)(2,1)S(1)} custom-call(bf16[2048,896]{1,0:T(8,128)(2,1)} %refs_0_.9), custom_call_target="tpu_custom_call" | custom-call | bytes 7340032 | tf_op jit(solution)/shard_map/fetch/pallas_call | solution.py:63
  71.2 2.0 %collective-permute-start.22 = (bf16[32,896]{1,0:T(8,128)(2,1)S(1)}, bf16[32,896]{1,0:T(8,128)(2,1)S(1)}, u32[]{:S(2)}, u32[]{:S(2)}) collective-permute-start(bf16[32,896]{1,0:T(8,128)(2,1)S(1)} %output_product.1.refs_1_.refs_0_), channel_id=1, source_target_pairs={{0,3},{1,2},{2,1},{3,0},{4,7},{5,6},{6,5},{7,4},{8,11},{9,10},{10,... | collective-permute-start | bytes 172040 | tf_op jit(solution)/shard_map/ppermute | solution.py:28
  73.2 2.5 %collective-permute-start.20 = (bf16[32,896]{1,0:T(8,128)(2,1)S(1)}, bf16[32,896]{1,0:T(8,128)(2,1)S(1)}, u32[]{:S(2)}, u32[]{:S(2)}) collective-permute-start(bf16[32,896]{1,0:T(8,128)(2,1)S(1)} %output_product.1.refs_1_.refs_0_), channel_id=1, source_target_pairs={{0,1},{1,0},{2,3},{3,2},{4,5},{5,4},{6,7},{7,6},{8,9},{9,8},{10,11... | collective-permute-start | bytes 172040 | tf_op jit(solution)/shard_map/ppermute | solution.py:28
  75.7 3.1 %fetch.6.refs_8_.refs_10_ = bf16[4,3584,256]{2,1,0:T(8,128)(2,1)S(1)} custom-call(bf16[4,3584,256]{2,1,0:T(8,128)(2,1)} %refs_0_.10, bf16[32,896]{1,0:T(8,128)(2,1)S(1)} %output_product.1.refs_1_.refs_0_), custom_call_target="tpu_custom_call" | custom-call | bytes 14680064 | tf_op jit(solution)/shard_map/fetch/pallas_call | solution.py:63
  81.6 3.1 %fetch.7.refs_11_ = bf16[4,256,3584]{2,1,0:T(8,128)(2,1)S(1)} custom-call(bf16[4,256,3584]{2,1,0:T(8,128)(2,1)} %refs_0_.11, bf16[4,8,896]{2,1,0:T(8,128)(2,1)S(1)} %mix.1.refs_1_.refs_0_), custom_call_target="tpu_custom_call" | custom-call | bytes 14680064 | tf_op jit(solution)/shard_map/fetch/pallas_call | solution.py:63
  85.2 5.0 %run_experts.1 = (bf16[16,8,896]{2,1,0:T(8,128)(2,1)S(1)}, bf16[4,8,896]{2,1,0:T(8,128)(2,1)S(1)}) custom-call(bf16[4,8,896]{2,1,0:T(8,128)(2,1)S(1)} %mix.1.refs_1_.refs_0_, bf16[4,8,896]{2,1,0:T(8,128)(2,1)S(1)} %collective-permute-done.23.refs_1_, bf16[4,8,896]{2,1,0:T(8,128)(2,1)S(1)} %collective-permute-done.24.refs_2_, ...), custom_call_target="tpu_custom_call" | custom-call | tf_op jit(solution)/shard_map/run_experts/pallas_call | solution.py:714
  90.2 12.3 %all_to_all.10.block_ref = bf16[16,8,896]{2,1,0:T(8,128)(2,1)S(1)} all-to-all(bf16[16,8,896]{2,1,0:T(8,128)(2,1)S(1)} %get-tuple-element.55), channel_id=1, replica_groups=mesh['groups'=2,'expert'=4,'section'=4] {'expert','section'}, dimensions={0} | all-to-all | bytes 458752 | tf_op jit(solution)/shard_map/all_to_all | solution.py:849
  (59 shorter events, 25.2 us)
Async XLA Ops:
  2.8 13.1 %collective-permute-start = (bf16[640,224]{1,0:T(8,128)(2,1)}, bf16[640,224]{1,0:T(8,128)(2,1)S(1)}, u32[]{:S(2)}, u32[]{:S(2)}) collective-permute-start(bf16[640,224]{1,0:T(8,128)(2,1)} %get-tuple-element.32), channel_id=1, source_target_pairs={{0,4},{4,0},{8,12},{12,8},{1,5},{5,1},{9,13},{13,9},{2,6},{6,2},{1... | collective-permute-start | bytes 860168 | tf_op jit(solution)/shard_map/ppermute | solution.py:28
  3.3 9.6 %collective-permute-start.3 = (bf16[8,128,128]{2,1,0:T(8,128)(2,1)S(1)}, bf16[8,128,128]{2,1,0:T(8,128)(2,1)S(1)}, u32[]{:S(2)}, u32[]{:S(2)}) collective-permute-start(bf16[8,128,128]{2,1,0:T(8,128)(2,1)S(1)} %get-tuple-element.35), channel_id=1, source_target_pairs={{0,8},{4,12},{8,0},{12,4},{1,9},{5,13},{9,1},{13,5},{2,10},{6,14},... | collective-permute-start | bytes 786440 | tf_op jit(solution)/shard_map/ppermute | solution.py:28
  5.8 14.2 %collective-permute-start.1 = (bf16[640,224]{1,0:T(8,128)(2,1)}, bf16[640,224]{1,0:T(8,128)(2,1)S(1)}, u32[]{:S(2)}, u32[]{:S(2)}) collective-permute-start(bf16[640,224]{1,0:T(8,128)(2,1)} %get-tuple-element.33), channel_id=1, source_target_pairs={{0,8},{4,12},{8,0},{12,4},{1,9},{5,13},{9,1},{13,5},{2,10},{6,14},... | collective-permute-start | bytes 860168 | tf_op jit(solution)/shard_map/ppermute | solution.py:28
  5.8 20.8 %collective-permute-start.2 = (bf16[640,224]{1,0:T(8,128)(2,1)}, bf16[640,224]{1,0:T(8,128)(2,1)S(1)}, u32[]{:S(2)}, u32[]{:S(2)}) collective-permute-start(bf16[640,224]{1,0:T(8,128)(2,1)} %get-tuple-element.34), channel_id=1, source_target_pairs={{0,12},{4,8},{8,4},{12,0},{1,13},{5,9},{9,5},{13,1},{2,14},{6,10},... | collective-permute-start | bytes 860168 | tf_op jit(solution)/shard_map/ppermute | solution.py:28
  8.5 29.1 %collective-permute-start.6 = (bf16[576,224]{1,0:T(8,128)(2,1)S(1)}, bf16[576,224]{1,0:T(8,128)(2,1)S(1)}, u32[]{:S(2)}, u32[]{:S(2)}) collective-permute-start(bf16[576,224]{1,0:T(8,128)(2,1)S(1)} %dynamic-slice_bitcast_fusion.refs_4_.refs_2_), channel_id=1, source_target_pairs={{0,3},{1,2},{2,1},{3,0},{4,7},{5,6},{6,5},{7,4},{8,11},{9,10},{10,... | collective-permute-start | bytes 774152 | tf_op jit(solution)/shard_map/ppermute | solution.py:28
  12.9 25.1 %collective-permute-start.5 = (bf16[576,224]{1,0:T(8,128)(2,1)S(1)}, bf16[576,224]{1,0:T(8,128)(2,1)S(1)}, u32[]{:S(2)}, u32[]{:S(2)}) collective-permute-start(bf16[576,224]{1,0:T(8,128)(2,1)S(1)} %dynamic-slice_bitcast_fusion.refs_4_.refs_2_), channel_id=1, source_target_pairs={{0,2},{1,3},{2,0},{3,1},{4,6},{5,7},{6,4},{7,5},{8,10},{9,11},{10,... | collective-permute-start | bytes 774152 | tf_op jit(solution)/shard_map/ppermute | solution.py:28
  16.0 22.1 %collective-permute-start.4 = (bf16[576,224]{1,0:T(8,128)(2,1)S(1)}, bf16[576,224]{1,0:T(8,128)(2,1)S(1)}, u32[]{:S(2)}, u32[]{:S(2)}) collective-permute-start(bf16[576,224]{1,0:T(8,128)(2,1)S(1)} %dynamic-slice_bitcast_fusion.refs_4_.refs_2_), channel_id=1, source_target_pairs={{0,1},{1,0},{2,3},{3,2},{4,5},{5,4},{6,7},{7,6},{8,9},{9,8},{10,11... | collective-permute-start | bytes 774152 | tf_op jit(solution)/shard_map/ppermute | solution.py:28
  30.1 14.1 %all-to-all-start = ((bf16[16,48,128]{2,1,0:T(8,128)(2,1)}), bf16[16,48,128]{2,1,0:T(8,128)(2,1)S(1)}, u32[]{:S(2)}, u32[]{:S(2)}) async-start(bf16[16,48,128]{2,1,0:T(8,128)(2,1)} %copy-done.1), calls=%async_computation | async-start | bytes 393216 | tf_op jit(solution)/shard_map/all_to_all | solution.py:800
  36.0 16.0 %collective-permute-start.13 = (bf16[8,128,128]{2,1,0:T(8,128)(2,1)S(1)}, bf16[8,128,128]{2,1,0:T(8,128)(2,1)}, u32[]{:S(2)}, u32[]{:S(2)}) collective-permute-start(bf16[8,128,128]{2,1,0:T(8,128)(2,1)S(1)} %collective-permute-done.3.refs_9_.refs_7_), channel_id=1, source_target_pairs={{0,16},{16,0},{1,17},{17,1},{2,18},{18,2},{3,19},{19,3},{4,20},{20... | collective-permute-start | bytes 786440 | tf_op jit(solution)/shard_map/ppermute | solution.py:28
  40.2 8.0 %collective-permute-start.8 = (bf16[144,576]{1,0:T(8,128)(2,1)}, bf16[144,576]{1,0:T(8,128)(2,1)S(1)}, u32[]{:S(2)}, u32[]{:S(2)}) collective-permute-start(bf16[144,576]{1,0:T(8,128)(2,1)} %get-tuple-element.39), channel_id=1, source_target_pairs={{0,8},{4,12},{8,0},{12,4},{1,9},{5,13},{9,1},{13,5},{2,10},{6,14},... | collective-permute-start | bytes 497672 | tf_op jit(solution)/shard_map/ppermute | solution.py:28
  41.7 8.5 %collective-permute-start.9 = (bf16[144,576]{1,0:T(8,128)(2,1)}, bf16[144,576]{1,0:T(8,128)(2,1)S(1)}, u32[]{:S(2)}, u32[]{:S(2)}) collective-permute-start(bf16[144,576]{1,0:T(8,128)(2,1)} %get-tuple-element.40), channel_id=1, source_target_pairs={{0,12},{4,8},{8,4},{12,0},{1,13},{5,9},{9,5},{13,1},{2,14},{6,10},... | collective-permute-start | bytes 497672 | tf_op jit(solution)/shard_map/ppermute | solution.py:28
  41.7 8.5 %collective-permute-start.7 = (bf16[144,576]{1,0:T(8,128)(2,1)}, bf16[144,576]{1,0:T(8,128)(2,1)S(1)}, u32[]{:S(2)}, u32[]{:S(2)}) collective-permute-start(bf16[144,576]{1,0:T(8,128)(2,1)} %get-tuple-element.38.refs_6_), channel_id=1, source_target_pairs={{0,4},{4,0},{8,12},{12,8},{1,5},{5,1},{9,13},{13,9},{2,6},{6,2},{1... | collective-permute-start | bytes 497672 | tf_op jit(solution)/shard_map/ppermute | solution.py:28
  52.1 12.0 %collective-permute-start.14 = (bf16[16,128,128]{2,1,0:T(8,128)(2,1)S(1)}, bf16[16,128,128]{2,1,0:T(8,128)(2,1)S(1)}, u32[]{:S(2)}, u32[]{:S(2)}) collective-permute-start(bf16[16,128,128]{2,1,0:T(8,128)(2,1)S(1)} %copy-done), channel_id=1, source_target_pairs={{0,4},{4,0},{8,12},{12,8},{1,5},{5,1},{9,13},{13,9},{2,6},{6,2},{1... | collective-permute-start | bytes 1572872 | tf_op jit(solution)/shard_map/ppermute | solution.py:28
  52.9 5.4 %collective-permute-start.10 = (bf16[32,512]{1,0:T(8,128)(2,1)S(1)}, bf16[32,512]{1,0:T(8,128)(2,1)S(1)}, u32[]{:S(2)}, u32[]{:S(2)}) collective-permute-start(bf16[32,512]{1,0:T(8,128)(2,1)S(1)} %get-tuple-element.47), channel_id=1, source_target_pairs={{0,1},{1,0},{2,3},{3,2},{4,5},{5,4},{6,7},{7,6},{8,9},{9,8},{10,11... | collective-permute-start | bytes 98312 | tf_op jit(solution)/shard_map/ppermute | solution.py:28
  54.4 9.7 %collective-permute-start.15 = (bf16[8,128,128]{2,1,0:T(8,128)(2,1)S(1)}, bf16[8,128,128]{2,1,0:T(8,128)(2,1)S(1)}, u32[]{:S(2)}, u32[]{:S(2)}) collective-permute-start(bf16[8,128,128]{2,1,0:T(8,128)(2,1)S(1)} %collective-permute-done.3.refs_9_.refs_7_), channel_id=1, source_target_pairs={{0,4},{4,0},{8,12},{12,8},{1,5},{5,1},{9,13},{13,9},{2,6},{6,2},{1... | collective-permute-start | bytes 786440 | tf_op jit(solution)/shard_map/ppermute | solution.py:28
  54.4 9.7 %collective-permute-start.16 = (bf16[8,128,128]{2,1,0:T(8,128)(2,1)}, bf16[8,128,128]{2,1,0:T(8,128)(2,1)S(1)}, u32[]{:S(2)}, u32[]{:S(2)}) collective-permute-start(bf16[8,128,128]{2,1,0:T(8,128)(2,1)} %collective-permute-done.13.refs_8_), channel_id=1, source_target_pairs={{0,4},{4,0},{8,12},{12,8},{1,5},{5,1},{9,13},{13,9},{2,6},{6,2},{1... | collective-permute-start | bytes 786440 | tf_op jit(solution)/shard_map/ppermute | solution.py:28
  56.3 6.5 %collective-permute-start.11 = (bf16[32,512]{1,0:T(8,128)(2,1)S(1)}, bf16[32,512]{1,0:T(8,128)(2,1)S(1)}, u32[]{:S(2)}, u32[]{:S(2)}) collective-permute-start(bf16[32,512]{1,0:T(8,128)(2,1)S(1)} %get-tuple-element.48), channel_id=1, source_target_pairs={{0,2},{1,3},{2,0},{3,1},{4,6},{5,7},{6,4},{7,5},{8,10},{9,11},{10,... | collective-permute-start | bytes 98312 | tf_op jit(solution)/shard_map/ppermute | solution.py:28
  58.3 5.7 %collective-permute-start.12 = (bf16[32,512]{1,0:T(8,128)(2,1)S(1)}, bf16[32,512]{1,0:T(8,128)(2,1)S(1)}, u32[]{:S(2)}, u32[]{:S(2)}) collective-permute-start(bf16[32,512]{1,0:T(8,128)(2,1)S(1)} %get-tuple-element.49), channel_id=1, source_target_pairs={{0,3},{1,2},{2,1},{3,0},{4,7},{5,6},{6,5},{7,4},{8,11},{9,10},{10,... | collective-permute-start | bytes 98312 | tf_op jit(solution)/shard_map/ppermute | solution.py:28
  66.3 4.1 %collective-permute-start.18 = (bf16[8,2176]{1,0:T(8,128)(2,1)S(1)}, bf16[8,2176]{1,0:T(8,128)(2,1)S(1)}, u32[]{:S(2)}, u32[]{:S(2)}) collective-permute-start(bf16[8,2176]{1,0:T(8,128)(2,1)S(1)} %head_products.1.refs_0_.refs_4_), channel_id=1, source_target_pairs={{0,8},{4,12},{8,0},{12,4},{1,9},{5,13},{9,1},{13,5},{2,10},{6,14},... | collective-permute-start | bytes 104456 | tf_op jit(solution)/shard_map/ppermute | solution.py:28
  71.2 7.6 %collective-permute-start.22 = (bf16[32,896]{1,0:T(8,128)(2,1)S(1)}, bf16[32,896]{1,0:T(8,128)(2,1)S(1)}, u32[]{:S(2)}, u32[]{:S(2)}) collective-permute-start(bf16[32,896]{1,0:T(8,128)(2,1)S(1)} %output_product.1.refs_1_.refs_0_), channel_id=1, source_target_pairs={{0,3},{1,2},{2,1},{3,0},{4,7},{5,6},{6,5},{7,4},{8,11},{9,10},{10,... | collective-permute-start | bytes 172040 | tf_op jit(solution)/shard_map/ppermute | solution.py:28
  73.2 6.4 %collective-permute-start.21 = (bf16[32,896]{1,0:T(8,128)(2,1)S(1)}, bf16[32,896]{1,0:T(8,128)(2,1)S(1)}, u32[]{:S(2)}, u32[]{:S(2)}) collective-permute-start(bf16[32,896]{1,0:T(8,128)(2,1)S(1)} %output_product.1.refs_1_.refs_0_), channel_id=1, source_target_pairs={{0,2},{1,3},{2,0},{3,1},{4,6},{5,7},{6,4},{7,5},{8,10},{9,11},{10,... | collective-permute-start | bytes 172040 | tf_op jit(solution)/shard_map/ppermute | solution.py:28
  73.2 6.4 %collective-permute-start.20 = (bf16[32,896]{1,0:T(8,128)(2,1)S(1)}, bf16[32,896]{1,0:T(8,128)(2,1)S(1)}, u32[]{:S(2)}, u32[]{:S(2)}) collective-permute-start(bf16[32,896]{1,0:T(8,128)(2,1)S(1)} %output_product.1.refs_1_.refs_0_), channel_id=1, source_target_pairs={{0,1},{1,0},{2,3},{3,2},{4,5},{5,4},{6,7},{7,6},{8,9},{9,8},{10,11... | collective-permute-start | bytes 172040 | tf_op jit(solution)/shard_map/ppermute | solution.py:28
  79.7 5.0 %collective-permute-start.25 = (bf16[4,8,896]{2,1,0:T(8,128)(2,1)S(1)}, bf16[4,8,896]{2,1,0:T(8,128)(2,1)S(1)}, u32[]{:S(2)}, u32[]{:S(2)}) collective-permute-start(bf16[4,8,896]{2,1,0:T(8,128)(2,1)S(1)} %mix.1.refs_1_.refs_0_), channel_id=1, source_target_pairs={{0,12},{4,8},{8,4},{12,0},{1,13},{5,9},{9,5},{13,1},{2,14},{6,10},... | collective-permute-start | bytes 172040 | tf_op jit(solution)/shard_map/ppermute | solution.py:28
  80.5 4.7 %collective-permute-start.24 = (bf16[4,8,896]{2,1,0:T(8,128)(2,1)S(1)}, bf16[4,8,896]{2,1,0:T(8,128)(2,1)S(1)}, u32[]{:S(2)}, u32[]{:S(2)}) collective-permute-start(bf16[4,8,896]{2,1,0:T(8,128)(2,1)S(1)} %mix.1.refs_1_.refs_0_), channel_id=1, source_target_pairs={{0,8},{4,12},{8,0},{12,4},{1,9},{5,13},{9,1},{13,5},{2,10},{6,14},... | collective-permute-start | bytes 172040 | tf_op jit(solution)/shard_map/ppermute | solution.py:28
  (7 other events, 64.3 us)

commit v13 on v12

--- a/solution.py
+++ b/solution.py
@@ -488,7 +488,8 @@
 
 
 def attend(
-    parts, positions, lengths, kv_gain, table, gathered, sources, steps, sections, score_scale
+    parts, positions, lengths, kv_gain, table, gathered, sources, steps, sections, score_scale,
+    after
 ):
     prompts, rows, latent = gathered[0].shape
     out = (rows // sections, latent)
@@ -502,17 +503,18 @@
         + [jax.ShapeDtypeStruct((8, 128), jnp.bfloat16)],
         in_specs=[held] * len(parts)
         + [pl.BlockSpec(memory_space=pltpu.SMEM)]
-        + [held] * 7,
+        + [held] * 7
+        + [pl.BlockSpec(memory_space=pl.ANY)] * len(after),
         out_specs=[held] * (sections + 1),
         scratch_shapes=[pltpu.VMEM((sections,) + out, jnp.bfloat16)],
         compiler_params=params(*parts, *gathered, scale=6),
         name="attend",
-    )(*parts, *at_home(lengths, kv_gain, *table), *gathered)
+    )(*parts, *at_home(lengths, kv_gain, *table), *gathered, *after)
 
 
 def value_kernel(experts, sections, heads, steps, sources, count, *refs):
     owner_ref, latent_refs, uv_refs = refs[0], refs[1 : 1 + sections], refs[1 + sections :]
-    route_ref = uv_refs[count]
+    name_ref, score_ref = uv_refs[count : count + 2]
     uv_refs = list(uv_refs[:count])
     out_ref, held = refs[-2:]
     group_rank, groups = lax.axis_index("groups"), lax.axis_size("groups")
@@ -568,10 +570,15 @@
     out_ref[:, :width] = jnp.dot(
         order.astype(bf16), values, preferred_element_type=f32
     ).astype(bf16)
-    out_ref[:, width:] = route_ref[...]
-
-
-def head_products(owners, latents, uv_parts, route, steps, sources, after):
+    names = jnp.concatenate([name_ref[step] for step in range(steps)], axis=0).astype(f32)
+    scores = jnp.concatenate([score_ref[step] for step in range(steps)], axis=0)
+    high = scores.astype(bf16).astype(f32)
+    spare = jnp.zeros((size, out_ref.shape[1] - width - 3 * names.shape[1]), f32)
+    route = jnp.concatenate([names, high, scores - high, spare], axis=1)
+    out_ref[:, width:] = route.astype(bf16)
+
+
+def head_products(owners, latents, uv_parts, names, scores, steps, sources, after):
     rows, width = latents[0].shape
     heads, value, _ = uv_parts[0][0].shape
     experts = len(uv_parts)
@@ -583,10 +590,10 @@
             value_kernel, experts, len(latents), heads, steps, sources, len(uv_parts)
         ),
         out_shape=jax.ShapeDtypeStruct(
-            (total // heads, heads * value + route.shape[1]), jnp.bfloat16
+            (total // heads, heads * value + 128), jnp.bfloat16
         ),
         in_specs=[pl.BlockSpec(memory_space=pltpu.SMEM)]
-        + [held] * (len(latents) + len(uv_parts) + 1)
+        + [held] * (len(latents) + len(uv_parts) + 2)
         + [pl.BlockSpec(memory_space=pl.ANY)] * len(after),
         out_specs=held,
         scratch_shapes=[
@@ -594,7 +601,7 @@
         ],
         compiler_params=params(*latents, *uv_parts, scale=4),
         name="head_products",
-    )(*at_home(owners), *latents, *uv_parts, route, *after)
+    )(*at_home(owners), *latents, *uv_parts, *at_home(names, scores), *after)
 
 
 def output_kernel(experts, *refs):
@@ -807,27 +814,23 @@
         blocks, lengths, owners, kv_gain, table, prompt_count, tokens_here, experts, sections,
         steps, heads
     ))
+    uv_shares = spread(uv_share, "groups")
+    later = masks[1:-1] + masks[:1]
+    held = [doubled({far: share}, "expert", later) for share in uv_shares]
+    uv_parts = {mask: [share[mask] for share in held] for mask in held[0]}
+    for mask, part in doubled({0: w_uv}, "expert", later).items():
+        uv_parts[mask] = [part]
     *out_latent, token = attend(
         parts, full_length, lengths, kv_gain, table, gathered, tokens_here, steps, sections,
         queries.shape[-1] ** (-0.5),
+        [share for mask in range(1, experts) for share in uv_parts[mask]],
     )
 
     (w_gate,) = fetch([w_gate], [token])
-    uv_shares = spread(uv_share, "groups")
-    *uv_shares, uv_own, token = lax.optimization_barrier((*uv_shares, w_uv, token))
-    later = masks[1:-1] + masks[:1]
-    held = [doubled({far: share}, "expert", later) for share in uv_shares]
-    uv_parts = {mask: [share[mask] for share in held] for mask in held[0]}
-    for mask, part in doubled({0: uv_own}, "expert", later).items():
-        uv_parts[mask] = [part]
     out_latent = deliver(out_latent, "section")
-    high = route_scores.astype(bf16)
-    low = (route_scores - high.astype(f32)).astype(bf16)
-    route = jnp.concatenate([expert_ids.astype(bf16), high, low], axis=2).reshape(own_rows, -1)
-    route = jnp.pad(route, ((0, 0), (0, 128 - route.shape[1])))
     head_values = head_products(
-        owners, out_latent, [uv_parts[mask] for mask in range(experts)], route, steps,
-        tokens_here, [w_gate, token],
+        owners, out_latent, [uv_parts[mask] for mask in range(experts)], expert_ids,
+        route_scores, steps, tokens_here, [w_gate],
     )
     head_values = spread(head_values, "expert")
 

time: 104 us -> 103 us (level)
  starting transfers between devices: 36.9 us -> 35.2 us
  other arithmetic: 1.53 us -> 0 us
  waiting for transfers between devices: 18.9 us -> 20.2 us
    ppermute x26, waiting for transfers between devices: 17.6 us -> 20.2 us  [swap(): return lax.ppermute(block, axis, [(i, i ^ mask) for i in range(size)])]
    ppermute x26, starting transfers between devices: 31 us -> 29.2 us  [swap(): return lax.ppermute(block, axis, [(i, i ^ mask) for i in range(size)])]
    convert_element_type x2 -> x0, other arithmetic: 1.45 us -> none  [the longest x1 0.77 us: local(): low = (route_scores - high.astype(f32)).astype(bf16)]
    all_to_all x1, waiting for transfers between devices: 1.29 us -> 0.01 us  [local(): blocks = lax.all_to_all(blocks, ('expert', 'section'), 0, 0, tiled=True)]
  transfers between devices with their start and end apart: 27 -> 27, of which waited for: 11 -> 10; matrix products, arithmetic and copies ran while one was open for 3% -> 1% of each run, Pallas kernels for 18% -> 17%
where the time goes in v13:
time: 103 us; the launch traced here: 102 us
  starting transfers between devices  35.2 us (34%)
  Pallas kernels  30.9 us (30%)
  waiting for transfers between devices  20.2 us (20%)
  blocking collectives  12.3 us (12%)
  local copies, waits for them, and re-layouts  3.36 us (3%)
    ppermute x26, starting transfers between devices, swap(): return lax.ppermute(block, axis, [(i, i ^ mask) for i in range(size)])  29.2 us
    ppermute x26, waiting for transfers between devices, swap(): return lax.ppermute(block, axis, [(i, i ^ mask) for i in range(size)])  20.2 us
    all_to_all x1, blocking collectives, local(): blocks = lax.all_to_all(blocks, ('expert', 'section'), 0, 0, tiled=True)  12.3 us
    pallas_call x4, Pallas kernels, fetch(): pl.pallas_call(functools.partial(fetch_kernel, len(arrays)), out_shape=[p...  11.4 us
    all_to_all x1, starting transfers between devices, local(): blocks = lax.all_to_all(blocks, ('expert', 'section'), 0, 0, tiled=True)  5.95 us
    pallas_call x1, Pallas kernels, run_experts(): pl.pallas_call(functools.partial(expert_kernel, experts, sections, picks)...  4.97 us
    pallas_call x1, Pallas kernels, cut_columns(): pl.pallas_call(functools.partial(cut_kernel, sections, experts, piece), o...  2.56 us
    pallas_call x1, Pallas kernels, absorb_queries(): pl.pallas_call(functools.partial(query_kernel, experts, sections, prompts...  2.2 us
  transfers between devices with their start and end apart: 27, of which 10 were waited for; matrix products, arithmetic and copies ran while one was open for 1% of the time, Pallas kernels for 17%

profile of v13, /device:TPU:0, one launch (start us, length us, event | category | flops | bytes accessed | tf_op | source)
XLA Modules:
  0.0 102.1 jit_solution(7211089994707857288)
XLA Ops:
  0.0 2.6 %cut_columns.1 = (bf16[8,128,128]{2,1,0:T(8,128)(2,1)S(1)}, bf16[640,224]{1,0:T(8,128)(2,1)S(1)}, bf16[640,224]{1,0:T(8,128)(2,1)S(1)}, bf16[640,224]{1,0:T(8,128)(2,1)S(1)}, bf16[640,224]{1,0:T(8,128)(2,1)}) custom-call(bf16[128,3584]{1,0:T(8,128)(2,1)} %bitcast.5, bf16[2,4,16,192]{3,2,1,0:T(8,128)(2,1)} %query_ref.1, bf16[16,128,128]{2,1,0:T(8,128)(2,1)} %refs_5_.5), custom_call_target="tpu_custom_call" | custom-call | tf_op jit(solution)/shard_map/cut_columns/pallas_call | solution.py:110
  3.0 2.5 %collective-permute-start.3 = (bf16[8,128,128]{2,1,0:T(8,128)(2,1)S(1)}, bf16[8,128,128]{2,1,0:T(8,128)(2,1)S(1)}, u32[]{:S(2)}, u32[]{:S(2)}) collective-permute-start(bf16[8,128,128]{2,1,0:T(8,128)(2,1)S(1)} %get-tuple-element.31), channel_id=1, source_target_pairs={{0,8},{4,12},{8,0},{12,4},{1,9},{5,13},{9,1},{13,5},{2,10},{6,14},... | collective-permute-start | bytes 786440 | tf_op jit(solution)/shard_map/ppermute | solution.py:28
  5.5 1.5 %collective-permute-start.2 = (bf16[640,224]{1,0:T(8,128)(2,1)}, bf16[640,224]{1,0:T(8,128)(2,1)S(1)}, u32[]{:S(2)}, u32[]{:S(2)}) collective-permute-start(bf16[640,224]{1,0:T(8,128)(2,1)} %get-tuple-element.30), channel_id=1, source_target_pairs={{0,12},{4,8},{8,4},{12,0},{1,13},{5,9},{9,5},{13,1},{2,14},{6,10},... | collective-permute-start | bytes 860168 | tf_op jit(solution)/shard_map/ppermute | solution.py:28
  8.2 3.7 %collective-permute-start.6 = (bf16[576,224]{1,0:T(8,128)(2,1)S(1)}, bf16[576,224]{1,0:T(8,128)(2,1)S(1)}, u32[]{:S(2)}, u32[]{:S(2)}) collective-permute-start(bf16[576,224]{1,0:T(8,128)(2,1)S(1)} %dynamic-slice_bitcast_fusion.refs_4_.refs_2_), channel_id=1, source_target_pairs={{0,3},{1,2},{2,1},{3,0},{4,7},{5,6},{6,5},{7,4},{8,11},{9,10},{10,... | collective-permute-start | bytes 774152 | tf_op jit(solution)/shard_map/ppermute | solution.py:28
  12.7 3.0 %collective-permute-start.5 = (bf16[576,224]{1,0:T(8,128)(2,1)S(1)}, bf16[576,224]{1,0:T(8,128)(2,1)S(1)}, u32[]{:S(2)}, u32[]{:S(2)}) collective-permute-start(bf16[576,224]{1,0:T(8,128)(2,1)S(1)} %dynamic-slice_bitcast_fusion.refs_4_.refs_2_), channel_id=1, source_target_pairs={{0,2},{1,3},{2,0},{3,1},{4,6},{5,7},{6,4},{7,5},{8,10},{9,11},{10,... | collective-permute-start | bytes 774152 | tf_op jit(solution)/shard_map/ppermute | solution.py:28
  15.7 1.6 %collective-permute-start.4 = (bf16[576,224]{1,0:T(8,128)(2,1)S(1)}, bf16[576,224]{1,0:T(8,128)(2,1)S(1)}, u32[]{:S(2)}, u32[]{:S(2)}) collective-permute-start(bf16[576,224]{1,0:T(8,128)(2,1)S(1)} %dynamic-slice_bitcast_fusion.refs_4_.refs_2_), channel_id=1, source_target_pairs={{0,1},{1,0},{2,3},{3,2},{4,5},{5,4},{6,7},{7,6},{8,9},{9,8},{10,11... | collective-permute-start | bytes 774152 | tf_op jit(solution)/shard_map/ppermute | solution.py:28
  17.3 2.4 %collective-permute-done.1.refs_3_.refs_1_ = bf16[640,224]{1,0:T(8,128)(2,1)S(1)} collective-permute-done((bf16[640,224]{1,0:T(8,128)(2,1)S(1)}, bf16[640,224]{1,0:T(8,128)(2,1)S(1)}, u32[]{:S(2)}, u32[]{:S(2)}) %collective-permute-start.1) | collective-permute-done | bytes 286752 | tf_op jit(solution)/shard_map/ppermute | solution.py:28
  19.7 6.7 %collective-permute-done.2.refs_4_.refs_2_ = bf16[640,224]{1,0:T(8,128)(2,1)S(1)} collective-permute-done((bf16[640,224]{1,0:T(8,128)(2,1)}, bf16[640,224]{1,0:T(8,128)(2,1)S(1)}, u32[]{:S(2)}, u32[]{:S(2)}) %collective-permute-start.2) | collective-permute-done | bytes 286752 | tf_op jit(solution)/shard_map/ppermute | solution.py:28
  26.3 1.6 %collective-permute-start.11 = (bf16[8,128,128]{2,1,0:T(8,128)(2,1)S(1)}, bf16[8,128,128]{2,1,0:T(8,128)(2,1)S(1)}, u32[]{:S(2)}, u32[]{:S(2)}) collective-permute-start(bf16[8,128,128]{2,1,0:T(8,128)(2,1)S(1)} %collective-permute-done.3.refs_9_.refs_13_.refs_7_), channel_id=1, source_target_pairs={{0,16},{16,0},{1,17},{17,1},{2,18},{18,2},{3,19},{19,3},{4,20},{20... | collective-permute-start | bytes 786440 | tf_op jit(solution)/shard_map/ppermute | solution.py:28
  27.9 2.2 %absorb_queries.1 = (bf16[16,48,128]{2,1,0:T(8,128)(2,1)S(1)}, bf16[4,16,576]{2,1,0:T(8,128)(2,1)S(1)}, bf16[8,128]{1,0:T(8,128)(2,1)S(1)}) custom-call(s32[16]{0:T(128)} %refs_0_.8, bf16[640,224]{1,0:T(8,128)(2,1)S(1)} %get-tuple-element.27.refs_1_.refs_0_, bf16[640,224]{1,0:T(8,128)(2,1)S(1)} %collective-permute-done.refs_2_.refs_0_, ...), custom_call_target="tpu_custom_call" | custom-call | tf_op jit(solution)/shard_map/absorb_queries/pallas_call | solution.py:287
  31.4 6.0 %all-to-all-start = ((bf16[16,48,128]{2,1,0:T(8,128)(2,1)}), bf16[16,48,128]{2,1,0:T(8,128)(2,1)}, u32[]{:S(2)}, u32[]{:S(2)}) async-start(bf16[16,48,128]{2,1,0:T(8,128)(2,1)} %copy-done.3), calls=%async_computation | async-start | bytes 393216 | tf_op jit(solution)/shard_map/all_to_all | solution.py:807
  42.3 6.0 %collective-permute-done.8.refs_2_.refs_6_ = bf16[144,576]{1,0:T(8,128)(2,1)S(1)} collective-permute-done((bf16[144,576]{1,0:T(8,128)(2,1)S(1)}, bf16[144,576]{1,0:T(8,128)(2,1)S(1)}, u32[]{:S(2)}, u32[]{:S(2)}) %collective-permute-start.8) | collective-permute-done | bytes 165920 | tf_op jit(solution)/shard_map/ppermute | solution.py:28
  51.0 2.0 %attend.1 = (bf16[32,512]{1,0:T(8,128)(2,1)S(1)}, bf16[32,512]{1,0:T(8,128)(2,1)S(1)}, bf16[32,512]{1,0:T(8,128)(2,1)S(1)}, bf16[32,512]{1,0:T(8,128)(2,1)S(1)}, bf16[8,128]{1,0:T(8,128)(2,1)S(1)}) custom-call(bf16[144,576]{1,0:T(8,128)(2,1)S(1)} %project.3.refs_0_.refs_4_, bf16[144,576]{1,0:T(8,128)(2,1)} %collective-permute-done.7.refs_1_.refs_5_, ...), custom_call_target="tpu_custom_call" | custom-call | tf_op jit(solution)/shard_map/attend/pallas_call | solution.py:497
  53.0 2.0 %collective-permute-start.14 = (bf16[32,512]{1,0:T(8,128)(2,1)S(1)}, bf16[32,512]{1,0:T(8,128)(2,1)S(1)}, u32[]{:S(2)}, u32[]{:S(2)}) collective-permute-start(bf16[32,512]{1,0:T(8,128)(2,1)S(1)} %get-tuple-element.43), channel_id=1, source_target_pairs={{0,1},{1,0},{2,3},{3,2},{4,5},{5,4},{6,7},{7,6},{8,9},{9,8},{10,11... | collective-permute-start | bytes 98312 | tf_op jit(solution)/shard_map/ppermute | solution.py:28
  54.9 2.0 %collective-permute-start.15 = (bf16[32,512]{1,0:T(8,128)(2,1)S(1)}, bf16[32,512]{1,0:T(8,128)(2,1)S(1)}, u32[]{:S(2)}, u32[]{:S(2)}) collective-permute-start(bf16[32,512]{1,0:T(8,128)(2,1)S(1)} %get-tuple-element.44), channel_id=1, source_target_pairs={{0,2},{1,3},{2,0},{3,1},{4,6},{5,7},{6,4},{7,5},{8,10},{9,11},{10,... | collective-permute-start | bytes 98312 | tf_op jit(solution)/shard_map/ppermute | solution.py:28
  57.4 3.1 %fetch.4.refs_13_.refs_9_ = bf16[4,3584,256]{2,1,0:T(8,128)(2,1)S(1)} custom-call(bf16[4,3584,256]{2,1,0:T(8,128)(2,1)} %refs_0_.7, bf16[8,128]{1,0:T(8,128)(2,1)S(1)} %get-tuple-element.46.refs_1_), custom_call_target="tpu_custom_call" | custom-call | bytes 14680064 | tf_op jit(solution)/shard_map/fetch/pallas_call | solution.py:63
  60.6 2.0 %collective-permute-done.16.refs_4_ = bf16[32,512]{1,0:T(8,128)(2,1)S(1)} collective-permute-done((bf16[32,512]{1,0:T(8,128)(2,1)S(1)}, bf16[32,512]{1,0:T(8,128)(2,1)S(1)}, u32[]{:S(2)}, u32[]{:S(2)}) %collective-permute-start.16) | collective-permute-done | bytes 32800 | tf_op jit(solution)/shard_map/ppermute | solution.py:28
  62.6 2.0 %head_products.1.refs_0_.refs_4_ = bf16[8,2176]{1,0:T(8,128)(2,1)S(1)} custom-call(s32[16]{0:T(128)} %refs_0_.8, bf16[32,512]{1,0:T(8,128)(2,1)S(1)} %get-tuple-element.42.refs_1_, bf16[32,512]{1,0:T(8,128)(2,1)S(1)} %collective-permute-done.14.refs_2_, bf16[32,512]{1,0:T(8,128)(2,1)S(1)} %collective-permute-done.15.refs_3_, ...), custom_call_target="tpu_custom_call" | custom-call | tf_op jit(solution)/shard_map/head_products/pallas_call | solution.py:588
  66.5 2.0 %fetch.5.refs_4_ = bf16[2048,896]{1,0:T(8,128)(2,1)S(1)} custom-call(bf16[2048,896]{1,0:T(8,128)(2,1)} %refs_0_.9), custom_call_target="tpu_custom_call" | custom-call | bytes 7340032 | tf_op jit(solution)/shard_map/fetch/pallas_call | solution.py:63
  70.9 3.1 %collective-permute-start.20 = (bf16[32,896]{1,0:T(8,128)(2,1)S(1)}, bf16[32,896]{1,0:T(8,128)(2,1)S(1)}, u32[]{:S(2)}, u32[]{:S(2)}) collective-permute-start(bf16[32,896]{1,0:T(8,128)(2,1)S(1)} %output_product.1.refs_1_.refs_0_), channel_id=1, source_target_pairs={{0,1},{1,0},{2,3},{3,2},{4,5},{5,4},{6,7},{7,6},{8,9},{9,8},{10,11... | collective-permute-start | bytes 172040 | tf_op jit(solution)/shard_map/ppermute | solution.py:28
  74.0 3.1 %fetch.6.refs_8_.refs_10_ = bf16[4,3584,256]{2,1,0:T(8,128)(2,1)S(1)} custom-call(bf16[4,3584,256]{2,1,0:T(8,128)(2,1)} %refs_0_.10, bf16[32,896]{1,0:T(8,128)(2,1)S(1)} %output_product.1.refs_1_.refs_0_), custom_call_target="tpu_custom_call" | custom-call | bytes 14680064 | tf_op jit(solution)/shard_map/fetch/pallas_call | solution.py:63
  80.6 3.1 %fetch.7.refs_11_ = bf16[4,256,3584]{2,1,0:T(8,128)(2,1)S(1)} custom-call(bf16[4,256,3584]{2,1,0:T(8,128)(2,1)} %refs_0_.11, bf16[4,8,896]{2,1,0:T(8,128)(2,1)S(1)} %mix.1.refs_1_.refs_0_), custom_call_target="tpu_custom_call" | custom-call | bytes 14680064 | tf_op jit(solution)/shard_map/fetch/pallas_call | solution.py:63
  84.2 5.0 %run_experts.1 = (bf16[16,8,896]{2,1,0:T(8,128)(2,1)S(1)}, bf16[4,8,896]{2,1,0:T(8,128)(2,1)S(1)}) custom-call(bf16[4,8,896]{2,1,0:T(8,128)(2,1)S(1)} %mix.1.refs_1_.refs_0_, bf16[4,8,896]{2,1,0:T(8,128)(2,1)S(1)} %collective-permute-done.23.refs_1_, bf16[4,8,896]{2,1,0:T(8,128)(2,1)S(1)} %collective-permute-done.24.refs_2_, ...), custom_call_target="tpu_custom_call" | custom-call | tf_op jit(solution)/shard_map/run_experts/pallas_call | solution.py:721
  89.2 12.3 %all_to_all.10.block_ref = bf16[16,8,896]{2,1,0:T(8,128)(2,1)S(1)} all-to-all(bf16[16,8,896]{2,1,0:T(8,128)(2,1)S(1)} %get-tuple-element.47), channel_id=1, replica_groups=mesh['groups'=2,'expert'=4,'section'=4] {'expert','section'}, dimensions={0} | all-to-all | bytes 458752 | tf_op jit(solution)/shard_map/all_to_all | solution.py:852
  (55 shorter events, 20.6 us)
Async XLA Ops:
  2.6 13.1 %collective-permute-start = (bf16[640,224]{1,0:T(8,128)(2,1)S(1)}, bf16[640,224]{1,0:T(8,128)(2,1)S(1)}, u32[]{:S(2)}, u32[]{:S(2)}) collective-permute-start(bf16[640,224]{1,0:T(8,128)(2,1)S(1)} %get-tuple-element.28), channel_id=1, source_target_pairs={{0,4},{4,0},{8,12},{12,8},{1,5},{5,1},{9,13},{13,9},{2,6},{6,2},{1... | collective-permute-start | bytes 860168 | tf_op jit(solution)/shard_map/ppermute | solution.py:28
  3.0 9.6 %collective-permute-start.3 = (bf16[8,128,128]{2,1,0:T(8,128)(2,1)S(1)}, bf16[8,128,128]{2,1,0:T(8,128)(2,1)S(1)}, u32[]{:S(2)}, u32[]{:S(2)}) collective-permute-start(bf16[8,128,128]{2,1,0:T(8,128)(2,1)S(1)} %get-tuple-element.31), channel_id=1, source_target_pairs={{0,8},{4,12},{8,0},{12,4},{1,9},{5,13},{9,1},{13,5},{2,10},{6,14},... | collective-permute-start | bytes 786440 | tf_op jit(solution)/shard_map/ppermute | solution.py:28
  5.5 14.2 %collective-permute-start.1 = (bf16[640,224]{1,0:T(8,128)(2,1)S(1)}, bf16[640,224]{1,0:T(8,128)(2,1)S(1)}, u32[]{:S(2)}, u32[]{:S(2)}) collective-permute-start(bf16[640,224]{1,0:T(8,128)(2,1)S(1)} %get-tuple-element.29), channel_id=1, source_target_pairs={{0,8},{4,12},{8,0},{12,4},{1,9},{5,13},{9,1},{13,5},{2,10},{6,14},... | collective-permute-start | bytes 860168 | tf_op jit(solution)/shard_map/ppermute | solution.py:28
  5.5 20.8 %collective-permute-start.2 = (bf16[640,224]{1,0:T(8,128)(2,1)}, bf16[640,224]{1,0:T(8,128)(2,1)S(1)}, u32[]{:S(2)}, u32[]{:S(2)}) collective-permute-start(bf16[640,224]{1,0:T(8,128)(2,1)} %get-tuple-element.30), channel_id=1, source_target_pairs={{0,12},{4,8},{8,4},{12,0},{1,13},{5,9},{9,5},{13,1},{2,14},{6,10},... | collective-permute-start | bytes 860168 | tf_op jit(solution)/shard_map/ppermute | solution.py:28
  8.2 29.1 %collective-permute-start.6 = (bf16[576,224]{1,0:T(8,128)(2,1)S(1)}, bf16[576,224]{1,0:T(8,128)(2,1)S(1)}, u32[]{:S(2)}, u32[]{:S(2)}) collective-permute-start(bf16[576,224]{1,0:T(8,128)(2,1)S(1)} %dynamic-slice_bitcast_fusion.refs_4_.refs_2_), channel_id=1, source_target_pairs={{0,3},{1,2},{2,1},{3,0},{4,7},{5,6},{6,5},{7,4},{8,11},{9,10},{10,... | collective-permute-start | bytes 774152 | tf_op jit(solution)/shard_map/ppermute | solution.py:28
  12.7 25.1 %collective-permute-start.5 = (bf16[576,224]{1,0:T(8,128)(2,1)S(1)}, bf16[576,224]{1,0:T(8,128)(2,1)S(1)}, u32[]{:S(2)}, u32[]{:S(2)}) collective-permute-start(bf16[576,224]{1,0:T(8,128)(2,1)S(1)} %dynamic-slice_bitcast_fusion.refs_4_.refs_2_), channel_id=1, source_target_pairs={{0,2},{1,3},{2,0},{3,1},{4,6},{5,7},{6,4},{7,5},{8,10},{9,11},{10,... | collective-permute-start | bytes 774152 | tf_op jit(solution)/shard_map/ppermute | solution.py:28
  15.7 22.1 %collective-permute-start.4 = (bf16[576,224]{1,0:T(8,128)(2,1)S(1)}, bf16[576,224]{1,0:T(8,128)(2,1)S(1)}, u32[]{:S(2)}, u32[]{:S(2)}) collective-permute-start(bf16[576,224]{1,0:T(8,128)(2,1)S(1)} %dynamic-slice_bitcast_fusion.refs_4_.refs_2_), channel_id=1, source_target_pairs={{0,1},{1,0},{2,3},{3,2},{4,5},{5,4},{6,7},{7,6},{8,9},{9,8},{10,11... | collective-permute-start | bytes 774152 | tf_op jit(solution)/shard_map/ppermute | solution.py:28
  19.7 31.3 %collective-permute-start.10 = (bf16[16,128,128]{2,1,0:T(8,128)(2,1)}, bf16[16,128,128]{2,1,0:T(8,128)(2,1)S(1)}, u32[]{:S(2)}, u32[]{:S(2)}) collective-permute-start(bf16[16,128,128]{2,1,0:T(8,128)(2,1)} %refs_5_.5), channel_id=1, source_target_pairs={{0,4},{4,0},{8,12},{12,8},{1,5},{5,1},{9,13},{13,9},{2,6},{6,2},{1... | collective-permute-start | bytes 1572872 | tf_op jit(solution)/shard_map/ppermute | solution.py:28
  26.3 15.3 %collective-permute-start.11 = (bf16[8,128,128]{2,1,0:T(8,128)(2,1)S(1)}, bf16[8,128,128]{2,1,0:T(8,128)(2,1)S(1)}, u32[]{:S(2)}, u32[]{:S(2)}) collective-permute-start(bf16[8,128,128]{2,1,0:T(8,128)(2,1)S(1)} %collective-permute-done.3.refs_9_.refs_13_.refs_7_), channel_id=1, source_target_pairs={{0,16},{16,0},{1,17},{17,1},{2,18},{18,2},{3,19},{19,3},{4,20},{20... | collective-permute-start | bytes 786440 | tf_op jit(solution)/shard_map/ppermute | solution.py:28
  31.4 17.3 %all-to-all-start = ((bf16[16,48,128]{2,1,0:T(8,128)(2,1)}), bf16[16,48,128]{2,1,0:T(8,128)(2,1)}, u32[]{:S(2)}, u32[]{:S(2)}) async-start(bf16[16,48,128]{2,1,0:T(8,128)(2,1)} %copy-done.3), calls=%async_computation | async-start | bytes 393216 | tf_op jit(solution)/shard_map/all_to_all | solution.py:807
  40.1 8.2 %collective-permute-start.8 = (bf16[144,576]{1,0:T(8,128)(2,1)S(1)}, bf16[144,576]{1,0:T(8,128)(2,1)S(1)}, u32[]{:S(2)}, u32[]{:S(2)}) collective-permute-start(bf16[144,576]{1,0:T(8,128)(2,1)S(1)} %get-tuple-element.35), channel_id=1, source_target_pairs={{0,8},{4,12},{8,0},{12,4},{1,9},{5,13},{9,1},{13,5},{2,10},{6,14},... | collective-permute-start | bytes 497672 | tf_op jit(solution)/shard_map/ppermute | solution.py:28
  41.6 9.3 %collective-permute-start.12 = (bf16[8,128,128]{2,1,0:T(8,128)(2,1)S(1)}, bf16[8,128,128]{2,1,0:T(8,128)(2,1)S(1)}, u32[]{:S(2)}, u32[]{:S(2)}) collective-permute-start(bf16[8,128,128]{2,1,0:T(8,128)(2,1)S(1)} %collective-permute-done.3.refs_9_.refs_13_.refs_7_), channel_id=1, source_target_pairs={{0,4},{4,0},{8,12},{12,8},{1,5},{5,1},{9,13},{13,9},{2,6},{6,2},{1... | collective-permute-start | bytes 786440 | tf_op jit(solution)/shard_map/ppermute | solution.py:28
  41.7 9.3 %collective-permute-start.13 = (bf16[8,128,128]{2,1,0:T(8,128)(2,1)S(1)}, bf16[8,128,128]{2,1,0:T(8,128)(2,1)S(1)}, u32[]{:S(2)}, u32[]{:S(2)}) collective-permute-start(bf16[8,128,128]{2,1,0:T(8,128)(2,1)S(1)} %collective-permute-done.11.refs_14_.refs_8_), channel_id=1, source_target_pairs={{0,4},{4,0},{8,12},{12,8},{1,5},{5,1},{9,13},{13,9},{2,6},{6,2},{1... | collective-permute-start | bytes 786440 | tf_op jit(solution)/shard_map/ppermute | solution.py:28
  42.2 8.8 %collective-permute-start.9 = (bf16[144,576]{1,0:T(8,128)(2,1)}, bf16[144,576]{1,0:T(8,128)(2,1)}, u32[]{:S(2)}, u32[]{:S(2)}) collective-permute-start(bf16[144,576]{1,0:T(8,128)(2,1)} %get-tuple-element.36), channel_id=1, source_target_pairs={{0,12},{4,8},{8,4},{12,0},{1,13},{5,9},{9,5},{13,1},{2,14},{6,10},... | collective-permute-start | bytes 497672 | tf_op jit(solution)/shard_map/ppermute | solution.py:28
  53.0 7.6 %collective-permute-start.14 = (bf16[32,512]{1,0:T(8,128)(2,1)S(1)}, bf16[32,512]{1,0:T(8,128)(2,1)S(1)}, u32[]{:S(2)}, u32[]{:S(2)}) collective-permute-start(bf16[32,512]{1,0:T(8,128)(2,1)S(1)} %get-tuple-element.43), channel_id=1, source_target_pairs={{0,1},{1,0},{2,3},{3,2},{4,5},{5,4},{6,7},{7,6},{8,9},{9,8},{10,11... | collective-permute-start | bytes 98312 | tf_op jit(solution)/shard_map/ppermute | solution.py:28
  54.9 5.6 %collective-permute-start.15 = (bf16[32,512]{1,0:T(8,128)(2,1)S(1)}, bf16[32,512]{1,0:T(8,128)(2,1)S(1)}, u32[]{:S(2)}, u32[]{:S(2)}) collective-permute-start(bf16[32,512]{1,0:T(8,128)(2,1)S(1)} %get-tuple-element.44), channel_id=1, source_target_pairs={{0,2},{1,3},{2,0},{3,1},{4,6},{5,7},{6,4},{7,5},{8,10},{9,11},{10,... | collective-permute-start | bytes 98312 | tf_op jit(solution)/shard_map/ppermute | solution.py:28
  56.9 5.7 %collective-permute-start.16 = (bf16[32,512]{1,0:T(8,128)(2,1)S(1)}, bf16[32,512]{1,0:T(8,128)(2,1)S(1)}, u32[]{:S(2)}, u32[]{:S(2)}) collective-permute-start(bf16[32,512]{1,0:T(8,128)(2,1)S(1)} %get-tuple-element.45), channel_id=1, source_target_pairs={{0,3},{1,2},{2,1},{3,0},{4,7},{5,6},{6,5},{7,4},{8,11},{9,10},{10,... | collective-permute-start | bytes 98312 | tf_op jit(solution)/shard_map/ppermute | solution.py:28
  64.7 3.9 %collective-permute-start.19 = (bf16[8,2176]{1,0:T(8,128)(2,1)S(1)}, bf16[8,2176]{1,0:T(8,128)(2,1)S(1)}, u32[]{:S(2)}, u32[]{:S(2)}) collective-permute-start(bf16[8,2176]{1,0:T(8,128)(2,1)S(1)} %head_products.1.refs_0_.refs_4_), channel_id=1, source_target_pairs={{0,12},{4,8},{8,4},{12,0},{1,13},{5,9},{9,5},{13,1},{2,14},{6,10},... | collective-permute-start | bytes 104456 | tf_op jit(solution)/shard_map/ppermute | solution.py:28
  64.7 4.1 %collective-permute-start.18 = (bf16[8,2176]{1,0:T(8,128)(2,1)S(1)}, bf16[8,2176]{1,0:T(8,128)(2,1)S(1)}, u32[]{:S(2)}, u32[]{:S(2)}) collective-permute-start(bf16[8,2176]{1,0:T(8,128)(2,1)S(1)} %head_products.1.refs_0_.refs_4_), channel_id=1, source_target_pairs={{0,8},{4,12},{8,0},{12,4},{1,9},{5,13},{9,1},{13,5},{2,10},{6,14},... | collective-permute-start | bytes 104456 | tf_op jit(solution)/shard_map/ppermute | solution.py:28
  69.5 7.6 %collective-permute-start.22 = (bf16[32,896]{1,0:T(8,128)(2,1)S(1)}, bf16[32,896]{1,0:T(8,128)(2,1)S(1)}, u32[]{:S(2)}, u32[]{:S(2)}) collective-permute-start(bf16[32,896]{1,0:T(8,128)(2,1)S(1)} %output_product.1.refs_1_.refs_0_), channel_id=1, source_target_pairs={{0,3},{1,2},{2,1},{3,0},{4,7},{5,6},{6,5},{7,4},{8,11},{9,10},{10,... | collective-permute-start | bytes 172040 | tf_op jit(solution)/shard_map/ppermute | solution.py:28
  70.9 6.7 %collective-permute-start.21 = (bf16[32,896]{1,0:T(8,128)(2,1)S(1)}, bf16[32,896]{1,0:T(8,128)(2,1)S(1)}, u32[]{:S(2)}, u32[]{:S(2)}) collective-permute-start(bf16[32,896]{1,0:T(8,128)(2,1)S(1)} %output_product.1.refs_1_.refs_0_), channel_id=1, source_target_pairs={{0,2},{1,3},{2,0},{3,1},{4,6},{5,7},{6,4},{7,5},{8,10},{9,11},{10,... | collective-permute-start | bytes 172040 | tf_op jit(solution)/shard_map/ppermute | solution.py:28
  70.9 6.7 %collective-permute-start.20 = (bf16[32,896]{1,0:T(8,128)(2,1)S(1)}, bf16[32,896]{1,0:T(8,128)(2,1)S(1)}, u32[]{:S(2)}, u32[]{:S(2)}) collective-permute-start(bf16[32,896]{1,0:T(8,128)(2,1)S(1)} %output_product.1.refs_1_.refs_0_), channel_id=1, source_target_pairs={{0,1},{1,0},{2,3},{3,2},{4,5},{5,4},{6,7},{7,6},{8,9},{9,8},{10,11... | collective-permute-start | bytes 172040 | tf_op jit(solution)/shard_map/ppermute | solution.py:28
  78.7 5.0 %collective-permute-start.25 = (bf16[4,8,896]{2,1,0:T(8,128)(2,1)S(1)}, bf16[4,8,896]{2,1,0:T(8,128)(2,1)S(1)}, u32[]{:S(2)}, u32[]{:S(2)}) collective-permute-start(bf16[4,8,896]{2,1,0:T(8,128)(2,1)S(1)} %mix.1.refs_1_.refs_0_), channel_id=1, source_target_pairs={{0,12},{4,8},{8,4},{12,0},{1,13},{5,9},{9,5},{13,1},{2,14},{6,10},... | collective-permute-start | bytes 172040 | tf_op jit(solution)/shard_map/ppermute | solution.py:28
  79.3 4.9 %collective-permute-start.24 = (bf16[4,8,896]{2,1,0:T(8,128)(2,1)S(1)}, bf16[4,8,896]{2,1,0:T(8,128)(2,1)S(1)}, u32[]{:S(2)}, u32[]{:S(2)}) collective-permute-start(bf16[4,8,896]{2,1,0:T(8,128)(2,1)S(1)} %mix.1.refs_1_.refs_0_), channel_id=1, source_target_pairs={{0,8},{4,12},{8,0},{12,4},{1,9},{5,13},{9,1},{13,5},{2,10},{6,14},... | collective-permute-start | bytes 172040 | tf_op jit(solution)/shard_map/ppermute | solution.py:28
  (7 other events, 17.5 us)

commit v14 on v13

--- a/solution.py
+++ b/solution.py
@@ -146,7 +146,7 @@
         + [pl.BlockSpec(memory_space=pl.ANY)] * len(after),
         compiler_params=params(*blocks, *w_parts, scale=6),
         name="project",
-    )(*blocks, riders, *w_parts, *after)
+    )(*blocks, *at_home(riders), *w_parts, *after)
 
 
 def query_kernel(
@@ -287,10 +287,8 @@
     return pl.pallas_call(
         functools.partial(query_kernel, experts, sections, prompts, nope, shape),
         out_shape=[
-            jax.ShapeDtypeStruct((experts * sections, rows, width), jnp.bfloat16),
-            jax.ShapeDtypeStruct(
-                (experts, block * -(-column // cache_width), cache_width), jnp.bfloat16
-            ),
+            pltpu.HBM((experts * sections, rows, width), jnp.bfloat16),
+            pltpu.HBM((experts, block * -(-column // cache_width), cache_width), jnp.bfloat16),
             jax.ShapeDtypeStruct((8, 128), jnp.bfloat16),
         ],
         in_specs=[pl.BlockSpec(memory_space=pltpu.SMEM)]

time: 103 us -> 102 us (level)
  Pallas kernels: 30.9 us -> 33.4 us
  local copies, waits for them, and re-layouts: 3.36 us -> 1.16 us
    unnamed x8 -> x2, local copies, waits for them, and re-layouts: 2.2 us -> 0.01 us
    pallas_call x2, Pallas kernels: 1.95 us -> 3.74 us  [project(): pl.pallas_call(functools.partial(project_kernel, len(blocks), first, rows...]
  transfers between devices with their start and end apart: 27 -> 27, of which waited for: 10 -> 9; matrix products, arithmetic and copies ran while one was open for 1% -> 1% of each run, Pallas kernels for 17% -> 19%
where the time goes in v14:
time: 102 us
  starting transfers between devices  35.2 us (35%)
  Pallas kernels  33.4 us (33%)
  waiting for transfers between devices  19.6 us (19%)
  blocking collectives  12 us (12%)
  local copies, waits for them, and re-layouts  1.16 us (1%)
    ppermute x26, starting transfers between devices, swap(): return lax.ppermute(block, axis, [(i, i ^ mask) for i in range(size)])  29.2 us
    ppermute x26, waiting for transfers between devices, swap(): return lax.ppermute(block, axis, [(i, i ^ mask) for i in range(size)])  19.6 us
    all_to_all x1, blocking collectives, local(): blocks = lax.all_to_all(blocks, ('expert', 'section'), 0, 0, tiled=True)  12 us
    pallas_call x4, Pallas kernels, fetch(): pl.pallas_call(functools.partial(fetch_kernel, len(arrays)), out_shape=[p...  11.4 us
    all_to_all x1, starting transfers between devices, local(): blocks = lax.all_to_all(blocks, ('expert', 'section'), 0, 0, tiled=True)  5.95 us
    pallas_call x1, Pallas kernels, run_experts(): pl.pallas_call(functools.partial(expert_kernel, experts, sections, picks)...  4.98 us
    pallas_call x2, Pallas kernels, project(): pl.pallas_call(functools.partial(project_kernel, len(blocks), first, rows...  3.74 us
    pallas_call x1, Pallas kernels, absorb_queries(): pl.pallas_call(functools.partial(query_kernel, experts, sections, prompts...  2.91 us
  transfers between devices with their start and end apart: 27, of which 9 were waited for; matrix products, arithmetic and copies ran while one was open for 1% of the time, Pallas kernels for 19%

profile of v14, /device:TPU:0, one launch (start us, length us, event | category | flops | bytes accessed | tf_op | source)
XLA Modules:
  0.0 101.6 jit_solution(7204890740479982217)
XLA Ops:
  0.0 2.6 %cut_columns.1 = (bf16[8,128,128]{2,1,0:T(8,128)(2,1)S(1)}, bf16[640,224]{1,0:T(8,128)(2,1)S(1)}, bf16[640,224]{1,0:T(8,128)(2,1)S(1)}, bf16[640,224]{1,0:T(8,128)(2,1)S(1)}, bf16[640,224]{1,0:T(8,128)(2,1)}) custom-call(bf16[128,3584]{1,0:T(8,128)(2,1)} %bitcast.5, bf16[2,4,16,192]{3,2,1,0:T(8,128)(2,1)} %query_ref.1, bf16[16,128,128]{2,1,0:T(8,128)(2,1)} %refs_5_.5), custom_call_target="tpu_custom_call" | custom-call | tf_op jit(solution)/shard_map/cut_columns/pallas_call | solution.py:110
  3.0 2.5 %collective-permute-start.3 = (bf16[8,128,128]{2,1,0:T(8,128)(2,1)S(1)}, bf16[8,128,128]{2,1,0:T(8,128)(2,1)S(1)}, u32[]{:S(2)}, u32[]{:S(2)}) collective-permute-start(bf16[8,128,128]{2,1,0:T(8,128)(2,1)S(1)} %get-tuple-element.31), channel_id=1, source_target_pairs={{0,8},{4,12},{8,0},{12,4},{1,9},{5,13},{9,1},{13,5},{2,10},{6,14},... | collective-permute-start | bytes 786440 | tf_op jit(solution)/shard_map/ppermute | solution.py:28
  5.5 1.5 %collective-permute-start.2 = (bf16[640,224]{1,0:T(8,128)(2,1)}, bf16[640,224]{1,0:T(8,128)(2,1)S(1)}, u32[]{:S(2)}, u32[]{:S(2)}) collective-permute-start(bf16[640,224]{1,0:T(8,128)(2,1)} %get-tuple-element.30), channel_id=1, source_target_pairs={{0,12},{4,8},{8,4},{12,0},{1,13},{5,9},{9,5},{13,1},{2,14},{6,10},... | collective-permute-start | bytes 860168 | tf_op jit(solution)/shard_map/ppermute | solution.py:28
  8.3 3.7 %collective-permute-start.6 = (bf16[576,224]{1,0:T(8,128)(2,1)S(1)}, bf16[576,224]{1,0:T(8,128)(2,1)S(1)}, u32[]{:S(2)}, u32[]{:S(2)}) collective-permute-start(bf16[576,224]{1,0:T(8,128)(2,1)S(1)} %dynamic-slice_bitcast_fusion.refs_4_.refs_2_), channel_id=1, source_target_pairs={{0,3},{1,2},{2,1},{3,0},{4,7},{5,6},{6,5},{7,4},{8,11},{9,10},{10,... | collective-permute-start | bytes 774152 | tf_op jit(solution)/shard_map/ppermute | solution.py:28
  12.7 3.0 %collective-permute-start.5 = (bf16[576,224]{1,0:T(8,128)(2,1)S(1)}, bf16[576,224]{1,0:T(8,128)(2,1)S(1)}, u32[]{:S(2)}, u32[]{:S(2)}) collective-permute-start(bf16[576,224]{1,0:T(8,128)(2,1)S(1)} %dynamic-slice_bitcast_fusion.refs_4_.refs_2_), channel_id=1, source_target_pairs={{0,2},{1,3},{2,0},{3,1},{4,6},{5,7},{6,4},{7,5},{8,10},{9,11},{10,... | collective-permute-start | bytes 774152 | tf_op jit(solution)/shard_map/ppermute | solution.py:28
  15.7 1.6 %collective-permute-start.4 = (bf16[576,224]{1,0:T(8,128)(2,1)S(1)}, bf16[576,224]{1,0:T(8,128)(2,1)S(1)}, u32[]{:S(2)}, u32[]{:S(2)}) collective-permute-start(bf16[576,224]{1,0:T(8,128)(2,1)S(1)} %dynamic-slice_bitcast_fusion.refs_4_.refs_2_), channel_id=1, source_target_pairs={{0,1},{1,0},{2,3},{3,2},{4,5},{5,4},{6,7},{7,6},{8,9},{9,8},{10,11... | collective-permute-start | bytes 774152 | tf_op jit(solution)/shard_map/ppermute | solution.py:28
  17.3 2.4 %collective-permute-done.1.refs_3_.refs_1_ = bf16[640,224]{1,0:T(8,128)(2,1)S(1)} collective-permute-done((bf16[640,224]{1,0:T(8,128)(2,1)S(1)}, bf16[640,224]{1,0:T(8,128)(2,1)S(1)}, u32[]{:S(2)}, u32[]{:S(2)}) %collective-permute-start.1) | collective-permute-done | bytes 286752 | tf_op jit(solution)/shard_map/ppermute | solution.py:28
  19.7 6.7 %collective-permute-done.2.refs_4_.refs_2_ = bf16[640,224]{1,0:T(8,128)(2,1)S(1)} collective-permute-done((bf16[640,224]{1,0:T(8,128)(2,1)}, bf16[640,224]{1,0:T(8,128)(2,1)S(1)}, u32[]{:S(2)}, u32[]{:S(2)}) %collective-permute-start.2) | collective-permute-done | bytes 286752 | tf_op jit(solution)/shard_map/ppermute | solution.py:28
  26.3 1.6 %collective-permute-start.11 = (bf16[8,128,128]{2,1,0:T(8,128)(2,1)S(1)}, bf16[8,128,128]{2,1,0:T(8,128)(2,1)S(1)}, u32[]{:S(2)}, u32[]{:S(2)}) collective-permute-start(bf16[8,128,128]{2,1,0:T(8,128)(2,1)S(1)} %collective-permute-done.3.refs_9_.refs_13_.refs_7_), channel_id=1, source_target_pairs={{0,16},{16,0},{1,17},{17,1},{2,18},{18,2},{3,19},{19,3},{4,20},{20... | collective-permute-start | bytes 786440 | tf_op jit(solution)/shard_map/ppermute | solution.py:28
  27.9 2.9 %absorb_queries.1 = (bf16[16,48,128]{2,1,0:T(8,128)(2,1)}, bf16[4,16,576]{2,1,0:T(8,128)(2,1)}, bf16[8,128]{1,0:T(8,128)(2,1)S(1)}) custom-call(s32[16]{0:T(128)} %refs_0_.8, bf16[640,224]{1,0:T(8,128)(2,1)S(1)} %get-tuple-element.27.refs_1_.refs_0_, bf16[640,224]{1,0:T(8,128)(2,1)S(1)} %collective-permute-done.refs_2_.refs_0_, ...), custom_call_target="tpu_custom_call" | custom-call | tf_op jit(solution)/shard_map/absorb_queries/pallas_call | solution.py:287
  30.8 6.0 %all-to-all-start = ((bf16[16,48,128]{2,1,0:T(8,128)(2,1)}), bf16[16,48,128]{2,1,0:T(8,128)(2,1)}, u32[]{:S(2)}, u32[]{:S(2)}) async-start(bf16[16,48,128]{2,1,0:T(8,128)(2,1)} %get-tuple-element.37), calls=%async_computation | async-start | bytes 393216 | tf_op jit(solution)/shard_map/all_to_all | solution.py:805
  37.8 2.3 %project.2 = (bf16[144,576]{1,0:T(8,128)(2,1)}, bf16[144,576]{1,0:T(8,128)(2,1)S(1)}, bf16[144,576]{1,0:T(8,128)(2,1)}) custom-call(bf16[640,224]{1,0:T(8,128)(2,1)S(1)} %collective-permute-done.refs_2_.refs_0_, bf16[640,224]{1,0:T(8,128)(2,1)S(1)} %collective-permute-done.1.refs_3_.refs_1_, bf16[640,224]{1,0:T(8,128)(2,1)S(1)} %collective-permute-done.2.refs_4_.refs_2_, ...), custom_call_target="tpu_custom_call" | custom-call | tf_op jit(solution)/shard_map/project/pallas_call | solution.py:142
  42.3 5.8 %collective-permute-done.8.refs_2_.refs_6_ = bf16[144,576]{1,0:T(8,128)(2,1)S(1)} collective-permute-done((bf16[144,576]{1,0:T(8,128)(2,1)S(1)}, bf16[144,576]{1,0:T(8,128)(2,1)S(1)}, u32[]{:S(2)}, u32[]{:S(2)}) %collective-permute-start.8) | collective-permute-done | bytes 165920 | tf_op jit(solution)/shard_map/ppermute | solution.py:28
  50.9 2.0 %attend.1 = (bf16[32,512]{1,0:T(8,128)(2,1)S(1)}, bf16[32,512]{1,0:T(8,128)(2,1)S(1)}, bf16[32,512]{1,0:T(8,128)(2,1)S(1)}, bf16[32,512]{1,0:T(8,128)(2,1)S(1)}, bf16[8,128]{1,0:T(8,128)(2,1)S(1)}) custom-call(bf16[144,576]{1,0:T(8,128)(2,1)S(1)} %project.3.refs_0_.refs_4_, bf16[144,576]{1,0:T(8,128)(2,1)} %collective-permute-done.7.refs_1_.refs_5_, ...), custom_call_target="tpu_custom_call" | custom-call | tf_op jit(solution)/shard_map/attend/pallas_call | solution.py:495
  54.3 2.0 %collective-permute-start.15 = (bf16[32,512]{1,0:T(8,128)(2,1)S(1)}, bf16[32,512]{1,0:T(8,128)(2,1)S(1)}, u32[]{:S(2)}, u32[]{:S(2)}) collective-permute-start(bf16[32,512]{1,0:T(8,128)(2,1)S(1)} %get-tuple-element.44), channel_id=1, source_target_pairs={{0,2},{1,3},{2,0},{3,1},{4,6},{5,7},{6,4},{7,5},{8,10},{9,11},{10,... | collective-permute-start | bytes 98312 | tf_op jit(solution)/shard_map/ppermute | solution.py:28
  57.3 3.1 %fetch.4.refs_13_.refs_9_ = bf16[4,3584,256]{2,1,0:T(8,128)(2,1)S(1)} custom-call(bf16[4,3584,256]{2,1,0:T(8,128)(2,1)} %refs_0_.7, bf16[8,128]{1,0:T(8,128)(2,1)S(1)} %get-tuple-element.46.refs_1_), custom_call_target="tpu_custom_call" | custom-call | bytes 14680064 | tf_op jit(solution)/shard_map/fetch/pallas_call | solution.py:63
  60.5 1.5 %collective-permute-done.16.refs_4_ = bf16[32,512]{1,0:T(8,128)(2,1)S(1)} collective-permute-done((bf16[32,512]{1,0:T(8,128)(2,1)S(1)}, bf16[32,512]{1,0:T(8,128)(2,1)S(1)}, u32[]{:S(2)}, u32[]{:S(2)}) %collective-permute-start.16) | collective-permute-done | bytes 32800 | tf_op jit(solution)/shard_map/ppermute | solution.py:28
  62.0 2.0 %head_products.1.refs_0_.refs_4_ = bf16[8,2176]{1,0:T(8,128)(2,1)S(1)} custom-call(s32[16]{0:T(128)} %refs_0_.8, bf16[32,512]{1,0:T(8,128)(2,1)S(1)} %get-tuple-element.42.refs_1_, bf16[32,512]{1,0:T(8,128)(2,1)S(1)} %collective-permute-done.14.refs_2_, bf16[32,512]{1,0:T(8,128)(2,1)S(1)} %collective-permute-done.15.refs_3_, ...), custom_call_target="tpu_custom_call" | custom-call | tf_op jit(solution)/shard_map/head_products/pallas_call | solution.py:586
  65.9 2.0 %fetch.5.refs_4_ = bf16[2048,896]{1,0:T(8,128)(2,1)S(1)} custom-call(bf16[2048,896]{1,0:T(8,128)(2,1)} %refs_0_.9), custom_call_target="tpu_custom_call" | custom-call | bytes 7340032 | tf_op jit(solution)/shard_map/fetch/pallas_call | solution.py:63
  70.6 3.0 %collective-permute-start.20 = (bf16[32,896]{1,0:T(8,128)(2,1)S(1)}, bf16[32,896]{1,0:T(8,128)(2,1)S(1)}, u32[]{:S(2)}, u32[]{:S(2)}) collective-permute-start(bf16[32,896]{1,0:T(8,128)(2,1)S(1)} %output_product.1.refs_1_.refs_0_), channel_id=1, source_target_pairs={{0,1},{1,0},{2,3},{3,2},{4,5},{5,4},{6,7},{7,6},{8,9},{9,8},{10,11... | collective-permute-start | bytes 172040 | tf_op jit(solution)/shard_map/ppermute | solution.py:28
  73.6 3.1 %fetch.6.refs_8_.refs_10_ = bf16[4,3584,256]{2,1,0:T(8,128)(2,1)S(1)} custom-call(bf16[4,3584,256]{2,1,0:T(8,128)(2,1)} %refs_0_.10, bf16[32,896]{1,0:T(8,128)(2,1)S(1)} %output_product.1.refs_1_.refs_0_), custom_call_target="tpu_custom_call" | custom-call | bytes 14680064 | tf_op jit(solution)/shard_map/fetch/pallas_call | solution.py:63
  80.4 3.1 %fetch.7.refs_11_ = bf16[4,256,3584]{2,1,0:T(8,128)(2,1)S(1)} custom-call(bf16[4,256,3584]{2,1,0:T(8,128)(2,1)} %refs_0_.11, bf16[4,8,896]{2,1,0:T(8,128)(2,1)S(1)} %mix.1.refs_1_.refs_0_), custom_call_target="tpu_custom_call" | custom-call | bytes 14680064 | tf_op jit(solution)/shard_map/fetch/pallas_call | solution.py:63
  84.0 5.0 %run_experts.1 = (bf16[16,8,896]{2,1,0:T(8,128)(2,1)S(1)}, bf16[4,8,896]{2,1,0:T(8,128)(2,1)S(1)}) custom-call(bf16[4,8,896]{2,1,0:T(8,128)(2,1)S(1)} %mix.1.refs_1_.refs_0_, bf16[4,8,896]{2,1,0:T(8,128)(2,1)S(1)} %collective-permute-done.23.refs_1_, bf16[4,8,896]{2,1,0:T(8,128)(2,1)S(1)} %collective-permute-done.24.refs_2_, ...), custom_call_target="tpu_custom_call" | custom-call | tf_op jit(solution)/shard_map/run_experts/pallas_call | solution.py:719
  89.0 12.0 %all_to_all.10.block_ref = bf16[16,8,896]{2,1,0:T(8,128)(2,1)S(1)} all-to-all(bf16[16,8,896]{2,1,0:T(8,128)(2,1)S(1)} %get-tuple-element.47), channel_id=1, replica_groups=mesh['groups'=2,'expert'=4,'section'=4] {'expert','section'}, dimensions={0} | all-to-all | bytes 458752 | tf_op jit(solution)/shard_map/all_to_all | solution.py:850
  (49 shorter events, 20.1 us)
Async XLA Ops:
  2.6 13.1 %collective-permute-start = (bf16[640,224]{1,0:T(8,128)(2,1)S(1)}, bf16[640,224]{1,0:T(8,128)(2,1)S(1)}, u32[]{:S(2)}, u32[]{:S(2)}) collective-permute-start(bf16[640,224]{1,0:T(8,128)(2,1)S(1)} %get-tuple-element.28), channel_id=1, source_target_pairs={{0,4},{4,0},{8,12},{12,8},{1,5},{5,1},{9,13},{13,9},{2,6},{6,2},{1... | collective-permute-start | bytes 860168 | tf_op jit(solution)/shard_map/ppermute | solution.py:28
  3.0 9.6 %collective-permute-start.3 = (bf16[8,128,128]{2,1,0:T(8,128)(2,1)S(1)}, bf16[8,128,128]{2,1,0:T(8,128)(2,1)S(1)}, u32[]{:S(2)}, u32[]{:S(2)}) collective-permute-start(bf16[8,128,128]{2,1,0:T(8,128)(2,1)S(1)} %get-tuple-element.31), channel_id=1, source_target_pairs={{0,8},{4,12},{8,0},{12,4},{1,9},{5,13},{9,1},{13,5},{2,10},{6,14},... | collective-permute-start | bytes 786440 | tf_op jit(solution)/shard_map/ppermute | solution.py:28
  5.5 14.2 %collective-permute-start.1 = (bf16[640,224]{1,0:T(8,128)(2,1)S(1)}, bf16[640,224]{1,0:T(8,128)(2,1)S(1)}, u32[]{:S(2)}, u32[]{:S(2)}) collective-permute-start(bf16[640,224]{1,0:T(8,128)(2,1)S(1)} %get-tuple-element.29), channel_id=1, source_target_pairs={{0,8},{4,12},{8,0},{12,4},{1,9},{5,13},{9,1},{13,5},{2,10},{6,14},... | collective-permute-start | bytes 860168 | tf_op jit(solution)/shard_map/ppermute | solution.py:28
  5.5 20.8 %collective-permute-start.2 = (bf16[640,224]{1,0:T(8,128)(2,1)}, bf16[640,224]{1,0:T(8,128)(2,1)S(1)}, u32[]{:S(2)}, u32[]{:S(2)}) collective-permute-start(bf16[640,224]{1,0:T(8,128)(2,1)} %get-tuple-element.30), channel_id=1, source_target_pairs={{0,12},{4,8},{8,4},{12,0},{1,13},{5,9},{9,5},{13,1},{2,14},{6,10},... | collective-permute-start | bytes 860168 | tf_op jit(solution)/shard_map/ppermute | solution.py:28
  8.3 28.5 %collective-permute-start.6 = (bf16[576,224]{1,0:T(8,128)(2,1)S(1)}, bf16[576,224]{1,0:T(8,128)(2,1)S(1)}, u32[]{:S(2)}, u32[]{:S(2)}) collective-permute-start(bf16[576,224]{1,0:T(8,128)(2,1)S(1)} %dynamic-slice_bitcast_fusion.refs_4_.refs_2_), channel_id=1, source_target_pairs={{0,3},{1,2},{2,1},{3,0},{4,7},{5,6},{6,5},{7,4},{8,11},{9,10},{10,... | collective-permute-start | bytes 774152 | tf_op jit(solution)/shard_map/ppermute | solution.py:28
  12.7 25.1 %collective-permute-start.5 = (bf16[576,224]{1,0:T(8,128)(2,1)S(1)}, bf16[576,224]{1,0:T(8,128)(2,1)S(1)}, u32[]{:S(2)}, u32[]{:S(2)}) collective-permute-start(bf16[576,224]{1,0:T(8,128)(2,1)S(1)} %dynamic-slice_bitcast_fusion.refs_4_.refs_2_), channel_id=1, source_target_pairs={{0,2},{1,3},{2,0},{3,1},{4,6},{5,7},{6,4},{7,5},{8,10},{9,11},{10,... | collective-permute-start | bytes 774152 | tf_op jit(solution)/shard_map/ppermute | solution.py:28
  15.7 22.1 %collective-permute-start.4 = (bf16[576,224]{1,0:T(8,128)(2,1)S(1)}, bf16[576,224]{1,0:T(8,128)(2,1)S(1)}, u32[]{:S(2)}, u32[]{:S(2)}) collective-permute-start(bf16[576,224]{1,0:T(8,128)(2,1)S(1)} %dynamic-slice_bitcast_fusion.refs_4_.refs_2_), channel_id=1, source_target_pairs={{0,1},{1,0},{2,3},{3,2},{4,5},{5,4},{6,7},{7,6},{8,9},{9,8},{10,11... | collective-permute-start | bytes 774152 | tf_op jit(solution)/shard_map/ppermute | solution.py:28
  19.7 31.2 %collective-permute-start.10 = (bf16[16,128,128]{2,1,0:T(8,128)(2,1)}, bf16[16,128,128]{2,1,0:T(8,128)(2,1)S(1)}, u32[]{:S(2)}, u32[]{:S(2)}) collective-permute-start(bf16[16,128,128]{2,1,0:T(8,128)(2,1)} %refs_5_.5), channel_id=1, source_target_pairs={{0,4},{4,0},{8,12},{12,8},{1,5},{5,1},{9,13},{13,9},{2,6},{6,2},{1... | collective-permute-start | bytes 1572872 | tf_op jit(solution)/shard_map/ppermute | solution.py:28
  26.3 14.7 %collective-permute-start.11 = (bf16[8,128,128]{2,1,0:T(8,128)(2,1)S(1)}, bf16[8,128,128]{2,1,0:T(8,128)(2,1)S(1)}, u32[]{:S(2)}, u32[]{:S(2)}) collective-permute-start(bf16[8,128,128]{2,1,0:T(8,128)(2,1)S(1)} %collective-permute-done.3.refs_9_.refs_13_.refs_7_), channel_id=1, source_target_pairs={{0,16},{16,0},{1,17},{17,1},{2,18},{18,2},{3,19},{19,3},{4,20},{20... | collective-permute-start | bytes 786440 | tf_op jit(solution)/shard_map/ppermute | solution.py:28
  30.8 18.6 %all-to-all-start = ((bf16[16,48,128]{2,1,0:T(8,128)(2,1)}), bf16[16,48,128]{2,1,0:T(8,128)(2,1)}, u32[]{:S(2)}, u32[]{:S(2)}) async-start(bf16[16,48,128]{2,1,0:T(8,128)(2,1)} %get-tuple-element.37), calls=%async_computation | async-start | bytes 393216 | tf_op jit(solution)/shard_map/all_to_all | solution.py:805
  40.1 7.9 %collective-permute-start.8 = (bf16[144,576]{1,0:T(8,128)(2,1)S(1)}, bf16[144,576]{1,0:T(8,128)(2,1)S(1)}, u32[]{:S(2)}, u32[]{:S(2)}) collective-permute-start(bf16[144,576]{1,0:T(8,128)(2,1)S(1)} %get-tuple-element.35), channel_id=1, source_target_pairs={{0,8},{4,12},{8,0},{12,4},{1,9},{5,13},{9,1},{13,5},{2,10},{6,14},... | collective-permute-start | bytes 497672 | tf_op jit(solution)/shard_map/ppermute | solution.py:28
  41.1 9.8 %collective-permute-start.12 = (bf16[8,128,128]{2,1,0:T(8,128)(2,1)S(1)}, bf16[8,128,128]{2,1,0:T(8,128)(2,1)S(1)}, u32[]{:S(2)}, u32[]{:S(2)}) collective-permute-start(bf16[8,128,128]{2,1,0:T(8,128)(2,1)S(1)} %collective-permute-done.3.refs_9_.refs_13_.refs_7_), channel_id=1, source_target_pairs={{0,4},{4,0},{8,12},{12,8},{1,5},{5,1},{9,13},{13,9},{2,6},{6,2},{1... | collective-permute-start | bytes 786440 | tf_op jit(solution)/shard_map/ppermute | solution.py:28
  41.1 9.8 %collective-permute-start.13 = (bf16[8,128,128]{2,1,0:T(8,128)(2,1)S(1)}, bf16[8,128,128]{2,1,0:T(8,128)(2,1)S(1)}, u32[]{:S(2)}, u32[]{:S(2)}) collective-permute-start(bf16[8,128,128]{2,1,0:T(8,128)(2,1)S(1)} %collective-permute-done.11.refs_14_.refs_8_), channel_id=1, source_target_pairs={{0,4},{4,0},{8,12},{12,8},{1,5},{5,1},{9,13},{13,9},{2,6},{6,2},{1... | collective-permute-start | bytes 786440 | tf_op jit(solution)/shard_map/ppermute | solution.py:28
  41.6 9.3 %collective-permute-start.9 = (bf16[144,576]{1,0:T(8,128)(2,1)}, bf16[144,576]{1,0:T(8,128)(2,1)}, u32[]{:S(2)}, u32[]{:S(2)}) collective-permute-start(bf16[144,576]{1,0:T(8,128)(2,1)} %get-tuple-element.36), channel_id=1, source_target_pairs={{0,12},{4,8},{8,4},{12,0},{1,13},{5,9},{9,5},{13,1},{2,14},{6,10},... | collective-permute-start | bytes 497672 | tf_op jit(solution)/shard_map/ppermute | solution.py:28
  52.9 7.6 %collective-permute-start.14 = (bf16[32,512]{1,0:T(8,128)(2,1)S(1)}, bf16[32,512]{1,0:T(8,128)(2,1)S(1)}, u32[]{:S(2)}, u32[]{:S(2)}) collective-permute-start(bf16[32,512]{1,0:T(8,128)(2,1)S(1)} %get-tuple-element.43), channel_id=1, source_target_pairs={{0,1},{1,0},{2,3},{3,2},{4,5},{5,4},{6,7},{7,6},{8,9},{9,8},{10,11... | collective-permute-start | bytes 98312 | tf_op jit(solution)/shard_map/ppermute | solution.py:28
  54.3 6.2 %collective-permute-start.15 = (bf16[32,512]{1,0:T(8,128)(2,1)S(1)}, bf16[32,512]{1,0:T(8,128)(2,1)S(1)}, u32[]{:S(2)}, u32[]{:S(2)}) collective-permute-start(bf16[32,512]{1,0:T(8,128)(2,1)S(1)} %get-tuple-element.44), channel_id=1, source_target_pairs={{0,2},{1,3},{2,0},{3,1},{4,6},{5,7},{6,4},{7,5},{8,10},{9,11},{10,... | collective-permute-start | bytes 98312 | tf_op jit(solution)/shard_map/ppermute | solution.py:28
  56.3 5.7 %collective-permute-start.16 = (bf16[32,512]{1,0:T(8,128)(2,1)S(1)}, bf16[32,512]{1,0:T(8,128)(2,1)S(1)}, u32[]{:S(2)}, u32[]{:S(2)}) collective-permute-start(bf16[32,512]{1,0:T(8,128)(2,1)S(1)} %get-tuple-element.45), channel_id=1, source_target_pairs={{0,3},{1,2},{2,1},{3,0},{4,7},{5,6},{6,5},{7,4},{8,11},{9,10},{10,... | collective-permute-start | bytes 98312 | tf_op jit(solution)/shard_map/ppermute | solution.py:28
  64.0 3.9 %collective-permute-start.19 = (bf16[8,2176]{1,0:T(8,128)(2,1)S(1)}, bf16[8,2176]{1,0:T(8,128)(2,1)S(1)}, u32[]{:S(2)}, u32[]{:S(2)}) collective-permute-start(bf16[8,2176]{1,0:T(8,128)(2,1)S(1)} %head_products.1.refs_0_.refs_4_), channel_id=1, source_target_pairs={{0,12},{4,8},{8,4},{12,0},{1,13},{5,9},{9,5},{13,1},{2,14},{6,10},... | collective-permute-start | bytes 104456 | tf_op jit(solution)/shard_map/ppermute | solution.py:28
  64.0 4.3 %collective-permute-start.18 = (bf16[8,2176]{1,0:T(8,128)(2,1)S(1)}, bf16[8,2176]{1,0:T(8,128)(2,1)S(1)}, u32[]{:S(2)}, u32[]{:S(2)}) collective-permute-start(bf16[8,2176]{1,0:T(8,128)(2,1)S(1)} %head_products.1.refs_0_.refs_4_), channel_id=1, source_target_pairs={{0,8},{4,12},{8,0},{12,4},{1,9},{5,13},{9,1},{13,5},{2,10},{6,14},... | collective-permute-start | bytes 104456 | tf_op jit(solution)/shard_map/ppermute | solution.py:28
  69.1 7.6 %collective-permute-start.22 = (bf16[32,896]{1,0:T(8,128)(2,1)S(1)}, bf16[32,896]{1,0:T(8,128)(2,1)S(1)}, u32[]{:S(2)}, u32[]{:S(2)}) collective-permute-start(bf16[32,896]{1,0:T(8,128)(2,1)S(1)} %output_product.1.refs_1_.refs_0_), channel_id=1, source_target_pairs={{0,3},{1,2},{2,1},{3,0},{4,7},{5,6},{6,5},{7,4},{8,11},{9,10},{10,... | collective-permute-start | bytes 172040 | tf_op jit(solution)/shard_map/ppermute | solution.py:28
  70.6 6.8 %collective-permute-start.21 = (bf16[32,896]{1,0:T(8,128)(2,1)S(1)}, bf16[32,896]{1,0:T(8,128)(2,1)S(1)}, u32[]{:S(2)}, u32[]{:S(2)}) collective-permute-start(bf16[32,896]{1,0:T(8,128)(2,1)S(1)} %output_product.1.refs_1_.refs_0_), channel_id=1, source_target_pairs={{0,2},{1,3},{2,0},{3,1},{4,6},{5,7},{6,4},{7,5},{8,10},{9,11},{10,... | collective-permute-start | bytes 172040 | tf_op jit(solution)/shard_map/ppermute | solution.py:28
  70.6 6.8 %collective-permute-start.20 = (bf16[32,896]{1,0:T(8,128)(2,1)S(1)}, bf16[32,896]{1,0:T(8,128)(2,1)S(1)}, u32[]{:S(2)}, u32[]{:S(2)}) collective-permute-start(bf16[32,896]{1,0:T(8,128)(2,1)S(1)} %output_product.1.refs_1_.refs_0_), channel_id=1, source_target_pairs={{0,1},{1,0},{2,3},{3,2},{4,5},{5,4},{6,7},{7,6},{8,9},{9,8},{10,11... | collective-permute-start | bytes 172040 | tf_op jit(solution)/shard_map/ppermute | solution.py:28
  78.5 5.0 %collective-permute-start.25 = (bf16[4,8,896]{2,1,0:T(8,128)(2,1)S(1)}, bf16[4,8,896]{2,1,0:T(8,128)(2,1)S(1)}, u32[]{:S(2)}, u32[]{:S(2)}) collective-permute-start(bf16[4,8,896]{2,1,0:T(8,128)(2,1)S(1)} %mix.1.refs_1_.refs_0_), channel_id=1, source_target_pairs={{0,12},{4,8},{8,4},{12,0},{1,13},{5,9},{9,5},{13,1},{2,14},{6,10},... | collective-permute-start | bytes 172040 | tf_op jit(solution)/shard_map/ppermute | solution.py:28
  79.0 5.0 %collective-permute-start.24 = (bf16[4,8,896]{2,1,0:T(8,128)(2,1)S(1)}, bf16[4,8,896]{2,1,0:T(8,128)(2,1)S(1)}, u32[]{:S(2)}, u32[]{:S(2)}) collective-permute-start(bf16[4,8,896]{2,1,0:T(8,128)(2,1)S(1)} %mix.1.refs_1_.refs_0_), channel_id=1, source_target_pairs={{0,8},{4,12},{8,0},{12,4},{1,9},{5,13},{9,1},{13,5},{2,10},{6,14},... | collective-permute-start | bytes 172040 | tf_op jit(solution)/shard_map/ppermute | solution.py:28
  (4 other events, 14.6 us)

commit v15 on v13

--- a/solution.py
+++ b/solution.py
@@ -81,8 +81,25 @@
     return held
 
 
-def cut_kernel(sections, experts, piece, x_ref, query_ref, uv_ref, half_ref, *refs):
-    out_refs, held = refs[-1 - experts : -1], refs[-1]
+def cut_kernel(
+    sections, experts, piece, x_ref, query_ref, uv_ref, w_ref, half_ref, w_out_ref, *refs
+):
+    out_refs, w_held, held = refs[:experts], refs[experts], refs[experts + 1]
+    for target in range(experts):
+        w_held[target] = w_ref[:, target * piece : (target + 1) * piece]
+    w_piece = w_held[lax.axis_index("expert")]
+    if w_out_ref.shape == w_piece.shape:
+        w_out_ref[...] = w_piece
+    else:
+        full = w_piece.shape[0]
+        few = full // 4
+        w_out_ref[:full, :] = w_piece[:, :128]
+        rest = jnp.concatenate(
+            [w_piece[index * few : (index + 1) * few, 128:] for index in range(4)], axis=1
+        )
+        for index in range(rest.shape[1] // 128):
+            to = full + index * few
+            w_out_ref[to : to + few, :] = rest[:, index * 128 : (index + 1) * 128]
     share = half_ref.shape[0]
     half_ref[...] = uv_ref[pl.ds(lax.axis_index("groups") * share, share)]
     rank = lax.axis_index("expert")
@@ -100,7 +117,27 @@
                 ref[at : at + heads, :wide] = query_ref[step, source]
 
 
-def cut_columns(x, queries, w_uv, sections, experts, groups):
+def folded(rows, piece):
+    if 128 < piece < 256 and (piece - 128) % 32 == 0 and rows % 64 == 0:
+        return rows + rows // 4 * ((piece - 128) // 32), 128
+    return rows, piece
+
+
+def unfolded(value, rows, piece):
+    if value.shape == (rows, piece):
+        return value
+    few = rows // 4
+    rest = jnp.concatenate(
+        [value[at : at + few] for at in range(rows, value.shape[0], few)], axis=1
+    )
+    wide = piece - 128
+    rest = jnp.concatenate(
+        [rest[:, index * wide : (index + 1) * wide] for index in range(4)], axis=0
+    )
+    return jnp.concatenate([value[:rows], rest], axis=1)
+
+
+def cut_columns(x, queries, w_uv, w_turned, sections, experts, groups):
     rows, width = x.shape
     piece = width // (sections * experts)
     steps, sources, heads, wide = queries.shape
@@ -110,37 +147,42 @@
     return pl.pallas_call(
         functools.partial(cut_kernel, sections, experts, piece),
         out_shape=[
-            jax.ShapeDtypeStruct((w_uv.shape[0] // groups,) + w_uv.shape[1:], w_uv.dtype)
+            jax.ShapeDtypeStruct((w_uv.shape[0] // groups,) + w_uv.shape[1:], w_uv.dtype),
+            jax.ShapeDtypeStruct(folded(w_turned.shape[0], piece), x.dtype),
         ]
         + [block] * experts,
-        scratch_shapes=[pltpu.VMEM((experts, sections * rows, piece), x.dtype)],
-        compiler_params=params(x, block, w_uv, scale=6),
+        scratch_shapes=[
+            pltpu.VMEM((experts, w_turned.shape[0], piece), x.dtype),
+            pltpu.VMEM((experts, sections * rows, piece), x.dtype),
+        ],
+        compiler_params=params(x, block, w_uv, w_turned, scale=6),
         name="cut_columns",
-    )(*at_home(x, queries, w_uv))
-
-
-def project_kernel(count, first, rows, *refs):
+    )(*at_home(x, queries, w_uv, w_turned))
+
+
+def project_kernel(count, first, rows, piece, *refs):
     x_refs, rider_ref, w_refs, out_refs = refs[:count], refs[count], refs[count + 1 :], refs[-count:]
     section_rank = lax.axis_index("section")
     sections = lax.axis_size("section")
-    piece = w_refs[0].shape[1]
+    width = rider_ref.shape[2]
     total = 0
     for mask in range(sections):
+        weights = unfolded(w_refs[mask][...], width, piece)
         at = pl.ds(pl.multiple_of((section_rank ^ mask) * rows, rows), rows)
         x = jnp.concatenate([ref[at, :piece] for ref in x_refs], axis=0)
         total = total + lax.dot_general(
-            x, w_refs[mask][...], (((1,), (1,)), ((), ())), preferred_element_type=jnp.float32
+            x, weights, (((1,), (1,)), ((), ())), preferred_element_type=jnp.float32
         )
     for index, ref in enumerate(out_refs):
         ref[:rows, :] = total[index * rows : (index + 1) * rows].astype(ref.dtype)
         ref[rows:, :] = rider_ref[first + index]
 
 
-def project(blocks, riders, w_parts, first, rows, after):
+def project(blocks, riders, w_parts, first, rows, piece, after):
     out = jax.ShapeDtypeStruct((rows + riders.shape[1], riders.shape[2]), jnp.bfloat16)
     held = pl.BlockSpec(memory_space=pltpu.VMEM)
     return pl.pallas_call(
-        functools.partial(project_kernel, len(blocks), first, rows),
+        functools.partial(project_kernel, len(blocks), first, rows, piece),
         out_shape=[out] * len(blocks),
         in_specs=[held] * (len(blocks) + 1 + len(w_parts))
         + [pl.BlockSpec(memory_space=pl.ANY)] * len(after),
@@ -790,13 +832,12 @@
     own_rows = steps * tokens_here
 
     w_turned = w_dkv.T
-    w_piece = lax.dynamic_slice_in_dim(w_turned, expert_rank * piece, piece, 1)
     masks = [1 << bit for bit in range(experts.bit_length() - 1)]
     far = masks[-1]
+    uv_share, w_piece, *cut = cut_columns(
+        prompts.reshape(rows, width), queries, w_uv, w_turned, sections, experts, groups
+    )
     w_parts = spread(w_piece, "section")
-    uv_share, *cut = cut_columns(
-        prompts.reshape(rows, width), queries, w_uv, sections, experts, groups
-    )
     uv_share = swap(uv_share, "expert", far)
     cut = deliver(cut, "expert")
 
@@ -806,8 +847,8 @@
     )
     blocks = lax.all_to_all(blocks, ("expert", "section"), 0, 0, tiled=True)
 
-    away = list(project(cut[1:], riders, w_parts, 1, rows, [token]))
-    near = list(project(cut[:1], riders, w_parts, 0, rows, away[:1]))
+    away = list(project(cut[1:], riders, w_parts, 1, rows, piece, [token]))
+    near = list(project(cut[:1], riders, w_parts, 0, rows, piece, away[:1]))
     parts = deliver(near + away, "expert")
     table = rotation(full_length + steps + -(full_length + steps) % 8, cache_width - latent)
     gathered = list(gather_queries(

time: 103 us -> 103 us (level)
  Pallas kernels: 30.9 us -> 32.9 us
  local copies, waits for them, and re-layouts: 3.36 us -> 1.56 us
    pallas_call x2, Pallas kernels: 1.95 us -> 4.01 us  [project(): pl.pallas_call(functools.partial(project_kernel, len(blocks), first, rows...]
    dynamic_slice x1 -> x0, local copies, waits for them, and re-layouts: 1.16 us -> none  [local(): w_piece = lax.dynamic_slice_in_dim(w_turned, expert_rank * piece, piece, 1)]
  transfers between devices with their start and end apart: 27 -> 27, of which waited for: 10 -> 8; matrix products, arithmetic and copies ran while one was open for 1% -> 0% of each run, Pallas kernels for 17% -> 18%
where the time goes in v15:
time: 103 us
  starting transfers between devices  35.5 us (34%)
  Pallas kernels  32.9 us (32%)
  waiting for transfers between devices  19.9 us (19%)
  blocking collectives  12.7 us (12%)
  local copies, waits for them, and re-layouts  1.56 us (2%)
    ppermute x26, starting transfers between devices, swap(): return lax.ppermute(block, axis, [(i, i ^ mask) for i in range(size)])  29.6 us
    ppermute x26, waiting for transfers between devices, swap(): return lax.ppermute(block, axis, [(i, i ^ mask) for i in range(size)])  19.9 us
    all_to_all x1, blocking collectives, local(): blocks = lax.all_to_all(blocks, ('expert', 'section'), 0, 0, tiled=True)  12.7 us
    pallas_call x4, Pallas kernels, fetch(): pl.pallas_call(functools.partial(fetch_kernel, len(arrays)), out_shape=[p...  11.4 us
    all_to_all x1, starting transfers between devices, local(): blocks = lax.all_to_all(blocks, ('expert', 'section'), 0, 0, tiled=True)  5.91 us
    pallas_call x1, Pallas kernels, run_experts(): pl.pallas_call(functools.partial(expert_kernel, experts, sections, picks)...  4.98 us
    pallas_call x2, Pallas kernels, project(): pl.pallas_call(functools.partial(project_kernel, len(blocks), first, rows...  4.01 us
    pallas_call x1, Pallas kernels, cut_columns(): pl.pallas_call(functools.partial(cut_kernel, sections, experts, piece), o...  2.68 us
  transfers between devices with their start and end apart: 27, of which 8 were waited for; matrix products, arithmetic and copies ran while one was open for 0% of the time, Pallas kernels for 18%

profile of v15, /device:TPU:0, one launch (start us, length us, event | category | flops | bytes accessed | tf_op | source)
XLA Modules:
  0.0 102.7 jit_solution(6220142674531867814)
XLA Ops:
  0.0 2.7 %cut_columns.1 = (bf16[8,128,128]{2,1,0:T(8,128)(2,1)S(1)}, bf16[1008,128]{1,0:T(8,128)(2,1)S(1)}, bf16[640,224]{1,0:T(8,128)(2,1)S(1)}, bf16[640,224]{1,0:T(8,1...) custom-call(bf16[128,3584]{1,0:T(8,128)(2,1)} %bitcast.4, bf16[2,4,16,192]{3,2,1,0:T(8,128)(2,1)} %query_ref.1, ...), custom_call_target="tpu_custom_call" | custom-call | tf_op jit(solution)/shard_map/cut_columns/pallas_call | solution.py:147
  3.2 2.6 %collective-permute-start.3 = (bf16[8,128,128]{2,1,0:T(8,128)(2,1)S(1)}, bf16[8,128,128]{2,1,0:T(8,128)(2,1)S(1)}, u32[]{:S(2)}, u32[]{:S(2)}) collective-permute-start(bf16[8,128,128]{2,1,0:T(8,128)(2,1)S(1)} %get-tuple-element.32), channel_id=1, source_target_pairs={{0,8},{4,12},{8,0},{12,4},{1,9},{5,13},{9,1},{13,5},{2,10},{6,14},... | collective-permute-start | bytes 786440 | tf_op jit(solution)/shard_map/ppermute | solution.py:28
  7.3 3.6 %collective-permute-start.6 = (bf16[1008,128]{1,0:T(8,128)(2,1)S(1)}, bf16[1008,128]{1,0:T(8,128)(2,1)S(1)}, u32[]{:S(2)}, u32[]{:S(2)}) collective-permute-start(bf16[1008,128]{1,0:T(8,128)(2,1)S(1)} %get-tuple-element.34.refs_4_.refs_2_), channel_id=1, source_target_pairs={{0,3},{1,2},{2,1},{3,0},{4,7},{5,6},{6,5},{7,4},{8,11},{9,10},{10,... | collective-permute-start | bytes 774152 | tf_op jit(solution)/shard_map/ppermute | solution.py:28
  10.9 2.0 %collective-permute-done.3.refs_9_.refs_13_.refs_7_ = bf16[8,128,128]{2,1,0:T(8,128)(2,1)S(1)} collective-permute-done((bf16[8,128,128]{2,1,0:T(8,128)(2,1)S(1)}, bf16[8,128,128]{2,1,0:T(8,128)(2,1)S(1)}, u32[]{:S(2)}, u32[]{:S(2)}) %collective-permute-start.3) | collective-permute-done | bytes 262176 | tf_op jit(solution)/shard_map/ppermute | solution.py:28
  12.9 3.0 %collective-permute-start.5 = (bf16[1008,128]{1,0:T(8,128)(2,1)S(1)}, bf16[1008,128]{1,0:T(8,128)(2,1)S(1)}, u32[]{:S(2)}, u32[]{:S(2)}) collective-permute-start(bf16[1008,128]{1,0:T(8,128)(2,1)S(1)} %get-tuple-element.34.refs_4_.refs_2_), channel_id=1, source_target_pairs={{0,2},{1,3},{2,0},{3,1},{4,6},{5,7},{6,4},{7,5},{8,10},{9,11},{10,... | collective-permute-start | bytes 774152 | tf_op jit(solution)/shard_map/ppermute | solution.py:28
  17.6 2.4 %collective-permute-done.1.refs_3_.refs_1_ = bf16[640,224]{1,0:T(8,128)(2,1)S(1)} collective-permute-done((bf16[640,224]{1,0:T(8,128)(2,1)S(1)}, bf16[640,224]{1,0:T(8,128)(2,1)S(1)}, u32[]{:S(2)}, u32[]{:S(2)}) %collective-permute-start.1) | collective-permute-done | bytes 286752 | tf_op jit(solution)/shard_map/ppermute | solution.py:28
  20.0 6.5 %collective-permute-done.2.refs_4_.refs_2_ = bf16[640,224]{1,0:T(8,128)(2,1)S(1)} collective-permute-done((bf16[640,224]{1,0:T(8,128)(2,1)S(1)}, bf16[640,224]{1,0:T(8,128)(2,1)S(1)}, u32[]{:S(2)}, u32[]{:S(2)}) %collective-permute-start.2) | collective-permute-done | bytes 286752 | tf_op jit(solution)/shard_map/ppermute | solution.py:28
  28.1 2.2 %absorb_queries.1 = (bf16[16,48,128]{2,1,0:T(8,128)(2,1)S(1)}, bf16[4,16,576]{2,1,0:T(8,128)(2,1)S(1)}, bf16[8,128]{1,0:T(8,128)(2,1)S(1)}) custom-call(s32[16]{0:T(128)} %refs_0_.8, bf16[640,224]{1,0:T(8,128)(2,1)S(1)} %get-tuple-element.28.refs_1_.refs_0_, bf16[640,224]{1,0:T(8,128)(2,1)S(1)} %collective-permute-done.refs_2_.refs_0_, ...), custom_call_target="tpu_custom_call" | custom-call | tf_op jit(solution)/shard_map/absorb_queries/pallas_call | solution.py:329
  30.9 5.9 %all-to-all-start = ((bf16[16,48,128]{2,1,0:T(8,128)(2,1)}), bf16[16,48,128]{2,1,0:T(8,128)(2,1)S(1)}, u32[]{:S(2)}, u32[]{:S(2)}) async-start(bf16[16,48,128]{2,1,0:T(8,128)(2,1)} %copy-done.3), calls=%async_computation | async-start | bytes 393216 | tf_op jit(solution)/shard_map/all_to_all | solution.py:848
  36.9 2.5 %project.2 = (bf16[144,576]{1,0:T(8,128)(2,1)}, bf16[144,576]{1,0:T(8,128)(2,1)S(1)}, bf16[144,576]{1,0:T(8,128)(2,1)}) custom-call(bf16[640,224]{1,0:T(8,128)(2,1)S(1)} %collective-permute-done.refs_2_.refs_0_, bf16[640,224]{1,0:T(8,128)(2,1)S(1)} %collective-permute-done.1.refs_3_.refs_1_, bf16[640,224]{1,0:T(8,128)(2,1)S(1)} %collective-permute-done.2.refs_4_.refs_2_, ...), custom_call_target="tpu_custom_call" | custom-call | tf_op jit(solution)/shard_map/project/pallas_call | solution.py:184
  39.4 1.9 %collective-permute-start.8 = (bf16[144,576]{1,0:T(8,128)(2,1)S(1)}, bf16[144,576]{1,0:T(8,128)(2,1)S(1)}, u32[]{:S(2)}, u32[]{:S(2)}) collective-permute-start(bf16[144,576]{1,0:T(8,128)(2,1)S(1)} %get-tuple-element.37), channel_id=1, source_target_pairs={{0,8},{4,12},{8,0},{12,4},{1,9},{5,13},{9,1},{13,5},{2,10},{6,14},... | collective-permute-start | bytes 497672 | tf_op jit(solution)/shard_map/ppermute | solution.py:28
  41.8 5.7 %collective-permute-done.8.refs_2_.refs_6_ = bf16[144,576]{1,0:T(8,128)(2,1)S(1)} collective-permute-done((bf16[144,576]{1,0:T(8,128)(2,1)S(1)}, bf16[144,576]{1,0:T(8,128)(2,1)S(1)}, u32[]{:S(2)}, u32[]{:S(2)}) %collective-permute-start.8) | collective-permute-done | bytes 165920 | tf_op jit(solution)/shard_map/ppermute | solution.py:28
  51.3 1.9 %attend.1 = (bf16[32,512]{1,0:T(8,128)(2,1)S(1)}, bf16[32,512]{1,0:T(8,128)(2,1)S(1)}, bf16[32,512]{1,0:T(8,128)(2,1)S(1)}, bf16[32,512]{1,0:T(8,128)(2,1)S(1)}, bf16[8,128]{1,0:T(8,128)(2,1)S(1)}) custom-call(bf16[144,576]{1,0:T(8,128)(2,1)S(1)} %project.3.refs_0_.refs_4_, bf16[144,576]{1,0:T(8,128)(2,1)} %collective-permute-done.7.refs_1_.refs_5_, ...), custom_call_target="tpu_custom_call" | custom-call | tf_op jit(solution)/shard_map/attend/pallas_call | solution.py:539
  54.9 2.0 %collective-permute-start.15 = (bf16[32,512]{1,0:T(8,128)(2,1)S(1)}, bf16[32,512]{1,0:T(8,128)(2,1)S(1)}, u32[]{:S(2)}, u32[]{:S(2)}) collective-permute-start(bf16[32,512]{1,0:T(8,128)(2,1)S(1)} %get-tuple-element.46), channel_id=1, source_target_pairs={{0,2},{1,3},{2,0},{3,1},{4,6},{5,7},{6,4},{7,5},{8,10},{9,11},{10,... | collective-permute-start | bytes 98312 | tf_op jit(solution)/shard_map/ppermute | solution.py:28
  57.6 3.1 %fetch.4.refs_13_.refs_9_ = bf16[4,3584,256]{2,1,0:T(8,128)(2,1)S(1)} custom-call(bf16[4,3584,256]{2,1,0:T(8,128)(2,1)} %refs_0_.7, bf16[8,128]{1,0:T(8,128)(2,1)S(1)} %get-tuple-element.48.refs_1_), custom_call_target="tpu_custom_call" | custom-call | bytes 14680064 | tf_op jit(solution)/shard_map/fetch/pallas_call | solution.py:63
  60.8 1.8 %collective-permute-done.16.refs_4_ = bf16[32,512]{1,0:T(8,128)(2,1)S(1)} collective-permute-done((bf16[32,512]{1,0:T(8,128)(2,1)S(1)}, bf16[32,512]{1,0:T(8,128)(2,1)S(1)}, u32[]{:S(2)}, u32[]{:S(2)}) %collective-permute-start.16) | collective-permute-done | bytes 32800 | tf_op jit(solution)/shard_map/ppermute | solution.py:28
  62.6 2.0 %head_products.1.refs_0_.refs_4_ = bf16[8,2176]{1,0:T(8,128)(2,1)S(1)} custom-call(s32[16]{0:T(128)} %refs_0_.8, bf16[32,512]{1,0:T(8,128)(2,1)S(1)} %get-tuple-element.44.refs_1_, bf16[32,512]{1,0:T(8,128)(2,1)S(1)} %collective-permute-done.14.refs_2_, bf16[32,512]{1,0:T(8,128)(2,1)S(1)} %collective-permute-done.15.refs_3_, ...), custom_call_target="tpu_custom_call" | custom-call | tf_op jit(solution)/shard_map/head_products/pallas_call | solution.py:630
  66.5 2.0 %fetch.5.refs_4_ = bf16[2048,896]{1,0:T(8,128)(2,1)S(1)} custom-call(bf16[2048,896]{1,0:T(8,128)(2,1)} %refs_0_.9), custom_call_target="tpu_custom_call" | custom-call | bytes 7340032 | tf_op jit(solution)/shard_map/fetch/pallas_call | solution.py:63
  69.5 2.2 %collective-permute-start.22 = (bf16[32,896]{1,0:T(8,128)(2,1)S(1)}, bf16[32,896]{1,0:T(8,128)(2,1)S(1)}, u32[]{:S(2)}, u32[]{:S(2)}) collective-permute-start(bf16[32,896]{1,0:T(8,128)(2,1)S(1)} %output_product.1.refs_1_.refs_0_), channel_id=1, source_target_pairs={{0,3},{1,2},{2,1},{3,0},{4,7},{5,6},{6,5},{7,4},{8,11},{9,10},{10,... | collective-permute-start | bytes 172040 | tf_op jit(solution)/shard_map/ppermute | solution.py:28
  71.7 2.3 %collective-permute-start.20 = (bf16[32,896]{1,0:T(8,128)(2,1)S(1)}, bf16[32,896]{1,0:T(8,128)(2,1)S(1)}, u32[]{:S(2)}, u32[]{:S(2)}) collective-permute-start(bf16[32,896]{1,0:T(8,128)(2,1)S(1)} %output_product.1.refs_1_.refs_0_), channel_id=1, source_target_pairs={{0,1},{1,0},{2,3},{3,2},{4,5},{5,4},{6,7},{7,6},{8,9},{9,8},{10,11... | collective-permute-start | bytes 172040 | tf_op jit(solution)/shard_map/ppermute | solution.py:28
  74.0 3.1 %fetch.6.refs_8_.refs_10_ = bf16[4,3584,256]{2,1,0:T(8,128)(2,1)S(1)} custom-call(bf16[4,3584,256]{2,1,0:T(8,128)(2,1)} %refs_0_.10, bf16[32,896]{1,0:T(8,128)(2,1)S(1)} %output_product.1.refs_1_.refs_0_), custom_call_target="tpu_custom_call" | custom-call | bytes 14680064 | tf_op jit(solution)/shard_map/fetch/pallas_call | solution.py:63
  80.9 3.1 %fetch.7.refs_11_ = bf16[4,256,3584]{2,1,0:T(8,128)(2,1)S(1)} custom-call(bf16[4,256,3584]{2,1,0:T(8,128)(2,1)} %refs_0_.11, bf16[4,8,896]{2,1,0:T(8,128)(2,1)S(1)} %mix.1.refs_1_.refs_0_), custom_call_target="tpu_custom_call" | custom-call | bytes 14680064 | tf_op jit(solution)/shard_map/fetch/pallas_call | solution.py:63
  84.5 5.0 %run_experts.1 = (bf16[16,8,896]{2,1,0:T(8,128)(2,1)S(1)}, bf16[4,8,896]{2,1,0:T(8,128)(2,1)S(1)}) custom-call(bf16[4,8,896]{2,1,0:T(8,128)(2,1)S(1)} %mix.1.refs_1_.refs_0_, bf16[4,8,896]{2,1,0:T(8,128)(2,1)S(1)} %collective-permute-done.23.refs_1_, bf16[4,8,896]{2,1,0:T(8,128)(2,1)S(1)} %collective-permute-done.24.refs_2_, ...), custom_call_target="tpu_custom_call" | custom-call | tf_op jit(solution)/shard_map/run_experts/pallas_call | solution.py:763
  89.4 12.7 %all_to_all.10.block_ref = bf16[16,8,896]{2,1,0:T(8,128)(2,1)S(1)} all-to-all(bf16[16,8,896]{2,1,0:T(8,128)(2,1)S(1)} %get-tuple-element.49), channel_id=1, replica_groups=mesh['groups'=2,'expert'=4,'section'=4] {'expert','section'}, dimensions={0} | all-to-all | bytes 458752 | tf_op jit(solution)/shard_map/all_to_all | solution.py:893
  (54 shorter events, 20.3 us)
Async XLA Ops:
  2.7 13.3 %collective-permute-start = (bf16[640,224]{1,0:T(8,128)(2,1)S(1)}, bf16[640,224]{1,0:T(8,128)(2,1)S(1)}, u32[]{:S(2)}, u32[]{:S(2)}) collective-permute-start(bf16[640,224]{1,0:T(8,128)(2,1)S(1)} %get-tuple-element.29), channel_id=1, source_target_pairs={{0,4},{4,0},{8,12},{12,8},{1,5},{5,1},{9,13},{13,9},{2,6},{6,2},{1... | collective-permute-start | bytes 860168 | tf_op jit(solution)/shard_map/ppermute | solution.py:28
  3.2 9.7 %collective-permute-start.3 = (bf16[8,128,128]{2,1,0:T(8,128)(2,1)S(1)}, bf16[8,128,128]{2,1,0:T(8,128)(2,1)S(1)}, u32[]{:S(2)}, u32[]{:S(2)}) collective-permute-start(bf16[8,128,128]{2,1,0:T(8,128)(2,1)S(1)} %get-tuple-element.32), channel_id=1, source_target_pairs={{0,8},{4,12},{8,0},{12,4},{1,9},{5,13},{9,1},{13,5},{2,10},{6,14},... | collective-permute-start | bytes 786440 | tf_op jit(solution)/shard_map/ppermute | solution.py:28
  5.8 14.2 %collective-permute-start.1 = (bf16[640,224]{1,0:T(8,128)(2,1)S(1)}, bf16[640,224]{1,0:T(8,128)(2,1)S(1)}, u32[]{:S(2)}, u32[]{:S(2)}) collective-permute-start(bf16[640,224]{1,0:T(8,128)(2,1)S(1)} %get-tuple-element.30), channel_id=1, source_target_pairs={{0,8},{4,12},{8,0},{12,4},{1,9},{5,13},{9,1},{13,5},{2,10},{6,14},... | collective-permute-start | bytes 860168 | tf_op jit(solution)/shard_map/ppermute | solution.py:28
  5.9 20.6 %collective-permute-start.2 = (bf16[640,224]{1,0:T(8,128)(2,1)S(1)}, bf16[640,224]{1,0:T(8,128)(2,1)S(1)}, u32[]{:S(2)}, u32[]{:S(2)}) collective-permute-start(bf16[640,224]{1,0:T(8,128)(2,1)S(1)} %get-tuple-element.31), channel_id=1, source_target_pairs={{0,12},{4,8},{8,4},{12,0},{1,13},{5,9},{9,5},{13,1},{2,14},{6,10},... | collective-permute-start | bytes 860168 | tf_op jit(solution)/shard_map/ppermute | solution.py:28
  7.3 29.6 %collective-permute-start.6 = (bf16[1008,128]{1,0:T(8,128)(2,1)S(1)}, bf16[1008,128]{1,0:T(8,128)(2,1)S(1)}, u32[]{:S(2)}, u32[]{:S(2)}) collective-permute-start(bf16[1008,128]{1,0:T(8,128)(2,1)S(1)} %get-tuple-element.34.refs_4_.refs_2_), channel_id=1, source_target_pairs={{0,3},{1,2},{2,1},{3,0},{4,7},{5,6},{6,5},{7,4},{8,11},{9,10},{10,... | collective-permute-start | bytes 774152 | tf_op jit(solution)/shard_map/ppermute | solution.py:28
  12.9 23.9 %collective-permute-start.5 = (bf16[1008,128]{1,0:T(8,128)(2,1)S(1)}, bf16[1008,128]{1,0:T(8,128)(2,1)S(1)}, u32[]{:S(2)}, u32[]{:S(2)}) collective-permute-start(bf16[1008,128]{1,0:T(8,128)(2,1)S(1)} %get-tuple-element.34.refs_4_.refs_2_), channel_id=1, source_target_pairs={{0,2},{1,3},{2,0},{3,1},{4,6},{5,7},{6,4},{7,5},{8,10},{9,11},{10,... | collective-permute-start | bytes 774152 | tf_op jit(solution)/shard_map/ppermute | solution.py:28
  16.0 20.9 %collective-permute-start.4 = (bf16[1008,128]{1,0:T(8,128)(2,1)S(1)}, bf16[1008,128]{1,0:T(8,128)(2,1)}, u32[]{:S(2)}, u32[]{:S(2)}) collective-permute-start(bf16[1008,128]{1,0:T(8,128)(2,1)S(1)} %get-tuple-element.34.refs_4_.refs_2_), channel_id=1, source_target_pairs={{0,1},{1,0},{2,3},{3,2},{4,5},{5,4},{6,7},{7,6},{8,9},{9,8},{10,11... | collective-permute-start | bytes 774152 | tf_op jit(solution)/shard_map/ppermute | solution.py:28
  20.0 31.3 %collective-permute-start.10 = (bf16[16,128,128]{2,1,0:T(8,128)(2,1)}, bf16[16,128,128]{2,1,0:T(8,128)(2,1)S(1)}, u32[]{:S(2)}, u32[]{:S(2)}) collective-permute-start(bf16[16,128,128]{2,1,0:T(8,128)(2,1)} %refs_5_.5), channel_id=1, source_target_pairs={{0,4},{4,0},{8,12},{12,8},{1,5},{5,1},{9,13},{13,9},{2,6},{6,2},{1... | collective-permute-start | bytes 1572872 | tf_op jit(solution)/shard_map/ppermute | solution.py:28
  26.5 14.9 %collective-permute-start.11 = (bf16[8,128,128]{2,1,0:T(8,128)(2,1)S(1)}, bf16[8,128,128]{2,1,0:T(8,128)(2,1)S(1)}, u32[]{:S(2)}, u32[]{:S(2)}) collective-permute-start(bf16[8,128,128]{2,1,0:T(8,128)(2,1)S(1)} %collective-permute-done.3.refs_9_.refs_13_.refs_7_), channel_id=1, source_target_pairs={{0,16},{16,0},{1,17},{17,1},{2,18},{18,2},{3,19},{19,3},{4,20},{20... | collective-permute-start | bytes 786440 | tf_op jit(solution)/shard_map/ppermute | solution.py:28
  30.9 19.0 %all-to-all-start = ((bf16[16,48,128]{2,1,0:T(8,128)(2,1)}), bf16[16,48,128]{2,1,0:T(8,128)(2,1)S(1)}, u32[]{:S(2)}, u32[]{:S(2)}) async-start(bf16[16,48,128]{2,1,0:T(8,128)(2,1)} %copy-done.3), calls=%async_computation | async-start | bytes 393216 | tf_op jit(solution)/shard_map/all_to_all | solution.py:848
  39.4 8.1 %collective-permute-start.8 = (bf16[144,576]{1,0:T(8,128)(2,1)S(1)}, bf16[144,576]{1,0:T(8,128)(2,1)S(1)}, u32[]{:S(2)}, u32[]{:S(2)}) collective-permute-start(bf16[144,576]{1,0:T(8,128)(2,1)S(1)} %get-tuple-element.37), channel_id=1, source_target_pairs={{0,8},{4,12},{8,0},{12,4},{1,9},{5,13},{9,1},{13,5},{2,10},{6,14},... | collective-permute-start | bytes 497672 | tf_op jit(solution)/shard_map/ppermute | solution.py:28
  41.3 10.0 %collective-permute-start.12 = (bf16[8,128,128]{2,1,0:T(8,128)(2,1)S(1)}, bf16[8,128,128]{2,1,0:T(8,128)(2,1)S(1)}, u32[]{:S(2)}, u32[]{:S(2)}) collective-permute-start(bf16[8,128,128]{2,1,0:T(8,128)(2,1)S(1)} %collective-permute-done.3.refs_9_.refs_13_.refs_7_), channel_id=1, source_target_pairs={{0,4},{4,0},{8,12},{12,8},{1,5},{5,1},{9,13},{13,9},{2,6},{6,2},{1... | collective-permute-start | bytes 786440 | tf_op jit(solution)/shard_map/ppermute | solution.py:28
  41.3 10.0 %collective-permute-start.13 = (bf16[8,128,128]{2,1,0:T(8,128)(2,1)S(1)}, bf16[8,128,128]{2,1,0:T(8,128)(2,1)S(1)}, u32[]{:S(2)}, u32[]{:S(2)}) collective-permute-start(bf16[8,128,128]{2,1,0:T(8,128)(2,1)S(1)} %collective-permute-done.11.refs_14_.refs_8_), channel_id=1, source_target_pairs={{0,4},{4,0},{8,12},{12,8},{1,5},{5,1},{9,13},{13,9},{2,6},{6,2},{1... | collective-permute-start | bytes 786440 | tf_op jit(solution)/shard_map/ppermute | solution.py:28
  41.8 9.4 %collective-permute-start.9 = (bf16[144,576]{1,0:T(8,128)(2,1)}, bf16[144,576]{1,0:T(8,128)(2,1)S(1)}, u32[]{:S(2)}, u32[]{:S(2)}) collective-permute-start(bf16[144,576]{1,0:T(8,128)(2,1)} %get-tuple-element.38), channel_id=1, source_target_pairs={{0,12},{4,8},{8,4},{12,0},{1,13},{5,9},{9,5},{13,1},{2,14},{6,10},... | collective-permute-start | bytes 497672 | tf_op jit(solution)/shard_map/ppermute | solution.py:28
  53.2 7.6 %collective-permute-start.14 = (bf16[32,512]{1,0:T(8,128)(2,1)S(1)}, bf16[32,512]{1,0:T(8,128)(2,1)S(1)}, u32[]{:S(2)}, u32[]{:S(2)}) collective-permute-start(bf16[32,512]{1,0:T(8,128)(2,1)S(1)} %get-tuple-element.45), channel_id=1, source_target_pairs={{0,1},{1,0},{2,3},{3,2},{4,5},{5,4},{6,7},{7,6},{8,9},{9,8},{10,11... | collective-permute-start | bytes 98312 | tf_op jit(solution)/shard_map/ppermute | solution.py:28
  54.9 5.9 %collective-permute-start.15 = (bf16[32,512]{1,0:T(8,128)(2,1)S(1)}, bf16[32,512]{1,0:T(8,128)(2,1)S(1)}, u32[]{:S(2)}, u32[]{:S(2)}) collective-permute-start(bf16[32,512]{1,0:T(8,128)(2,1)S(1)} %get-tuple-element.46), channel_id=1, source_target_pairs={{0,2},{1,3},{2,0},{3,1},{4,6},{5,7},{6,4},{7,5},{8,10},{9,11},{10,... | collective-permute-start | bytes 98312 | tf_op jit(solution)/shard_map/ppermute | solution.py:28
  56.9 5.7 %collective-permute-start.16 = (bf16[32,512]{1,0:T(8,128)(2,1)S(1)}, bf16[32,512]{1,0:T(8,128)(2,1)S(1)}, u32[]{:S(2)}, u32[]{:S(2)}) collective-permute-start(bf16[32,512]{1,0:T(8,128)(2,1)S(1)} %get-tuple-element.47), channel_id=1, source_target_pairs={{0,3},{1,2},{2,1},{3,0},{4,7},{5,6},{6,5},{7,4},{8,11},{9,10},{10,... | collective-permute-start | bytes 98312 | tf_op jit(solution)/shard_map/ppermute | solution.py:28
  64.6 3.9 %collective-permute-start.19 = (bf16[8,2176]{1,0:T(8,128)(2,1)S(1)}, bf16[8,2176]{1,0:T(8,128)(2,1)S(1)}, u32[]{:S(2)}, u32[]{:S(2)}) collective-permute-start(bf16[8,2176]{1,0:T(8,128)(2,1)S(1)} %head_products.1.refs_0_.refs_4_), channel_id=1, source_target_pairs={{0,12},{4,8},{8,4},{12,0},{1,13},{5,9},{9,5},{13,1},{2,14},{6,10},... | collective-permute-start | bytes 104456 | tf_op jit(solution)/shard_map/ppermute | solution.py:28
  64.6 4.1 %collective-permute-start.18 = (bf16[8,2176]{1,0:T(8,128)(2,1)S(1)}, bf16[8,2176]{1,0:T(8,128)(2,1)S(1)}, u32[]{:S(2)}, u32[]{:S(2)}) collective-permute-start(bf16[8,2176]{1,0:T(8,128)(2,1)S(1)} %head_products.1.refs_0_.refs_4_), channel_id=1, source_target_pairs={{0,8},{4,12},{8,0},{12,4},{1,9},{5,13},{9,1},{13,5},{2,10},{6,14},... | collective-permute-start | bytes 104456 | tf_op jit(solution)/shard_map/ppermute | solution.py:28
  69.5 7.6 %collective-permute-start.22 = (bf16[32,896]{1,0:T(8,128)(2,1)S(1)}, bf16[32,896]{1,0:T(8,128)(2,1)S(1)}, u32[]{:S(2)}, u32[]{:S(2)}) collective-permute-start(bf16[32,896]{1,0:T(8,128)(2,1)S(1)} %output_product.1.refs_1_.refs_0_), channel_id=1, source_target_pairs={{0,3},{1,2},{2,1},{3,0},{4,7},{5,6},{6,5},{7,4},{8,11},{9,10},{10,... | collective-permute-start | bytes 172040 | tf_op jit(solution)/shard_map/ppermute | solution.py:28
  71.7 6.2 %collective-permute-start.21 = (bf16[32,896]{1,0:T(8,128)(2,1)S(1)}, bf16[32,896]{1,0:T(8,128)(2,1)S(1)}, u32[]{:S(2)}, u32[]{:S(2)}) collective-permute-start(bf16[32,896]{1,0:T(8,128)(2,1)S(1)} %output_product.1.refs_1_.refs_0_), channel_id=1, source_target_pairs={{0,2},{1,3},{2,0},{3,1},{4,6},{5,7},{6,4},{7,5},{8,10},{9,11},{10,... | collective-permute-start | bytes 172040 | tf_op jit(solution)/shard_map/ppermute | solution.py:28
  71.7 6.2 %collective-permute-start.20 = (bf16[32,896]{1,0:T(8,128)(2,1)S(1)}, bf16[32,896]{1,0:T(8,128)(2,1)S(1)}, u32[]{:S(2)}, u32[]{:S(2)}) collective-permute-start(bf16[32,896]{1,0:T(8,128)(2,1)S(1)} %output_product.1.refs_1_.refs_0_), channel_id=1, source_target_pairs={{0,1},{1,0},{2,3},{3,2},{4,5},{5,4},{6,7},{7,6},{8,9},{9,8},{10,11... | collective-permute-start | bytes 172040 | tf_op jit(solution)/shard_map/ppermute | solution.py:28
  78.9 5.0 %collective-permute-start.25 = (bf16[4,8,896]{2,1,0:T(8,128)(2,1)S(1)}, bf16[4,8,896]{2,1,0:T(8,128)(2,1)S(1)}, u32[]{:S(2)}, u32[]{:S(2)}) collective-permute-start(bf16[4,8,896]{2,1,0:T(8,128)(2,1)S(1)} %mix.1.refs_1_.refs_0_), channel_id=1, source_target_pairs={{0,12},{4,8},{8,4},{12,0},{1,13},{5,9},{9,5},{13,1},{2,14},{6,10},... | collective-permute-start | bytes 172040 | tf_op jit(solution)/shard_map/ppermute | solution.py:28
  79.8 4.7 %collective-permute-start.24 = (bf16[4,8,896]{2,1,0:T(8,128)(2,1)S(1)}, bf16[4,8,896]{2,1,0:T(8,128)(2,1)S(1)}, u32[]{:S(2)}, u32[]{:S(2)}) collective-permute-start(bf16[4,8,896]{2,1,0:T(8,128)(2,1)S(1)} %mix.1.refs_1_.refs_0_), channel_id=1, source_target_pairs={{0,8},{4,12},{8,0},{12,4},{1,9},{5,13},{9,1},{13,5},{2,10},{6,14},... | collective-permute-start | bytes 172040 | tf_op jit(solution)/shard_map/ppermute | solution.py:28
  (7 other events, 33.3 us)
